TPU v7x, 256 devices: a whole 4x4x8 slice. The times are simulated.
256 devices in a mesh: dp: 32 (over x, z_hi, core), seq: 8 (over z_lo, y).
Axes of the slice: x: 4, y: 4, z: 8 (z_hi: 4, z_lo: 2; z = z_hi * 2 + z_lo), core: 2. Of those that a mesh axis runs over, the one named last changes fastest.
Arguments:
- normed: bfloat16 [32, 2048, 1536], P('dp', 'seq'), may hold values from -6 to 6
- w_query: bfloat16 [1536, 512], replicated, may hold values from -1.5 to 1.5
- w_key: bfloat16 [1536, 128], replicated, may hold values from -1.5 to 1.5
- w_value: bfloat16 [1536, 128], replicated, may hold values from -0.15625 to 0.15625
- w_out: bfloat16 [1536, 512], replicated, may hold values from -0.25 to 0.25
- cotangent: bfloat16 [32, 2048, 1536], P('dp', 'seq'), may hold values from -6 to 6
Outputs:
- branch: bfloat16 [32, 2048, 1536], P('dp', 'seq')
- grad_query: float32 [1536, 512], P(('dp', 'seq'))
- grad_key: float32 [1536, 128], P(('dp', 'seq'))
- grad_value: float32 [1536, 128], P(('dp', 'seq'))
- grad_out: float32 [1536, 512], P(('dp', 'seq'))
All inputs are finite; a program needn't handle non-finite values.
Results may differ from a plain program's by a relative error of at most 0.006.
The roundings to bfloat16 on the way count: a program that leaves them out, or rounds other values in their place, can miss the bound.
Values may be sent and summed in bfloat16 or wider, within the bound.
No kernel may reach another device: no remote copies, remote signals or barrier semaphores. Data moves between devices by JAX's collectives and lax.ppermute only.
A program may use at most 64 MiB of HBM per device.

v0:
```python
import jax
import jax.numpy as jnp
from jax import lax
from jax.sharding import PartitionSpec as P

HEADS = 4
HD = 128


def contract_rows(left, right):
    return lax.dot_general(
        left, right, (((0,), (0,)), ((), ())), preferred_element_type=jnp.float32
    )


def contract_rows_exact(left, right):
    return lax.dot_general(
        left.astype(jnp.float32),
        right,
        (((0,), (0,)), ((), ())),
        precision=lax.Precision.HIGHEST,
        preferred_element_type=jnp.float32,
    )


def local(normed, w_query, w_key, w_value, w_out, cotangent):
    hidden = normed[0]
    grads_in = cotangent[0]
    tokens = hidden.shape[0]
    scale = HD ** (-0.5)
    queries = jnp.dot(hidden, w_query, preferred_element_type=jnp.float32).astype(jnp.bfloat16)
    own_keys = jnp.dot(hidden, w_key, preferred_element_type=jnp.float32).astype(jnp.bfloat16)
    own_values = jnp.dot(hidden, w_value, preferred_element_type=jnp.float32).astype(jnp.bfloat16)
    keys, values = (
        lax.all_gather(own_keys, "seq", axis=0, tiled=True),
        lax.all_gather(own_values, "seq", axis=0, tiled=True),
    )
    length = keys.shape[0]
    d_att = jnp.dot(grads_in, w_out, preferred_element_type=jnp.float32).astype(jnp.bfloat16)
    rows = tokens * HEADS
    block = min(512, rows)
    count = rows // block
    query_blocks = queries.reshape(count, block, HD)
    grad_blocks = d_att.reshape(count, block, HD)

    def step(carry, item):
        key_total, value_total = carry
        query_rows, grad_rows = item
        scores = jnp.dot(query_rows, keys.T, preferred_element_type=jnp.float32) * scale
        shifted = jnp.exp(scores - jnp.max(scores, axis=1, keepdims=True))
        probs = shifted / jnp.sum(shifted, axis=1, keepdims=True)
        probs_b = probs.astype(jnp.bfloat16)
        attended = jnp.dot(probs_b, values, preferred_element_type=jnp.float32).astype(jnp.bfloat16)
        d_probs = jnp.dot(grad_rows, values.T, preferred_element_type=jnp.float32)
        delta = jnp.sum(d_probs * probs, axis=1, keepdims=True)
        d_scores = (probs * (d_probs - delta)).astype(jnp.bfloat16)
        d_query = (jnp.dot(d_scores, keys, preferred_element_type=jnp.float32) * scale).astype(
            jnp.bfloat16
        )
        key_total = key_total + contract_rows(d_scores, query_rows) * scale
        value_total = value_total + contract_rows(probs_b, grad_rows)
        return ((key_total, value_total), (attended, d_query))

    start = (jnp.zeros((length, HD), jnp.float32), jnp.zeros((length, HD), jnp.float32))
    (key_terms, value_terms), (attended, d_query) = lax.scan(
        step, start, (query_blocks, grad_blocks)
    )
    attended = attended.reshape(tokens, HEADS * HD)
    d_query = d_query.reshape(tokens, HEADS * HD)
    branch = lax.dot_general(
        attended, w_out, (((1,), (1,)), ((), ())), preferred_element_type=jnp.float32
    ).astype(jnp.bfloat16)
    grad_query = contract_rows(hidden, d_query)
    grad_out = contract_rows(grads_in, attended)
    own_key_terms, own_value_terms = (
        lax.psum_scatter(key_terms, "seq", scatter_dimension=0, tiled=True),
        lax.psum_scatter(value_terms, "seq", scatter_dimension=0, tiled=True),
    )
    grad_key = contract_rows_exact(hidden, own_key_terms)
    grad_value = contract_rows_exact(hidden, own_value_terms)
    summed = (
        lax.psum_scatter(grad_query, ("dp", "seq"), scatter_dimension=0, tiled=True),
        lax.psum_scatter(grad_key, ("dp", "seq"), scatter_dimension=0, tiled=True),
        lax.psum_scatter(grad_value, ("dp", "seq"), scatter_dimension=0, tiled=True),
        lax.psum_scatter(grad_out, ("dp", "seq"), scatter_dimension=0, tiled=True),
    )
    return (branch[None], summed[0], summed[1], summed[2], summed[3])


def solution(mesh):
    return jax.shard_map(
        local,
        mesh=mesh,
        in_specs=(P("dp", "seq", None), P(), P(), P(), P(), P("dp", "seq", None)),
        out_specs=(
            P("dp", "seq", None),
            P(("dp", "seq"), None),
            P(("dp", "seq"), None),
            P(("dp", "seq"), None),
            P(("dp", "seq"), None),
        ),
        check_vma=False,
    )
```

profile of v0, /device:TPU:32, one launch (start us, length us, event | category | flops | bytes accessed | tf_op | source)
XLA Modules:
  0.0 493.3 jit_solution(17905329457975755462)
XLA Ops:
  7.3 1.7 convolution_convert_fusion.5
  9.0 31.1 %all_gather.6 = bf16[2048,128]{1,0:T(8,128)(2,1)} all-gather(bf16[256,128]{1,0:T(8,128)(2,1)S(1)} %convolution_convert_fusion.5), channel_id=1, replica_groups=mesh['dp'=32,'seq'=8] {'seq'}, dimensions={0}, use_global_device_ids=true | all-gather | bytes 589824 | tf_op jit(solution)/shard_map/all_gather | solution.py:35
  40.1 1.6 convolution_convert_fusion.4
  41.7 31.1 %all_gather.7 = bf16[2048,128]{1,0:T(8,128)(2,1)} all-gather(bf16[256,128]{1,0:T(8,128)(2,1)S(1)} %convolution_convert_fusion.4), channel_id=1, replica_groups=mesh['dp'=32,'seq'=8] {'seq'}, dimensions={0}, use_global_device_ids=true | all-gather | bytes 589824 | tf_op jit(solution)/shard_map/all_gather | solution.py:36
  72.8 1.3 convolution_convert_fusion.3
  74.1 1.9 reshape.25
  75.9 2.4 convolution_convert_fusion.2
  78.4 1.8 reshape.26
  80.2 32.7 %while.17 = (s32[]{:T(128)}, f32[2048,128]{1,0:T(8,128)S(1)}, f32[2048,128]{1,0:T(8,128)}, bf16[2,512,128]{2,1,0:T(8,128)(2,1)}, bf16[2,512,128]{2,1,0:T(8,128)(...) while((s32[]{:T(128)}, f32[2048,128]{1,0:T(8,128)S(1)}, ...), condition=%wide.region_4.5_spmd.clone, body=%wide.region_0.4_spmd.clone.sunk | while | flops 1627847168 | bytes 101466472 | solution.py:65
  80.2 1.9 multiply_reduce_fusion.4
  82.1 0.8 fusion.74
  82.9 0.2 copy-done.7
  83.1 0.1 copy-done.9
  83.2 1.5 multiply_reduce_fusion.5
  84.7 1.9 copy-done.1
  86.7 1.8 multiply_convert_fusion.2
  88.4 2.9 fusion.75
  91.4 1.4 fusion.77
  92.7 1.8 convolution_add_fusion.2
  94.5 1.4 fusion.76
  95.9 1.9 multiply_reduce_fusion.4
  97.8 0.8 fusion.74
  98.6 0.2 copy-done.7
  98.8 0.1 copy-done.9
  98.9 1.5 multiply_reduce_fusion.5
  100.4 1.9 copy-done.1
  102.4 1.8 multiply_convert_fusion.2
  104.1 2.9 fusion.75
  107.1 1.4 fusion.77
  108.4 3.0 convolution_add_fusion.2
  111.5 1.4 fusion.76
  112.9 0.9 copy-done.4
  113.9 1.1 reshape.27
  115.1 1.1 reshape.28
  116.2 3.4 convolution_bitcast_fusion
  119.6 2.2 convolution_bitcast_fusion.1
  121.8 34.4 %reduce-scatter.9.cloned.1.call-done = f32[256,128]{1,0:T(8,128)} async-done(((f32[2048,128]{1,0:T(8,128)}), f32[256,128]{1,0:T(8,128)}) %reduce-scatter.9.cloned.1.call-update) | async-done | bytes 131088 | tf_op jit(solution)/shard_map/reduce_scatter | solution.py:77
  156.2 2.4 convolution_bitcast_fusion.2
  158.6 40.6 %reduce-scatter.7.cloned.1.call-done = f32[256,128]{1,0:T(8,128)} async-done(((f32[2048,128]{1,0:T(8,128)}), f32[256,128]{1,0:T(8,128)}) %reduce-scatter.7.cloned.1.call-update) | async-done | bytes 131088 | tf_op jit(solution)/shard_map/reduce_scatter | solution.py:76
  199.1 2.3 convolution_bitcast_fusion.3
  201.5 1.5 fusion.24
  203.0 278.5 %all-reduce.7.cloned.1.call-done = (f32[1536,512]{0,1:T(8,128)}, f32[1536,128]{0,1:T(8,128)}, f32[1536,128]{0,1:T(8,128)}, f32[1536,512]{0,1:T(8,128)}) async-done(((f32[1536,512]{0,1:T(8,128)}, f32[1536,128]{0,1:T(8,128)}, f32[1536,128]{0,1:T(8,128)}, f32[1536,512]{0,1:T(8,128)}), (f32[1536,512]{0,1:T(8,128)}, f32[1536,128]{0,1:T(8,128)}, f32[1536,128]{0,1:T(8,128)}, ...) | async-done | bytes 7864336
  481.5 1.1 constant_dynamic-slice_fusion.1
  482.5 0.7 copy.16
  483.2 0.7 copy.17
  483.9 1.4 constant_dynamic-slice_fusion
  485.3 0.7 copy.15
  486.0 0.7 copy.18
  (43 shorter events, 0.2 us)
Async XLA Ops:
  7.2 68.8 %copy-start = (bf16[1536,512]{1,0:T(8,128)(2,1)S(1)}, bf16[1536,512]{1,0:T(8,128)(2,1)}, u32[]{:S(2)}) copy-start(bf16[1536,512]{1,0:T(8,128)(2,1)} %param.12) | copy-start | bytes 4718596
  7.2 65.6 %copy-start.5 = (bf16[1,256,1536]{2,1,0:T(8,128)(2,1)S(1)}, bf16[1,256,1536]{2,1,0:T(8,128)(2,1)}, u32[]{:S(2)}) copy-start(bf16[1,256,1536]{2,1,0:T(8,128)(2,1)} %param.8) | copy-start | bytes 2359300
  7.2 149.0 %reduce-scatter.9.cloned.1.call-start = ((), (), s32[]{:S(2)}) async-start(), calls=%async_computation.3 | async-start | bytes 1179648 | tf_op jit(solution)/shard_map/reduce_scatter | solution.py:77
  7.3 65.5 %copy-start.11 = (bf16[1536,512]{1,0:T(8,128)(2,1)S(1)}, bf16[1536,512]{1,0:T(8,128)(2,1)}, u32[]{:S(2)}) copy-start(bf16[1536,512]{1,0:T(8,128)(2,1)} %param.9) | copy-start | bytes 4718596
  82.1 1.0 copy-start.7
  82.1 1.1 copy-start.9
  84.7 1.9 copy-start.1
  88.4 2.9 copy-start.3
  88.4 2.9 copy-start.6
  88.4 4.3 copy-start.2
  88.4 4.3 copy-start.10
  92.7 1.8 copy-start.8
  97.8 1.0 copy-start.7
  97.8 1.1 copy-start.9
  100.4 1.9 copy-start.1
  104.1 2.9 copy-start.3
  104.1 2.9 copy-start.6
  104.1 4.3 copy-start.2
  104.1 4.3 copy-start.10
  108.4 3.1 copy-start.8
  112.8 1.0 copy-start.4
  112.9 86.3 %reduce-scatter.7.cloned.1.call-start = ((), (), s32[]{:S(2)}) async-start(), calls=%async_computation.2 | async-start | bytes 1179648 | tf_op jit(solution)/shard_map/reduce_scatter | solution.py:76
  113.9 367.6 %all-reduce.7.cloned.1.call-start = ((), (), s32[]{:S(2)}) async-start(), calls=%async_computation.4 | async-start | bytes 15728640
Sparse Core Ops, SparseCore 0:
  113.0 43.1 reduce-scatter.8
  158.7 40.3 reduce-scatter.6
  205.1 276.3 all-reduce.6
where the time goes:
time: 496 us; the launch traced here: 493 us
  waiting for transfers between devices  353 us (71%)
  blocking collectives  62.2 us (13%)
  matrix products  41.8 us (8%)
  local copies, waits for them, and re-layouts  16.6 us (3%)
  between operations  13.8 us (3%)
  other arithmetic  5.15 us (1%)
    unnamed x4, waiting for transfers between devices  279 us
    reduce_scatter x1, waiting for transfers between devices, local(): lax.psum_scatter(key_terms, 'seq', scatter_dimension=0, tiled=True)  40.6 us
    reduce_scatter x1, waiting for transfers between devices, local(): lax.psum_scatter(value_terms, 'seq', scatter_dimension=0, tiled=True)  34.4 us
    all_gather x1, blocking collectives, local(): lax.all_gather(own_values, 'seq', axis=0, tiled=True)  31.1 us
    all_gather x1, blocking collectives, local(): lax.all_gather(own_keys, 'seq', axis=0, tiled=True)  31.1 us
    dot_general x6, matrix products, contract_rows(): lax.dot_general(left, right, (((0,), (0,)), ((), ())), preferred_element_...  16.2 us
  transfers between devices with their start and end apart: 3, of which 3 were waited for; matrix products, arithmetic and copies ran while one was open for 2% of the time, Pallas kernels for 0%

commit v1 on v0

v1 whole, which is shorter than its diff:
```python
import jax
import jax.numpy as jnp
import numpy as np
from jax import lax
from jax.experimental import pallas as pl
from jax.experimental.pallas import tpu as pltpu
from jax.sharding import PartitionSpec as P

HEADS = 4
HD = 128
SCALE = HD ** (-0.5)
LOG2_E = 1.4426950408889634
AXES = ("dp", "seq")
MIB = 1024 * 1024


def place(x, y, z, core):
    return x * 64 + (z >> 1) * 16 + core * 8 + (z & 1) * 4 + y


YZ_GROUPS = [[place(x, y, z, c) for y in range(4) for z in range(8)] for x in range(4) for c in range(2)]
ROW_ORDER = np.concatenate(
    [
        np.arange(6) + 6 * place(x, y, z, c)
        for c in range(2)
        for x in range(4)
        for y in range(4)
        for z in range(8)
    ]
)


def dot(left, right, dims):
    return lax.dot_general(left, right, (dims, ((), ())), preferred_element_type=jnp.float32)


def exchange(value, mask):
    return lax.ppermute(value, AXES, [(i, i ^ mask) for i in range(256)])


def from_other_core(value):
    return exchange(value, 8)


def exponent(values):
    top = jnp.max(jnp.max(jnp.abs(values), axis=0, keepdims=True), axis=1, keepdims=True)
    return jnp.ceil(jnp.log2(jnp.maximum(top, 1e-30))) - 13.0


def unscaled(ref, block, values, exponents):
    return ref[block, values, :] * jnp.exp2(ref[block, exponents, :])


def attention_kernel(q_ref, da_ref, k_ref, v_ref, factor_ref, copy_ref, dkv_ref):
    step = pl.program_id(0)
    keys = k_ref[...]
    values = v_ref[...]
    bf = jnp.bfloat16
    heads = range(q_ref.shape[1] // HD)
    q = [q_ref[:, h * HD : (h + 1) * HD] for h in heads]
    da = [da_ref[:, h * HD : (h + 1) * HD] for h in heads]

    def softmax(scores):
        shifted = jnp.exp2((scores - jnp.max(scores, axis=1, keepdims=True)) * (SCALE * LOG2_E))
        return shifted * (1.0 / jnp.sum(shifted, axis=1, keepdims=True))

    def store(side, h, value):
        factor_ref[side, :, h * HD : (h + 1) * HD] = value
        copy_ref[side, :, h * HD : (h + 1) * HD] = value

    scores = [dot(q[h], keys, ((1,), (1,))) for h in heads]
    probs, probs_b, d_probs, d_scores = [], [], [], []
    for h in heads:
        probs.append(softmax(scores[h]))
        probs_b.append(probs[h].astype(bf))
        d_probs.append(dot(da[h], values, ((1,), (1,))))
    d_value = None
    for h in heads:
        store(1, h, dot(probs_b[h], values, ((1,), (0,))).astype(bf))
        term = dot(da[h], probs_b[h], ((0,), (0,)))
        d_value = term if d_value is None else d_value + term
        delta = jnp.sum(d_probs[h] * probs[h], axis=1, keepdims=True)
        d_scores.append((probs[h] * (d_probs[h] - delta)).astype(bf))
    d_key = None
    for h in heads:
        store(0, h, (dot(d_scores[h], keys, ((1,), (0,))) * SCALE).astype(bf))
        term = dot(q[h], d_scores[h], ((0,), (0,)))
        d_key = term if d_key is None else d_key + term
    blocks, _, tokens = dkv_ref.shape

    @pl.when(step == 0)
    def _():
        for b in range(blocks):
            dkv_ref[b, :HD, :] = d_key[:, b * tokens : (b + 1) * tokens]
            dkv_ref[b, HD : 2 * HD, :] = d_value[:, b * tokens : (b + 1) * tokens]

    @pl.when(step != 0)
    def _():
        for b in range(blocks):
            dkv_ref[b, :HD, :] += d_key[:, b * tokens : (b + 1) * tokens]
            dkv_ref[b, HD : 2 * HD, :] += d_value[:, b * tokens : (b + 1) * tokens]

    @pl.when(step == pl.num_programs(0) - 1)
    def _():
        for i, scale in enumerate((SCALE, 1.0)):
            rows = pl.ds(i * HD, HD)
            top = jnp.abs(dkv_ref[0, rows, :])
            for b in range(1, blocks):
                top = jnp.maximum(top, jnp.abs(dkv_ref[b, rows, :]))
            power = exponent(top * scale)
            factor = jnp.exp2(-power) * scale
            for b in range(blocks):
                dkv_ref[b, rows, :] = dkv_ref[b, rows, :] * factor
                dkv_ref[b, pl.ds(2 * HD + 8 * i, 8), :] = jnp.broadcast_to(power, (8, tokens))


def attention(queries, d_att, keys_values):
    tokens, inner = queries.shape
    length = keys_values.shape[0]
    by_pair = pl.BlockSpec((tokens, 2 * HD), lambda j: (0, j))
    terms = (length // tokens, 2 * HD + 16, tokens)
    return pl.pallas_call(
        attention_kernel,
        grid=(HEADS // 2,),
        in_specs=[
            by_pair,
            by_pair,
            pl.BlockSpec((length, HD), lambda j: (0, 0)),
            pl.BlockSpec((length, HD), lambda j: (0, 1)),
        ],
        out_specs=[
            pl.BlockSpec((2, tokens, 2 * HD), lambda j: (0, 0, j)),
            pl.BlockSpec((2, tokens, 2 * HD), lambda j: (0, 0, j)),
            pl.BlockSpec(terms, lambda j: (0, 0, 0)),
        ],
        out_shape=[
            jax.ShapeDtypeStruct((2, tokens, inner), jnp.bfloat16),
            jax.ShapeDtypeStruct((2, tokens, inner), jnp.bfloat16),
            jax.ShapeDtypeStruct(terms, jnp.float32),
        ],
        compiler_params=pltpu.CompilerParams(vmem_limit_bytes=32 * MIB),
        cost_estimate=pl.CostEstimate(
            flops=12 * tokens * inner * length, bytes_accessed=4 << 20, transcendentals=tokens * HEADS * length
        ),
        name="attention",
    )(queries, d_att, keys_values, keys_values)


def store_scaled(product, out_ref, first, cols, mask):
    power = exponent(product)
    scaled = product * jnp.exp2(-power)
    receivers, padded, _ = out_ref.shape
    rows = padded - 8
    for i in range(receivers):
        out_ref[i ^ mask, :rows, pl.ds(first, cols)] = scaled[i * rows : (i + 1) * rows]
        out_ref[i, rows:, pl.ds(first, cols)] = jnp.broadcast_to(power, (8, cols))


def wide_kernel(x_ref, mine_ref, theirs_ref, own_ref, other_ref, out_ref):
    product = dot(mine_ref[0], own_ref[0], ((1,), (0,))) + dot(theirs_ref[0], other_ref[0], ((1,), (0,)))
    store_scaled(product, out_ref, 0, product.shape[1], x_ref[0])


def wide_products(x, mine, theirs, own, other):
    _, rows, tokens = mine.shape
    inner = own.shape[2]
    side = pl.BlockSpec((1, rows, tokens), lambda i, x: (i, 0, 0))
    factor = pl.BlockSpec((1, tokens, inner), lambda i, x: (i, 0, 0))
    return pl.pallas_call(
        wide_kernel,
        grid_spec=pltpu.PrefetchScalarGridSpec(
            num_scalar_prefetch=1,
            grid=(2,),
            in_specs=[side, side, factor, factor],
            out_specs=pl.BlockSpec((4, rows // 4 + 8, inner), lambda i, x: (0, 0, i)),
        ),
        out_shape=jax.ShapeDtypeStruct((4, rows // 4 + 8, 2 * inner), jnp.float32),
        compiler_params=pltpu.CompilerParams(vmem_limit_bytes=16 * MIB),
        cost_estimate=pl.CostEstimate(flops=8 * rows * tokens * inner, bytes_accessed=5 << 20, transcendentals=0),
        name="wide",
    )(x.reshape(1), mine, theirs, own, other)


def narrow_kernel(x_ref, mine_ref, theirs_ref, own_ref, other_ref, out_ref):
    product = None
    for side_ref, terms_ref in ((mine_ref, own_ref), (theirs_ref, other_ref)):
        side = side_ref[0]
        rest = terms_ref[...]
        for _ in range(3):
            piece = rest.astype(jnp.bfloat16)
            rest = rest - piece.astype(jnp.float32)
            term = dot(side, piece, ((1,), (1,)))
            product = term if product is None else product + term
    for i in range(2):
        store_scaled(product[:, i * HD : (i + 1) * HD], out_ref, i * HD, HD, x_ref[0])


def narrow_products(x, mine, theirs, own, other):
    _, rows, tokens = mine.shape
    cols = own.shape[0]
    side = pl.BlockSpec((1, rows, tokens), lambda i, x: (0, 0, 0))
    whole = pl.BlockSpec((cols, tokens), lambda i, x: (0, 0))
    shape = (4, rows // 4 + 8, cols)
    return pl.pallas_call(
        narrow_kernel,
        grid_spec=pltpu.PrefetchScalarGridSpec(
            num_scalar_prefetch=1,
            grid=(1,),
            in_specs=[side, side, whole, whole],
            out_specs=pl.BlockSpec(shape, lambda i, x: (0, 0, 0)),
        ),
        out_shape=jax.ShapeDtypeStruct(shape, jnp.float32),
        compiler_params=pltpu.CompilerParams(vmem_limit_bytes=16 * MIB),
        cost_estimate=pl.CostEstimate(flops=1, bytes_accessed=1, transcendentals=0),
        name="narrow",
    )(x.reshape(1), mine, theirs, own, other)


def own_terms_kernel(terms_ref, out_ref):
    for i in range(2):
        rows, powers = pl.ds(i * HD, HD), pl.ds(2 * HD + 8 * i, 1)
        total = unscaled(terms_ref, 0, rows, powers)
        for b in range(1, terms_ref.shape[0]):
            total = total + unscaled(terms_ref, b, rows, powers)
        out_ref[rows, :] = total


def own_terms(terms):
    return pl.pallas_call(
        own_terms_kernel,
        out_shape=jax.ShapeDtypeStruct((2 * HD, terms.shape[2]), jnp.float32),
        compiler_params=pltpu.CompilerParams(vmem_limit_bytes=8 * MIB),
        cost_estimate=pl.CostEstimate(flops=1, bytes_accessed=1, transcendentals=0),
        name="own_terms",
    )(terms)


def after_x_kernel(wide_ref, wide_got_ref, narrow_ref, narrow_got_ref, out_ref, total_ref):
    receivers = out_ref.shape[0]
    rows = total_ref.shape[0]
    first = 0
    for i, (own_ref, got_ref, start, cols) in enumerate(
        (
            (wide_ref, wide_got_ref, 0, 4 * HD),
            (wide_ref, wide_got_ref, 4 * HD, 4 * HD),
            (narrow_ref, narrow_got_ref, 0, HD),
            (narrow_ref, narrow_got_ref, HD, HD),
        )
    ):
        sent = [(own_ref, 0)] + [(got_ref, m) for m in range(3)]
        here = pl.ds(start, cols)
        powers = [ref[m, rows : rows + 1, here] for ref, m in sent]
        top = jnp.maximum(jnp.maximum(powers[0], powers[1]), jnp.maximum(powers[2], powers[3])) + 2.0
        total = sum(ref[m, :rows, here] * jnp.exp2(power - top) for (ref, m), power in zip(sent, powers))
        total_ref[:, pl.ds(first, cols)] = total
        out_ref[:, 60 + i, :] = jnp.broadcast_to(top[:, :HD], (receivers, HD))
        first += cols
    for k in range(receivers):
        for j in range(10):
            out_ref[k, 6 * j : 6 * j + 6, :] = total_ref[6 * k : 6 * k + 6, j * HD : (j + 1) * HD]


def after_x(wide, wide_got, narrow, narrow_got):
    _, padded, wide_cols = wide.shape
    narrow_cols = narrow.shape[2]
    rows = padded - 8
    shape = (rows // 6, 64, HD)
    spec = lambda count, cols: pl.BlockSpec((count, padded, cols), lambda i: (0, 0, 0))
    return pl.pallas_call(
        after_x_kernel,
        grid=(1,),
        in_specs=[spec(1, wide_cols), spec(3, wide_cols), spec(1, narrow_cols), spec(3, narrow_cols)],
        out_specs=pl.BlockSpec(shape, lambda i: (0, 0, 0)),
        out_shape=jax.ShapeDtypeStruct(shape, jnp.float32),
        scratch_shapes=[pltpu.VMEM((rows, wide_cols + narrow_cols), jnp.float32)],
        compiler_params=pltpu.CompilerParams(vmem_limit_bytes=16 * MIB),
        name="after_x",
    )(wide, wide_got, narrow, narrow_got)


def last_sum_kernel(got_ref, query_ref, out_ref, key_ref, value_ref):
    first = 0
    for i, ref in enumerate((query_ref, out_ref, key_ref, value_ref)):
        tiles = ref.shape[1] // HD
        rows = pl.ds(first, 6 * tiles)
        total = unscaled(got_ref, 0, rows, pl.ds(60 + i, 1))
        for b in range(1, got_ref.shape[0]):
            total = total + unscaled(got_ref, b, rows, pl.ds(60 + i, 1))
        for j in range(tiles):
            ref[:, j * HD : (j + 1) * HD] = total[6 * j : 6 * j + 6]
        first += 6 * tiles


def last_sum(got):
    shape = lambda cols: jax.ShapeDtypeStruct((6, cols), jnp.float32)
    return pl.pallas_call(
        last_sum_kernel,
        out_shape=[shape(4 * HD), shape(4 * HD), shape(HD), shape(HD)],
        compiler_params=pltpu.CompilerParams(vmem_limit_bytes=8 * MIB),
        name="last_sum",
    )(got)


def local(normed, w_query, w_key, w_value, w_out, cotangent):
    hidden = normed[0]
    grads_in = cotangent[0]
    tokens, width = hidden.shape
    bf, half = jnp.bfloat16, jnp.float16
    dp = lax.axis_index("dp")
    x, core = dp >> 3, dp & 1
    f32 = jnp.float32

    own = dot(hidden, jnp.concatenate([w_key, w_value], axis=1), ((1,), (0,))).astype(bf)
    gathered = lax.all_to_all(jnp.broadcast_to(own, (8,) + own.shape), "seq", 0, 0, tiled=True)

    queries = dot(hidden, w_query, ((1,), (0,))).astype(bf)
    d_att = dot(grads_in, w_out, ((1,), (0,))).astype(bf)
    pick = (jnp.asarray(ROW_ORDER)[:, None] == jnp.arange(width)[None, :]).astype(bf)
    sides = jnp.stack([dot(pick, side, ((1,), (1,))).astype(bf) for side in (hidden, grads_in)])
    sides = sides.reshape(2, 2, width // 2, tokens)
    mine = lax.dynamic_index_in_dim(sides, core, 1, keepdims=False)
    theirs = from_other_core(lax.dynamic_index_in_dim(sides, 1 - core, 1, keepdims=False))
    queries, d_att, mine, theirs = lax.optimization_barrier((queries, d_att, mine, theirs))

    factors, factors_sent, terms = attention(queries, d_att, gathered.reshape(8 * tokens, 2 * HD))
    terms = lax.all_to_all(terms.astype(half), "seq", 0, 0, tiled=True)
    wide = wide_products(x, mine, theirs, factors, from_other_core(factors_sent))
    sent = [wide[m].astype(half) for m in (1, 2, 3)]
    got = [exchange(block, m << 6) for m, block in zip((1, 2, 3), sent)]
    branch = dot(factors[1], w_out, ((1,), (1,))).astype(bf)

    terms, _ = lax.optimization_barrier((terms, sent))
    d_kv = own_terms(terms.astype(f32))
    narrow = narrow_products(x, mine, theirs, d_kv, from_other_core(d_kv))
    narrow_sent = [narrow[m].astype(half) for m in (1, 2, 3)]
    got, _ = lax.optimization_barrier((got, narrow_sent))
    narrow_got = [exchange(block, m << 6) for m, block in zip((1, 2, 3), narrow_sent)]

    part = after_x(wide, jnp.stack(got).astype(f32), narrow, jnp.stack(narrow_got).astype(f32))
    part = lax.all_to_all(part.astype(half), AXES, 0, 0, axis_index_groups=YZ_GROUPS, tiled=True)
    grad_query, grad_out, grad_key, grad_value = last_sum(part.astype(f32))
    return branch[None], grad_query, grad_key, grad_value, grad_out


def solution(mesh):
    return jax.shard_map(
        local,
        mesh=mesh,
        in_specs=(P("dp", "seq", None), P(), P(), P(), P(), P("dp", "seq", None)),
        out_specs=(
            P("dp", "seq", None),
            P(("dp", "seq"), None),
            P(("dp", "seq"), None),
            P(("dp", "seq"), None),
            P(("dp", "seq"), None),
        ),
        check_vma=False,
    )
```

time: 496 us -> 115 us (0.23)
  waiting for transfers between devices: 353 us -> 47.1 us
  blocking collectives: 62.2 us -> 0 us
  matrix products: 41.8 us -> 8.85 us
  starting transfers between devices: 0.12 us -> 28.8 us
  Pallas kernels: 0 us -> 14.4 us
  between operations: 13.8 us -> 0.93 us
  local copies, waits for them, and re-layouts: 16.6 us -> 9.47 us
    unnamed x4 -> x0, waiting for transfers between devices: 279 us -> none
    reduce_scatter x2 -> x0, waiting for transfers between devices: 75 us -> none  [the longest x1 40.6 us: local(): lax.psum_scatter(key_terms, 'seq', scatter_dimension=0, tiled=True)]
    all_gather x2 -> x0, blocking collectives: 62.2 us -> none  [the longest x1 31.1 us: local(): lax.all_gather(own_values, 'seq', axis=0, tiled=True)]
    dot_general x21 -> x6, matrix products: 41.8 us -> 8.85 us  [dot(): lax.dot_general(left, right, (dims, ((), ())), preferred_element_type=jnp...]
    all_to_all x0 -> x3, waiting for transfers between devices: none -> 27.7 us  [the longest x1 14.4 us: local(): lax.all_to_all(part.astype(half), AXES, 0, 0, axis_index_groups=YZ_GROUPS...]
    all_to_all x0 -> x3, starting transfers between devices: none -> 20.3 us  [the longest x1 9.66 us: local(): lax.all_to_all(part.astype(half), AXES, 0, 0, axis_index_groups=YZ_GROUPS...]
    ppermute x0 -> x9, waiting for transfers between devices: none -> 19.4 us  [exchange(): return lax.ppermute(value, AXES, [(i, i ^ mask) for i in range(256)])]
    pallas_call x0 -> x6, Pallas kernels: none -> 14.4 us  [the longest x1 9.15 us: attention(): pl.pallas_call(attention_kernel, grid=(HEADS // 2,), in_specs=[by_pair, b...]
  transfers between devices with their start and end apart: 3 -> 12, of which waited for: 3 -> 9; matrix products, arithmetic and copies ran while one was open for 2% -> 8% of each run, Pallas kernels for 0% -> 3%
where the time goes in v1:
time: 115 us; the launch traced here: 114 us
  waiting for transfers between devices  47.1 us (41%)
  starting transfers between devices  28.8 us (25%)
  Pallas kernels  14.4 us (13%)
  local copies, waits for them, and re-layouts  9.47 us (8%)
  matrix products  8.85 us (8%)
  other arithmetic  4.57 us (4%)
    ppermute x9, waiting for transfers between devices, exchange(): return lax.ppermute(value, AXES, [(i, i ^ mask) for i in range(256)])  19.4 us
    all_to_all x1, waiting for transfers between devices, local(): lax.all_to_all(part.astype(half), AXES, 0, 0, axis_index_groups=YZ_GROUPS...  14.4 us
    all_to_all x1, starting transfers between devices, local(): lax.all_to_all(part.astype(half), AXES, 0, 0, axis_index_groups=YZ_GROUPS...  9.66 us
    pallas_call x1, Pallas kernels, attention(): pl.pallas_call(attention_kernel, grid=(HEADS // 2,), in_specs=[by_pair, b...  9.15 us
    dot_general x6, matrix products, dot(): lax.dot_general(left, right, (dims, ((), ())), preferred_element_type=jnp...  8.85 us
    ppermute x9, starting transfers between devices, exchange(): return lax.ppermute(value, AXES, [(i, i ^ mask) for i in range(256)])  8.42 us
    all_to_all x1, waiting for transfers between devices, local(): lax.all_to_all(jnp.broadcast_to(own, (8,) + own.shape), 'seq', 0, 0, tile...  7.16 us
    unnamed x30, local copies, waits for them, and re-layouts  7.03 us
  transfers between devices with their start and end apart: 12, of which 9 were waited for; matrix products, arithmetic and copies ran while one was open for 8% of the time, Pallas kernels for 3%

profile of v1, /device:TPU:32, one launch (start us, length us, event | category | flops | bytes accessed | tf_op | source)
XLA Modules:
  0.0 114.0 jit_solution(18138410407535175423)
XLA Ops:
  0.6 1.9 %fusion.7 = bf16[256,256]{0,1:T(8,128)(2,1)S(1)} fusion(bf16[1536,128]{1,0:T(8,128)(2,1)} %param.10, bf16[1536,128]{1,0:T(8,128)(2,1)} %param.9, bf16[1,256,1536]{2,1,0:T(8,128)(2,1)} %param.7), kind=kOutput, calls=%fused_computation.17 | convolution fusion | flops 202964992 | bytes 1703936 | tf_op jit(solution)/shard_map/dot_general | solution.py:34
  2.6 0.1 copy.14
  2.7 1.0 broadcast_in_dim.8
  3.7 6.0 %all-to-all-start = ((bf16[8,256,256]{2,1,0:T(8,128)(2,1)}), bf16[8,256,256]{2,1,0:T(8,128)(2,1)}, u32[]{:S(2)}, u32[]{:S(2)}) async-start(bf16[8,256,256]{2,1,0:T(8,128)(2,1)} %broadcast_in_dim.8), calls=%async_computation | async-start | bytes 2097152 | tf_op jit(solution)/shard_map/all_to_all | solution.py:314
  9.7 1.8 %fusion.4 = bf16[1536,256]{1,0:T(8,128)(2,1)S(1)} fusion(s32[1536]{0:T(1024)S(1)} %copy-done.14, bf16[1,256,1536]{2,1,0:T(8,128)(2,1)S(1)} %copy-done.11), kind=kOutput, calls=%fused_computation.5 | convolution fusion | flops 1210712064 | bytes 1579008 | tf_op jit(solution)/shard_map/dot_general | solution.py:34
  11.5 1.8 %fusion.5 = bf16[1536,256]{1,0:T(8,128)(2,1)S(1)} fusion(s32[1536]{0:T(1024)S(1)} %copy-done.14, bf16[1,256,1536]{2,1,0:T(8,128)(2,1)S(1)} %copy-done.13), kind=kOutput, calls=%fused_computation.6 | convolution fusion | flops 1210712064 | bytes 1579008 | tf_op jit(solution)/shard_map/dot_general | solution.py:34
  13.4 0.1 fusion.9
  13.5 0.1 collective-permute-start
  13.6 1.1 copy-done.10
  14.8 0.2 copy-done.12
  15.0 0.6 convolution_convert_fusion.2.q_ref
  15.6 1.3 %convolution_convert_fusion.1.da_ref = bf16[256,512]{1,0:T(8,128)(2,1)} fusion(bf16[1536,512]{1,0:T(8,128)(2,1)S(1)} %copy-done, bf16[1,256,1536]{2,1,0:T(8,128)(2,1)S(1)} %copy-done.13), kind=kOutput, calls=%fused_computation.14 | convolution fusion | flops 402784256 | bytes 2621440 | tf_op jit(solution)/shard_map/dot_general | solution.py:34
  16.8 7.2 %all-to-all-done = bf16[8,256,256]{2,1,0:T(8,128)(2,1)} async-done(((bf16[8,256,256]{2,1,0:T(8,128)(2,1)}), bf16[8,256,256]{2,1,0:T(8,128)(2,1)}, u32[]{:S(2)}, u32[]{:S(2)}) %all-to-all-start) | async-done | bytes 1048608 | tf_op jit(solution)/shard_map/all_to_all | solution.py:314
  24.0 0.9 copy-done.7
  25.0 9.2 %attention.1 = (bf16[2,256,512]{2,1,0:T(8,128)(2,1)S(1)}, bf16[2,256,512]{2,1,0:T(8,128)(2,1)S(1)}, f32[8,272,256]{2,1,0:T(8,128)S(1)}) custom-call(bf16[256,512]{1,0:T(8,128)(2,1)S(1)} %convolution_convert_fusion.2.q_ref, bf16[256,512]{1,0:T(8,128)(2,1)S(1)} %copy-done.7, bf16[2048,256]{1,0:T(8,128)(2,1)} %bitcast.9.k_ref.v_ref, ...), custom_call_target="tpu_custom_call" | custom-call | flops 3221225472 | bytes 4194304 | tf_op jit(solution)/shard_map/attention/pallas_call | solution.py:122
  34.1 0.8 copy-done.3
  34.9 0.8 copy-done.6
  35.7 1.2 %convert_element_type.74 = f16[8,272,256]{2,1,0:T(8,128)(2,1)} convert(f32[8,272,256]{2,1,0:T(8,128)S(1)} %get-tuple-element.26) | non-fusion elementwise | flops 557056 | bytes 3342336 | tf_op jit(solution)/shard_map/convert_element_type | solution.py:326
  36.9 4.7 %all-to-all-start.1 = ((f16[8,272,256]{2,1,0:T(8,128)(2,1)}), f16[8,272,256]{2,1,0:T(8,128)(2,1)}, u32[]{:S(2)}, u32[]{:S(2)}) async-start(f16[8,272,256]{2,1,0:T(8,128)(2,1)} %convert_element_type.74), calls=%async_computation.1 | async-start | bytes 2228224 | tf_op jit(solution)/shard_map/all_to_all | solution.py:326
  41.6 2.2 %collective-permute-done.1.other_ref = bf16[2,256,512]{2,1,0:T(8,128)(2,1)} collective-permute-done((bf16[2,256,512]{2,1,0:T(8,128)(2,1)}, bf16[2,256,512]{2,1,0:T(8,128)(2,1)}, u32[]{:S(2)}, u32[]{:S(2)}) %collective-permute-start.1) | collective-permute-done | bytes 524320 | tf_op jit(solution)/shard_map/ppermute | solution.py:38
  43.9 1.0 copy-done.4
  44.9 2.7 %wide.1.wide_ref = f32[4,200,1024]{2,1,0:T(8,128)S(1)} custom-call(s32[1]{0:T(128)} %bitcast.12.x_ref, bf16[2,768,256]{2,1,0:T(8,128)(2,1)S(1)} %get-tuple-element.23.mine_ref, bf16[2,768,256]{2,1,0:T(8,128)(2,1)S(1)} %collective-permute-done.theirs_ref, bf16[2,256,512]{2,1,0:T(8,128)(2,1)S(1)} %copy-done.4, ...), custom_call_target="tpu_custom_call" | custom-call | flops 805306368 | bytes 5242880 | tf_op jit(solution)/shard_map/wide/pallas_call | solution.py:169
  47.7 0.3 convert.10
  48.0 1.3 %copy-done.1 = f32[4,200,1024]{2,1,0:T(8,128)} copy-done((f32[4,200,1024]{2,1,0:T(8,128)}, f32[4,200,1024]{2,1,0:T(8,128)S(1)}, u32[]{:S(2)}) %copy-start.1) | copy-done | bytes 3276824
  49.3 1.2 %slice_bitcast_fusion = (f16[200,1024]{1,0:T(8,128)(2,1)}, f16[200,1024]{1,0:T(8,128)(2,1)}, f16[200,1024]{1,0:T(8,128)(2,1)S(1)}) fusion(f16[4,200,1024]{2,1,0:T(8,128)(2,1)S(1)} %convert.10), kind=kLoop, calls=%fused_computation.30 | loop fusion | bytes 2457600 | tf_op jit(solution)/shard_map/convert_element_type | solution.py:328
  50.6 6.1 %all-to-all-done.1 = f16[8,272,256]{2,1,0:T(8,128)(2,1)} async-done(((f16[8,272,256]{2,1,0:T(8,128)(2,1)}), f16[8,272,256]{2,1,0:T(8,128)(2,1)}, u32[]{:S(2)}, u32[]{:S(2)}) %all-to-all-start.1) | async-done | bytes 1114144 | tf_op jit(solution)/shard_map/all_to_all | solution.py:326
  56.7 1.4 %convert_element_type.75.terms_ref = f32[8,272,256]{2,1,0:T(8,128)S(1)} convert(f16[8,272,256]{2,1,0:T(8,128)(2,1)} %all-to-all-done.1) | non-fusion elementwise | flops 557056 | bytes 3342336 | tf_op jit(solution)/shard_map/convert_element_type | solution.py:333
  58.2 0.1 own_terms.1.own_ref
  58.4 0.7 copy-done.9
  59.1 2.9 %collective-permute-start.4 = (f16[200,1024]{1,0:T(8,128)(2,1)S(1)}, f16[200,1024]{1,0:T(8,128)(2,1)S(1)}, u32[]{:S(2)}, u32[]{:S(2)}) collective-permute-start(f16[200,1024]{1,0:T(8,128)(2,1)S(1)} %copy-done.9), channel_id=1, source_target_pairs={{0,192},{1,193},{2,194},{3,195},{4,196},{5,197},{6,198},{7,199},{8... | collective-permute-start | bytes 1228808 | tf_op jit(solution)/shard_map/ppermute | solution.py:38
  62.0 0.8 collective-permute-start.3
  62.8 0.4 collective-permute-start.2
  63.2 1.0 narrow.1.narrow_ref
  64.4 2.9 %collective-permute-start.8 = (f16[200,256]{1,0:T(8,128)(2,1)S(1)}, f16[200,256]{1,0:T(8,128)(2,1)S(1)}, u32[]{:S(2)}, u32[]{:S(2)}) collective-permute-start(f16[200,256]{1,0:T(8,128)(2,1)S(1)} %get-tuple-element.40), channel_id=1, source_target_pairs={{0,192},{1,193},{2,194},{3,195},{4,196},{5,197},{6,198},{7,199},{8... | collective-permute-start | bytes 307208 | tf_op jit(solution)/shard_map/ppermute | solution.py:38
  67.3 0.8 collective-permute-start.7
  68.1 13.3 %collective-permute-done.4 = f16[200,1024]{1,0:T(8,128)(2,1)S(1)} collective-permute-done((f16[200,1024]{1,0:T(8,128)(2,1)S(1)}, f16[200,1024]{1,0:T(8,128)(2,1)S(1)}, u32[]{:S(2)}, u32[]{:S(2)}) %collective-permute-start.4) | collective-permute-done | bytes 409632 | tf_op jit(solution)/shard_map/ppermute | solution.py:38
  81.4 0.4 collective-permute-start.6
  81.8 0.4 collective-permute-done.2
  82.2 0.3 maximum_convert_fusion.wide_got_ref
  82.5 1.3 %collective-permute-done.8 = f16[200,256]{1,0:T(8,128)(2,1)S(1)} collective-permute-done((f16[200,256]{1,0:T(8,128)(2,1)S(1)}, f16[200,256]{1,0:T(8,128)(2,1)S(1)}, u32[]{:S(2)}, u32[]{:S(2)}) %collective-permute-start.8) | collective-permute-done | bytes 102432 | tf_op jit(solution)/shard_map/ppermute | solution.py:38
  83.9 1.6 %collective-permute-done.7 = f16[200,256]{1,0:T(8,128)(2,1)S(1)} collective-permute-done((f16[200,256]{1,0:T(8,128)(2,1)S(1)}, f16[200,256]{1,0:T(8,128)(2,1)S(1)}, u32[]{:S(2)}, u32[]{:S(2)}) %collective-permute-start.7) | collective-permute-done | bytes 102432 | tf_op jit(solution)/shard_map/ppermute | solution.py:38
  85.4 0.6 collective-permute-done.6
  86.1 0.6 after_x.1
  86.8 0.9 convert_element_type.81
  87.7 9.7 %all-to-all-start.2 = ((f16[32,64,128]{2,1,0:T(8,128)(2,1)}), f16[32,64,128]{2,1,0:T(8,128)(2,1)S(1)}, u32[]{:S(2)}, u32[]{:S(2)}) async-start(f16[32,64,128]{2,1,0:T(8,128)(2,1)} %convert_element_type.81), calls=%async_computation.2 | async-start | bytes 1048576 | tf_op jit(solution)/shard_map/all_to_all | solution.py:340
  97.3 1.5 %fusion.6 = bf16[1,256,1536]{2,1,0:T(8,128)(2,1)} fusion(bf16[1536,512]{1,0:T(8,128)(2,1)S(1)} %copy-done, bf16[2,256,512]{2,1,0:T(8,128)(2,1)S(1)} %copy-done.5), kind=kOutput, calls=%fused_computation.8 | convolution fusion | flops 403046400 | bytes 2621440 | tf_op jit(solution)/shard_map/dot_general | solution.py:34
  98.8 14.4 %all-to-all-done.2 = f16[32,64,128]{2,1,0:T(8,128)(2,1)S(1)} async-done(((f16[32,64,128]{2,1,0:T(8,128)(2,1)}), f16[32,64,128]{2,1,0:T(8,128)(2,1)S(1)}, u32[]{:S(2)}, u32[]{:S(2)}) %all-to-all-start.2) | async-done | bytes 524320 | tf_op jit(solution)/shard_map/all_to_all | solution.py:340
  113.3 0.7 last_sum.1
  (31 shorter events, 0.4 us)
Async XLA Ops:
  0.6 14.9 %copy-start = (bf16[1536,512]{1,0:T(8,128)(2,1)S(1)}, bf16[1536,512]{1,0:T(8,128)(2,1)}, u32[]{:S(2)}) copy-start(bf16[1536,512]{1,0:T(8,128)(2,1)} %param.11) | copy-start | bytes 4718596
  2.7 7.0 %copy-start.11 = (bf16[1,256,1536]{2,1,0:T(8,128)(2,1)S(1)}, bf16[1,256,1536]{2,1,0:T(8,128)(2,1)}, u32[]{:S(2)}) copy-start(bf16[1,256,1536]{2,1,0:T(8,128)(2,1)} %param.7) | copy-start | bytes 2359300
  2.7 7.0 %copy-start.14 = (s32[1536]{0:T(1024)S(1)}, s32[1536]{0:T(1024)}, u32[]{:S(2)}) copy-start(s32[1536]{0:T(1024)} %constant.21.clone) | copy-start | bytes 18436
  3.7 20.3 %all-to-all-start = ((bf16[8,256,256]{2,1,0:T(8,128)(2,1)}), bf16[8,256,256]{2,1,0:T(8,128)(2,1)}, u32[]{:S(2)}, u32[]{:S(2)}) async-start(bf16[8,256,256]{2,1,0:T(8,128)(2,1)} %broadcast_in_dim.8), calls=%async_computation | async-start | bytes 2097152 | tf_op jit(solution)/shard_map/all_to_all | solution.py:314
  9.7 1.8 %copy-start.13 = (bf16[1,256,1536]{2,1,0:T(8,128)(2,1)S(1)}, bf16[1,256,1536]{2,1,0:T(8,128)(2,1)}, u32[]{:S(2)}) copy-start(bf16[1,256,1536]{2,1,0:T(8,128)(2,1)} %param.12) | copy-start | bytes 2359300
  13.4 1.4 %copy-start.10 = (bf16[1536,512]{1,0:T(8,128)(2,1)S(1)}, bf16[1536,512]{1,0:T(8,128)(2,1)}, u32[]{:S(2)}) copy-start(bf16[1536,512]{1,0:T(8,128)(2,1)} %param.8) | copy-start | bytes 4718596
  13.4 1.6 %copy-start.12 = (bf16[1,256,1536]{2,1,0:T(8,128)(2,1)S(1)}, bf16[1,256,1536]{2,1,0:T(8,128)(2,1)}, u32[]{:S(2)}) copy-start(bf16[1,256,1536]{2,1,0:T(8,128)(2,1)} %param.7) | copy-start | bytes 2359300
  13.5 3.3 %collective-permute-start = (bf16[2,768,256]{2,1,0:T(8,128)(2,1)S(1)}, bf16[2,768,256]{2,1,0:T(8,128)(2,1)S(1)}, u32[]{:S(2)}, u32[]{:S(2)}) collective-permute-start(bf16[2,768,256]{2,1,0:T(8,128)(2,1)S(1)} %get-tuple-element.38), channel_id=1, source_target_pairs={{0,8},{1,9},{2,10},{3,11},{4,12},{5,13},{6,14},{7,15},{8,0},{9,1},... | collective-permute-start | bytes 2359304 | tf_op jit(solution)/shard_map/ppermute | solution.py:38
  24.0 1.0 copy-start.7
  34.1 0.8 copy-start.3
  34.9 0.8 copy-start.6
  36.9 19.8 %all-to-all-start.1 = ((f16[8,272,256]{2,1,0:T(8,128)(2,1)}), f16[8,272,256]{2,1,0:T(8,128)(2,1)}, u32[]{:S(2)}, u32[]{:S(2)}) async-start(f16[8,272,256]{2,1,0:T(8,128)(2,1)} %convert_element_type.74), calls=%async_computation.1 | async-start | bytes 2228224 | tf_op jit(solution)/shard_map/all_to_all | solution.py:326
  41.6 2.3 %collective-permute-start.1 = (bf16[2,256,512]{2,1,0:T(8,128)(2,1)}, bf16[2,256,512]{2,1,0:T(8,128)(2,1)}, u32[]{:S(2)}, u32[]{:S(2)}) collective-permute-start(bf16[2,256,512]{2,1,0:T(8,128)(2,1)} %copy-done.6), channel_id=1, source_target_pairs={{0,8},{1,9},{2,10},{3,11},{4,12},{5,13},{6,14},{7,15},{8,0},{9,1},... | collective-permute-start | bytes 1572872 | tf_op jit(solution)/shard_map/ppermute | solution.py:38
  43.9 1.0 copy-start.4
  47.7 1.7 %copy-start.1 = (f32[4,200,1024]{2,1,0:T(8,128)}, f32[4,200,1024]{2,1,0:T(8,128)S(1)}, u32[]{:S(2)}) copy-start(f32[4,200,1024]{2,1,0:T(8,128)S(1)} %wide.1.wide_ref) | copy-start | bytes 9830404
  58.1 1.0 copy-start.9
  58.1 3.9 %copy-start.8 = (f16[200,1024]{1,0:T(8,128)(2,1)S(1)}, f16[200,1024]{1,0:T(8,128)(2,1)}, u32[]{:S(2)}) copy-start(f16[200,1024]{1,0:T(8,128)(2,1)} %get-tuple-element.36) | copy-start | bytes 1228804
  58.3 4.9 %collective-permute-start.5 = (f32[256,256]{1,0:T(8,128)S(1)}, f32[256,256]{1,0:T(8,128)S(1)}, u32[]{:S(2)}, u32[]{:S(2)}) collective-permute-start(f32[256,256]{1,0:T(8,128)S(1)} %own_terms.1.own_ref), channel_id=1, source_target_pairs={{0,8},{1,9},{2,10},{3,11},{4,12},{5,13},{6,14},{7,15},{8,0},{9,1},... | collective-permute-start | bytes 786440 | tf_op jit(solution)/shard_map/ppermute | solution.py:38
  59.1 22.2 %collective-permute-start.4 = (f16[200,1024]{1,0:T(8,128)(2,1)S(1)}, f16[200,1024]{1,0:T(8,128)(2,1)S(1)}, u32[]{:S(2)}, u32[]{:S(2)}) collective-permute-start(f16[200,1024]{1,0:T(8,128)(2,1)S(1)} %copy-done.9), channel_id=1, source_target_pairs={{0,192},{1,193},{2,194},{3,195},{4,196},{5,197},{6,198},{7,199},{8... | collective-permute-start | bytes 1228808 | tf_op jit(solution)/shard_map/ppermute | solution.py:38
  62.0 19.8 %collective-permute-start.3 = (f16[200,1024]{1,0:T(8,128)(2,1)S(1)}, f16[200,1024]{1,0:T(8,128)(2,1)S(1)}, u32[]{:S(2)}, u32[]{:S(2)}) collective-permute-start(f16[200,1024]{1,0:T(8,128)(2,1)S(1)} %copy-done.8), channel_id=1, source_target_pairs={{0,128},{1,129},{2,130},{3,131},{4,132},{5,133},{6,134},{7,135},{8... | collective-permute-start | bytes 1228808 | tf_op jit(solution)/shard_map/ppermute | solution.py:38
  62.8 19.4 %collective-permute-start.2 = (f16[200,1024]{1,0:T(8,128)(2,1)S(1)}, f16[200,1024]{1,0:T(8,128)(2,1)S(1)}, u32[]{:S(2)}, u32[]{:S(2)}) collective-permute-start(f16[200,1024]{1,0:T(8,128)(2,1)S(1)} %get-tuple-element.37), channel_id=1, source_target_pairs={{0,64},{1,65},{2,66},{3,67},{4,68},{5,69},{6,70},{7,71},{8,72},{9,... | collective-permute-start | bytes 1228808 | tf_op jit(solution)/shard_map/ppermute | solution.py:38
  64.4 19.5 %collective-permute-start.8 = (f16[200,256]{1,0:T(8,128)(2,1)S(1)}, f16[200,256]{1,0:T(8,128)(2,1)S(1)}, u32[]{:S(2)}, u32[]{:S(2)}) collective-permute-start(f16[200,256]{1,0:T(8,128)(2,1)S(1)} %get-tuple-element.40), channel_id=1, source_target_pairs={{0,192},{1,193},{2,194},{3,195},{4,196},{5,197},{6,198},{7,199},{8... | collective-permute-start | bytes 307208 | tf_op jit(solution)/shard_map/ppermute | solution.py:38
  67.3 18.1 %collective-permute-start.7 = (f16[200,256]{1,0:T(8,128)(2,1)S(1)}, f16[200,256]{1,0:T(8,128)(2,1)S(1)}, u32[]{:S(2)}, u32[]{:S(2)}) collective-permute-start(f16[200,256]{1,0:T(8,128)(2,1)S(1)} %get-tuple-element.41), channel_id=1, source_target_pairs={{0,128},{1,129},{2,130},{3,131},{4,132},{5,133},{6,134},{7,135},{8... | collective-permute-start | bytes 307208 | tf_op jit(solution)/shard_map/ppermute | solution.py:38
  81.4 4.7 %collective-permute-start.6 = (f16[200,256]{1,0:T(8,128)(2,1)S(1)}, f16[200,256]{1,0:T(8,128)(2,1)S(1)}, u32[]{:S(2)}, u32[]{:S(2)}) collective-permute-start(f16[200,256]{1,0:T(8,128)(2,1)S(1)} %get-tuple-element.42), channel_id=1, source_target_pairs={{0,64},{1,65},{2,66},{3,67},{4,68},{5,69},{6,70},{7,71},{8,72},{9,... | collective-permute-start | bytes 307208 | tf_op jit(solution)/shard_map/ppermute | solution.py:38
  82.2 3.9 %copy-start.2 = (f32[4,200,1024]{2,1,0:T(8,128)S(1)}, f32[4,200,1024]{2,1,0:T(8,128)}, u32[]{:S(2)}) copy-start(f32[4,200,1024]{2,1,0:T(8,128)} %copy-done.1) | copy-start | bytes 9830404
  86.7 10.6 %copy-start.5 = (bf16[2,256,512]{2,1,0:T(8,128)(2,1)S(1)}, bf16[2,256,512]{2,1,0:T(8,128)(2,1)}, u32[]{:S(2)}) copy-start(bf16[2,256,512]{2,1,0:T(8,128)(2,1)} %copy-done.3) | copy-start | bytes 1572868
  87.7 25.6 %all-to-all-start.2 = ((f16[32,64,128]{2,1,0:T(8,128)(2,1)}), f16[32,64,128]{2,1,0:T(8,128)(2,1)S(1)}, u32[]{:S(2)}, u32[]{:S(2)}) async-start(f16[32,64,128]{2,1,0:T(8,128)(2,1)} %convert_element_type.81), calls=%async_computation.2 | async-start | bytes 1048576 | tf_op jit(solution)/shard_map/all_to_all | solution.py:340

commit v2 on v1

--- a/solution.py
+++ b/solution.py
@@ -51,7 +51,25 @@
     return ref[block, values, :] * jnp.exp2(ref[block, exponents, :])
 
 
-def attention_kernel(q_ref, da_ref, k_ref, v_ref, factor_ref, copy_ref, dkv_ref):
+def project_kernel(hidden_ref, w_key_ref, w_value_ref, out_ref):
+    hidden = hidden_ref[...]
+    for i, ref in enumerate((w_key_ref, w_value_ref)):
+        block = dot(hidden, ref[...], ((1,), (0,))).astype(jnp.bfloat16)
+        for b in range(out_ref.shape[0]):
+            out_ref[b, :, i * HD : (i + 1) * HD] = block
+
+
+def project(hidden, w_key, w_value):
+    hidden, w_key, w_value = (pltpu.with_memory_space_constraint(v, pltpu.HBM) for v in (hidden, w_key, w_value))
+    return pl.pallas_call(
+        project_kernel,
+        out_shape=jax.ShapeDtypeStruct((8, hidden.shape[0], 2 * HD), jnp.bfloat16),
+        compiler_params=pltpu.CompilerParams(vmem_limit_bytes=16 * MIB),
+        name="project",
+    )(hidden, w_key, w_value)
+
+
+def attention_kernel(q_ref, da_ref, k_ref, v_ref, factor_ref, dkv_ref):
     step = pl.program_id(0)
     keys = k_ref[...]
     values = v_ref[...]
@@ -66,7 +84,6 @@
 
     def store(side, h, value):
         factor_ref[side, :, h * HD : (h + 1) * HD] = value
-        copy_ref[side, :, h * HD : (h + 1) * HD] = value
 
     scores = [dot(q[h], keys, ((1,), (1,))) for h in heads]
     probs, probs_b, d_probs, d_scores = [], [], [], []
@@ -130,12 +147,10 @@
         ],
         out_specs=[
             pl.BlockSpec((2, tokens, 2 * HD), lambda j: (0, 0, j)),
-            pl.BlockSpec((2, tokens, 2 * HD), lambda j: (0, 0, j)),
             pl.BlockSpec(terms, lambda j: (0, 0, 0)),
         ],
         out_shape=[
-            jax.ShapeDtypeStruct((2, tokens, inner), jnp.bfloat16),
-            jax.ShapeDtypeStruct((2, tokens, inner), jnp.bfloat16),
+            pltpu.HBM((2, tokens, inner), jnp.bfloat16),
             jax.ShapeDtypeStruct(terms, jnp.float32),
         ],
         compiler_params=pltpu.CompilerParams(vmem_limit_bytes=32 * MIB),
@@ -156,9 +171,26 @@
         out_ref[i, rows:, pl.ds(first, cols)] = jnp.broadcast_to(power, (8, cols))
 
 
-def wide_kernel(x_ref, mine_ref, theirs_ref, own_ref, other_ref, out_ref):
+def scaled_rows(values, out_ref, first):
+    power = exponent(values)
+    rows = values.shape[0]
+    out_ref[0, first : first + rows, :] = values * jnp.exp2(-power)
+    out_ref[0, first + rows :, :] = jnp.broadcast_to(power, (8, values.shape[1]))
+
+
+def wide_kernel(x_ref, mine_ref, theirs_ref, own_ref, other_ref, keep_ref, send_ref, product_ref):
     product = dot(mine_ref[0], own_ref[0], ((1,), (0,))) + dot(theirs_ref[0], other_ref[0], ((1,), (0,)))
-    store_scaled(product, out_ref, 0, product.shape[1], x_ref[0])
+    product_ref[...] = product
+    power = exponent(product)
+    factor = jnp.exp2(-power)
+    first = 1 + 2 * pl.program_id(0)
+    rows = keep_ref.shape[2]
+    block = lambda mask: product_ref[pl.ds(pl.multiple_of((x_ref[0] ^ mask) * rows, 8), rows), :]
+    keep_ref[0, 0] = block(0)
+    keep_ref[0, 1] = block(4 - first)
+    send_ref[0, :rows] = block(first) * factor
+    send_ref[0, rows : 2 * rows] = block(2) * factor
+    send_ref[0, 2 * rows :] = jnp.broadcast_to(power, (8, product.shape[1]))
 
 
 def wide_products(x, mine, theirs, own, other):
@@ -172,13 +204,48 @@
             num_scalar_prefetch=1,
             grid=(2,),
             in_specs=[side, side, factor, factor],
-            out_specs=pl.BlockSpec((4, rows // 4 + 8, inner), lambda i, x: (0, 0, i)),
+            out_specs=[
+                pl.BlockSpec((1, 2, rows // 4, inner), lambda i, x: (i, 0, 0, 0)),
+                pl.BlockSpec((1, rows // 2 + 8, inner), lambda i, x: (i, 0, 0)),
+            ],
+            scratch_shapes=[pltpu.VMEM((rows, inner), jnp.float32)],
         ),
-        out_shape=jax.ShapeDtypeStruct((4, rows // 4 + 8, 2 * inner), jnp.float32),
+        out_shape=[
+            pltpu.HBM((2, 2, rows // 4, inner), jnp.float32),
+            jax.ShapeDtypeStruct((2, rows // 2 + 8, inner), jnp.float32),
+        ],
         compiler_params=pltpu.CompilerParams(vmem_limit_bytes=16 * MIB),
         cost_estimate=pl.CostEstimate(flops=8 * rows * tokens * inner, bytes_accessed=5 << 20, transcendentals=0),
         name="wide",
     )(x.reshape(1), mine, theirs, own, other)
+
+
+def middle_kernel(keep_ref, got_ref, total_ref, send_ref):
+    rows = keep_ref.shape[2]
+    powers = pl.ds(2 * rows, 1)
+    total_ref[0] = keep_ref[0, 0] + unscaled(got_ref, 0, pl.ds(0, rows), powers)
+    scaled_rows(keep_ref[0, 1] + unscaled(got_ref, 0, pl.ds(rows, rows), powers), send_ref, 0)
+
+
+def middle(keep, got):
+    _, _, rows, cols = keep.shape
+    shapes = (rows, rows + 8)
+    return pl.pallas_call(
+        middle_kernel,
+        grid=(2,),
+        in_specs=[
+            pl.BlockSpec((1, 2, rows, cols), lambda i: (i, 0, 0, 0)),
+            pl.BlockSpec((1, 2 * rows + 8, cols), lambda i: (i, 0, 0)),
+        ],
+        out_specs=[pl.BlockSpec((1, r, cols), lambda i: (i, 0, 0)) for r in shapes],
+        out_shape=[
+            pltpu.HBM((2, rows, cols), jnp.float32),
+            jax.ShapeDtypeStruct((2, rows + 8, cols), jnp.float32),
+        ],
+        compiler_params=pltpu.CompilerParams(vmem_limit_bytes=16 * MIB),
+        cost_estimate=pl.CostEstimate(flops=1, bytes_accessed=1, transcendentals=0),
+        name="middle",
+    )(keep, got)
 
 
 def narrow_kernel(x_ref, mine_ref, theirs_ref, own_ref, other_ref, out_ref):
@@ -237,42 +304,43 @@
 
 def after_x_kernel(wide_ref, wide_got_ref, narrow_ref, narrow_got_ref, out_ref, total_ref):
     receivers = out_ref.shape[0]
-    rows = total_ref.shape[0]
-    first = 0
-    for i, (own_ref, got_ref, start, cols) in enumerate(
-        (
-            (wide_ref, wide_got_ref, 0, 4 * HD),
-            (wide_ref, wide_got_ref, 4 * HD, 4 * HD),
-            (narrow_ref, narrow_got_ref, 0, HD),
-            (narrow_ref, narrow_got_ref, HD, HD),
-        )
-    ):
-        sent = [(own_ref, 0)] + [(got_ref, m) for m in range(3)]
-        here = pl.ds(start, cols)
-        powers = [ref[m, rows : rows + 1, here] for ref, m in sent]
-        top = jnp.maximum(jnp.maximum(powers[0], powers[1]), jnp.maximum(powers[2], powers[3])) + 2.0
-        total = sum(ref[m, :rows, here] * jnp.exp2(power - top) for (ref, m), power in zip(sent, powers))
-        total_ref[:, pl.ds(first, cols)] = total
-        out_ref[:, 60 + i, :] = jnp.broadcast_to(top[:, :HD], (receivers, HD))
-        first += cols
+    rows, cols = wide_ref.shape[1:]
+    for i in range(2):
+        power = wide_got_ref[i, rows : rows + 1, :]
+        total = wide_ref[i] + wide_got_ref[i, :rows, :] * jnp.exp2(power)
+        top = exponent(total)
+        total_ref[:, pl.ds(i * cols, cols)] = total * jnp.exp2(-top)
+        out_ref[:, 60 + i, :] = jnp.broadcast_to(top, (receivers, HD))
+    for i in range(2):
+        here = pl.ds(i * HD, HD)
+        total = unscaled(narrow_ref, 0, pl.ds(0, rows), pl.ds(rows, 1))[:, i * HD : (i + 1) * HD]
+        for m in range(3):
+            total = total + narrow_got_ref[m, :rows, here] * jnp.exp2(narrow_got_ref[m, rows : rows + 1, here])
+        top = exponent(total)
+        total_ref[:, pl.ds(2 * cols + i * HD, HD)] = total * jnp.exp2(-top)
+        out_ref[:, 62 + i, :] = jnp.broadcast_to(top, (receivers, HD))
     for k in range(receivers):
         for j in range(10):
             out_ref[k, 6 * j : 6 * j + 6, :] = total_ref[6 * k : 6 * k + 6, j * HD : (j + 1) * HD]
 
 
 def after_x(wide, wide_got, narrow, narrow_got):
-    _, padded, wide_cols = wide.shape
+    _, rows, wide_cols = wide.shape
     narrow_cols = narrow.shape[2]
-    rows = padded - 8
     shape = (rows // 6, 64, HD)
-    spec = lambda count, cols: pl.BlockSpec((count, padded, cols), lambda i: (0, 0, 0))
+    spec = lambda *sizes: pl.BlockSpec(sizes, lambda i: (0, 0, 0))
     return pl.pallas_call(
         after_x_kernel,
         grid=(1,),
-        in_specs=[spec(1, wide_cols), spec(3, wide_cols), spec(1, narrow_cols), spec(3, narrow_cols)],
-        out_specs=pl.BlockSpec(shape, lambda i: (0, 0, 0)),
+        in_specs=[
+            spec(2, rows, wide_cols),
+            spec(2, rows + 8, wide_cols),
+            spec(1, rows + 8, narrow_cols),
+            spec(3, rows + 8, narrow_cols),
+        ],
+        out_specs=spec(*shape),
         out_shape=jax.ShapeDtypeStruct(shape, jnp.float32),
-        scratch_shapes=[pltpu.VMEM((rows, wide_cols + narrow_cols), jnp.float32)],
+        scratch_shapes=[pltpu.VMEM((rows, 2 * wide_cols + narrow_cols), jnp.float32)],
         compiler_params=pltpu.CompilerParams(vmem_limit_bytes=16 * MIB),
         name="after_x",
     )(wide, wide_got, narrow, narrow_got)
@@ -310,8 +378,7 @@
     x, core = dp >> 3, dp & 1
     f32 = jnp.float32
 
-    own = dot(hidden, jnp.concatenate([w_key, w_value], axis=1), ((1,), (0,))).astype(bf)
-    gathered = lax.all_to_all(jnp.broadcast_to(own, (8,) + own.shape), "seq", 0, 0, tiled=True)
+    gathered = lax.all_to_all(project(hidden, w_key, w_value), "seq", 0, 0, tiled=True)
 
     queries = dot(hidden, w_query, ((1,), (0,))).astype(bf)
     d_att = dot(grads_in, w_out, ((1,), (0,))).astype(bf)
@@ -322,19 +389,23 @@
     theirs = from_other_core(lax.dynamic_index_in_dim(sides, 1 - core, 1, keepdims=False))
     queries, d_att, mine, theirs = lax.optimization_barrier((queries, d_att, mine, theirs))
 
-    factors, factors_sent, terms = attention(queries, d_att, gathered.reshape(8 * tokens, 2 * HD))
+    queries, d_att = (pltpu.with_memory_space_constraint(v, pltpu.HBM) for v in (queries, d_att))
+    factors, terms = attention(queries, d_att, gathered.reshape(8 * tokens, 2 * HD))
     terms = lax.all_to_all(terms.astype(half), "seq", 0, 0, tiled=True)
-    wide = wide_products(x, mine, theirs, factors, from_other_core(factors_sent))
-    sent = [wide[m].astype(half) for m in (1, 2, 3)]
-    got = [exchange(block, m << 6) for m, block in zip((1, 2, 3), sent)]
+    keep, send = wide_products(x, mine, theirs, factors, from_other_core(factors))
+    send = send.astype(half)
+    got = [exchange(send[0], 1 << 6), exchange(send[1], 3 << 6)]
     branch = dot(factors[1], w_out, ((1,), (1,))).astype(bf)
 
-    terms, _ = lax.optimization_barrier((terms, sent))
-    d_kv = own_terms(terms.astype(f32))
+    terms, _ = lax.optimization_barrier((terms, send))
+    terms, got = lax.optimization_barrier((terms.astype(f32), got))
+    d_kv = own_terms(terms)
     narrow = narrow_products(x, mine, theirs, d_kv, from_other_core(d_kv))
     narrow_sent = [narrow[m].astype(half) for m in (1, 2, 3)]
-    got, _ = lax.optimization_barrier((got, narrow_sent))
     narrow_got = [exchange(block, m << 6) for m, block in zip((1, 2, 3), narrow_sent)]
+    wide, send = middle(keep, jnp.stack(got).astype(f32))
+    send = send.astype(half)
+    got = [exchange(send[0], 3 << 6), exchange(send[1], 1 << 6)]
 
     part = after_x(wide, jnp.stack(got).astype(f32), narrow, jnp.stack(narrow_got).astype(f32))
     part = lax.all_to_all(part.astype(half), AXES, 0, 0, axis_index_groups=YZ_GROUPS, tiled=True)

time: 115 us -> 109 us (0.948)
  waiting for transfers between devices: 47.1 us -> 40.1 us
  local copies, waits for them, and re-layouts: 9.47 us -> 4.65 us
  Pallas kernels: 14.4 us -> 19.2 us
  starting transfers between devices: 28.8 us -> 30.5 us
  matrix products: 8.85 us -> 7.67 us
    ppermute x9 -> x10, waiting for transfers between devices: 19.4 us -> 14.7 us  [exchange(): return lax.ppermute(value, AXES, [(i, i ^ mask) for i in range(256)])]
    pallas_call x1 -> x3, Pallas kernels: 0.64 us -> 4.55 us  [the longest x1 3.02 us: project(): pl.pallas_call(project_kernel, out_shape=jax.ShapeDtypeStruct((8, hidden....]
    unnamed x30 -> x24, local copies, waits for them, and re-layouts: 7.03 us -> 3.46 us
    all_to_all x1, waiting for transfers between devices: 7.16 us -> 5.47 us  [local(): lax.all_to_all(project(hidden, w_key, w_value), 'seq', 0, 0, tiled=True)]
    all_to_all x1, waiting for transfers between devices: 6.09 us -> 4.41 us  [local(): terms = lax.all_to_all(terms.astype(half), 'seq', 0, 0, tiled=True)]
    convert_element_type x1 -> x4, other arithmetic: 1.44 us -> 2.99 us  [the longest x1 1.44 us: local(): terms, got = lax.optimization_barrier((terms.astype(f32), got))]
    convert_element_type x2 -> x0, local copies, waits for them, and re-layouts: 1.34 us -> none  [the longest x1 1.24 us: local(): sent = [wide[m].astype(half) for m in (1, 2, 3)]]
    dot_general x6 -> x5, matrix products: 8.85 us -> 7.67 us  [dot(): lax.dot_general(left, right, (dims, ((), ())), preferred_element_type=jnp...]
  transfers between devices with their start and end apart: 12 -> 13, of which waited for: 9 -> 10; matrix products, arithmetic and copies ran while one was open for 8% -> 11% of each run, Pallas kernels for 3% -> 5%
where the time goes in v2:
time: 109 us; the launch traced here: 108 us
  waiting for transfers between devices  40.1 us (37%)
  starting transfers between devices  30.5 us (28%)
  Pallas kernels  19.2 us (18%)
  matrix products  7.67 us (7%)
  other arithmetic  5.52 us (5%)
  local copies, waits for them, and re-layouts  4.65 us (4%)
    all_to_all x1, waiting for transfers between devices, local(): lax.all_to_all(part.astype(half), AXES, 0, 0, axis_index_groups=YZ_GROUPS...  15.5 us
    ppermute x10, waiting for transfers between devices, exchange(): return lax.ppermute(value, AXES, [(i, i ^ mask) for i in range(256)])  14.7 us
    all_to_all x1, starting transfers between devices, local(): lax.all_to_all(part.astype(half), AXES, 0, 0, axis_index_groups=YZ_GROUPS...  10.7 us
    pallas_call x1, Pallas kernels, attention(): pl.pallas_call(attention_kernel, grid=(HEADS // 2,), in_specs=[by_pair, b...  9.53 us
    ppermute x10, starting transfers between devices, exchange(): return lax.ppermute(value, AXES, [(i, i ^ mask) for i in range(256)])  8.93 us
    dot_general x5, matrix products, dot(): lax.dot_general(left, right, (dims, ((), ())), preferred_element_type=jnp...  7.67 us
    all_to_all x1, starting transfers between devices, local(): lax.all_to_all(project(hidden, w_key, w_value), 'seq', 0, 0, tiled=True)  6.06 us
    all_to_all x1, waiting for transfers between devices, local(): lax.all_to_all(project(hidden, w_key, w_value), 'seq', 0, 0, tiled=True)  5.47 us
  transfers between devices with their start and end apart: 13, of which 10 were waited for; matrix products, arithmetic and copies ran while one was open for 11% of the time, Pallas kernels for 5%

profile of v2, /device:TPU:32, one launch (start us, length us, event | category | flops | bytes accessed | tf_op | source)
XLA Modules:
  0.0 108.5 jit_solution(4965030640432469871)
XLA Ops:
  0.6 3.0 %project.1 = bf16[8,256,256]{2,1,0:T(8,128)(2,1)} custom-call(bf16[256,1536]{1,0:T(8,128)(2,1)} %bitcast.53, bf16[1536,128]{1,0:T(8,128)(2,1)} %w_key_ref.1, bf16[1536,128]{1,0:T(8,128)(2,1)} %w_value_ref.1), custom_call_target="tpu_custom_call" | custom-call | tf_op jit(solution)/shard_map/project/pallas_call | solution.py:64
  3.7 6.1 %all-to-all-start = ((bf16[8,256,256]{2,1,0:T(8,128)(2,1)}), bf16[8,256,256]{2,1,0:T(8,128)(2,1)S(1)}, u32[]{:S(2)}, u32[]{:S(2)}) async-start(bf16[8,256,256]{2,1,0:T(8,128)(2,1)} %project.1), calls=%async_computation | async-start | bytes 2097152 | tf_op jit(solution)/shard_map/all_to_all | solution.py:381
  9.7 1.8 %fusion.4 = bf16[1536,256]{1,0:T(8,128)(2,1)S(1)} fusion(s32[1536]{0:T(1024)S(1)} %copy-done.11, bf16[1,256,1536]{2,1,0:T(8,128)(2,1)S(1)} %copy-done.7), kind=kOutput, calls=%fused_computation.5 | convolution fusion | flops 1210712064 | bytes 1579008 | tf_op jit(solution)/shard_map/dot_general | solution.py:34
  11.6 1.8 %fusion.5 = bf16[1536,256]{1,0:T(8,128)(2,1)S(1)} fusion(s32[1536]{0:T(1024)S(1)} %copy-done.11, bf16[1,256,1536]{2,1,0:T(8,128)(2,1)S(1)} %copy-done.10), kind=kOutput, calls=%fused_computation.6 | convolution fusion | flops 1210712064 | bytes 1579008 | tf_op jit(solution)/shard_map/dot_general | solution.py:34
  13.4 0.1 fusion.8
  13.6 0.1 collective-permute-start
  13.7 0.9 copy-done.8
  14.5 0.5 copy-done.9
  15.1 1.3 %convolution_convert_fusion.2.q_ref = bf16[256,512]{1,0:T(8,128)(2,1)} fusion(bf16[1536,512]{1,0:T(8,128)(2,1)S(1)} %copy-done.9, bf16[1,256,1536]{2,1,0:T(8,128)(2,1)S(1)} %copy-done.8), kind=kOutput, calls=%fused_computation.14 | convolution fusion | flops 402784256 | bytes 2621440 | tf_op jit(solution)/shard_map/dot_general | solution.py:34
  16.3 1.3 %convolution_convert_fusion.1.da_ref = bf16[256,512]{1,0:T(8,128)(2,1)} fusion(bf16[1536,512]{1,0:T(8,128)(2,1)S(1)} %copy-done, bf16[1,256,1536]{2,1,0:T(8,128)(2,1)S(1)} %copy-done.10), kind=kOutput, calls=%fused_computation.13 | convolution fusion | flops 402784256 | bytes 2621440 | tf_op jit(solution)/shard_map/dot_general | solution.py:34
  17.6 0.9 copy-done.2
  18.5 5.5 %all-to-all-done = bf16[8,256,256]{2,1,0:T(8,128)(2,1)S(1)} async-done(((bf16[8,256,256]{2,1,0:T(8,128)(2,1)}), bf16[8,256,256]{2,1,0:T(8,128)(2,1)S(1)}, u32[]{:S(2)}, u32[]{:S(2)}) %all-to-all-start) | async-done | bytes 1048608 | tf_op jit(solution)/shard_map/all_to_all | solution.py:381
  24.0 9.5 %attention.1 = (bf16[2,256,512]{2,1,0:T(8,128)(2,1)}, f32[8,272,256]{2,1,0:T(8,128)S(1)}) custom-call(bf16[256,512]{1,0:T(8,128)(2,1)} %convolution_convert_fusion.2.q_ref, bf16[256,512]{1,0:T(8,128)(2,1)} %convolution_convert_fusion.1.da_ref, bf16[2048,256]{1,0:T(8,128)(2,1)S(1)} %bitcast.51, bf16[2048,256]{1,0:T(8,128)(2,1)S(1)} %bitcast.52), custom_call_target="tpu_custom_call" | custom-call | flops 3221225472 | bytes 4194304 | tf_op jit(solution)/shard_map/attention/pallas_call | solution.py:139
  33.5 1.2 %convert_element_type.60 = f16[8,272,256]{2,1,0:T(8,128)(2,1)} convert(f32[8,272,256]{2,1,0:T(8,128)S(1)} %get-tuple-element.29) | non-fusion elementwise | flops 557056 | bytes 3342336 | tf_op jit(solution)/shard_map/convert_element_type | solution.py:394
  34.7 4.8 %all-to-all-start.1 = ((f16[8,272,256]{2,1,0:T(8,128)(2,1)}), f16[8,272,256]{2,1,0:T(8,128)(2,1)}, u32[]{:S(2)}, u32[]{:S(2)}) async-start(f16[8,272,256]{2,1,0:T(8,128)(2,1)} %convert_element_type.60), calls=%async_computation.1 | async-start | bytes 2228224 | tf_op jit(solution)/shard_map/all_to_all | solution.py:394
  39.5 2.2 %collective-permute-done.1.other_ref = bf16[2,256,512]{2,1,0:T(8,128)(2,1)} collective-permute-done((bf16[2,256,512]{2,1,0:T(8,128)(2,1)}, bf16[2,256,512]{2,1,0:T(8,128)(2,1)}, u32[]{:S(2)}, u32[]{:S(2)}) %collective-permute-start.1) | collective-permute-done | bytes 524320 | tf_op jit(solution)/shard_map/ppermute | solution.py:38
  41.8 1.0 copy-done.5
  42.8 3.2 %wide.1 = (f32[2,2,192,512]{3,2,1,0:T(8,128)}, f32[2,392,512]{2,1,0:T(8,128)S(1)}) custom-call(s32[1]{0:T(128)} %bitcast.11.x_ref, bf16[2,768,256]{2,1,0:T(8,128)(2,1)S(1)} %get-tuple-element.26.mine_ref, bf16[2,768,256]{2,1,0:T(8,128)(2,1)S(1)} %copy-done.3, bf16[2,256,512]{2,1,0:T(8,128)(2,1)S(1)} %copy-done.5, ...), custom_call_target="tpu_custom_call" | custom-call | flops 805306368 | bytes 5242880 | tf_op jit(solution)/shard_map/wide/pallas_call | solution.py:201
  46.1 0.2 convert_element_type.61
  46.2 1.1 slice_bitcast_fusion
  47.3 2.8 %collective-permute-start.3 = (f16[392,512]{1,0:T(8,128)(2,1)}, f16[392,512]{1,0:T(8,128)(2,1)S(1)}, u32[]{:S(2)}, u32[]{:S(2)}) collective-permute-start(f16[392,512]{1,0:T(8,128)(2,1)} %get-tuple-element.43), channel_id=1, source_target_pairs={{0,192},{1,193},{2,194},{3,195},{4,196},{5,197},{6,198},{7,199},{8... | collective-permute-start | bytes 1204232 | tf_op jit(solution)/shard_map/ppermute | solution.py:38
  50.1 0.2 collective-permute-start.2
  50.3 4.4 %all-to-all-done.1 = f16[8,272,256]{2,1,0:T(8,128)(2,1)} async-done(((f16[8,272,256]{2,1,0:T(8,128)(2,1)}), f16[8,272,256]{2,1,0:T(8,128)(2,1)}, u32[]{:S(2)}, u32[]{:S(2)}) %all-to-all-start.1) | async-done | bytes 1114144 | tf_op jit(solution)/shard_map/all_to_all | solution.py:394
  54.7 1.4 %convert_element_type.62.terms_ref = f32[8,272,256]{2,1,0:T(8,128)S(1)} convert(f16[8,272,256]{2,1,0:T(8,128)(2,1)} %all-to-all-done.1) | non-fusion elementwise | flops 557056 | bytes 3342336 | tf_op jit(solution)/shard_map/convert_element_type | solution.py:401
  56.2 3.9 %collective-permute-done.3 = f16[392,512]{1,0:T(8,128)(2,1)S(1)} collective-permute-done((f16[392,512]{1,0:T(8,128)(2,1)}, f16[392,512]{1,0:T(8,128)(2,1)S(1)}, u32[]{:S(2)}, u32[]{:S(2)}) %collective-permute-start.3) | collective-permute-done | bytes 401440 | tf_op jit(solution)/shard_map/ppermute | solution.py:38
  60.1 1.4 %collective-permute-done.2 = f16[392,512]{1,0:T(8,128)(2,1)} collective-permute-done((f16[392,512]{1,0:T(8,128)(2,1)}, f16[392,512]{1,0:T(8,128)(2,1)}, u32[]{:S(2)}, u32[]{:S(2)}) %collective-permute-start.2) | collective-permute-done | bytes 401440 | tf_op jit(solution)/shard_map/ppermute | solution.py:38
  61.4 0.1 own_terms.1.own_ref
  61.6 0.1 collective-permute-start.6
  61.7 1.3 %maximum_convert_fusion.got_ref = f32[2,392,512]{2,1,0:T(8,128)S(1)} fusion(f16[1,392,512]{2,1,0:T(8,128)(2,1)S(1)} %bitcast.56, f16[1,392,512]{2,1,0:T(8,128)(2,1)} %bitcast.14), kind=kLoop, calls=%fused_computation.15 | loop fusion | flops 802816 | bytes 2408448 | tf_op jit(solution)/shard_map/convert_element_type | solution.py:406
  63.0 0.1 copy-done.1
  63.1 1.0 middle.1
  64.3 1.5 %collective-permute-start.4 = (f16[200,512]{1,0:T(8,128)(2,1)S(1)}, f16[200,512]{1,0:T(8,128)(2,1)S(1)}, u32[]{:S(2)}, u32[]{:S(2)}) collective-permute-start(f16[200,512]{1,0:T(8,128)(2,1)S(1)} %get-tuple-element.48), channel_id=1, source_target_pairs={{0,192},{1,193},{2,194},{3,195},{4,196},{5,197},{6,198},{7,199},{8... | collective-permute-start | bytes 614408 | tf_op jit(solution)/shard_map/ppermute | solution.py:38
  65.8 1.0 narrow.1.narrow_ref
  66.9 2.1 %collective-permute-start.7 = (f16[200,256]{1,0:T(8,128)(2,1)S(1)}, f16[200,256]{1,0:T(8,128)(2,1)S(1)}, u32[]{:S(2)}, u32[]{:S(2)}) collective-permute-start(f16[200,256]{1,0:T(8,128)(2,1)S(1)} %get-tuple-element.45), channel_id=1, source_target_pairs={{0,64},{1,65},{2,66},{3,67},{4,68},{5,69},{6,70},{7,71},{8,72},{9,... | collective-permute-start | bytes 307208 | tf_op jit(solution)/shard_map/ppermute | solution.py:38
  69.0 1.8 %collective-permute-start.9 = (f16[200,256]{1,0:T(8,128)(2,1)S(1)}, f16[200,256]{1,0:T(8,128)(2,1)S(1)}, u32[]{:S(2)}, u32[]{:S(2)}) collective-permute-start(f16[200,256]{1,0:T(8,128)(2,1)S(1)} %get-tuple-element.46), channel_id=1, source_target_pairs={{0,192},{1,193},{2,194},{3,195},{4,196},{5,197},{6,198},{7,199},{8... | collective-permute-start | bytes 307208 | tf_op jit(solution)/shard_map/ppermute | solution.py:38
  70.8 0.3 collective-permute-start.8
  71.2 2.3 %collective-permute-done.4 = f16[200,512]{1,0:T(8,128)(2,1)S(1)} collective-permute-done((f16[200,512]{1,0:T(8,128)(2,1)S(1)}, f16[200,512]{1,0:T(8,128)(2,1)S(1)}, u32[]{:S(2)}, u32[]{:S(2)}) %collective-permute-start.4) | collective-permute-done | bytes 204832 | tf_op jit(solution)/shard_map/ppermute | solution.py:38
  73.5 0.2 collective-permute-done.5
  73.7 0.1 maximum_convert_fusion.1.wide_got_ref
  73.8 2.1 %collective-permute-done.7 = f16[200,256]{1,0:T(8,128)(2,1)S(1)} collective-permute-done((f16[200,256]{1,0:T(8,128)(2,1)S(1)}, f16[200,256]{1,0:T(8,128)(2,1)S(1)}, u32[]{:S(2)}, u32[]{:S(2)}) %collective-permute-start.7) | collective-permute-done | bytes 102432 | tf_op jit(solution)/shard_map/ppermute | solution.py:38
  75.9 2.6 %collective-permute-done.8 = f16[200,256]{1,0:T(8,128)(2,1)S(1)} collective-permute-done((f16[200,256]{1,0:T(8,128)(2,1)S(1)}, f16[200,256]{1,0:T(8,128)(2,1)S(1)}, u32[]{:S(2)}, u32[]{:S(2)}) %collective-permute-start.8) | collective-permute-done | bytes 102432 | tf_op jit(solution)/shard_map/ppermute | solution.py:38
  78.5 0.5 after_x.1
  79.1 0.9 convert_element_type.70
  79.9 10.7 %all-to-all-start.2 = ((f16[32,64,128]{2,1,0:T(8,128)(2,1)}), f16[32,64,128]{2,1,0:T(8,128)(2,1)S(1)}, u32[]{:S(2)}, u32[]{:S(2)}) async-start(f16[32,64,128]{2,1,0:T(8,128)(2,1)} %convert_element_type.70), calls=%async_computation.2 | async-start | bytes 1048576 | tf_op jit(solution)/shard_map/all_to_all | solution.py:411
  90.7 1.5 %fusion.6 = bf16[1,256,1536]{2,1,0:T(8,128)(2,1)} fusion(bf16[1536,512]{1,0:T(8,128)(2,1)S(1)} %copy-done, bf16[2,256,512]{2,1,0:T(8,128)(2,1)S(1)} %copy-done.6), kind=kOutput, calls=%fused_computation.8 | convolution fusion | flops 403046400 | bytes 2621440 | tf_op jit(solution)/shard_map/dot_general | solution.py:34
  92.2 15.5 %all-to-all-done.2 = f16[32,64,128]{2,1,0:T(8,128)(2,1)S(1)} async-done(((f16[32,64,128]{2,1,0:T(8,128)(2,1)}), f16[32,64,128]{2,1,0:T(8,128)(2,1)S(1)}, u32[]{:S(2)}, u32[]{:S(2)}) %all-to-all-start.2) | async-done | bytes 524320 | tf_op jit(solution)/shard_map/all_to_all | solution.py:411
  107.6 0.1 convert_element_type.71.got_ref
  107.7 0.7 last_sum.1
  (29 shorter events, 0.4 us)
Async XLA Ops:
  0.6 15.7 %copy-start = (bf16[1536,512]{1,0:T(8,128)(2,1)S(1)}, bf16[1536,512]{1,0:T(8,128)(2,1)}, u32[]{:S(2)}) copy-start(bf16[1536,512]{1,0:T(8,128)(2,1)} %param.11) | copy-start | bytes 4718596
  3.7 6.1 %copy-start.7 = (bf16[1,256,1536]{2,1,0:T(8,128)(2,1)S(1)}, bf16[1,256,1536]{2,1,0:T(8,128)(2,1)}, u32[]{:S(2)}) copy-start(bf16[1,256,1536]{2,1,0:T(8,128)(2,1)} %param.7) | copy-start | bytes 2359300
  3.7 6.1 %copy-start.11 = (s32[1536]{0:T(1024)S(1)}, s32[1536]{0:T(1024)}, u32[]{:S(2)}) copy-start(s32[1536]{0:T(1024)} %constant.21.clone) | copy-start | bytes 18436
  3.7 20.3 %all-to-all-start = ((bf16[8,256,256]{2,1,0:T(8,128)(2,1)}), bf16[8,256,256]{2,1,0:T(8,128)(2,1)S(1)}, u32[]{:S(2)}, u32[]{:S(2)}) async-start(bf16[8,256,256]{2,1,0:T(8,128)(2,1)} %project.1), calls=%async_computation | async-start | bytes 2097152 | tf_op jit(solution)/shard_map/all_to_all | solution.py:381
  9.7 1.8 %copy-start.10 = (bf16[1,256,1536]{2,1,0:T(8,128)(2,1)S(1)}, bf16[1,256,1536]{2,1,0:T(8,128)(2,1)}, u32[]{:S(2)}) copy-start(bf16[1,256,1536]{2,1,0:T(8,128)(2,1)} %param.12) | copy-start | bytes 2359300
  13.4 1.1 %copy-start.8 = (bf16[1,256,1536]{2,1,0:T(8,128)(2,1)S(1)}, bf16[1,256,1536]{2,1,0:T(8,128)(2,1)}, u32[]{:S(2)}) copy-start(bf16[1,256,1536]{2,1,0:T(8,128)(2,1)} %param.7) | copy-start | bytes 2359300
  13.4 1.6 %copy-start.9 = (bf16[1536,512]{1,0:T(8,128)(2,1)S(1)}, bf16[1536,512]{1,0:T(8,128)(2,1)}, u32[]{:S(2)}) copy-start(bf16[1536,512]{1,0:T(8,128)(2,1)} %param.8) | copy-start | bytes 4718596
  13.6 4.1 %collective-permute-start = (bf16[2,768,256]{2,1,0:T(8,128)(2,1)S(1)}, bf16[2,768,256]{2,1,0:T(8,128)(2,1)S(1)}, u32[]{:S(2)}, u32[]{:S(2)}) collective-permute-start(bf16[2,768,256]{2,1,0:T(8,128)(2,1)S(1)} %get-tuple-element.41), channel_id=1, source_target_pairs={{0,8},{1,9},{2,10},{3,11},{4,12},{5,13},{6,14},{7,15},{8,0},{9,1},... | collective-permute-start | bytes 2359304 | tf_op jit(solution)/shard_map/ppermute | solution.py:38
  17.6 0.9 copy-start.2
  34.7 7.1 %copy-start.3 = (bf16[2,768,256]{2,1,0:T(8,128)(2,1)S(1)}, bf16[2,768,256]{2,1,0:T(8,128)(2,1)}, u32[]{:S(2)}) copy-start(bf16[2,768,256]{2,1,0:T(8,128)(2,1)} %copy-done.2) | copy-start | bytes 2359300
  34.7 20.0 %all-to-all-start.1 = ((f16[8,272,256]{2,1,0:T(8,128)(2,1)}), f16[8,272,256]{2,1,0:T(8,128)(2,1)}, u32[]{:S(2)}, u32[]{:S(2)}) async-start(f16[8,272,256]{2,1,0:T(8,128)(2,1)} %convert_element_type.60), calls=%async_computation.1 | async-start | bytes 2228224 | tf_op jit(solution)/shard_map/all_to_all | solution.py:394
  39.5 2.3 %collective-permute-start.1 = (bf16[2,256,512]{2,1,0:T(8,128)(2,1)}, bf16[2,256,512]{2,1,0:T(8,128)(2,1)}, u32[]{:S(2)}, u32[]{:S(2)}) collective-permute-start(bf16[2,256,512]{2,1,0:T(8,128)(2,1)} %get-tuple-element.25.own_ref), channel_id=1, source_target_pairs={{0,8},{1,9},{2,10},{3,11},{4,12},{5,13},{6,14},{7,15},{8,0},{9,1},... | collective-permute-start | bytes 1572872 | tf_op jit(solution)/shard_map/ppermute | solution.py:38
  41.8 1.0 copy-start.5
  47.3 12.7 %collective-permute-start.3 = (f16[392,512]{1,0:T(8,128)(2,1)}, f16[392,512]{1,0:T(8,128)(2,1)S(1)}, u32[]{:S(2)}, u32[]{:S(2)}) collective-permute-start(f16[392,512]{1,0:T(8,128)(2,1)} %get-tuple-element.43), channel_id=1, source_target_pairs={{0,192},{1,193},{2,194},{3,195},{4,196},{5,197},{6,198},{7,199},{8... | collective-permute-start | bytes 1204232 | tf_op jit(solution)/shard_map/ppermute | solution.py:38
  50.1 11.4 %collective-permute-start.2 = (f16[392,512]{1,0:T(8,128)(2,1)}, f16[392,512]{1,0:T(8,128)(2,1)}, u32[]{:S(2)}, u32[]{:S(2)}) collective-permute-start(f16[392,512]{1,0:T(8,128)(2,1)} %get-tuple-element.44), channel_id=1, source_target_pairs={{0,64},{1,65},{2,66},{3,67},{4,68},{5,69},{6,70},{7,71},{8,72},{9,... | collective-permute-start | bytes 1204232 | tf_op jit(solution)/shard_map/ppermute | solution.py:38
  61.6 1.5 %copy-start.1 = (f32[2,2,192,512]{3,2,1,0:T(8,128)S(1)}, f32[2,2,192,512]{3,2,1,0:T(8,128)}, u32[]{:S(2)}) copy-start(f32[2,2,192,512]{3,2,1,0:T(8,128)} %get-tuple-element.28.keep_ref) | copy-start | bytes 4718596
  61.6 4.2 %collective-permute-start.6 = (f32[256,256]{1,0:T(8,128)S(1)}, f32[256,256]{1,0:T(8,128)S(1)}, u32[]{:S(2)}, u32[]{:S(2)}) collective-permute-start(f32[256,256]{1,0:T(8,128)S(1)} %own_terms.1.own_ref), channel_id=1, source_target_pairs={{0,8},{1,9},{2,10},{3,11},{4,12},{5,13},{6,14},{7,15},{8,0},{9,1},... | collective-permute-start | bytes 786440 | tf_op jit(solution)/shard_map/ppermute | solution.py:38
  64.3 9.2 %collective-permute-start.4 = (f16[200,512]{1,0:T(8,128)(2,1)S(1)}, f16[200,512]{1,0:T(8,128)(2,1)S(1)}, u32[]{:S(2)}, u32[]{:S(2)}) collective-permute-start(f16[200,512]{1,0:T(8,128)(2,1)S(1)} %get-tuple-element.48), channel_id=1, source_target_pairs={{0,192},{1,193},{2,194},{3,195},{4,196},{5,197},{6,198},{7,199},{8... | collective-permute-start | bytes 614408 | tf_op jit(solution)/shard_map/ppermute | solution.py:38
  65.8 7.9 %collective-permute-start.5 = (f16[200,512]{1,0:T(8,128)(2,1)S(1)}, f16[200,512]{1,0:T(8,128)(2,1)S(1)}, u32[]{:S(2)}, u32[]{:S(2)}) collective-permute-start(f16[200,512]{1,0:T(8,128)(2,1)S(1)} %get-tuple-element.49), channel_id=1, source_target_pairs={{0,64},{1,65},{2,66},{3,67},{4,68},{5,69},{6,70},{7,71},{8,72},{9,... | collective-permute-start | bytes 614408 | tf_op jit(solution)/shard_map/ppermute | solution.py:38
  66.8 11.7 %copy-start.4 = (f32[2,192,512]{2,1,0:T(8,128)S(1)}, f32[2,192,512]{2,1,0:T(8,128)}, u32[]{:S(2)}) copy-start(f32[2,192,512]{2,1,0:T(8,128)} %get-tuple-element.34.wide_ref) | copy-start | bytes 2359300
  66.9 9.0 %collective-permute-start.7 = (f16[200,256]{1,0:T(8,128)(2,1)S(1)}, f16[200,256]{1,0:T(8,128)(2,1)S(1)}, u32[]{:S(2)}, u32[]{:S(2)}) collective-permute-start(f16[200,256]{1,0:T(8,128)(2,1)S(1)} %get-tuple-element.45), channel_id=1, source_target_pairs={{0,64},{1,65},{2,66},{3,67},{4,68},{5,69},{6,70},{7,71},{8,72},{9,... | collective-permute-start | bytes 307208 | tf_op jit(solution)/shard_map/ppermute | solution.py:38
  69.0 6.9 %collective-permute-start.9 = (f16[200,256]{1,0:T(8,128)(2,1)S(1)}, f16[200,256]{1,0:T(8,128)(2,1)S(1)}, u32[]{:S(2)}, u32[]{:S(2)}) collective-permute-start(f16[200,256]{1,0:T(8,128)(2,1)S(1)} %get-tuple-element.46), channel_id=1, source_target_pairs={{0,192},{1,193},{2,194},{3,195},{4,196},{5,197},{6,198},{7,199},{8... | collective-permute-start | bytes 307208 | tf_op jit(solution)/shard_map/ppermute | solution.py:38
  70.8 7.6 %collective-permute-start.8 = (f16[200,256]{1,0:T(8,128)(2,1)S(1)}, f16[200,256]{1,0:T(8,128)(2,1)S(1)}, u32[]{:S(2)}, u32[]{:S(2)}) collective-permute-start(f16[200,256]{1,0:T(8,128)(2,1)S(1)} %get-tuple-element.47), channel_id=1, source_target_pairs={{0,128},{1,129},{2,130},{3,131},{4,132},{5,133},{6,134},{7,135},{8... | collective-permute-start | bytes 307208 | tf_op jit(solution)/shard_map/ppermute | solution.py:38
  79.0 11.6 %copy-start.6 = (bf16[2,256,512]{2,1,0:T(8,128)(2,1)S(1)}, bf16[2,256,512]{2,1,0:T(8,128)(2,1)}, u32[]{:S(2)}) copy-start(bf16[2,256,512]{2,1,0:T(8,128)(2,1)} %get-tuple-element.25.own_ref) | copy-start | bytes 1572868
  79.9 27.7 %all-to-all-start.2 = ((f16[32,64,128]{2,1,0:T(8,128)(2,1)}), f16[32,64,128]{2,1,0:T(8,128)(2,1)S(1)}, u32[]{:S(2)}, u32[]{:S(2)}) async-start(f16[32,64,128]{2,1,0:T(8,128)(2,1)} %convert_element_type.70), calls=%async_computation.2 | async-start | bytes 1048576 | tf_op jit(solution)/shard_map/all_to_all | solution.py:411

commit v3 on v1

v3 whole, which is shorter than its diff:
```python
import functools

import jax
import jax.numpy as jnp
from jax import lax
from jax.experimental import pallas as pl
from jax.experimental.pallas import tpu as pltpu
from jax.sharding import PartitionSpec as P

HEADS = 4
HD = 128
SCALE = HD ** (-0.5)
LOG2_E = 1.4426950408889634
AXES = ("dp", "seq")
MIB = 1024 * 1024


def place(x, y, z, core):
    return x * 64 + (z >> 1) * 16 + core * 8 + (z & 1) * 4 + y


Z_HI_GROUPS = [
    [place(x, y, 2 * z + low, c) for z in range(4)] for x in range(4) for y in range(4) for low in range(2) for c in range(2)
]


def dot(left, right, dims):
    return lax.dot_general(left, right, (dims, ((), ())), preferred_element_type=jnp.float32)


def exchange(value, mask):
    return lax.ppermute(value, AXES, [(i, i ^ mask) for i in range(256)])


def from_other_core(value):
    return exchange(value, 8)


def exponent(values):
    top = jnp.max(jnp.max(jnp.abs(values), axis=0, keepdims=True), axis=1, keepdims=True)
    return jnp.ceil(jnp.log2(jnp.maximum(top, 1e-30))) - 13.0


def unscaled(ref, block, values, exponents):
    return ref[block, values, :] * jnp.exp2(ref[block, exponents, :])


def project_kernel(hidden_ref, w_key_ref, w_value_ref, out_ref):
    hidden = hidden_ref[...]
    for i, ref in enumerate((w_key_ref, w_value_ref)):
        block = dot(hidden, ref[...], ((1,), (0,))).astype(jnp.bfloat16)
        for b in range(out_ref.shape[0]):
            out_ref[b, :, i * HD : (i + 1) * HD] = block


def project(hidden, w_key, w_value):
    hidden, w_key, w_value = (pltpu.with_memory_space_constraint(v, pltpu.HBM) for v in (hidden, w_key, w_value))
    return pl.pallas_call(
        project_kernel,
        out_shape=jax.ShapeDtypeStruct((8, hidden.shape[0], 2 * HD), jnp.bfloat16),
        compiler_params=pltpu.CompilerParams(vmem_limit_bytes=16 * MIB),
        name="project",
    )(hidden, w_key, w_value)


def turn_kernel(pieces, place_ref, side_ref, *refs):
    turned_ref = refs[-1]
    turned_ref[...] = side_ref[...].T
    for ref, (far, masks) in zip(refs, pieces):
        for i, mask in enumerate(masks):
            for z_hi in range(4):
                start = 384 * (place_ref[0] ^ mask) + 96 * z_hi + 48 * (place_ref[1] ^ far)
                first = 192 * i + 48 * z_hi
                ref[first : first + 48, :] = turned_ref[pl.ds(pl.multiple_of(start, 16), 48), :]


def turn(place, side, pieces):
    tokens, width = side.shape
    shapes = [(len(masks) * width // 8, tokens) for _, masks in pieces]
    return pl.pallas_call(
        functools.partial(turn_kernel, pieces),
        grid_spec=pltpu.PrefetchScalarGridSpec(
            num_scalar_prefetch=1,
            grid=(1,),
            in_specs=[pl.BlockSpec((tokens, width), lambda i, place: (0, 0))],
            out_specs=[pl.BlockSpec(shape, lambda i, place: (0, 0)) for shape in shapes],
            scratch_shapes=[pltpu.VMEM((width, tokens), side.dtype)],
        ),
        out_shape=[jax.ShapeDtypeStruct(shape, side.dtype) for shape in shapes],
        compiler_params=pltpu.CompilerParams(vmem_limit_bytes=12 * MIB),
        name="turn",
    )(place, side)


def attention_kernel(q_ref, da_ref, k_ref, v_ref, d_query_ref, attended_ref, dkv_ref):
    step = pl.program_id(0)
    keys = k_ref[...]
    values = v_ref[...]
    bf = jnp.bfloat16
    heads = range(q_ref.shape[1] // HD)
    q = [q_ref[:, h * HD : (h + 1) * HD] for h in heads]
    da = [da_ref[:, h * HD : (h + 1) * HD] for h in heads]

    def softmax(scores):
        shifted = jnp.exp2((scores - jnp.max(scores, axis=1, keepdims=True)) * (SCALE * LOG2_E))
        return shifted * (1.0 / jnp.sum(shifted, axis=1, keepdims=True))

    scores = [dot(q[h], keys, ((1,), (1,))) for h in heads]
    probs, probs_b, d_probs, d_scores = [], [], [], []
    for h in heads:
        probs.append(softmax(scores[h]))
        probs_b.append(probs[h].astype(bf))
        d_probs.append(dot(da[h], values, ((1,), (1,))))
    d_value = None
    for h in heads:
        attended_ref[:, h * HD : (h + 1) * HD] = dot(probs_b[h], values, ((1,), (0,))).astype(bf)
        term = dot(da[h], probs_b[h], ((0,), (0,)))
        d_value = term if d_value is None else d_value + term
        delta = jnp.sum(d_probs[h] * probs[h], axis=1, keepdims=True)
        d_scores.append((probs[h] * (d_probs[h] - delta)).astype(bf))
    d_key = None
    for h in heads:
        d_query_ref[:, h * HD : (h + 1) * HD] = (dot(d_scores[h], keys, ((1,), (0,))) * SCALE).astype(bf)
        term = dot(q[h], d_scores[h], ((0,), (0,)))
        d_key = term if d_key is None else d_key + term
    blocks, _, tokens = dkv_ref.shape

    @pl.when(step == 0)
    def _():
        for b in range(blocks):
            dkv_ref[b, :HD, :] = d_key[:, b * tokens : (b + 1) * tokens]
            dkv_ref[b, HD : 2 * HD, :] = d_value[:, b * tokens : (b + 1) * tokens]

    @pl.when(step != 0)
    def _():
        for b in range(blocks):
            dkv_ref[b, :HD, :] += d_key[:, b * tokens : (b + 1) * tokens]
            dkv_ref[b, HD : 2 * HD, :] += d_value[:, b * tokens : (b + 1) * tokens]

    @pl.when(step == pl.num_programs(0) - 1)
    def _():
        for i, scale in enumerate((SCALE, 1.0)):
            rows = pl.ds(i * HD, HD)
            top = jnp.abs(dkv_ref[0, rows, :])
            for b in range(1, blocks):
                top = jnp.maximum(top, jnp.abs(dkv_ref[b, rows, :]))
            power = exponent(top * scale)
            factor = jnp.exp2(-power) * scale
            for b in range(blocks):
                dkv_ref[b, rows, :] = dkv_ref[b, rows, :] * factor
                dkv_ref[b, pl.ds(2 * HD + 8 * i, 8), :] = jnp.broadcast_to(power, (8, tokens))


def attention(queries, d_att, keys_values):
    tokens, inner = queries.shape
    length = keys_values.shape[0]
    by_pair = pl.BlockSpec((tokens, 2 * HD), lambda j: (0, j))
    terms = (length // tokens, 2 * HD + 16, tokens)
    return pl.pallas_call(
        attention_kernel,
        grid=(HEADS // 2,),
        in_specs=[
            by_pair,
            by_pair,
            pl.BlockSpec((length, HD), lambda j: (0, 0)),
            pl.BlockSpec((length, HD), lambda j: (0, 1)),
        ],
        out_specs=[
            by_pair,
            by_pair,
            pl.BlockSpec(terms, lambda j: (0, 0, 0)),
        ],
        out_shape=[
            pltpu.HBM((tokens, inner), jnp.bfloat16),
            pltpu.HBM((tokens, inner), jnp.bfloat16),
            jax.ShapeDtypeStruct(terms, jnp.float32),
        ],
        compiler_params=pltpu.CompilerParams(vmem_limit_bytes=32 * MIB),
        cost_estimate=pl.CostEstimate(
            flops=12 * tokens * inner * length, bytes_accessed=4 << 20, transcendentals=tokens * HEADS * length
        ),
        name="attention",
    )(queries, d_att, keys_values, keys_values)


def store_scaled(values, ref):
    power = exponent(values)
    ref[:-8, :] = values * jnp.exp2(-power)
    ref[-8:, :] = jnp.broadcast_to(power, (8, values.shape[1]))


def wide_kernel(*refs):
    keep_ref, *send_refs = refs[16:]
    rows, cols = keep_ref.shape[0], send_refs[0].shape[1]
    for i in range(2):
        product = None
        for side_ref, factor_ref in zip(refs[8 * i : 8 * i + 4], refs[8 * i + 4 : 8 * i + 8]):
            term = dot(side_ref[: 2 * rows], factor_ref[...], ((1,), (0,)))
            product = term if product is None else product + term
        keep_ref[:, i * cols : (i + 1) * cols] = product[:rows]
        store_scaled(product[rows:], send_refs[i])


def wide_products(query, out):
    rows = out[0].shape[0] // 2
    cols = out[4].shape[1]
    query, out = (v[:4] + [pltpu.with_memory_space_constraint(f, pltpu.HBM) for f in v[4:]] for v in (query, out))
    return pl.pallas_call(
        wide_kernel,
        out_shape=[
            pltpu.HBM((rows, 2 * cols), jnp.float32),
            jax.ShapeDtypeStruct((rows + 8, cols), jnp.float32),
            jax.ShapeDtypeStruct((rows + 8, cols), jnp.float32),
        ],
        compiler_params=pltpu.CompilerParams(vmem_limit_bytes=20 * MIB),
        cost_estimate=pl.CostEstimate(flops=1 << 30, bytes_accessed=5 << 20, transcendentals=0),
        name="wide",
    )(*query, *out)


def narrow_kernel(mine_ref, theirs_ref, own_ref, other_ref, keep_ref, three_ref, one_ref, two_ref):
    product = None
    for side_ref, terms_ref in ((mine_ref, own_ref), (theirs_ref, other_ref)):
        side = side_ref[...]
        rest = terms_ref[...]
        for _ in range(2):
            piece = rest.astype(jnp.bfloat16)
            rest = rest - piece.astype(jnp.float32)
            term = dot(side, piece, ((1,), (1,)))
            product = term if product is None else product + term
    rows = keep_ref.shape[0]
    keep_ref[...] = product[:rows]
    powers = [jnp.broadcast_to(exponent(product[:, i * HD : (i + 1) * HD]), (8, HD)) for i in range(2)]
    power = jnp.concatenate(powers, axis=1)
    factor = jnp.exp2(-power[:1])
    for i, ref in enumerate((three_ref, one_ref, two_ref)):
        ref[:rows, :] = product[(i + 1) * rows : (i + 2) * rows] * factor
        ref[rows:, :] = power


def narrow_products(mine, theirs, own, other):
    rows = mine.shape[0] // 4
    cols = own.shape[0]
    sent = jax.ShapeDtypeStruct((rows + 8, cols), jnp.float32)
    return pl.pallas_call(
        narrow_kernel,
        out_shape=[pltpu.HBM((rows, cols), jnp.float32), sent, sent, sent],
        compiler_params=pltpu.CompilerParams(vmem_limit_bytes=16 * MIB),
        cost_estimate=pl.CostEstimate(flops=1, bytes_accessed=1, transcendentals=0),
        name="narrow",
    )(mine, theirs, own, other)


def own_terms_kernel(terms_ref, out_ref):
    for i in range(2):
        rows, powers = pl.ds(i * HD, HD), pl.ds(2 * HD + 8 * i, 1)
        total = unscaled(terms_ref, 0, rows, powers)
        for b in range(1, terms_ref.shape[0]):
            total = total + unscaled(terms_ref, b, rows, powers)
        out_ref[rows, :] = total


def own_terms(terms):
    return pl.pallas_call(
        own_terms_kernel,
        out_shape=jax.ShapeDtypeStruct((2 * HD, terms.shape[2]), jnp.float32),
        compiler_params=pltpu.CompilerParams(vmem_limit_bytes=8 * MIB),
        cost_estimate=pl.CostEstimate(flops=1, bytes_accessed=1, transcendentals=0),
        name="own_terms",
    )(terms)


def after_x_kernel(wide_ref, wide_got_ref, narrow_ref, narrow_got_ref, out_ref, total_ref):
    rows = wide_ref.shape[0]
    cols = 4 * HD
    scaled = lambda ref, i, here: ref[i, :rows, here] * jnp.exp2(ref[i, rows : rows + 1, here])
    for i, (first, width) in enumerate(((0, cols), (cols, cols), (2 * cols, HD), (2 * cols + HD, HD))):
        if i < 2:
            total = wide_ref[:, first : first + width] + scaled(wide_got_ref, i, pl.ds(0, cols))
        else:
            here = pl.ds(first - 2 * cols, HD)
            total = narrow_ref[:, here]
            for m in range(3):
                total = total + scaled(narrow_got_ref, m, here)
        top = exponent(total)
        total_ref[:, first : first + width] = total * jnp.exp2(-top)
        out_ref[:, 240 + i, :] = jnp.broadcast_to(top, (out_ref.shape[0], HD))
    out_ref[:, 244:, :] = jnp.zeros((out_ref.shape[0], 4, HD), jnp.float32)
    for k in range(out_ref.shape[0]):
        for j in range(10):
            for z_hi in range(4):
                to, start = 24 * j + 6 * z_hi, 48 * z_hi + 6 * k
                out_ref[k, to : to + 6, :] = total_ref[start : start + 6, j * HD : (j + 1) * HD]


def after_x(wide, wide_got, narrow, narrow_got):
    rows, cols = wide.shape
    shape = (rows // 24, 248, HD)
    return pl.pallas_call(
        after_x_kernel,
        out_shape=jax.ShapeDtypeStruct(shape, jnp.float32),
        scratch_shapes=[pltpu.VMEM((rows, cols + narrow.shape[1]), jnp.float32)],
        compiler_params=pltpu.CompilerParams(vmem_limit_bytes=16 * MIB),
        name="after_x",
    )(wide, wide_got, narrow, narrow_got)


def after_seq_kernel(got_ref, out_ref, total_ref):
    for i, (first, count) in enumerate(((0, 96), (96, 96), (192, 24), (216, 24))):
        rows = pl.ds(first, count)
        total = unscaled(got_ref, 0, rows, pl.ds(240 + i, 1))
        for b in range(1, got_ref.shape[0]):
            total = total + unscaled(got_ref, b, rows, pl.ds(240 + i, 1))
        total_ref[rows, :] = total
    for k in range(4):
        for j in range(10):
            out_ref[k, 6 * j : 6 * j + 6, :] = total_ref[24 * j + 6 * k : 24 * j + 6 * k + 6, :]
        out_ref[k, 60:, :] = jnp.zeros((4, HD), jnp.float32)


def after_seq(got):
    return pl.pallas_call(
        after_seq_kernel,
        out_shape=jax.ShapeDtypeStruct((4, 64, HD), jnp.float32),
        scratch_shapes=[pltpu.VMEM((240, HD), jnp.float32)],
        compiler_params=pltpu.CompilerParams(vmem_limit_bytes=8 * MIB),
        name="after_seq",
    )(got)


def last_sum_kernel(got_ref, query_ref, out_ref, key_ref, value_ref):
    total = (got_ref[0] + got_ref[1]) + (got_ref[2] + got_ref[3])
    first = 0
    for ref in (query_ref, out_ref, key_ref, value_ref):
        for j in range(ref.shape[1] // HD):
            ref[:, j * HD : (j + 1) * HD] = total[first : first + 6]
            first += 6


def last_sum(got):
    shape = lambda cols: jax.ShapeDtypeStruct((6, cols), jnp.float32)
    return pl.pallas_call(
        last_sum_kernel,
        out_shape=[shape(4 * HD), shape(4 * HD), shape(HD), shape(HD)],
        compiler_params=pltpu.CompilerParams(vmem_limit_bytes=8 * MIB),
        name="last_sum",
    )(got)


def local(normed, w_query, w_key, w_value, w_out, cotangent):
    hidden = normed[0]
    grads_in = cotangent[0]
    tokens = hidden.shape[0]
    bf, half = jnp.bfloat16, jnp.float16
    dp = lax.axis_index("dp")
    x, core = dp >> 3, dp & 1
    f32 = jnp.float32

    gathered = lax.all_to_all(project(hidden, w_key, w_value), "seq", 0, 0, tiled=True)

    queries = dot(hidden, w_query, ((1,), (0,))).astype(bf)
    d_att = dot(grads_in, w_out, ((1,), (0,))).astype(bf)
    place_now = jnp.stack([x, core])
    h, h_core, *h_far = turn(place_now, hidden, ((0, (0, 3, 1, 2)), (1, (0, 3, 1, 2)), (0, (1, 2)), (1, (1, 2))))
    g, g_core, *g_far = turn(place_now, grads_in, ((0, (0, 1)), (1, (0, 1)), (0, (3, 2)), (1, (3, 2))))
    h_from = [exchange(h_far[0], 1 << 6), exchange(h_far[1], (1 << 6) | 8)]
    g_from = [exchange(g_far[0], 3 << 6), exchange(g_far[1], (3 << 6) | 8)]
    h_core, g_core = from_other_core(h_core), from_other_core(g_core)

    queries, d_att = (pltpu.with_memory_space_constraint(v, pltpu.HBM) for v in (queries, d_att))
    d_query, attended, terms = attention(queries, d_att, gathered.reshape(8 * tokens, 2 * HD))
    terms, d_query, attended, h_from, g_from, h_core, g_core = lax.optimization_barrier(
        (terms, d_query, attended, h_from, g_from, h_core, g_core)
    )
    terms = lax.all_to_all(terms.astype(half), "seq", 0, 0, tiled=True)

    def factors(own, first):
        beside = exchange(own, first << 6)
        return [own, from_other_core(own), beside, from_other_core(beside)]

    keep, *sent = wide_products(
        [h, h_core, *h_from] + factors(d_query, 1),
        [g, g_core, *g_from] + factors(attended, 3),
    )
    sent = [block.astype(half) for block in sent]
    wide_got = [exchange(block, m << 6) for m, block in zip((3, 1), sent)]
    branch = dot(attended, w_out, ((1,), (1,))).astype(bf)

    terms, _, branch = lax.optimization_barrier((terms, sent, branch))
    d_kv = own_terms(terms.astype(f32))
    narrow, *sent = narrow_products(h, h_core, d_kv, from_other_core(d_kv))
    narrow_got = [exchange(block.astype(half), m << 6) for m, block in zip((3, 1, 2), sent)]

    part = after_x(keep, jnp.stack(wide_got).astype(f32), narrow, jnp.stack(narrow_got).astype(f32))
    part = after_seq(lax.all_to_all(part.astype(half), "seq", 0, 0, tiled=True).astype(f32))
    part = lax.all_to_all(part, AXES, 0, 0, axis_index_groups=Z_HI_GROUPS, tiled=True)
    grad_query, grad_out, grad_key, grad_value = last_sum(part)
    return branch[None], grad_query, grad_key, grad_value, grad_out


def solution(mesh):
    return jax.shard_map(
        local,
        mesh=mesh,
        in_specs=(P("dp", "seq", None), P(), P(), P(), P(), P("dp", "seq", None)),
        out_specs=(
            P("dp", "seq", None),
            P(("dp", "seq"), None),
            P(("dp", "seq"), None),
            P(("dp", "seq"), None),
            P(("dp", "seq"), None),
        ),
        check_vma=False,
    )
```

time: 115 us -> 103 us (0.90)
  waiting for transfers between devices: 47.1 us -> 14.2 us
  blocking collectives: 0 us -> 29.7 us
  local copies, waits for them, and re-layouts: 9.47 us -> 1.03 us
  Pallas kernels: 14.4 us -> 22.2 us
  matrix products: 8.85 us -> 4.03 us
  starting transfers between devices: 28.8 us -> 27.3 us
  other arithmetic: 4.57 us -> 3.1 us
    all_to_all x0 -> x2, blocking collectives: none -> 29.7 us  [the longest x1 15.9 us: local(): lax.all_to_all(part, AXES, 0, 0, axis_index_groups=Z_HI_GROUPS, tiled=True)]
    all_to_all x2 -> x1, waiting for transfers between devices: 21.6 us -> 2.89 us  [local(): lax.all_to_all(project(hidden, w_key, w_value), 'seq', 0, 0, tiled=True)]
    all_to_all x2 -> x1, starting transfers between devices: 15.6 us -> 6.1 us  [local(): lax.all_to_all(project(hidden, w_key, w_value), 'seq', 0, 0, tiled=True)]
    ppermute x9 -> x18, waiting for transfers between devices: 19.4 us -> 11.3 us  [exchange(): return lax.ppermute(value, AXES, [(i, i ^ mask) for i in range(256)])]
    ppermute x9 -> x18, starting transfers between devices: 8.42 us -> 16.4 us  [exchange(): return lax.ppermute(value, AXES, [(i, i ^ mask) for i in range(256)])]
    pallas_call x3 -> x7, Pallas kernels: 4.35 us -> 11.5 us  [the longest x1 3.49 us: wide_products(): pl.pallas_call(wide_kernel, out_shape=[pltpu.HBM((rows, 2 * cols), jnp.fl...]
    all_to_all x1, waiting for transfers between devices: 6.09 us -> 0.01 us  [local(): terms = lax.all_to_all(terms.astype(half), 'seq', 0, 0, tiled=True)]
    unnamed x30, local copies, waits for them, and re-layouts: 7.03 us -> 1.03 us
  transfers between devices with their start and end apart: 12 -> 20, of which waited for: 9 -> 8; matrix products, arithmetic and copies ran while one was open for 8% -> 4% of each run, Pallas kernels for 3% -> 17%
where the time goes in v3:
time: 103 us; the launch traced here: 102 us
  blocking collectives  29.7 us (29%)
  starting transfers between devices  27.3 us (27%)
  Pallas kernels  22.2 us (22%)
  waiting for transfers between devices  14.2 us (14%)
  matrix products  4.03 us (4%)
  other arithmetic  3.1 us (3%)
  local copies, waits for them, and re-layouts  1.03 us (1%)
    ppermute x18, starting transfers between devices, exchange(): return lax.ppermute(value, AXES, [(i, i ^ mask) for i in range(256)])  16.4 us
    all_to_all x1, blocking collectives, local(): lax.all_to_all(part, AXES, 0, 0, axis_index_groups=Z_HI_GROUPS, tiled=True)  15.9 us
    all_to_all x1, blocking collectives, local(): lax.all_to_all(part.astype(half), 'seq', 0, 0, tiled=True).astype(f32)  13.9 us
    ppermute x18, waiting for transfers between devices, exchange(): return lax.ppermute(value, AXES, [(i, i ^ mask) for i in range(256)])  11.3 us
    pallas_call x1, Pallas kernels, attention(): pl.pallas_call(attention_kernel, grid=(HEADS // 2,), in_specs=[by_pair, b...  9.9 us
    all_to_all x1, starting transfers between devices, local(): lax.all_to_all(project(hidden, w_key, w_value), 'seq', 0, 0, tiled=True)  6.1 us
    all_to_all x1, starting transfers between devices, local(): terms = lax.all_to_all(terms.astype(half), 'seq', 0, 0, tiled=True)  4.83 us
    dot_general x3, matrix products, dot(): lax.dot_general(left, right, (dims, ((), ())), preferred_element_type=jnp...  4.03 us
  transfers between devices with their start and end apart: 20, of which 8 were waited for; matrix products, arithmetic and copies ran while one was open for 4% of the time, Pallas kernels for 17%

profile of v3, /device:TPU:32, one launch (start us, length us, event | category | flops | bytes accessed | tf_op | source)
XLA Modules:
  0.0 102.4 jit_solution(13814694151426905207)
XLA Ops:
  0.6 3.0 %project.1 = bf16[8,256,256]{2,1,0:T(8,128)(2,1)} custom-call(bf16[256,1536]{1,0:T(8,128)(2,1)} %bitcast.19, bf16[1536,128]{1,0:T(8,128)(2,1)} %w_key_ref.1, bf16[1536,128]{1,0:T(8,128)(2,1)} %w_value_ref.1), custom_call_target="tpu_custom_call" | custom-call | tf_op jit(solution)/shard_map/project/pallas_call | solution.py:58
  3.7 6.1 %all-to-all-start = ((bf16[8,256,256]{2,1,0:T(8,128)(2,1)}), bf16[8,256,256]{2,1,0:T(8,128)(2,1)}, u32[]{:S(2)}, u32[]{:S(2)}) async-start(bf16[8,256,256]{2,1,0:T(8,128)(2,1)} %project.1), calls=%async_computation | async-start | bytes 2097152 | tf_op jit(solution)/shard_map/all_to_all | solution.py:359
  9.8 0.1 pad_add_fusion.place_ref
  9.8 1.6 %turn.3 = (bf16[384,256]{1,0:T(8,128)(2,1)S(1)}, bf16[384,256]{1,0:T(8,128)(2,1)}, bf16[384,256]{1,0:T(8,128)(2,1)S(1)}, bf16[384,256]{1,0:T(8,128)(2,1)}) custom-call(s32[2]{0:T(128)S(1)} %pad_add_fusion.place_ref, bf16[256,1536]{1,0:T(8,128)(2,1)S(1)} %bitcast.21), custom_call_target="tpu_custom_call" | custom-call | tf_op jit(solution)/shard_map/turn/pallas_call | solution.py:80
  11.4 2.7 %collective-permute-start.2 = (bf16[384,256]{1,0:T(8,128)(2,1)S(1)}, bf16[384,256]{1,0:T(8,128)(2,1)S(1)}, u32[]{:S(2)}, u32[]{:S(2)}) collective-permute-start(bf16[384,256]{1,0:T(8,128)(2,1)S(1)} %get-tuple-element.43), channel_id=1, source_target_pairs={{0,192},{1,193},{2,194},{3,195},{4,196},{5,197},{6,198},{7,199},{8... | collective-permute-start | bytes 589832 | tf_op jit(solution)/shard_map/ppermute | solution.py:32
  14.2 0.6 collective-permute-start.5
  14.8 1.7 %turn.2 = (bf16[768,256]{1,0:T(8,128)(2,1)S(1)}, bf16[768,256]{1,0:T(8,128)(2,1)}, bf16[384,256]{1,0:T(8,128)(2,1)}, bf16[384,256]{1,0:T(8,128)(2,1)}) custom-call(s32[2]{0:T(128)S(1)} %pad_add_fusion.place_ref, bf16[256,1536]{1,0:T(8,128)(2,1)S(1)} %bitcast.20), custom_call_target="tpu_custom_call" | custom-call | tf_op jit(solution)/shard_map/turn/pallas_call | solution.py:80
  16.5 0.2 collective-permute-start
  16.7 1.3 %convolution_convert_fusion.2.q_ref = bf16[256,512]{1,0:T(8,128)(2,1)} fusion(bf16[1536,512]{1,0:T(8,128)(2,1)S(1)} %copy-done.14, bf16[1,256,1536]{2,1,0:T(8,128)(2,1)S(1)} %copy-done.1), kind=kOutput, calls=%fused_computation.2 | convolution fusion | flops 402784256 | bytes 2621440 | tf_op jit(solution)/shard_map/dot_general | solution.py:28
  18.0 1.3 %convolution_convert_fusion.1.da_ref = bf16[256,512]{1,0:T(8,128)(2,1)} fusion(bf16[1536,512]{1,0:T(8,128)(2,1)S(1)} %copy-done, bf16[1,256,1536]{2,1,0:T(8,128)(2,1)S(1)} %copy-done.3), kind=kOutput, calls=%fused_computation.1 | convolution fusion | flops 402784256 | bytes 2621440 | tf_op jit(solution)/shard_map/dot_general | solution.py:28
  19.3 0.2 collective-permute-done.2.refs_10_
  19.5 1.7 %collective-permute-start.1 = (bf16[384,256]{1,0:T(8,128)(2,1)}, bf16[384,256]{1,0:T(8,128)(2,1)S(1)}, u32[]{:S(2)}, u32[]{:S(2)}) collective-permute-start(bf16[384,256]{1,0:T(8,128)(2,1)} %get-tuple-element.42), channel_id=1, source_target_pairs={{0,72},{1,73},{2,74},{3,75},{4,76},{5,77},{6,78},{7,79},{8,64},{9,... | collective-permute-start | bytes 589832 | tf_op jit(solution)/shard_map/ppermute | solution.py:32
  21.2 2.9 %all-to-all-done = bf16[8,256,256]{2,1,0:T(8,128)(2,1)} async-done(((bf16[8,256,256]{2,1,0:T(8,128)(2,1)}), bf16[8,256,256]{2,1,0:T(8,128)(2,1)}, u32[]{:S(2)}, u32[]{:S(2)}) %all-to-all-start) | async-done | bytes 1048608 | tf_op jit(solution)/shard_map/all_to_all | solution.py:359
  24.1 9.9 %attention.1 = (bf16[256,512]{1,0:T(8,128)(2,1)}, bf16[256,512]{1,0:T(8,128)(2,1)}, f32[8,272,256]{2,1,0:T(8,128)S(1)}) custom-call(bf16[256,512]{1,0:T(8,128)(2,1)} %convolution_convert_fusion.2.q_ref, bf16[256,512]{1,0:T(8,128)(2,1)} %convolution_convert_fusion.1.da_ref, bf16[2048,256]{1,0:T(8,128)(2,1)} %bitcast.2.k_ref.v_ref, ...), custom_call_target="tpu_custom_call" | custom-call | flops 3221225472 | bytes 4194304 | tf_op jit(solution)/shard_map/attention/pallas_call | solution.py:159
  34.0 1.2 %convert_element_type.44 = f16[8,272,256]{2,1,0:T(8,128)(2,1)} convert(f32[8,272,256]{2,1,0:T(8,128)S(1)} %get-tuple-element.47) | non-fusion elementwise | flops 557056 | bytes 3342336 | tf_op jit(solution)/shard_map/convert_element_type | solution.py:375
  35.2 4.8 %all-to-all-start.1 = ((f16[8,272,256]{2,1,0:T(8,128)(2,1)}), f16[8,272,256]{2,1,0:T(8,128)(2,1)}, u32[]{:S(2)}, u32[]{:S(2)}) async-start(f16[8,272,256]{2,1,0:T(8,128)(2,1)} %convert_element_type.44), calls=%async_computation.1 | async-start | bytes 2228224 | tf_op jit(solution)/shard_map/all_to_all | solution.py:375
  40.0 1.5 %collective-permute-start.7 = (bf16[256,512]{1,0:T(8,128)(2,1)S(1)}, bf16[256,512]{1,0:T(8,128)(2,1)S(1)}, u32[]{:S(2)}, u32[]{:S(2)}) collective-permute-start(bf16[256,512]{1,0:T(8,128)(2,1)S(1)} %copy-done.7), channel_id=1, source_target_pairs={{0,64},{1,65},{2,66},{3,67},{4,68},{5,69},{6,70},{7,71},{8,72},{9,... | collective-permute-start | bytes 786440 | tf_op jit(solution)/shard_map/ppermute | solution.py:32
  41.5 2.1 %collective-permute-start.10 = (bf16[256,512]{1,0:T(8,128)(2,1)S(1)}, bf16[256,512]{1,0:T(8,128)(2,1)S(1)}, u32[]{:S(2)}, u32[]{:S(2)}) collective-permute-start(bf16[256,512]{1,0:T(8,128)(2,1)S(1)} %copy-done.6), channel_id=1, source_target_pairs={{0,192},{1,193},{2,194},{3,195},{4,196},{5,197},{6,198},{7,199},{8... | collective-permute-start | bytes 786440 | tf_op jit(solution)/shard_map/ppermute | solution.py:32
  43.6 0.5 collective-permute-start.9
  44.1 3.4 %collective-permute-done.7.refs_6_ = bf16[256,512]{1,0:T(8,128)(2,1)S(1)} collective-permute-done((bf16[256,512]{1,0:T(8,128)(2,1)S(1)}, bf16[256,512]{1,0:T(8,128)(2,1)S(1)}, u32[]{:S(2)}, u32[]{:S(2)}) %collective-permute-start.7) | collective-permute-done | bytes 262176 | tf_op jit(solution)/shard_map/ppermute | solution.py:32
  47.5 2.5 %collective-permute-done.10.refs_14_ = bf16[256,512]{1,0:T(8,128)(2,1)S(1)} collective-permute-done((bf16[256,512]{1,0:T(8,128)(2,1)S(1)}, bf16[256,512]{1,0:T(8,128)(2,1)S(1)}, u32[]{:S(2)}, u32[]{:S(2)}) %collective-permute-start.10) | collective-permute-done | bytes 262176 | tf_op jit(solution)/shard_map/ppermute | solution.py:32
  50.1 1.5 %convolution_convert_fusion = bf16[256,1536]{1,0:T(8,128)(2,1)} fusion(bf16[256,512]{1,0:T(8,128)(2,1)S(1)} %copy-done.6, bf16[1536,512]{1,0:T(8,128)(2,1)S(1)} %copy-done), kind=kOutput, calls=%fused_computation | convolution fusion | flops 403046400 | bytes 2621440 | tf_op jit(solution)/shard_map/dot_general | solution.py:28
  51.6 0.6 copy-done.10
  52.2 0.1 copy-done.11
  52.4 0.1 copy-done.12
  52.5 0.2 copy-done.13
  52.6 3.5 %wide.1 = (f32[192,1024]{1,0:T(8,128)}, f32[200,512]{1,0:T(8,128)S(1)}, f32[200,512]{1,0:T(8,128)S(1)}) custom-call(bf16[768,256]{1,0:T(8,128)(2,1)S(1)} %get-tuple-element.48.refs_0_.mine_ref, bf16[768,256]{1,0:T(8,128)(2,1)S(1)} %collective-permute-done.4.refs_1_.theirs_ref, bf16[384,256]{1,0:T(8,128)(2,1)} %collective-permute-done.refs_2_, ...), custom_call_target="tpu_custom_call" | custom-call | flops 1073741824 | bytes 5242880 | tf_op jit(solution)/shard_map/wide/pallas_call | solution.py:208
  56.2 1.4 %convert_element_type.49.terms_ref = f32[8,272,256]{2,1,0:T(8,128)S(1)} convert(f16[8,272,256]{2,1,0:T(8,128)(2,1)} %all-to-all-done.1) | non-fusion elementwise | flops 557056 | bytes 3342336 | tf_op jit(solution)/shard_map/convert_element_type | solution.py:390
  57.6 0.1 own_terms.1.own_ref
  57.8 0.6 collective-permute-start.14
  58.4 0.1 collective-permute-start.13
  58.5 2.1 %collective-permute-start.12 = (f16[200,512]{1,0:T(8,128)(2,1)S(1)}, f16[200,512]{1,0:T(8,128)(2,1)S(1)}, u32[]{:S(2)}, u32[]{:S(2)}) collective-permute-start(f16[200,512]{1,0:T(8,128)(2,1)S(1)} %convert_element_type.45), channel_id=1, source_target_pairs={{0,192},{1,193},{2,194},{3,195},{4,196},{5,197},{6,198},{7,199},{8... | collective-permute-start | bytes 614408 | tf_op jit(solution)/shard_map/ppermute | solution.py:32
  60.6 1.2 %narrow.1 = (f32[192,256]{1,0:T(8,128)}, f32[200,256]{1,0:T(8,128)S(1)}, f32[200,256]{1,0:T(8,128)S(1)}, f32[200,256]{1,0:T(8,128)S(1)}) custom-call(bf16[768,256]{1,0:T(8,128)(2,1)S(1)} %get-tuple-element.48.refs_0_.mine_ref, bf16[768,256]{1,0:T(8,128)(2,1)S(1)} %collective-permute-done.4.refs_1_.theirs_ref, f32[256,256]{1,0:T(8,128)S(1)} %own_terms.1.own_ref, ...), custom_call_target="tpu_custom_call" | custom-call | flops 1 | bytes 1 | tf_op jit(solution)/shard_map/narrow/pallas_call | solution.py:245
  61.8 2.0 %collective-permute-start.17 = (f16[200,256]{1,0:T(8,128)(2,1)S(1)}, f16[200,256]{1,0:T(8,128)(2,1)S(1)}, u32[]{:S(2)}, u32[]{:S(2)}) collective-permute-start(f16[200,256]{1,0:T(8,128)(2,1)S(1)} %convert_element_type.52), channel_id=1, source_target_pairs={{0,128},{1,129},{2,130},{3,131},{4,132},{5,133},{6,134},{7,135},{8... | collective-permute-start | bytes 307208 | tf_op jit(solution)/shard_map/ppermute | solution.py:32
  63.8 0.1 collective-permute-start.16
  63.9 2.1 %collective-permute-start.15 = (f16[200,256]{1,0:T(8,128)(2,1)S(1)}, f16[200,256]{1,0:T(8,128)(2,1)S(1)}, u32[]{:S(2)}, u32[]{:S(2)}) collective-permute-start(f16[200,256]{1,0:T(8,128)(2,1)S(1)} %convert_element_type.50), channel_id=1, source_target_pairs={{0,192},{1,193},{2,194},{3,195},{4,196},{5,197},{6,198},{7,199},{8... | collective-permute-start | bytes 307208 | tf_op jit(solution)/shard_map/ppermute | solution.py:32
  66.0 0.1 collective-permute-done.13
  66.1 1.8 %collective-permute-done.12 = f16[200,512]{1,0:T(8,128)(2,1)S(1)} collective-permute-done((f16[200,512]{1,0:T(8,128)(2,1)S(1)}, f16[200,512]{1,0:T(8,128)(2,1)S(1)}, u32[]{:S(2)}, u32[]{:S(2)}) %collective-permute-start.12) | collective-permute-done | bytes 204832 | tf_op jit(solution)/shard_map/ppermute | solution.py:32
  67.9 0.1 maximum_convert_fusion.wide_got_ref
  68.0 2.0 %collective-permute-done.17 = f16[200,256]{1,0:T(8,128)(2,1)S(1)} collective-permute-done((f16[200,256]{1,0:T(8,128)(2,1)S(1)}, f16[200,256]{1,0:T(8,128)(2,1)S(1)}, u32[]{:S(2)}, u32[]{:S(2)}) %collective-permute-start.17) | collective-permute-done | bytes 102432 | tf_op jit(solution)/shard_map/ppermute | solution.py:32
  70.1 1.2 %collective-permute-done.15 = f16[200,256]{1,0:T(8,128)(2,1)S(1)} collective-permute-done((f16[200,256]{1,0:T(8,128)(2,1)S(1)}, f16[200,256]{1,0:T(8,128)(2,1)S(1)}, u32[]{:S(2)}, u32[]{:S(2)}) %collective-permute-start.15) | collective-permute-done | bytes 102432 | tf_op jit(solution)/shard_map/ppermute | solution.py:32
  71.3 0.5 after_x.1
  71.8 0.1 convert_element_type.54
  71.8 13.9 %all_to_all.20 = f16[8,248,128]{2,1,0:T(8,128)(2,1)S(1)} all-to-all(f16[8,248,128]{2,1,0:T(8,128)(2,1)S(1)} %convert_element_type.54), channel_id=1, replica_groups=mesh['dp'=32,'seq'=8] {'seq'}, dimensions={0} | all-to-all | bytes 1015808 | tf_op jit(solution)/shard_map/all_to_all | solution.py:395
  85.7 0.1 convert_element_type.55.got_ref
  85.8 0.1 after_seq.1
  85.9 15.9 %all_to_all.21.got_ref = f32[4,64,128]{2,1,0:T(8,128)S(1)} all-to-all(f32[4,64,128]{2,1,0:T(8,128)S(1)} %after_seq.1), channel_id=1, replica_groups={{0,16,32,48},{8,24,40,56},{4,20,36,52},{12,28,44,60},{1,17,33,49},{9,25..., dimensions={0} | all-to-all | bytes 262144 | tf_op jit(solution)/shard_map/all_to_all | solution.py:396
  101.8 0.6 last_sum.1
  (49 shorter events, 0.3 us)
Async XLA Ops:
  0.6 17.4 %copy-start = (bf16[1536,512]{1,0:T(8,128)(2,1)S(1)}, bf16[1536,512]{1,0:T(8,128)(2,1)}, u32[]{:S(2)}) copy-start(bf16[1536,512]{1,0:T(8,128)(2,1)} %param.10) | copy-start | bytes 4718596
  3.7 6.2 %copy-start.2 = (bf16[1,256,1536]{2,1,0:T(8,128)(2,1)S(1)}, bf16[1,256,1536]{2,1,0:T(8,128)(2,1)}, u32[]{:S(2)}) copy-start(bf16[1,256,1536]{2,1,0:T(8,128)(2,1)} %param.11) | copy-start | bytes 2359300
  3.7 11.1 %copy-start.1 = (bf16[1,256,1536]{2,1,0:T(8,128)(2,1)S(1)}, bf16[1,256,1536]{2,1,0:T(8,128)(2,1)}, u32[]{:S(2)}) copy-start(bf16[1,256,1536]{2,1,0:T(8,128)(2,1)} %param.6) | copy-start | bytes 2359300
  3.7 20.4 %all-to-all-start = ((bf16[8,256,256]{2,1,0:T(8,128)(2,1)}), bf16[8,256,256]{2,1,0:T(8,128)(2,1)}, u32[]{:S(2)}, u32[]{:S(2)}) async-start(bf16[8,256,256]{2,1,0:T(8,128)(2,1)} %project.1), calls=%async_computation | async-start | bytes 2097152 | tf_op jit(solution)/shard_map/all_to_all | solution.py:359
  9.8 7.0 %copy-start.14 = (bf16[1536,512]{1,0:T(8,128)(2,1)S(1)}, bf16[1536,512]{1,0:T(8,128)(2,1)}, u32[]{:S(2)}) copy-start(bf16[1536,512]{1,0:T(8,128)(2,1)} %param.7) | copy-start | bytes 4718596
  11.4 8.1 %collective-permute-start.2 = (bf16[384,256]{1,0:T(8,128)(2,1)S(1)}, bf16[384,256]{1,0:T(8,128)(2,1)S(1)}, u32[]{:S(2)}, u32[]{:S(2)}) collective-permute-start(bf16[384,256]{1,0:T(8,128)(2,1)S(1)} %get-tuple-element.43), channel_id=1, source_target_pairs={{0,192},{1,193},{2,194},{3,195},{4,196},{5,197},{6,198},{7,199},{8... | collective-permute-start | bytes 589832 | tf_op jit(solution)/shard_map/ppermute | solution.py:32
  14.2 19.8 %collective-permute-start.3 = (bf16[384,256]{1,0:T(8,128)(2,1)}, bf16[384,256]{1,0:T(8,128)(2,1)}, u32[]{:S(2)}, u32[]{:S(2)}) collective-permute-start(bf16[384,256]{1,0:T(8,128)(2,1)} %get-tuple-element.44), channel_id=1, source_target_pairs={{0,200},{1,201},{2,202},{3,203},{4,204},{5,205},{6,206},{7,207},{8... | collective-permute-start | bytes 589832 | tf_op jit(solution)/shard_map/ppermute | solution.py:32
  14.2 3.8 %copy-start.3 = (bf16[1,256,1536]{2,1,0:T(8,128)(2,1)S(1)}, bf16[1,256,1536]{2,1,0:T(8,128)(2,1)}, u32[]{:S(2)}) copy-start(bf16[1,256,1536]{2,1,0:T(8,128)(2,1)} %param.11) | copy-start | bytes 2359300
  14.2 19.8 %collective-permute-start.5 = (bf16[384,256]{1,0:T(8,128)(2,1)}, bf16[384,256]{1,0:T(8,128)(2,1)}, u32[]{:S(2)}, u32[]{:S(2)}) collective-permute-start(bf16[384,256]{1,0:T(8,128)(2,1)} %get-tuple-element.46), channel_id=1, source_target_pairs={{0,8},{1,9},{2,10},{3,11},{4,12},{5,13},{6,14},{7,15},{8,0},{9,1},... | collective-permute-start | bytes 589832 | tf_op jit(solution)/shard_map/ppermute | solution.py:32
  16.5 17.5 %collective-permute-start = (bf16[384,256]{1,0:T(8,128)(2,1)}, bf16[384,256]{1,0:T(8,128)(2,1)}, u32[]{:S(2)}, u32[]{:S(2)}) collective-permute-start(bf16[384,256]{1,0:T(8,128)(2,1)} %get-tuple-element.41), channel_id=1, source_target_pairs={{0,64},{1,65},{2,66},{3,67},{4,68},{5,69},{6,70},{7,71},{8,72},{9,... | collective-permute-start | bytes 589832 | tf_op jit(solution)/shard_map/ppermute | solution.py:32
  16.7 17.3 %collective-permute-start.4 = (bf16[768,256]{1,0:T(8,128)(2,1)}, bf16[768,256]{1,0:T(8,128)(2,1)S(1)}, u32[]{:S(2)}, u32[]{:S(2)}) collective-permute-start(bf16[768,256]{1,0:T(8,128)(2,1)} %get-tuple-element.45), channel_id=1, source_target_pairs={{0,8},{1,9},{2,10},{3,11},{4,12},{5,13},{6,14},{7,15},{8,0},{9,1},... | collective-permute-start | bytes 1179656 | tf_op jit(solution)/shard_map/ppermute | solution.py:32
  19.5 14.5 %collective-permute-start.1 = (bf16[384,256]{1,0:T(8,128)(2,1)}, bf16[384,256]{1,0:T(8,128)(2,1)S(1)}, u32[]{:S(2)}, u32[]{:S(2)}) collective-permute-start(bf16[384,256]{1,0:T(8,128)(2,1)} %get-tuple-element.42), channel_id=1, source_target_pairs={{0,72},{1,73},{2,74},{3,75},{4,76},{5,77},{6,78},{7,79},{8,64},{9,... | collective-permute-start | bytes 589832 | tf_op jit(solution)/shard_map/ppermute | solution.py:32
  35.2 4.8 %copy-start.7 = (bf16[256,512]{1,0:T(8,128)(2,1)S(1)}, bf16[256,512]{1,0:T(8,128)(2,1)}, u32[]{:S(2)}) copy-start(bf16[256,512]{1,0:T(8,128)(2,1)} %get-tuple-element.52.refs_4_) | copy-start | bytes 786436
  35.2 6.3 %copy-start.6 = (bf16[256,512]{1,0:T(8,128)(2,1)S(1)}, bf16[256,512]{1,0:T(8,128)(2,1)}, u32[]{:S(2)}) copy-start(bf16[256,512]{1,0:T(8,128)(2,1)} %get-tuple-element.57.refs_12_) | copy-start | bytes 786436
  35.2 21.0 %all-to-all-start.1 = ((f16[8,272,256]{2,1,0:T(8,128)(2,1)}), f16[8,272,256]{2,1,0:T(8,128)(2,1)}, u32[]{:S(2)}, u32[]{:S(2)}) async-start(f16[8,272,256]{2,1,0:T(8,128)(2,1)} %convert_element_type.44), calls=%async_computation.1 | async-start | bytes 2228224 | tf_op jit(solution)/shard_map/all_to_all | solution.py:375
  40.0 7.5 %collective-permute-start.7 = (bf16[256,512]{1,0:T(8,128)(2,1)S(1)}, bf16[256,512]{1,0:T(8,128)(2,1)S(1)}, u32[]{:S(2)}, u32[]{:S(2)}) collective-permute-start(bf16[256,512]{1,0:T(8,128)(2,1)S(1)} %copy-done.7), channel_id=1, source_target_pairs={{0,64},{1,65},{2,66},{3,67},{4,68},{5,69},{6,70},{7,71},{8,72},{9,... | collective-permute-start | bytes 786440 | tf_op jit(solution)/shard_map/ppermute | solution.py:32
  41.5 8.5 %collective-permute-start.10 = (bf16[256,512]{1,0:T(8,128)(2,1)S(1)}, bf16[256,512]{1,0:T(8,128)(2,1)S(1)}, u32[]{:S(2)}, u32[]{:S(2)}) collective-permute-start(bf16[256,512]{1,0:T(8,128)(2,1)S(1)} %copy-done.6), channel_id=1, source_target_pairs={{0,192},{1,193},{2,194},{3,195},{4,196},{5,197},{6,198},{7,199},{8... | collective-permute-start | bytes 786440 | tf_op jit(solution)/shard_map/ppermute | solution.py:32
  43.6 7.9 %collective-permute-start.6 = (bf16[256,512]{1,0:T(8,128)(2,1)S(1)}, bf16[256,512]{1,0:T(8,128)(2,1)S(1)}, u32[]{:S(2)}, u32[]{:S(2)}) collective-permute-start(bf16[256,512]{1,0:T(8,128)(2,1)S(1)} %copy-done.7), channel_id=1, source_target_pairs={{0,8},{1,9},{2,10},{3,11},{4,12},{5,13},{6,14},{7,15},{8,0},{9,1},... | collective-permute-start | bytes 786440 | tf_op jit(solution)/shard_map/ppermute | solution.py:32
  43.6 7.9 %collective-permute-start.9 = (bf16[256,512]{1,0:T(8,128)(2,1)S(1)}, bf16[256,512]{1,0:T(8,128)(2,1)S(1)}, u32[]{:S(2)}, u32[]{:S(2)}) collective-permute-start(bf16[256,512]{1,0:T(8,128)(2,1)S(1)} %copy-done.6), channel_id=1, source_target_pairs={{0,8},{1,9},{2,10},{3,11},{4,12},{5,13},{6,14},{7,15},{8,0},{9,1},... | collective-permute-start | bytes 786440 | tf_op jit(solution)/shard_map/ppermute | solution.py:32
  47.5 4.1 %copy-start.8 = (bf16[256,512]{1,0:T(8,128)(2,1)}, bf16[256,512]{1,0:T(8,128)(2,1)S(1)}, u32[]{:S(2)}) copy-start(bf16[256,512]{1,0:T(8,128)(2,1)S(1)} %collective-permute-done.7.refs_6_) | copy-start | bytes 786436
  47.5 4.0 %collective-permute-start.8 = (bf16[256,512]{1,0:T(8,128)(2,1)S(1)}, bf16[256,512]{1,0:T(8,128)(2,1)S(1)}, u32[]{:S(2)}, u32[]{:S(2)}) collective-permute-start(bf16[256,512]{1,0:T(8,128)(2,1)S(1)} %collective-permute-done.7.refs_6_), channel_id=1, source_target_pairs={{0,8},{1,9},{2,10},{3,11},{4,12},{5,13},{6,14},{7,15},{8,0},{9,1},... | collective-permute-start | bytes 786440 | tf_op jit(solution)/shard_map/ppermute | solution.py:32
  50.1 1.6 %copy-start.9 = (bf16[256,512]{1,0:T(8,128)(2,1)}, bf16[256,512]{1,0:T(8,128)(2,1)S(1)}, u32[]{:S(2)}) copy-start(bf16[256,512]{1,0:T(8,128)(2,1)S(1)} %collective-permute-done.10.refs_14_) | copy-start | bytes 786436
  50.1 1.5 %collective-permute-start.11 = (bf16[256,512]{1,0:T(8,128)(2,1)S(1)}, bf16[256,512]{1,0:T(8,128)(2,1)S(1)}, u32[]{:S(2)}, u32[]{:S(2)}) collective-permute-start(bf16[256,512]{1,0:T(8,128)(2,1)S(1)} %collective-permute-done.10.refs_14_), channel_id=1, source_target_pairs={{0,8},{1,9},{2,10},{3,11},{4,12},{5,13},{6,14},{7,15},{8,0},{9,1},... | collective-permute-start | bytes 786440 | tf_op jit(solution)/shard_map/ppermute | solution.py:32
  51.6 0.7 copy-start.10
  51.6 0.8 copy-start.11
  51.6 0.9 copy-start.12
  51.6 1.0 copy-start.13
  57.8 2.8 %collective-permute-start.14 = (f32[256,256]{1,0:T(8,128)S(1)}, f32[256,256]{1,0:T(8,128)S(1)}, u32[]{:S(2)}, u32[]{:S(2)}) collective-permute-start(f32[256,256]{1,0:T(8,128)S(1)} %own_terms.1.own_ref), channel_id=1, source_target_pairs={{0,8},{1,9},{2,10},{3,11},{4,12},{5,13},{6,14},{7,15},{8,0},{9,1},... | collective-permute-start | bytes 786440 | tf_op jit(solution)/shard_map/ppermute | solution.py:32
  58.4 7.7 %collective-permute-start.13 = (f16[200,512]{1,0:T(8,128)(2,1)S(1)}, f16[200,512]{1,0:T(8,128)(2,1)S(1)}, u32[]{:S(2)}, u32[]{:S(2)}) collective-permute-start(f16[200,512]{1,0:T(8,128)(2,1)S(1)} %convert_element_type.46), channel_id=1, source_target_pairs={{0,64},{1,65},{2,66},{3,67},{4,68},{5,69},{6,70},{7,71},{8,72},{9,... | collective-permute-start | bytes 614408 | tf_op jit(solution)/shard_map/ppermute | solution.py:32
  58.5 9.4 %collective-permute-start.12 = (f16[200,512]{1,0:T(8,128)(2,1)S(1)}, f16[200,512]{1,0:T(8,128)(2,1)S(1)}, u32[]{:S(2)}, u32[]{:S(2)}) collective-permute-start(f16[200,512]{1,0:T(8,128)(2,1)S(1)} %convert_element_type.45), channel_id=1, source_target_pairs={{0,192},{1,193},{2,194},{3,195},{4,196},{5,197},{6,198},{7,199},{8... | collective-permute-start | bytes 614408 | tf_op jit(solution)/shard_map/ppermute | solution.py:32
  61.8 9.5 %copy-start.4 = (f32[192,1024]{1,0:T(8,128)S(1)}, f32[192,1024]{1,0:T(8,128)}, u32[]{:S(2)}) copy-start(f32[192,1024]{1,0:T(8,128)} %get-tuple-element.61.wide_ref) | copy-start | bytes 2359300
  61.8 9.5 %copy-start.5 = (f32[192,256]{1,0:T(8,128)S(1)}, f32[192,256]{1,0:T(8,128)}, u32[]{:S(2)}) copy-start(f32[192,256]{1,0:T(8,128)} %get-tuple-element.63.narrow_ref) | copy-start | bytes 589828
  61.8 8.2 %collective-permute-start.17 = (f16[200,256]{1,0:T(8,128)(2,1)S(1)}, f16[200,256]{1,0:T(8,128)(2,1)S(1)}, u32[]{:S(2)}, u32[]{:S(2)}) collective-permute-start(f16[200,256]{1,0:T(8,128)(2,1)S(1)} %convert_element_type.52), channel_id=1, source_target_pairs={{0,128},{1,129},{2,130},{3,131},{4,132},{5,133},{6,134},{7,135},{8... | collective-permute-start | bytes 307208 | tf_op jit(solution)/shard_map/ppermute | solution.py:32
  63.8 6.3 %collective-permute-start.16 = (f16[200,256]{1,0:T(8,128)(2,1)S(1)}, f16[200,256]{1,0:T(8,128)(2,1)S(1)}, u32[]{:S(2)}, u32[]{:S(2)}) collective-permute-start(f16[200,256]{1,0:T(8,128)(2,1)S(1)} %convert_element_type.51), channel_id=1, source_target_pairs={{0,64},{1,65},{2,66},{3,67},{4,68},{5,69},{6,70},{7,71},{8,72},{9,... | collective-permute-start | bytes 307208 | tf_op jit(solution)/shard_map/ppermute | solution.py:32
  63.9 7.3 %collective-permute-start.15 = (f16[200,256]{1,0:T(8,128)(2,1)S(1)}, f16[200,256]{1,0:T(8,128)(2,1)S(1)}, u32[]{:S(2)}, u32[]{:S(2)}) collective-permute-start(f16[200,256]{1,0:T(8,128)(2,1)S(1)} %convert_element_type.50), channel_id=1, source_target_pairs={{0,192},{1,193},{2,194},{3,195},{4,196},{5,197},{6,198},{7,199},{8... | collective-permute-start | bytes 307208 | tf_op jit(solution)/shard_map/ppermute | solution.py:32

commit v4 on v3

--- a/solution.py
+++ b/solution.py
@@ -92,89 +92,112 @@
     )(place, side)
 
 
-def attention_kernel(q_ref, da_ref, k_ref, v_ref, d_query_ref, attended_ref, dkv_ref):
-    step = pl.program_id(0)
-    keys = k_ref[...]
-    values = v_ref[...]
+def attention_kernel(
+    q_ref, da_ref, k_ref, v_ref, d_query_ref, attended_ref, dkv_ref, scores_ref, d_probs_ref, probs_ref, d_scores_ref
+):
     bf = jnp.bfloat16
-    heads = range(q_ref.shape[1] // HD)
-    q = [q_ref[:, h * HD : (h + 1) * HD] for h in heads]
-    da = [da_ref[:, h * HD : (h + 1) * HD] for h in heads]
-
-    def softmax(scores):
+    blocks, _, tokens = dkv_ref.shape
+    chunk = 16
+    head_cols = lambda h: slice(h * HD, (h + 1) * HD)
+    block_rows = lambda b: slice(b * tokens, (b + 1) * tokens)
+
+    def ahead(h):
+        def make(b, side_ref, other_ref, to_ref):
+            def run():
+                to_ref[h % 2, :, block_rows(b)] = dot(side_ref[:, head_cols(h)], other_ref[block_rows(b), :], ((1,), (1,)))
+
+            return run
+
+        return [
+            make(b, *refs)
+            for b in range(blocks)
+            for refs in ((q_ref, k_ref, scores_ref), (da_ref, v_ref, d_probs_ref))
+        ]
+
+    def softmax(h, i):
+        rows = slice(i * chunk, (i + 1) * chunk)
+        scores = scores_ref[h % 2, rows, :]
         shifted = jnp.exp2((scores - jnp.max(scores, axis=1, keepdims=True)) * (SCALE * LOG2_E))
-        return shifted * (1.0 / jnp.sum(shifted, axis=1, keepdims=True))
-
-    scores = [dot(q[h], keys, ((1,), (1,))) for h in heads]
-    probs, probs_b, d_probs, d_scores = [], [], [], []
-    for h in heads:
-        probs.append(softmax(scores[h]))
-        probs_b.append(probs[h].astype(bf))
-        d_probs.append(dot(da[h], values, ((1,), (1,))))
-    d_value = None
-    for h in heads:
-        attended_ref[:, h * HD : (h + 1) * HD] = dot(probs_b[h], values, ((1,), (0,))).astype(bf)
-        term = dot(da[h], probs_b[h], ((0,), (0,)))
-        d_value = term if d_value is None else d_value + term
-        delta = jnp.sum(d_probs[h] * probs[h], axis=1, keepdims=True)
-        d_scores.append((probs[h] * (d_probs[h] - delta)).astype(bf))
-    d_key = None
-    for h in heads:
-        d_query_ref[:, h * HD : (h + 1) * HD] = (dot(d_scores[h], keys, ((1,), (0,))) * SCALE).astype(bf)
-        term = dot(q[h], d_scores[h], ((0,), (0,)))
-        d_key = term if d_key is None else d_key + term
-    blocks, _, tokens = dkv_ref.shape
-
-    @pl.when(step == 0)
-    def _():
+        probs = shifted * (1.0 / jnp.sum(shifted, axis=1, keepdims=True))
+        d_probs = d_probs_ref[h % 2, rows, :]
+        delta = jnp.sum(d_probs * probs, axis=1, keepdims=True)
+        probs_ref[h % 2, rows, :] = probs.astype(bf)
+        d_scores_ref[h % 2, rows, :] = (probs * (d_probs - delta)).astype(bf)
+
+    def behind(h):
+        sides = [ref[:, head_cols(h)].T for ref in (q_ref, da_ref)]
+
+        def terms(b, i, from_ref):
+            def run():
+                term = dot(sides[i], from_ref[h % 2, :, block_rows(b)], ((1,), (0,)))
+                rows = slice(i * HD, (i + 1) * HD)
+                dkv_ref[b, rows, :] = term if h == 0 else dkv_ref[b, rows, :] + term
+
+            return run
+
+        def rows_of(from_ref, other_ref, to_ref, scale):
+            def run():
+                product = dot(from_ref[h % 2], other_ref[...], ((1,), (0,)))
+                to_ref[:, head_cols(h)] = (product * scale if scale else product).astype(bf)
+
+            return run
+
+        work = [terms(b, i, ref) for b in range(blocks) for i, ref in enumerate((d_scores_ref, probs_ref))]
+        work.insert(4, rows_of(probs_ref, v_ref, attended_ref, None))
+        work.insert(13, rows_of(d_scores_ref, k_ref, d_query_ref, SCALE))
+        return work
+
+    for run in ahead(0):
+        run()
+    for h in range(HEADS):
+        beside = []
+        if h + 1 < HEADS:
+            beside += [(n / 16, run) for n, run in enumerate(ahead(h + 1))]
+        if h > 0:
+            beside += [(n / 18, run) for n, run in enumerate(behind(h - 1))]
+        beside.sort(key=lambda entry: entry[0])
+        steps = tokens // chunk
+        for i in range(steps):
+            softmax(h, i)
+            for at, run in beside:
+                if i <= at * steps < i + 1:
+                    run()
+    for run in behind(HEADS - 1):
+        run()
+
+    for i, scale in enumerate((SCALE, 1.0)):
+        rows = pl.ds(i * HD, HD)
+        top = jnp.abs(dkv_ref[0, rows, :])
+        for b in range(1, blocks):
+            top = jnp.maximum(top, jnp.abs(dkv_ref[b, rows, :]))
+        power = exponent(top * scale)
+        factor = jnp.exp2(-power) * scale
         for b in range(blocks):
-            dkv_ref[b, :HD, :] = d_key[:, b * tokens : (b + 1) * tokens]
-            dkv_ref[b, HD : 2 * HD, :] = d_value[:, b * tokens : (b + 1) * tokens]
-
-    @pl.when(step != 0)
-    def _():
-        for b in range(blocks):
-            dkv_ref[b, :HD, :] += d_key[:, b * tokens : (b + 1) * tokens]
-            dkv_ref[b, HD : 2 * HD, :] += d_value[:, b * tokens : (b + 1) * tokens]
-
-    @pl.when(step == pl.num_programs(0) - 1)
-    def _():
-        for i, scale in enumerate((SCALE, 1.0)):
-            rows = pl.ds(i * HD, HD)
-            top = jnp.abs(dkv_ref[0, rows, :])
-            for b in range(1, blocks):
-                top = jnp.maximum(top, jnp.abs(dkv_ref[b, rows, :]))
-            power = exponent(top * scale)
-            factor = jnp.exp2(-power) * scale
-            for b in range(blocks):
-                dkv_ref[b, rows, :] = dkv_ref[b, rows, :] * factor
-                dkv_ref[b, pl.ds(2 * HD + 8 * i, 8), :] = jnp.broadcast_to(power, (8, tokens))
+            dkv_ref[b, rows, :] = dkv_ref[b, rows, :] * factor
+            dkv_ref[b, pl.ds(2 * HD + 8 * i, 8), :] = jnp.broadcast_to(power, (8, tokens))
 
 
 def attention(queries, d_att, keys_values):
     tokens, inner = queries.shape
     length = keys_values.shape[0]
-    by_pair = pl.BlockSpec((tokens, 2 * HD), lambda j: (0, j))
+    whole = pl.BlockSpec((tokens, inner), lambda i: (0, 0))
     terms = (length // tokens, 2 * HD + 16, tokens)
     return pl.pallas_call(
         attention_kernel,
-        grid=(HEADS // 2,),
+        grid=(1,),
         in_specs=[
-            by_pair,
-            by_pair,
-            pl.BlockSpec((length, HD), lambda j: (0, 0)),
-            pl.BlockSpec((length, HD), lambda j: (0, 1)),
+            whole,
+            whole,
+            pl.BlockSpec((length, HD), lambda i: (0, 0)),
+            pl.BlockSpec((length, HD), lambda i: (0, 1)),
         ],
-        out_specs=[
-            by_pair,
-            by_pair,
-            pl.BlockSpec(terms, lambda j: (0, 0, 0)),
-        ],
+        out_specs=[whole, whole, pl.BlockSpec(terms, lambda i: (0, 0, 0))],
         out_shape=[
             pltpu.HBM((tokens, inner), jnp.bfloat16),
             pltpu.HBM((tokens, inner), jnp.bfloat16),
             jax.ShapeDtypeStruct(terms, jnp.float32),
         ],
+        scratch_shapes=[pltpu.VMEM((2, tokens, length), jnp.float32)] * 2 + [pltpu.VMEM((2, tokens, length), jnp.bfloat16)] * 2,
         compiler_params=pltpu.CompilerParams(vmem_limit_bytes=32 * MIB),
         cost_estimate=pl.CostEstimate(
             flops=12 * tokens * inner * length, bytes_accessed=4 << 20, transcendentals=tokens * HEADS * length

time: 103 us -> 103 us (level)
  no operation moved by 1% of the time
where the time goes in v4:
time: 103 us; the launch traced here: 102 us
  blocking collectives  29.8 us (29%)
  starting transfers between devices  27.3 us (27%)
  Pallas kernels  21.8 us (21%)
  waiting for transfers between devices  14.2 us (14%)
  matrix products  4.03 us (4%)
  other arithmetic  3.1 us (3%)
  local copies, waits for them, and re-layouts  1.03 us (1%)
    ppermute x18, starting transfers between devices, exchange(): return lax.ppermute(value, AXES, [(i, i ^ mask) for i in range(256)])  16.4 us
    all_to_all x1, blocking collectives, local(): lax.all_to_all(part, AXES, 0, 0, axis_index_groups=Z_HI_GROUPS, tiled=True)  15.9 us
    all_to_all x1, blocking collectives, local(): lax.all_to_all(part.astype(half), 'seq', 0, 0, tiled=True).astype(f32)  13.9 us
    ppermute x18, waiting for transfers between devices, exchange(): return lax.ppermute(value, AXES, [(i, i ^ mask) for i in range(256)])  11.3 us
    pallas_call x1, Pallas kernels, attention(): pl.pallas_call(attention_kernel, grid=(1,), in_specs=[whole, whole, pl.Bl...  9.57 us
    all_to_all x1, starting transfers between devices, local(): lax.all_to_all(project(hidden, w_key, w_value), 'seq', 0, 0, tiled=True)  6.1 us
    all_to_all x1, starting transfers between devices, local(): terms = lax.all_to_all(terms.astype(half), 'seq', 0, 0, tiled=True)  4.82 us
    dot_general x3, matrix products, dot(): lax.dot_general(left, right, (dims, ((), ())), preferred_element_type=jnp...  4.03 us
  transfers between devices with their start and end apart: 20, of which 8 were waited for; matrix products, arithmetic and copies ran while one was open for 4% of the time, Pallas kernels for 17%

profile of v4, /device:TPU:32, one launch (start us, length us, event | category | flops | bytes accessed | tf_op | source)
XLA Modules:
  0.0 102.1 jit_solution(11168965242053553431)
XLA Ops:
  0.6 3.0 %project.1 = bf16[8,256,256]{2,1,0:T(8,128)(2,1)} custom-call(bf16[256,1536]{1,0:T(8,128)(2,1)} %bitcast.19, bf16[1536,128]{1,0:T(8,128)(2,1)} %w_key_ref.1, bf16[1536,128]{1,0:T(8,128)(2,1)} %w_value_ref.1), custom_call_target="tpu_custom_call" | custom-call | tf_op jit(solution)/shard_map/project/pallas_call | solution.py:58
  3.7 6.1 %all-to-all-start = ((bf16[8,256,256]{2,1,0:T(8,128)(2,1)}), bf16[8,256,256]{2,1,0:T(8,128)(2,1)}, u32[]{:S(2)}, u32[]{:S(2)}) async-start(bf16[8,256,256]{2,1,0:T(8,128)(2,1)} %project.1), calls=%async_computation | async-start | bytes 2097152 | tf_op jit(solution)/shard_map/all_to_all | solution.py:382
  9.8 0.1 pad_add_fusion.place_ref
  9.8 1.6 %turn.3 = (bf16[384,256]{1,0:T(8,128)(2,1)S(1)}, bf16[384,256]{1,0:T(8,128)(2,1)}, bf16[384,256]{1,0:T(8,128)(2,1)S(1)}, bf16[384,256]{1,0:T(8,128)(2,1)}) custom-call(s32[2]{0:T(128)S(1)} %pad_add_fusion.place_ref, bf16[256,1536]{1,0:T(8,128)(2,1)S(1)} %bitcast.21), custom_call_target="tpu_custom_call" | custom-call | tf_op jit(solution)/shard_map/turn/pallas_call | solution.py:80
  11.4 2.7 %collective-permute-start.2 = (bf16[384,256]{1,0:T(8,128)(2,1)S(1)}, bf16[384,256]{1,0:T(8,128)(2,1)S(1)}, u32[]{:S(2)}, u32[]{:S(2)}) collective-permute-start(bf16[384,256]{1,0:T(8,128)(2,1)S(1)} %get-tuple-element.43), channel_id=1, source_target_pairs={{0,192},{1,193},{2,194},{3,195},{4,196},{5,197},{6,198},{7,199},{8... | collective-permute-start | bytes 589832 | tf_op jit(solution)/shard_map/ppermute | solution.py:32
  14.2 0.6 collective-permute-start.5
  14.8 1.7 %turn.2 = (bf16[768,256]{1,0:T(8,128)(2,1)S(1)}, bf16[768,256]{1,0:T(8,128)(2,1)}, bf16[384,256]{1,0:T(8,128)(2,1)}, bf16[384,256]{1,0:T(8,128)(2,1)}) custom-call(s32[2]{0:T(128)S(1)} %pad_add_fusion.place_ref, bf16[256,1536]{1,0:T(8,128)(2,1)S(1)} %bitcast.20), custom_call_target="tpu_custom_call" | custom-call | tf_op jit(solution)/shard_map/turn/pallas_call | solution.py:80
  16.5 0.2 collective-permute-start
  16.7 1.3 %convolution_convert_fusion.2.q_ref = bf16[256,512]{1,0:T(8,128)(2,1)} fusion(bf16[1536,512]{1,0:T(8,128)(2,1)S(1)} %copy-done.14, bf16[1,256,1536]{2,1,0:T(8,128)(2,1)S(1)} %copy-done.1), kind=kOutput, calls=%fused_computation.2 | convolution fusion | flops 402784256 | bytes 2621440 | tf_op jit(solution)/shard_map/dot_general | solution.py:28
  18.0 1.3 %convolution_convert_fusion.1.da_ref = bf16[256,512]{1,0:T(8,128)(2,1)} fusion(bf16[1536,512]{1,0:T(8,128)(2,1)S(1)} %copy-done, bf16[1,256,1536]{2,1,0:T(8,128)(2,1)S(1)} %copy-done.3), kind=kOutput, calls=%fused_computation.1 | convolution fusion | flops 402784256 | bytes 2621440 | tf_op jit(solution)/shard_map/dot_general | solution.py:28
  19.3 0.2 collective-permute-done.2.refs_10_
  19.5 1.7 %collective-permute-start.1 = (bf16[384,256]{1,0:T(8,128)(2,1)}, bf16[384,256]{1,0:T(8,128)(2,1)S(1)}, u32[]{:S(2)}, u32[]{:S(2)}) collective-permute-start(bf16[384,256]{1,0:T(8,128)(2,1)} %get-tuple-element.42), channel_id=1, source_target_pairs={{0,72},{1,73},{2,74},{3,75},{4,76},{5,77},{6,78},{7,79},{8,64},{9,... | collective-permute-start | bytes 589832 | tf_op jit(solution)/shard_map/ppermute | solution.py:32
  21.2 2.9 %all-to-all-done = bf16[8,256,256]{2,1,0:T(8,128)(2,1)} async-done(((bf16[8,256,256]{2,1,0:T(8,128)(2,1)}), bf16[8,256,256]{2,1,0:T(8,128)(2,1)}, u32[]{:S(2)}, u32[]{:S(2)}) %all-to-all-start) | async-done | bytes 1048608 | tf_op jit(solution)/shard_map/all_to_all | solution.py:382
  24.1 9.6 %attention.1 = (bf16[256,512]{1,0:T(8,128)(2,1)}, bf16[256,512]{1,0:T(8,128)(2,1)}, f32[8,272,256]{2,1,0:T(8,128)S(1)}) custom-call(bf16[256,512]{1,0:T(8,128)(2,1)} %convolution_convert_fusion.2.q_ref, bf16[256,512]{1,0:T(8,128)(2,1)} %convolution_convert_fusion.1.da_ref, bf16[2048,256]{1,0:T(8,128)(2,1)} %bitcast.2.k_ref.v_ref, ...), custom_call_target="tpu_custom_call" | custom-call | flops 3221225472 | bytes 4194304 | tf_op jit(solution)/shard_map/attention/pallas_call | solution.py:185
  33.7 1.2 %convert_element_type.44 = f16[8,272,256]{2,1,0:T(8,128)(2,1)} convert(f32[8,272,256]{2,1,0:T(8,128)S(1)} %get-tuple-element.47) | non-fusion elementwise | flops 557056 | bytes 3342336 | tf_op jit(solution)/shard_map/convert_element_type | solution.py:398
  34.9 4.8 %all-to-all-start.1 = ((f16[8,272,256]{2,1,0:T(8,128)(2,1)}), f16[8,272,256]{2,1,0:T(8,128)(2,1)}, u32[]{:S(2)}, u32[]{:S(2)}) async-start(f16[8,272,256]{2,1,0:T(8,128)(2,1)} %convert_element_type.44), calls=%async_computation.1 | async-start | bytes 2228224 | tf_op jit(solution)/shard_map/all_to_all | solution.py:398
  39.7 1.5 %collective-permute-start.7 = (bf16[256,512]{1,0:T(8,128)(2,1)S(1)}, bf16[256,512]{1,0:T(8,128)(2,1)S(1)}, u32[]{:S(2)}, u32[]{:S(2)}) collective-permute-start(bf16[256,512]{1,0:T(8,128)(2,1)S(1)} %copy-done.7), channel_id=1, source_target_pairs={{0,64},{1,65},{2,66},{3,67},{4,68},{5,69},{6,70},{7,71},{8,72},{9,... | collective-permute-start | bytes 786440 | tf_op jit(solution)/shard_map/ppermute | solution.py:32
  41.2 2.1 %collective-permute-start.10 = (bf16[256,512]{1,0:T(8,128)(2,1)S(1)}, bf16[256,512]{1,0:T(8,128)(2,1)S(1)}, u32[]{:S(2)}, u32[]{:S(2)}) collective-permute-start(bf16[256,512]{1,0:T(8,128)(2,1)S(1)} %copy-done.6), channel_id=1, source_target_pairs={{0,192},{1,193},{2,194},{3,195},{4,196},{5,197},{6,198},{7,199},{8... | collective-permute-start | bytes 786440 | tf_op jit(solution)/shard_map/ppermute | solution.py:32
  43.3 0.5 collective-permute-start.9
  43.8 3.4 %collective-permute-done.7.refs_6_ = bf16[256,512]{1,0:T(8,128)(2,1)S(1)} collective-permute-done((bf16[256,512]{1,0:T(8,128)(2,1)S(1)}, bf16[256,512]{1,0:T(8,128)(2,1)S(1)}, u32[]{:S(2)}, u32[]{:S(2)}) %collective-permute-start.7) | collective-permute-done | bytes 262176 | tf_op jit(solution)/shard_map/ppermute | solution.py:32
  47.2 2.5 %collective-permute-done.10.refs_14_ = bf16[256,512]{1,0:T(8,128)(2,1)S(1)} collective-permute-done((bf16[256,512]{1,0:T(8,128)(2,1)S(1)}, bf16[256,512]{1,0:T(8,128)(2,1)S(1)}, u32[]{:S(2)}, u32[]{:S(2)}) %collective-permute-start.10) | collective-permute-done | bytes 262176 | tf_op jit(solution)/shard_map/ppermute | solution.py:32
  49.7 1.5 %convolution_convert_fusion = bf16[256,1536]{1,0:T(8,128)(2,1)} fusion(bf16[256,512]{1,0:T(8,128)(2,1)S(1)} %copy-done.6, bf16[1536,512]{1,0:T(8,128)(2,1)S(1)} %copy-done), kind=kOutput, calls=%fused_computation | convolution fusion | flops 403046400 | bytes 2621440 | tf_op jit(solution)/shard_map/dot_general | solution.py:28
  51.3 0.6 copy-done.10
  51.9 0.1 copy-done.11
  52.0 0.1 copy-done.12
  52.1 0.2 copy-done.13
  52.3 3.5 %wide.1 = (f32[192,1024]{1,0:T(8,128)}, f32[200,512]{1,0:T(8,128)S(1)}, f32[200,512]{1,0:T(8,128)S(1)}) custom-call(bf16[768,256]{1,0:T(8,128)(2,1)S(1)} %get-tuple-element.48.refs_0_.mine_ref, bf16[768,256]{1,0:T(8,128)(2,1)S(1)} %collective-permute-done.4.refs_1_.theirs_ref, bf16[384,256]{1,0:T(8,128)(2,1)} %collective-permute-done.refs_2_, ...), custom_call_target="tpu_custom_call" | custom-call | flops 1073741824 | bytes 5242880 | tf_op jit(solution)/shard_map/wide/pallas_call | solution.py:231
  55.9 1.4 %convert_element_type.49.terms_ref = f32[8,272,256]{2,1,0:T(8,128)S(1)} convert(f16[8,272,256]{2,1,0:T(8,128)(2,1)} %all-to-all-done.1) | non-fusion elementwise | flops 557056 | bytes 3342336 | tf_op jit(solution)/shard_map/convert_element_type | solution.py:413
  57.3 0.1 own_terms.1.own_ref
  57.5 0.6 collective-permute-start.14
  58.1 0.1 collective-permute-start.13
  58.2 2.1 %collective-permute-start.12 = (f16[200,512]{1,0:T(8,128)(2,1)S(1)}, f16[200,512]{1,0:T(8,128)(2,1)S(1)}, u32[]{:S(2)}, u32[]{:S(2)}) collective-permute-start(f16[200,512]{1,0:T(8,128)(2,1)S(1)} %convert_element_type.45), channel_id=1, source_target_pairs={{0,192},{1,193},{2,194},{3,195},{4,196},{5,197},{6,198},{7,199},{8... | collective-permute-start | bytes 614408 | tf_op jit(solution)/shard_map/ppermute | solution.py:32
  60.3 1.2 %narrow.1 = (f32[192,256]{1,0:T(8,128)}, f32[200,256]{1,0:T(8,128)S(1)}, f32[200,256]{1,0:T(8,128)S(1)}, f32[200,256]{1,0:T(8,128)S(1)}) custom-call(bf16[768,256]{1,0:T(8,128)(2,1)S(1)} %get-tuple-element.48.refs_0_.mine_ref, bf16[768,256]{1,0:T(8,128)(2,1)S(1)} %collective-permute-done.4.refs_1_.theirs_ref, f32[256,256]{1,0:T(8,128)S(1)} %own_terms.1.own_ref, ...), custom_call_target="tpu_custom_call" | custom-call | flops 1 | bytes 1 | tf_op jit(solution)/shard_map/narrow/pallas_call | solution.py:268
  61.5 2.0 %collective-permute-start.17 = (f16[200,256]{1,0:T(8,128)(2,1)S(1)}, f16[200,256]{1,0:T(8,128)(2,1)S(1)}, u32[]{:S(2)}, u32[]{:S(2)}) collective-permute-start(f16[200,256]{1,0:T(8,128)(2,1)S(1)} %convert_element_type.52), channel_id=1, source_target_pairs={{0,128},{1,129},{2,130},{3,131},{4,132},{5,133},{6,134},{7,135},{8... | collective-permute-start | bytes 307208 | tf_op jit(solution)/shard_map/ppermute | solution.py:32
  63.5 0.1 collective-permute-start.16
  63.6 2.1 %collective-permute-start.15 = (f16[200,256]{1,0:T(8,128)(2,1)S(1)}, f16[200,256]{1,0:T(8,128)(2,1)S(1)}, u32[]{:S(2)}, u32[]{:S(2)}) collective-permute-start(f16[200,256]{1,0:T(8,128)(2,1)S(1)} %convert_element_type.50), channel_id=1, source_target_pairs={{0,192},{1,193},{2,194},{3,195},{4,196},{5,197},{6,198},{7,199},{8... | collective-permute-start | bytes 307208 | tf_op jit(solution)/shard_map/ppermute | solution.py:32
  65.7 0.1 collective-permute-done.13
  65.8 1.8 %collective-permute-done.12 = f16[200,512]{1,0:T(8,128)(2,1)S(1)} collective-permute-done((f16[200,512]{1,0:T(8,128)(2,1)S(1)}, f16[200,512]{1,0:T(8,128)(2,1)S(1)}, u32[]{:S(2)}, u32[]{:S(2)}) %collective-permute-start.12) | collective-permute-done | bytes 204832 | tf_op jit(solution)/shard_map/ppermute | solution.py:32
  67.6 0.1 maximum_convert_fusion.wide_got_ref
  67.7 2.0 %collective-permute-done.17 = f16[200,256]{1,0:T(8,128)(2,1)S(1)} collective-permute-done((f16[200,256]{1,0:T(8,128)(2,1)S(1)}, f16[200,256]{1,0:T(8,128)(2,1)S(1)}, u32[]{:S(2)}, u32[]{:S(2)}) %collective-permute-start.17) | collective-permute-done | bytes 102432 | tf_op jit(solution)/shard_map/ppermute | solution.py:32
  69.7 1.2 %collective-permute-done.15 = f16[200,256]{1,0:T(8,128)(2,1)S(1)} collective-permute-done((f16[200,256]{1,0:T(8,128)(2,1)S(1)}, f16[200,256]{1,0:T(8,128)(2,1)S(1)}, u32[]{:S(2)}, u32[]{:S(2)}) %collective-permute-start.15) | collective-permute-done | bytes 102432 | tf_op jit(solution)/shard_map/ppermute | solution.py:32
  71.0 0.5 after_x.1
  71.4 0.1 convert_element_type.54
  71.5 13.9 %all_to_all.20 = f16[8,248,128]{2,1,0:T(8,128)(2,1)S(1)} all-to-all(f16[8,248,128]{2,1,0:T(8,128)(2,1)S(1)} %convert_element_type.54), channel_id=1, replica_groups=mesh['dp'=32,'seq'=8] {'seq'}, dimensions={0} | all-to-all | bytes 1015808 | tf_op jit(solution)/shard_map/all_to_all | solution.py:418
  85.4 0.1 convert_element_type.55.got_ref
  85.5 0.1 after_seq.1
  85.6 15.9 %all_to_all.21.got_ref = f32[4,64,128]{2,1,0:T(8,128)S(1)} all-to-all(f32[4,64,128]{2,1,0:T(8,128)S(1)} %after_seq.1), channel_id=1, replica_groups={{0,16,32,48},{8,24,40,56},{4,20,36,52},{12,28,44,60},{1,17,33,49},{9,25..., dimensions={0} | all-to-all | bytes 262144 | tf_op jit(solution)/shard_map/all_to_all | solution.py:419
  101.4 0.6 last_sum.1
  (49 shorter events, 0.3 us)
Async XLA Ops:
  0.6 17.4 %copy-start = (bf16[1536,512]{1,0:T(8,128)(2,1)S(1)}, bf16[1536,512]{1,0:T(8,128)(2,1)}, u32[]{:S(2)}) copy-start(bf16[1536,512]{1,0:T(8,128)(2,1)} %param.10) | copy-start | bytes 4718596
  3.7 6.2 %copy-start.2 = (bf16[1,256,1536]{2,1,0:T(8,128)(2,1)S(1)}, bf16[1,256,1536]{2,1,0:T(8,128)(2,1)}, u32[]{:S(2)}) copy-start(bf16[1,256,1536]{2,1,0:T(8,128)(2,1)} %param.11) | copy-start | bytes 2359300
  3.7 11.1 %copy-start.1 = (bf16[1,256,1536]{2,1,0:T(8,128)(2,1)S(1)}, bf16[1,256,1536]{2,1,0:T(8,128)(2,1)}, u32[]{:S(2)}) copy-start(bf16[1,256,1536]{2,1,0:T(8,128)(2,1)} %param.6) | copy-start | bytes 2359300
  3.7 20.4 %all-to-all-start = ((bf16[8,256,256]{2,1,0:T(8,128)(2,1)}), bf16[8,256,256]{2,1,0:T(8,128)(2,1)}, u32[]{:S(2)}, u32[]{:S(2)}) async-start(bf16[8,256,256]{2,1,0:T(8,128)(2,1)} %project.1), calls=%async_computation | async-start | bytes 2097152 | tf_op jit(solution)/shard_map/all_to_all | solution.py:382
  9.8 7.0 %copy-start.14 = (bf16[1536,512]{1,0:T(8,128)(2,1)S(1)}, bf16[1536,512]{1,0:T(8,128)(2,1)}, u32[]{:S(2)}) copy-start(bf16[1536,512]{1,0:T(8,128)(2,1)} %param.7) | copy-start | bytes 4718596
  11.4 8.1 %collective-permute-start.2 = (bf16[384,256]{1,0:T(8,128)(2,1)S(1)}, bf16[384,256]{1,0:T(8,128)(2,1)S(1)}, u32[]{:S(2)}, u32[]{:S(2)}) collective-permute-start(bf16[384,256]{1,0:T(8,128)(2,1)S(1)} %get-tuple-element.43), channel_id=1, source_target_pairs={{0,192},{1,193},{2,194},{3,195},{4,196},{5,197},{6,198},{7,199},{8... | collective-permute-start | bytes 589832 | tf_op jit(solution)/shard_map/ppermute | solution.py:32
  14.2 19.5 %collective-permute-start.3 = (bf16[384,256]{1,0:T(8,128)(2,1)}, bf16[384,256]{1,0:T(8,128)(2,1)}, u32[]{:S(2)}, u32[]{:S(2)}) collective-permute-start(bf16[384,256]{1,0:T(8,128)(2,1)} %get-tuple-element.44), channel_id=1, source_target_pairs={{0,200},{1,201},{2,202},{3,203},{4,204},{5,205},{6,206},{7,207},{8... | collective-permute-start | bytes 589832 | tf_op jit(solution)/shard_map/ppermute | solution.py:32
  14.2 3.8 %copy-start.3 = (bf16[1,256,1536]{2,1,0:T(8,128)(2,1)S(1)}, bf16[1,256,1536]{2,1,0:T(8,128)(2,1)}, u32[]{:S(2)}) copy-start(bf16[1,256,1536]{2,1,0:T(8,128)(2,1)} %param.11) | copy-start | bytes 2359300
  14.2 19.5 %collective-permute-start.5 = (bf16[384,256]{1,0:T(8,128)(2,1)}, bf16[384,256]{1,0:T(8,128)(2,1)}, u32[]{:S(2)}, u32[]{:S(2)}) collective-permute-start(bf16[384,256]{1,0:T(8,128)(2,1)} %get-tuple-element.46), channel_id=1, source_target_pairs={{0,8},{1,9},{2,10},{3,11},{4,12},{5,13},{6,14},{7,15},{8,0},{9,1},... | collective-permute-start | bytes 589832 | tf_op jit(solution)/shard_map/ppermute | solution.py:32
  16.5 17.2 %collective-permute-start = (bf16[384,256]{1,0:T(8,128)(2,1)}, bf16[384,256]{1,0:T(8,128)(2,1)}, u32[]{:S(2)}, u32[]{:S(2)}) collective-permute-start(bf16[384,256]{1,0:T(8,128)(2,1)} %get-tuple-element.41), channel_id=1, source_target_pairs={{0,64},{1,65},{2,66},{3,67},{4,68},{5,69},{6,70},{7,71},{8,72},{9,... | collective-permute-start | bytes 589832 | tf_op jit(solution)/shard_map/ppermute | solution.py:32
  16.7 17.0 %collective-permute-start.4 = (bf16[768,256]{1,0:T(8,128)(2,1)}, bf16[768,256]{1,0:T(8,128)(2,1)S(1)}, u32[]{:S(2)}, u32[]{:S(2)}) collective-permute-start(bf16[768,256]{1,0:T(8,128)(2,1)} %get-tuple-element.45), channel_id=1, source_target_pairs={{0,8},{1,9},{2,10},{3,11},{4,12},{5,13},{6,14},{7,15},{8,0},{9,1},... | collective-permute-start | bytes 1179656 | tf_op jit(solution)/shard_map/ppermute | solution.py:32
  19.5 14.2 %collective-permute-start.1 = (bf16[384,256]{1,0:T(8,128)(2,1)}, bf16[384,256]{1,0:T(8,128)(2,1)S(1)}, u32[]{:S(2)}, u32[]{:S(2)}) collective-permute-start(bf16[384,256]{1,0:T(8,128)(2,1)} %get-tuple-element.42), channel_id=1, source_target_pairs={{0,72},{1,73},{2,74},{3,75},{4,76},{5,77},{6,78},{7,79},{8,64},{9,... | collective-permute-start | bytes 589832 | tf_op jit(solution)/shard_map/ppermute | solution.py:32
  34.9 4.8 %copy-start.7 = (bf16[256,512]{1,0:T(8,128)(2,1)S(1)}, bf16[256,512]{1,0:T(8,128)(2,1)}, u32[]{:S(2)}) copy-start(bf16[256,512]{1,0:T(8,128)(2,1)} %get-tuple-element.52.refs_4_) | copy-start | bytes 786436
  34.9 6.3 %copy-start.6 = (bf16[256,512]{1,0:T(8,128)(2,1)S(1)}, bf16[256,512]{1,0:T(8,128)(2,1)}, u32[]{:S(2)}) copy-start(bf16[256,512]{1,0:T(8,128)(2,1)} %get-tuple-element.57.refs_12_) | copy-start | bytes 786436
  34.9 21.0 %all-to-all-start.1 = ((f16[8,272,256]{2,1,0:T(8,128)(2,1)}), f16[8,272,256]{2,1,0:T(8,128)(2,1)}, u32[]{:S(2)}, u32[]{:S(2)}) async-start(f16[8,272,256]{2,1,0:T(8,128)(2,1)} %convert_element_type.44), calls=%async_computation.1 | async-start | bytes 2228224 | tf_op jit(solution)/shard_map/all_to_all | solution.py:398
  39.7 7.5 %collective-permute-start.7 = (bf16[256,512]{1,0:T(8,128)(2,1)S(1)}, bf16[256,512]{1,0:T(8,128)(2,1)S(1)}, u32[]{:S(2)}, u32[]{:S(2)}) collective-permute-start(bf16[256,512]{1,0:T(8,128)(2,1)S(1)} %copy-done.7), channel_id=1, source_target_pairs={{0,64},{1,65},{2,66},{3,67},{4,68},{5,69},{6,70},{7,71},{8,72},{9,... | collective-permute-start | bytes 786440 | tf_op jit(solution)/shard_map/ppermute | solution.py:32
  41.2 8.5 %collective-permute-start.10 = (bf16[256,512]{1,0:T(8,128)(2,1)S(1)}, bf16[256,512]{1,0:T(8,128)(2,1)S(1)}, u32[]{:S(2)}, u32[]{:S(2)}) collective-permute-start(bf16[256,512]{1,0:T(8,128)(2,1)S(1)} %copy-done.6), channel_id=1, source_target_pairs={{0,192},{1,193},{2,194},{3,195},{4,196},{5,197},{6,198},{7,199},{8... | collective-permute-start | bytes 786440 | tf_op jit(solution)/shard_map/ppermute | solution.py:32
  43.3 7.9 %collective-permute-start.6 = (bf16[256,512]{1,0:T(8,128)(2,1)S(1)}, bf16[256,512]{1,0:T(8,128)(2,1)S(1)}, u32[]{:S(2)}, u32[]{:S(2)}) collective-permute-start(bf16[256,512]{1,0:T(8,128)(2,1)S(1)} %copy-done.7), channel_id=1, source_target_pairs={{0,8},{1,9},{2,10},{3,11},{4,12},{5,13},{6,14},{7,15},{8,0},{9,1},... | collective-permute-start | bytes 786440 | tf_op jit(solution)/shard_map/ppermute | solution.py:32
  43.3 7.9 %collective-permute-start.9 = (bf16[256,512]{1,0:T(8,128)(2,1)S(1)}, bf16[256,512]{1,0:T(8,128)(2,1)S(1)}, u32[]{:S(2)}, u32[]{:S(2)}) collective-permute-start(bf16[256,512]{1,0:T(8,128)(2,1)S(1)} %copy-done.6), channel_id=1, source_target_pairs={{0,8},{1,9},{2,10},{3,11},{4,12},{5,13},{6,14},{7,15},{8,0},{9,1},... | collective-permute-start | bytes 786440 | tf_op jit(solution)/shard_map/ppermute | solution.py:32
  47.2 4.1 %copy-start.8 = (bf16[256,512]{1,0:T(8,128)(2,1)}, bf16[256,512]{1,0:T(8,128)(2,1)S(1)}, u32[]{:S(2)}) copy-start(bf16[256,512]{1,0:T(8,128)(2,1)S(1)} %collective-permute-done.7.refs_6_) | copy-start | bytes 786436
  47.2 4.0 %collective-permute-start.8 = (bf16[256,512]{1,0:T(8,128)(2,1)S(1)}, bf16[256,512]{1,0:T(8,128)(2,1)S(1)}, u32[]{:S(2)}, u32[]{:S(2)}) collective-permute-start(bf16[256,512]{1,0:T(8,128)(2,1)S(1)} %collective-permute-done.7.refs_6_), channel_id=1, source_target_pairs={{0,8},{1,9},{2,10},{3,11},{4,12},{5,13},{6,14},{7,15},{8,0},{9,1},... | collective-permute-start | bytes 786440 | tf_op jit(solution)/shard_map/ppermute | solution.py:32
  49.7 1.6 %copy-start.9 = (bf16[256,512]{1,0:T(8,128)(2,1)}, bf16[256,512]{1,0:T(8,128)(2,1)S(1)}, u32[]{:S(2)}) copy-start(bf16[256,512]{1,0:T(8,128)(2,1)S(1)} %collective-permute-done.10.refs_14_) | copy-start | bytes 786436
  49.7 1.5 %collective-permute-start.11 = (bf16[256,512]{1,0:T(8,128)(2,1)S(1)}, bf16[256,512]{1,0:T(8,128)(2,1)S(1)}, u32[]{:S(2)}, u32[]{:S(2)}) collective-permute-start(bf16[256,512]{1,0:T(8,128)(2,1)S(1)} %collective-permute-done.10.refs_14_), channel_id=1, source_target_pairs={{0,8},{1,9},{2,10},{3,11},{4,12},{5,13},{6,14},{7,15},{8,0},{9,1},... | collective-permute-start | bytes 786440 | tf_op jit(solution)/shard_map/ppermute | solution.py:32
  51.2 0.7 copy-start.10
  51.2 0.8 copy-start.11
  51.3 0.9 copy-start.12
  51.3 1.0 copy-start.13
  57.5 2.8 %collective-permute-start.14 = (f32[256,256]{1,0:T(8,128)S(1)}, f32[256,256]{1,0:T(8,128)S(1)}, u32[]{:S(2)}, u32[]{:S(2)}) collective-permute-start(f32[256,256]{1,0:T(8,128)S(1)} %own_terms.1.own_ref), channel_id=1, source_target_pairs={{0,8},{1,9},{2,10},{3,11},{4,12},{5,13},{6,14},{7,15},{8,0},{9,1},... | collective-permute-start | bytes 786440 | tf_op jit(solution)/shard_map/ppermute | solution.py:32
  58.1 7.7 %collective-permute-start.13 = (f16[200,512]{1,0:T(8,128)(2,1)S(1)}, f16[200,512]{1,0:T(8,128)(2,1)S(1)}, u32[]{:S(2)}, u32[]{:S(2)}) collective-permute-start(f16[200,512]{1,0:T(8,128)(2,1)S(1)} %convert_element_type.46), channel_id=1, source_target_pairs={{0,64},{1,65},{2,66},{3,67},{4,68},{5,69},{6,70},{7,71},{8,72},{9,... | collective-permute-start | bytes 614408 | tf_op jit(solution)/shard_map/ppermute | solution.py:32
  58.2 9.4 %collective-permute-start.12 = (f16[200,512]{1,0:T(8,128)(2,1)S(1)}, f16[200,512]{1,0:T(8,128)(2,1)S(1)}, u32[]{:S(2)}, u32[]{:S(2)}) collective-permute-start(f16[200,512]{1,0:T(8,128)(2,1)S(1)} %convert_element_type.45), channel_id=1, source_target_pairs={{0,192},{1,193},{2,194},{3,195},{4,196},{5,197},{6,198},{7,199},{8... | collective-permute-start | bytes 614408 | tf_op jit(solution)/shard_map/ppermute | solution.py:32
  61.4 9.5 %copy-start.4 = (f32[192,1024]{1,0:T(8,128)S(1)}, f32[192,1024]{1,0:T(8,128)}, u32[]{:S(2)}) copy-start(f32[192,1024]{1,0:T(8,128)} %get-tuple-element.61.wide_ref) | copy-start | bytes 2359300
  61.4 9.5 %copy-start.5 = (f32[192,256]{1,0:T(8,128)S(1)}, f32[192,256]{1,0:T(8,128)}, u32[]{:S(2)}) copy-start(f32[192,256]{1,0:T(8,128)} %get-tuple-element.63.narrow_ref) | copy-start | bytes 589828
  61.5 8.2 %collective-permute-start.17 = (f16[200,256]{1,0:T(8,128)(2,1)S(1)}, f16[200,256]{1,0:T(8,128)(2,1)S(1)}, u32[]{:S(2)}, u32[]{:S(2)}) collective-permute-start(f16[200,256]{1,0:T(8,128)(2,1)S(1)} %convert_element_type.52), channel_id=1, source_target_pairs={{0,128},{1,129},{2,130},{3,131},{4,132},{5,133},{6,134},{7,135},{8... | collective-permute-start | bytes 307208 | tf_op jit(solution)/shard_map/ppermute | solution.py:32
  63.5 6.3 %collective-permute-start.16 = (f16[200,256]{1,0:T(8,128)(2,1)S(1)}, f16[200,256]{1,0:T(8,128)(2,1)S(1)}, u32[]{:S(2)}, u32[]{:S(2)}) collective-permute-start(f16[200,256]{1,0:T(8,128)(2,1)S(1)} %convert_element_type.51), channel_id=1, source_target_pairs={{0,64},{1,65},{2,66},{3,67},{4,68},{5,69},{6,70},{7,71},{8,72},{9,... | collective-permute-start | bytes 307208 | tf_op jit(solution)/shard_map/ppermute | solution.py:32
  63.6 7.3 %collective-permute-start.15 = (f16[200,256]{1,0:T(8,128)(2,1)S(1)}, f16[200,256]{1,0:T(8,128)(2,1)S(1)}, u32[]{:S(2)}, u32[]{:S(2)}) collective-permute-start(f16[200,256]{1,0:T(8,128)(2,1)S(1)} %convert_element_type.50), channel_id=1, source_target_pairs={{0,192},{1,193},{2,194},{3,195},{4,196},{5,197},{6,198},{7,199},{8... | collective-permute-start | bytes 307208 | tf_op jit(solution)/shard_map/ppermute | solution.py:32

commit v5 on v4

--- a/solution.py
+++ b/solution.py
@@ -45,19 +45,51 @@
     return ref[block, values, :] * jnp.exp2(ref[block, exponents, :])
 
 
-def project_kernel(hidden_ref, w_key_ref, w_value_ref, out_ref):
-    hidden = hidden_ref[...]
-    for i, ref in enumerate((w_key_ref, w_value_ref)):
-        block = dot(hidden, ref[...], ((1,), (0,))).astype(jnp.bfloat16)
-        for b in range(out_ref.shape[0]):
-            out_ref[b, :, i * HD : (i + 1) * HD] = block
+def project_kernel(hidden_hbm, w_key_hbm, w_value_hbm, out_hbm, hidden_ref, weight_ref, block_ref, in_sems, out_sems):
+    chunks = in_sems.shape[0]
+    depth = hidden_ref.shape[1] // chunks
+    copies = []
+    for c in range(chunks):
+        part = pl.ds(c * depth, depth)
+        copies.append(
+            [
+                pltpu.make_async_copy(hidden_hbm.at[:, part], hidden_ref.at[:, part], in_sems.at[c, 0]),
+                pltpu.make_async_copy(w_key_hbm.at[part, :], weight_ref.at[part, pl.ds(0, HD)], in_sems.at[c, 1]),
+                pltpu.make_async_copy(w_value_hbm.at[part, :], weight_ref.at[part, pl.ds(HD, HD)], in_sems.at[c, 2]),
+            ]
+        )
+        for copy in copies[-1]:
+            copy.start()
+    total = None
+    for c in range(chunks):
+        for copy in copies[c]:
+            copy.wait()
+        term = dot(hidden_ref[:, c * depth : (c + 1) * depth], weight_ref[c * depth : (c + 1) * depth, :], ((1,), (0,)))
+        total = term if total is None else total + term
+    block_ref[...] = total.astype(jnp.bfloat16)
+    copies = [pltpu.make_async_copy(block_ref, out_hbm.at[b], out_sems.at[b]) for b in range(out_hbm.shape[0])]
+    for copy in copies:
+        copy.start()
+    for copy in copies:
+        copy.wait()
 
 
 def project(hidden, w_key, w_value):
     hidden, w_key, w_value = (pltpu.with_memory_space_constraint(v, pltpu.HBM) for v in (hidden, w_key, w_value))
+    tokens, width = hidden.shape
+    anywhere = pl.BlockSpec(memory_space=pl.ANY)
     return pl.pallas_call(
         project_kernel,
-        out_shape=jax.ShapeDtypeStruct((8, hidden.shape[0], 2 * HD), jnp.bfloat16),
+        in_specs=[anywhere] * 3,
+        out_specs=anywhere,
+        out_shape=pltpu.HBM((8, tokens, 2 * HD), jnp.bfloat16),
+        scratch_shapes=[
+            pltpu.VMEM((tokens, width), jnp.bfloat16),
+            pltpu.VMEM((width, 2 * HD), jnp.bfloat16),
+            pltpu.VMEM((tokens, 2 * HD), jnp.bfloat16),
+            pltpu.SemaphoreType.DMA((3, 3)),
+            pltpu.SemaphoreType.DMA((8,)),
+        ],
         compiler_params=pltpu.CompilerParams(vmem_limit_bytes=16 * MIB),
         name="project",
     )(hidden, w_key, w_value)
@@ -93,17 +125,44 @@
 
 
 def attention_kernel(
-    q_ref, da_ref, k_ref, v_ref, d_query_ref, attended_ref, dkv_ref, scores_ref, d_probs_ref, probs_ref, d_scores_ref
+    q_hbm, da_hbm, kv_hbm, d_query_hbm, attended_hbm, dkv_ref,
+    q_ref, da_ref, k_ref, v_ref, d_query_ref, attended_ref, scores_ref, d_probs_ref, probs_ref, d_scores_ref,
+    side_sems, block_sems, out_sems,
 ):
     bf = jnp.bfloat16
     blocks, _, tokens = dkv_ref.shape
     chunk = 16
     head_cols = lambda h: slice(h * HD, (h + 1) * HD)
     block_rows = lambda b: slice(b * tokens, (b + 1) * tokens)
+    sides_in = [
+        pltpu.make_async_copy(source, ref, side_sems.at[i])
+        for i, (source, ref) in enumerate(((q_hbm, q_ref), (da_hbm, da_ref)))
+    ]
+    blocks_in = [
+        [
+            pltpu.make_async_copy(
+                kv_hbm.at[pl.ds(b * tokens, tokens), pl.ds(i * HD, HD)],
+                ref.at[pl.ds(b * tokens, tokens), :],
+                block_sems.at[i, b],
+            )
+            for b in range(blocks)
+        ]
+        for i, ref in enumerate((k_ref, v_ref))
+    ]
+    for copy in sides_in:
+        copy.start()
+    for b in range(blocks):
+        for i in range(2):
+            blocks_in[i][b].start()
+    leaving = []
 
     def ahead(h):
-        def make(b, side_ref, other_ref, to_ref):
+        def make(b, i, side_ref, other_ref, to_ref):
             def run():
+                if h == 0:
+                    blocks_in[i][b].wait()
+                    if b == 0:
+                        sides_in[i].wait()
                 to_ref[h % 2, :, block_rows(b)] = dot(side_ref[:, head_cols(h)], other_ref[block_rows(b), :], ((1,), (1,)))
 
             return run
@@ -111,7 +170,7 @@
         return [
             make(b, *refs)
             for b in range(blocks)
-            for refs in ((q_ref, k_ref, scores_ref), (da_ref, v_ref, d_probs_ref))
+            for refs in ((0, q_ref, k_ref, scores_ref), (1, da_ref, v_ref, d_probs_ref))
         ]
 
     def softmax(h, i):
@@ -135,16 +194,19 @@
 
             return run
 
-        def rows_of(from_ref, other_ref, to_ref, scale):
+        def rows_of(from_ref, other_ref, to_ref, scale, to_hbm, i):
             def run():
                 product = dot(from_ref[h % 2], other_ref[...], ((1,), (0,)))
                 to_ref[:, head_cols(h)] = (product * scale if scale else product).astype(bf)
+                here = (slice(None), pl.ds(h * HD, HD))
+                leaving.append(pltpu.make_async_copy(to_ref.at[here], to_hbm.at[here], out_sems.at[i, h]))
+                leaving[-1].start()
 
             return run
 
         work = [terms(b, i, ref) for b in range(blocks) for i, ref in enumerate((d_scores_ref, probs_ref))]
-        work.insert(4, rows_of(probs_ref, v_ref, attended_ref, None))
-        work.insert(13, rows_of(d_scores_ref, k_ref, d_query_ref, SCALE))
+        work.insert(4, rows_of(probs_ref, v_ref, attended_ref, None, attended_hbm, 0))
+        work.insert(13, rows_of(d_scores_ref, k_ref, d_query_ref, SCALE, d_query_hbm, 1))
         return work
 
     for run in ahead(0):
@@ -174,36 +236,36 @@
         factor = jnp.exp2(-power) * scale
         for b in range(blocks):
             dkv_ref[b, rows, :] = dkv_ref[b, rows, :] * factor
-            dkv_ref[b, pl.ds(2 * HD + 8 * i, 8), :] = jnp.broadcast_to(power, (8, tokens))
+            dkv_ref[b, pl.ds(2 * HD + 4 * i, 4), :] = jnp.broadcast_to(power, (4, tokens))
+    for copy in leaving:
+        copy.wait()
 
 
 def attention(queries, d_att, keys_values):
     tokens, inner = queries.shape
     length = keys_values.shape[0]
-    whole = pl.BlockSpec((tokens, inner), lambda i: (0, 0))
-    terms = (length // tokens, 2 * HD + 16, tokens)
+    blocks = length // tokens
+    anywhere = pl.BlockSpec(memory_space=pl.ANY)
+    small, large = pltpu.VMEM((tokens, inner), jnp.bfloat16), pltpu.VMEM((length, HD), jnp.bfloat16)
+    wide, half = pltpu.VMEM((2, tokens, length), jnp.float32), pltpu.VMEM((2, tokens, length), jnp.bfloat16)
+    operands = [pltpu.with_memory_space_constraint(v, pltpu.HBM) for v in (queries, d_att, keys_values)]
     return pl.pallas_call(
         attention_kernel,
-        grid=(1,),
-        in_specs=[
-            whole,
-            whole,
-            pl.BlockSpec((length, HD), lambda i: (0, 0)),
-            pl.BlockSpec((length, HD), lambda i: (0, 1)),
-        ],
-        out_specs=[whole, whole, pl.BlockSpec(terms, lambda i: (0, 0, 0))],
+        in_specs=[anywhere] * 3,
+        out_specs=[anywhere, anywhere, pl.BlockSpec(memory_space=pltpu.VMEM)],
         out_shape=[
             pltpu.HBM((tokens, inner), jnp.bfloat16),
             pltpu.HBM((tokens, inner), jnp.bfloat16),
-            jax.ShapeDtypeStruct(terms, jnp.float32),
+            jax.ShapeDtypeStruct((blocks, 2 * HD + 8, tokens), jnp.float32),
         ],
-        scratch_shapes=[pltpu.VMEM((2, tokens, length), jnp.float32)] * 2 + [pltpu.VMEM((2, tokens, length), jnp.bfloat16)] * 2,
+        scratch_shapes=[small, small, large, large, small, small, wide, wide, half, half]
+        + [pltpu.SemaphoreType.DMA((2,)), pltpu.SemaphoreType.DMA((2, blocks)), pltpu.SemaphoreType.DMA((2, HEADS))],
         compiler_params=pltpu.CompilerParams(vmem_limit_bytes=32 * MIB),
         cost_estimate=pl.CostEstimate(
             flops=12 * tokens * inner * length, bytes_accessed=4 << 20, transcendentals=tokens * HEADS * length
         ),
         name="attention",
-    )(queries, d_att, keys_values, keys_values)
+    )(*operands)
 
 
 def store_scaled(values, ref):
@@ -276,7 +338,7 @@
 
 def own_terms_kernel(terms_ref, out_ref):
     for i in range(2):
-        rows, powers = pl.ds(i * HD, HD), pl.ds(2 * HD + 8 * i, 1)
+        rows, powers = pl.ds(i * HD, HD), pl.ds(2 * HD + 4 * i, 1)
         total = unscaled(terms_ref, 0, rows, powers)
         for b in range(1, terms_ref.shape[0]):
             total = total + unscaled(terms_ref, b, rows, powers)
@@ -390,7 +452,6 @@
     g_from = [exchange(g_far[0], 3 << 6), exchange(g_far[1], (3 << 6) | 8)]
     h_core, g_core = from_other_core(h_core), from_other_core(g_core)
 
-    queries, d_att = (pltpu.with_memory_space_constraint(v, pltpu.HBM) for v in (queries, d_att))
     d_query, attended, terms = attention(queries, d_att, gathered.reshape(8 * tokens, 2 * HD))
     terms, d_query, attended, h_from, g_from, h_core, g_core = lax.optimization_barrier(
         (terms, d_query, attended, h_from, g_from, h_core, g_core)

time: 103 us -> 106 us (1.029)
  Pallas kernels: 21.8 us -> 24.8 us
    pallas_call x2, Pallas kernels: 12.6 us -> 15.6 us  [the longest x1 12.5 us: attention(): pl.pallas_call(attention_kernel, in_specs=[anywhere] * 3, out_specs=[anyw...]
  transfers between devices with their start and end apart: 20 -> 20, of which waited for: 8 -> 8; matrix products, arithmetic and copies ran while one was open for 4% -> 4% of each run, Pallas kernels for 17% -> 19%
where the time goes in v5:
time: 106 us; the launch traced here: 105 us
  blocking collectives  29.8 us (28%)
  starting transfers between devices  27.2 us (26%)
  Pallas kernels  24.8 us (23%)
  waiting for transfers between devices  14.2 us (13%)
  matrix products  4.03 us (4%)
  other arithmetic  3.02 us (3%)
    ppermute x18, starting transfers between devices, exchange(): return lax.ppermute(value, AXES, [(i, i ^ mask) for i in range(256)])  16.2 us
    all_to_all x1, blocking collectives, local(): lax.all_to_all(part, AXES, 0, 0, axis_index_groups=Z_HI_GROUPS, tiled=True)  15.9 us
    all_to_all x1, blocking collectives, local(): lax.all_to_all(part.astype(half), 'seq', 0, 0, tiled=True).astype(f32)  13.9 us
    pallas_call x1, Pallas kernels, attention(): pl.pallas_call(attention_kernel, in_specs=[anywhere] * 3, out_specs=[anyw...  12.5 us
    ppermute x18, waiting for transfers between devices, exchange(): return lax.ppermute(value, AXES, [(i, i ^ mask) for i in range(256)])  11.4 us
    all_to_all x1, starting transfers between devices, local(): lax.all_to_all(project(hidden, w_key, w_value), 'seq', 0, 0, tiled=True)  6.11 us
    all_to_all x1, starting transfers between devices, local(): terms = lax.all_to_all(terms.astype(half), 'seq', 0, 0, tiled=True)  4.83 us
    dot_general x3, matrix products, dot(): lax.dot_general(left, right, (dims, ((), ())), preferred_element_type=jnp...  4.03 us
  transfers between devices with their start and end apart: 20, of which 8 were waited for; matrix products, arithmetic and copies ran while one was open for 4% of the time, Pallas kernels for 19%

profile of v5, /device:TPU:32, one launch (start us, length us, event | category | flops | bytes accessed | tf_op | source)
XLA Modules:
  0.0 105.0 jit_solution(16481211701839912213)
XLA Ops:
  0.6 3.1 %project.1 = bf16[8,256,256]{2,1,0:T(8,128)(2,1)} custom-call(bf16[256,1536]{1,0:T(8,128)(2,1)} %bitcast.19, bf16[1536,128]{1,0:T(8,128)(2,1)} %w_key_hbm.1, bf16[1536,128]{1,0:T(8,128)(2,1)} %w_value_hbm.1), custom_call_target="tpu_custom_call" | custom-call | tf_op jit(solution)/shard_map/project/pallas_call | solution.py:81
  3.8 6.1 %all-to-all-start = ((bf16[8,256,256]{2,1,0:T(8,128)(2,1)}), bf16[8,256,256]{2,1,0:T(8,128)(2,1)}, u32[]{:S(2)}, u32[]{:S(2)}) async-start(bf16[8,256,256]{2,1,0:T(8,128)(2,1)} %project.1), calls=%async_computation | async-start | bytes 2097152 | tf_op jit(solution)/shard_map/all_to_all | solution.py:444
  9.9 0.1 pad_add_fusion.place_ref
  10.0 1.6 %turn.3 = (bf16[384,256]{1,0:T(8,128)(2,1)S(1)}, bf16[384,256]{1,0:T(8,128)(2,1)}, bf16[384,256]{1,0:T(8,128)(2,1)S(1)}, bf16[384,256]{1,0:T(8,128)(2,1)}) custom-call(s32[2]{0:T(128)S(1)} %pad_add_fusion.place_ref, bf16[256,1536]{1,0:T(8,128)(2,1)S(1)} %bitcast.21), custom_call_target="tpu_custom_call" | custom-call | tf_op jit(solution)/shard_map/turn/pallas_call | solution.py:112
  11.6 2.7 %collective-permute-start.2 = (bf16[384,256]{1,0:T(8,128)(2,1)S(1)}, bf16[384,256]{1,0:T(8,128)(2,1)S(1)}, u32[]{:S(2)}, u32[]{:S(2)}) collective-permute-start(bf16[384,256]{1,0:T(8,128)(2,1)S(1)} %get-tuple-element.43), channel_id=1, source_target_pairs={{0,192},{1,193},{2,194},{3,195},{4,196},{5,197},{6,198},{7,199},{8... | collective-permute-start | bytes 589832 | tf_op jit(solution)/shard_map/ppermute | solution.py:32
  14.3 0.6 collective-permute-start.5
  14.9 1.7 %turn.2 = (bf16[768,256]{1,0:T(8,128)(2,1)S(1)}, bf16[768,256]{1,0:T(8,128)(2,1)}, bf16[384,256]{1,0:T(8,128)(2,1)}, bf16[384,256]{1,0:T(8,128)(2,1)}) custom-call(s32[2]{0:T(128)S(1)} %pad_add_fusion.place_ref, bf16[256,1536]{1,0:T(8,128)(2,1)S(1)} %bitcast.20), custom_call_target="tpu_custom_call" | custom-call | tf_op jit(solution)/shard_map/turn/pallas_call | solution.py:112
  16.6 0.2 collective-permute-start
  16.9 1.3 %convolution_convert_fusion.2.q_hbm = bf16[256,512]{1,0:T(8,128)(2,1)} fusion(bf16[1536,512]{1,0:T(8,128)(2,1)S(1)} %copy-done.14, bf16[1,256,1536]{2,1,0:T(8,128)(2,1)S(1)} %copy-done.1), kind=kOutput, calls=%fused_computation.2 | convolution fusion | flops 402784256 | bytes 2621440 | tf_op jit(solution)/shard_map/dot_general | solution.py:28
  18.1 1.3 %convolution_convert_fusion.1.da_hbm = bf16[256,512]{1,0:T(8,128)(2,1)} fusion(bf16[1536,512]{1,0:T(8,128)(2,1)S(1)} %copy-done, bf16[1,256,1536]{2,1,0:T(8,128)(2,1)S(1)} %copy-done.3), kind=kOutput, calls=%fused_computation.1 | convolution fusion | flops 402784256 | bytes 2621440 | tf_op jit(solution)/shard_map/dot_general | solution.py:28
  19.4 0.2 collective-permute-done.2.refs_10_
  19.7 1.7 %collective-permute-start.1 = (bf16[384,256]{1,0:T(8,128)(2,1)}, bf16[384,256]{1,0:T(8,128)(2,1)S(1)}, u32[]{:S(2)}, u32[]{:S(2)}) collective-permute-start(bf16[384,256]{1,0:T(8,128)(2,1)} %get-tuple-element.42), channel_id=1, source_target_pairs={{0,72},{1,73},{2,74},{3,75},{4,76},{5,77},{6,78},{7,79},{8,64},{9,... | collective-permute-start | bytes 589832 | tf_op jit(solution)/shard_map/ppermute | solution.py:32
  21.3 2.9 %all-to-all-done = bf16[8,256,256]{2,1,0:T(8,128)(2,1)} async-done(((bf16[8,256,256]{2,1,0:T(8,128)(2,1)}), bf16[8,256,256]{2,1,0:T(8,128)(2,1)}, u32[]{:S(2)}, u32[]{:S(2)}) %all-to-all-start) | async-done | bytes 1048608 | tf_op jit(solution)/shard_map/all_to_all | solution.py:444
  24.2 12.5 %attention.1 = (bf16[256,512]{1,0:T(8,128)(2,1)}, bf16[256,512]{1,0:T(8,128)(2,1)}, f32[8,264,256]{2,1,0:T(8,128)S(1)}) custom-call(bf16[256,512]{1,0:T(8,128)(2,1)} %convolution_convert_fusion.2.q_hbm, bf16[256,512]{1,0:T(8,128)(2,1)} %convolution_convert_fusion.1.da_hbm, bf16[2048,256]{1,0:T(8,128)(2,1)} %bitcast.2.kv_hbm), custom_call_target="tpu_custom_call" | custom-call | flops 3221225472 | bytes 4194304 | tf_op jit(solution)/shard_map/attention/pallas_call | solution.py:252
  36.7 1.2 %convert_element_type.44 = f16[8,264,256]{2,1,0:T(8,128)(2,1)} convert(f32[8,264,256]{2,1,0:T(8,128)S(1)} %get-tuple-element.47) | non-fusion elementwise | flops 540672 | bytes 3244032 | tf_op jit(solution)/shard_map/convert_element_type | solution.py:459
  37.9 4.8 %all-to-all-start.1 = ((f16[8,264,256]{2,1,0:T(8,128)(2,1)}), f16[8,264,256]{2,1,0:T(8,128)(2,1)}, u32[]{:S(2)}, u32[]{:S(2)}) async-start(f16[8,264,256]{2,1,0:T(8,128)(2,1)} %convert_element_type.44), calls=%async_computation.1 | async-start | bytes 2162688 | tf_op jit(solution)/shard_map/all_to_all | solution.py:459
  42.7 1.5 %collective-permute-start.7 = (bf16[256,512]{1,0:T(8,128)(2,1)S(1)}, bf16[256,512]{1,0:T(8,128)(2,1)S(1)}, u32[]{:S(2)}, u32[]{:S(2)}) collective-permute-start(bf16[256,512]{1,0:T(8,128)(2,1)S(1)} %copy-done.7), channel_id=1, source_target_pairs={{0,64},{1,65},{2,66},{3,67},{4,68},{5,69},{6,70},{7,71},{8,72},{9,... | collective-permute-start | bytes 786440 | tf_op jit(solution)/shard_map/ppermute | solution.py:32
  44.2 2.1 %collective-permute-start.10 = (bf16[256,512]{1,0:T(8,128)(2,1)S(1)}, bf16[256,512]{1,0:T(8,128)(2,1)S(1)}, u32[]{:S(2)}, u32[]{:S(2)}) collective-permute-start(bf16[256,512]{1,0:T(8,128)(2,1)S(1)} %copy-done.6), channel_id=1, source_target_pairs={{0,192},{1,193},{2,194},{3,195},{4,196},{5,197},{6,198},{7,199},{8... | collective-permute-start | bytes 786440 | tf_op jit(solution)/shard_map/ppermute | solution.py:32
  46.3 0.5 collective-permute-start.9
  46.8 3.4 %collective-permute-done.7.refs_6_ = bf16[256,512]{1,0:T(8,128)(2,1)S(1)} collective-permute-done((bf16[256,512]{1,0:T(8,128)(2,1)S(1)}, bf16[256,512]{1,0:T(8,128)(2,1)S(1)}, u32[]{:S(2)}, u32[]{:S(2)}) %collective-permute-start.7) | collective-permute-done | bytes 262176 | tf_op jit(solution)/shard_map/ppermute | solution.py:32
  50.2 2.5 %collective-permute-done.10.refs_14_ = bf16[256,512]{1,0:T(8,128)(2,1)S(1)} collective-permute-done((bf16[256,512]{1,0:T(8,128)(2,1)S(1)}, bf16[256,512]{1,0:T(8,128)(2,1)S(1)}, u32[]{:S(2)}, u32[]{:S(2)}) %collective-permute-start.10) | collective-permute-done | bytes 262176 | tf_op jit(solution)/shard_map/ppermute | solution.py:32
  52.8 1.5 %convolution_convert_fusion = bf16[256,1536]{1,0:T(8,128)(2,1)} fusion(bf16[256,512]{1,0:T(8,128)(2,1)S(1)} %copy-done.6, bf16[1536,512]{1,0:T(8,128)(2,1)S(1)} %copy-done), kind=kOutput, calls=%fused_computation | convolution fusion | flops 403046400 | bytes 2621440 | tf_op jit(solution)/shard_map/dot_general | solution.py:28
  54.3 0.6 copy-done.10
  54.9 0.1 copy-done.11
  55.1 0.1 copy-done.12
  55.2 0.1 copy-done.13
  55.3 3.5 %wide.1 = (f32[192,1024]{1,0:T(8,128)}, f32[200,512]{1,0:T(8,128)S(1)}, f32[200,512]{1,0:T(8,128)S(1)}) custom-call(bf16[768,256]{1,0:T(8,128)(2,1)S(1)} %get-tuple-element.48.refs_0_.mine_ref, bf16[768,256]{1,0:T(8,128)(2,1)S(1)} %collective-permute-done.4.refs_1_.theirs_ref, bf16[384,256]{1,0:T(8,128)(2,1)} %collective-permute-done.refs_2_, ...), custom_call_target="tpu_custom_call" | custom-call | flops 1073741824 | bytes 5242880 | tf_op jit(solution)/shard_map/wide/pallas_call | solution.py:293
  58.8 1.4 %convert_element_type.49.terms_ref = f32[8,264,256]{2,1,0:T(8,128)S(1)} convert(f16[8,264,256]{2,1,0:T(8,128)(2,1)} %all-to-all-done.1) | non-fusion elementwise | flops 540672 | bytes 3244032 | tf_op jit(solution)/shard_map/convert_element_type | solution.py:474
  60.2 0.1 own_terms.1.own_ref
  60.4 0.6 collective-permute-start.14
  61.0 2.1 %collective-permute-start.12 = (f16[200,512]{1,0:T(8,128)(2,1)S(1)}, f16[200,512]{1,0:T(8,128)(2,1)S(1)}, u32[]{:S(2)}, u32[]{:S(2)}) collective-permute-start(f16[200,512]{1,0:T(8,128)(2,1)S(1)} %convert_element_type.45), channel_id=1, source_target_pairs={{0,192},{1,193},{2,194},{3,195},{4,196},{5,197},{6,198},{7,199},{8... | collective-permute-start | bytes 614408 | tf_op jit(solution)/shard_map/ppermute | solution.py:32
  63.1 1.2 %narrow.1 = (f32[192,256]{1,0:T(8,128)}, f32[200,256]{1,0:T(8,128)S(1)}, f32[200,256]{1,0:T(8,128)S(1)}, f32[200,256]{1,0:T(8,128)S(1)}) custom-call(bf16[768,256]{1,0:T(8,128)(2,1)S(1)} %get-tuple-element.48.refs_0_.mine_ref, bf16[768,256]{1,0:T(8,128)(2,1)S(1)} %collective-permute-done.4.refs_1_.theirs_ref, f32[256,256]{1,0:T(8,128)S(1)} %own_terms.1.own_ref, ...), custom_call_target="tpu_custom_call" | custom-call | flops 1 | bytes 1 | tf_op jit(solution)/shard_map/narrow/pallas_call | solution.py:330
  64.3 2.1 %collective-permute-start.17 = (f16[200,256]{1,0:T(8,128)(2,1)S(1)}, f16[200,256]{1,0:T(8,128)(2,1)S(1)}, u32[]{:S(2)}, u32[]{:S(2)}) collective-permute-start(f16[200,256]{1,0:T(8,128)(2,1)S(1)} %convert_element_type.52), channel_id=1, source_target_pairs={{0,128},{1,129},{2,130},{3,131},{4,132},{5,133},{6,134},{7,135},{8... | collective-permute-start | bytes 307208 | tf_op jit(solution)/shard_map/ppermute | solution.py:32
  66.4 0.0 collective-permute-start.16
  66.4 2.1 %collective-permute-start.15 = (f16[200,256]{1,0:T(8,128)(2,1)S(1)}, f16[200,256]{1,0:T(8,128)(2,1)S(1)}, u32[]{:S(2)}, u32[]{:S(2)}) collective-permute-start(f16[200,256]{1,0:T(8,128)(2,1)S(1)} %convert_element_type.50), channel_id=1, source_target_pairs={{0,192},{1,193},{2,194},{3,195},{4,196},{5,197},{6,198},{7,199},{8... | collective-permute-start | bytes 307208 | tf_op jit(solution)/shard_map/ppermute | solution.py:32
  68.5 0.2 collective-permute-done.13
  68.7 1.7 %collective-permute-done.12 = f16[200,512]{1,0:T(8,128)(2,1)S(1)} collective-permute-done((f16[200,512]{1,0:T(8,128)(2,1)S(1)}, f16[200,512]{1,0:T(8,128)(2,1)S(1)}, u32[]{:S(2)}, u32[]{:S(2)}) %collective-permute-start.12) | collective-permute-done | bytes 204832 | tf_op jit(solution)/shard_map/ppermute | solution.py:32
  70.4 0.1 maximum_convert_fusion.wide_got_ref
  70.5 2.1 %collective-permute-done.17 = f16[200,256]{1,0:T(8,128)(2,1)S(1)} collective-permute-done((f16[200,256]{1,0:T(8,128)(2,1)S(1)}, f16[200,256]{1,0:T(8,128)(2,1)S(1)}, u32[]{:S(2)}, u32[]{:S(2)}) %collective-permute-start.17) | collective-permute-done | bytes 102432 | tf_op jit(solution)/shard_map/ppermute | solution.py:32
  72.7 1.1 %collective-permute-done.15 = f16[200,256]{1,0:T(8,128)(2,1)S(1)} collective-permute-done((f16[200,256]{1,0:T(8,128)(2,1)S(1)}, f16[200,256]{1,0:T(8,128)(2,1)S(1)}, u32[]{:S(2)}, u32[]{:S(2)}) %collective-permute-start.15) | collective-permute-done | bytes 102432 | tf_op jit(solution)/shard_map/ppermute | solution.py:32
  73.8 0.1 maximum_convert_fusion.1.narrow_got_ref
  73.9 0.5 after_x.1
  74.3 0.1 convert_element_type.54
  74.4 13.9 %all_to_all.20 = f16[8,248,128]{2,1,0:T(8,128)(2,1)S(1)} all-to-all(f16[8,248,128]{2,1,0:T(8,128)(2,1)S(1)} %convert_element_type.54), channel_id=1, replica_groups=mesh['dp'=32,'seq'=8] {'seq'}, dimensions={0} | all-to-all | bytes 1015808 | tf_op jit(solution)/shard_map/all_to_all | solution.py:479
  88.3 0.1 convert_element_type.55.got_ref
  88.4 0.1 after_seq.1
  88.5 15.9 %all_to_all.21.got_ref = f32[4,64,128]{2,1,0:T(8,128)S(1)} all-to-all(f32[4,64,128]{2,1,0:T(8,128)S(1)} %after_seq.1), channel_id=1, replica_groups={{0,16,32,48},{8,24,40,56},{4,20,36,52},{12,28,44,60},{1,17,33,49},{9,25..., dimensions={0} | all-to-all | bytes 262144 | tf_op jit(solution)/shard_map/all_to_all | solution.py:480
  104.4 0.6 last_sum.1
  (49 shorter events, 0.2 us)
Async XLA Ops:
  0.6 17.5 %copy-start = (bf16[1536,512]{1,0:T(8,128)(2,1)S(1)}, bf16[1536,512]{1,0:T(8,128)(2,1)}, u32[]{:S(2)}) copy-start(bf16[1536,512]{1,0:T(8,128)(2,1)} %param.10) | copy-start | bytes 4718596
  3.8 6.2 %copy-start.2 = (bf16[1,256,1536]{2,1,0:T(8,128)(2,1)S(1)}, bf16[1,256,1536]{2,1,0:T(8,128)(2,1)}, u32[]{:S(2)}) copy-start(bf16[1,256,1536]{2,1,0:T(8,128)(2,1)} %param.11) | copy-start | bytes 2359300
  3.8 11.1 %copy-start.1 = (bf16[1,256,1536]{2,1,0:T(8,128)(2,1)S(1)}, bf16[1,256,1536]{2,1,0:T(8,128)(2,1)}, u32[]{:S(2)}) copy-start(bf16[1,256,1536]{2,1,0:T(8,128)(2,1)} %param.6) | copy-start | bytes 2359300
  3.8 20.4 %all-to-all-start = ((bf16[8,256,256]{2,1,0:T(8,128)(2,1)}), bf16[8,256,256]{2,1,0:T(8,128)(2,1)}, u32[]{:S(2)}, u32[]{:S(2)}) async-start(bf16[8,256,256]{2,1,0:T(8,128)(2,1)} %project.1), calls=%async_computation | async-start | bytes 2097152 | tf_op jit(solution)/shard_map/all_to_all | solution.py:444
  9.9 7.0 %copy-start.14 = (bf16[1536,512]{1,0:T(8,128)(2,1)S(1)}, bf16[1536,512]{1,0:T(8,128)(2,1)}, u32[]{:S(2)}) copy-start(bf16[1536,512]{1,0:T(8,128)(2,1)} %param.7) | copy-start | bytes 4718596
  11.6 8.1 %collective-permute-start.2 = (bf16[384,256]{1,0:T(8,128)(2,1)S(1)}, bf16[384,256]{1,0:T(8,128)(2,1)S(1)}, u32[]{:S(2)}, u32[]{:S(2)}) collective-permute-start(bf16[384,256]{1,0:T(8,128)(2,1)S(1)} %get-tuple-element.43), channel_id=1, source_target_pairs={{0,192},{1,193},{2,194},{3,195},{4,196},{5,197},{6,198},{7,199},{8... | collective-permute-start | bytes 589832 | tf_op jit(solution)/shard_map/ppermute | solution.py:32
  14.3 22.4 %collective-permute-start.3 = (bf16[384,256]{1,0:T(8,128)(2,1)}, bf16[384,256]{1,0:T(8,128)(2,1)}, u32[]{:S(2)}, u32[]{:S(2)}) collective-permute-start(bf16[384,256]{1,0:T(8,128)(2,1)} %get-tuple-element.44), channel_id=1, source_target_pairs={{0,200},{1,201},{2,202},{3,203},{4,204},{5,205},{6,206},{7,207},{8... | collective-permute-start | bytes 589832 | tf_op jit(solution)/shard_map/ppermute | solution.py:32
  14.3 3.8 %copy-start.3 = (bf16[1,256,1536]{2,1,0:T(8,128)(2,1)S(1)}, bf16[1,256,1536]{2,1,0:T(8,128)(2,1)}, u32[]{:S(2)}) copy-start(bf16[1,256,1536]{2,1,0:T(8,128)(2,1)} %param.11) | copy-start | bytes 2359300
  14.3 22.4 %collective-permute-start.5 = (bf16[384,256]{1,0:T(8,128)(2,1)}, bf16[384,256]{1,0:T(8,128)(2,1)}, u32[]{:S(2)}, u32[]{:S(2)}) collective-permute-start(bf16[384,256]{1,0:T(8,128)(2,1)} %get-tuple-element.46), channel_id=1, source_target_pairs={{0,8},{1,9},{2,10},{3,11},{4,12},{5,13},{6,14},{7,15},{8,0},{9,1},... | collective-permute-start | bytes 589832 | tf_op jit(solution)/shard_map/ppermute | solution.py:32
  16.6 20.1 %collective-permute-start = (bf16[384,256]{1,0:T(8,128)(2,1)}, bf16[384,256]{1,0:T(8,128)(2,1)}, u32[]{:S(2)}, u32[]{:S(2)}) collective-permute-start(bf16[384,256]{1,0:T(8,128)(2,1)} %get-tuple-element.41), channel_id=1, source_target_pairs={{0,64},{1,65},{2,66},{3,67},{4,68},{5,69},{6,70},{7,71},{8,72},{9,... | collective-permute-start | bytes 589832 | tf_op jit(solution)/shard_map/ppermute | solution.py:32
  16.9 19.9 %collective-permute-start.4 = (bf16[768,256]{1,0:T(8,128)(2,1)}, bf16[768,256]{1,0:T(8,128)(2,1)S(1)}, u32[]{:S(2)}, u32[]{:S(2)}) collective-permute-start(bf16[768,256]{1,0:T(8,128)(2,1)} %get-tuple-element.45), channel_id=1, source_target_pairs={{0,8},{1,9},{2,10},{3,11},{4,12},{5,13},{6,14},{7,15},{8,0},{9,1},... | collective-permute-start | bytes 1179656 | tf_op jit(solution)/shard_map/ppermute | solution.py:32
  19.7 17.1 %collective-permute-start.1 = (bf16[384,256]{1,0:T(8,128)(2,1)}, bf16[384,256]{1,0:T(8,128)(2,1)S(1)}, u32[]{:S(2)}, u32[]{:S(2)}) collective-permute-start(bf16[384,256]{1,0:T(8,128)(2,1)} %get-tuple-element.42), channel_id=1, source_target_pairs={{0,72},{1,73},{2,74},{3,75},{4,76},{5,77},{6,78},{7,79},{8,64},{9,... | collective-permute-start | bytes 589832 | tf_op jit(solution)/shard_map/ppermute | solution.py:32
  37.9 4.8 %copy-start.7 = (bf16[256,512]{1,0:T(8,128)(2,1)S(1)}, bf16[256,512]{1,0:T(8,128)(2,1)}, u32[]{:S(2)}) copy-start(bf16[256,512]{1,0:T(8,128)(2,1)} %get-tuple-element.52.refs_4_) | copy-start | bytes 786436
  37.9 6.3 %copy-start.6 = (bf16[256,512]{1,0:T(8,128)(2,1)S(1)}, bf16[256,512]{1,0:T(8,128)(2,1)}, u32[]{:S(2)}) copy-start(bf16[256,512]{1,0:T(8,128)(2,1)} %get-tuple-element.57.refs_12_) | copy-start | bytes 786436
  37.9 20.9 %all-to-all-start.1 = ((f16[8,264,256]{2,1,0:T(8,128)(2,1)}), f16[8,264,256]{2,1,0:T(8,128)(2,1)}, u32[]{:S(2)}, u32[]{:S(2)}) async-start(f16[8,264,256]{2,1,0:T(8,128)(2,1)} %convert_element_type.44), calls=%async_computation.1 | async-start | bytes 2162688 | tf_op jit(solution)/shard_map/all_to_all | solution.py:459
  42.7 7.5 %collective-permute-start.7 = (bf16[256,512]{1,0:T(8,128)(2,1)S(1)}, bf16[256,512]{1,0:T(8,128)(2,1)S(1)}, u32[]{:S(2)}, u32[]{:S(2)}) collective-permute-start(bf16[256,512]{1,0:T(8,128)(2,1)S(1)} %copy-done.7), channel_id=1, source_target_pairs={{0,64},{1,65},{2,66},{3,67},{4,68},{5,69},{6,70},{7,71},{8,72},{9,... | collective-permute-start | bytes 786440 | tf_op jit(solution)/shard_map/ppermute | solution.py:32
  44.2 8.5 %collective-permute-start.10 = (bf16[256,512]{1,0:T(8,128)(2,1)S(1)}, bf16[256,512]{1,0:T(8,128)(2,1)S(1)}, u32[]{:S(2)}, u32[]{:S(2)}) collective-permute-start(bf16[256,512]{1,0:T(8,128)(2,1)S(1)} %copy-done.6), channel_id=1, source_target_pairs={{0,192},{1,193},{2,194},{3,195},{4,196},{5,197},{6,198},{7,199},{8... | collective-permute-start | bytes 786440 | tf_op jit(solution)/shard_map/ppermute | solution.py:32
  46.3 7.9 %collective-permute-start.6 = (bf16[256,512]{1,0:T(8,128)(2,1)S(1)}, bf16[256,512]{1,0:T(8,128)(2,1)S(1)}, u32[]{:S(2)}, u32[]{:S(2)}) collective-permute-start(bf16[256,512]{1,0:T(8,128)(2,1)S(1)} %copy-done.7), channel_id=1, source_target_pairs={{0,8},{1,9},{2,10},{3,11},{4,12},{5,13},{6,14},{7,15},{8,0},{9,1},... | collective-permute-start | bytes 786440 | tf_op jit(solution)/shard_map/ppermute | solution.py:32
  46.3 7.9 %collective-permute-start.9 = (bf16[256,512]{1,0:T(8,128)(2,1)S(1)}, bf16[256,512]{1,0:T(8,128)(2,1)S(1)}, u32[]{:S(2)}, u32[]{:S(2)}) collective-permute-start(bf16[256,512]{1,0:T(8,128)(2,1)S(1)} %copy-done.6), channel_id=1, source_target_pairs={{0,8},{1,9},{2,10},{3,11},{4,12},{5,13},{6,14},{7,15},{8,0},{9,1},... | collective-permute-start | bytes 786440 | tf_op jit(solution)/shard_map/ppermute | solution.py:32
  50.2 4.1 %copy-start.8 = (bf16[256,512]{1,0:T(8,128)(2,1)}, bf16[256,512]{1,0:T(8,128)(2,1)S(1)}, u32[]{:S(2)}) copy-start(bf16[256,512]{1,0:T(8,128)(2,1)S(1)} %collective-permute-done.7.refs_6_) | copy-start | bytes 786436
  50.2 4.0 %collective-permute-start.8 = (bf16[256,512]{1,0:T(8,128)(2,1)S(1)}, bf16[256,512]{1,0:T(8,128)(2,1)S(1)}, u32[]{:S(2)}, u32[]{:S(2)}) collective-permute-start(bf16[256,512]{1,0:T(8,128)(2,1)S(1)} %collective-permute-done.7.refs_6_), channel_id=1, source_target_pairs={{0,8},{1,9},{2,10},{3,11},{4,12},{5,13},{6,14},{7,15},{8,0},{9,1},... | collective-permute-start | bytes 786440 | tf_op jit(solution)/shard_map/ppermute | solution.py:32
  52.8 1.6 %copy-start.9 = (bf16[256,512]{1,0:T(8,128)(2,1)}, bf16[256,512]{1,0:T(8,128)(2,1)S(1)}, u32[]{:S(2)}) copy-start(bf16[256,512]{1,0:T(8,128)(2,1)S(1)} %collective-permute-done.10.refs_14_) | copy-start | bytes 786436
  52.8 1.5 %collective-permute-start.11 = (bf16[256,512]{1,0:T(8,128)(2,1)S(1)}, bf16[256,512]{1,0:T(8,128)(2,1)S(1)}, u32[]{:S(2)}, u32[]{:S(2)}) collective-permute-start(bf16[256,512]{1,0:T(8,128)(2,1)S(1)} %collective-permute-done.10.refs_14_), channel_id=1, source_target_pairs={{0,8},{1,9},{2,10},{3,11},{4,12},{5,13},{6,14},{7,15},{8,0},{9,1},... | collective-permute-start | bytes 786440 | tf_op jit(solution)/shard_map/ppermute | solution.py:32
  54.2 0.7 copy-start.10
  54.3 0.8 copy-start.11
  54.3 0.9 copy-start.12
  54.3 1.0 copy-start.13
  60.4 2.7 %collective-permute-start.14 = (f32[256,256]{1,0:T(8,128)S(1)}, f32[256,256]{1,0:T(8,128)S(1)}, u32[]{:S(2)}, u32[]{:S(2)}) collective-permute-start(f32[256,256]{1,0:T(8,128)S(1)} %own_terms.1.own_ref), channel_id=1, source_target_pairs={{0,8},{1,9},{2,10},{3,11},{4,12},{5,13},{6,14},{7,15},{8,0},{9,1},... | collective-permute-start | bytes 786440 | tf_op jit(solution)/shard_map/ppermute | solution.py:32
  61.0 7.7 %collective-permute-start.13 = (f16[200,512]{1,0:T(8,128)(2,1)S(1)}, f16[200,512]{1,0:T(8,128)(2,1)S(1)}, u32[]{:S(2)}, u32[]{:S(2)}) collective-permute-start(f16[200,512]{1,0:T(8,128)(2,1)S(1)} %convert_element_type.46), channel_id=1, source_target_pairs={{0,64},{1,65},{2,66},{3,67},{4,68},{5,69},{6,70},{7,71},{8,72},{9,... | collective-permute-start | bytes 614408 | tf_op jit(solution)/shard_map/ppermute | solution.py:32
  61.0 9.4 %collective-permute-start.12 = (f16[200,512]{1,0:T(8,128)(2,1)S(1)}, f16[200,512]{1,0:T(8,128)(2,1)S(1)}, u32[]{:S(2)}, u32[]{:S(2)}) collective-permute-start(f16[200,512]{1,0:T(8,128)(2,1)S(1)} %convert_element_type.45), channel_id=1, source_target_pairs={{0,192},{1,193},{2,194},{3,195},{4,196},{5,197},{6,198},{7,199},{8... | collective-permute-start | bytes 614408 | tf_op jit(solution)/shard_map/ppermute | solution.py:32
  64.3 9.6 %copy-start.4 = (f32[192,1024]{1,0:T(8,128)S(1)}, f32[192,1024]{1,0:T(8,128)}, u32[]{:S(2)}) copy-start(f32[192,1024]{1,0:T(8,128)} %get-tuple-element.61.wide_ref) | copy-start | bytes 2359300
  64.3 9.6 %copy-start.5 = (f32[192,256]{1,0:T(8,128)S(1)}, f32[192,256]{1,0:T(8,128)}, u32[]{:S(2)}) copy-start(f32[192,256]{1,0:T(8,128)} %get-tuple-element.63.narrow_ref) | copy-start | bytes 589828
  64.3 8.3 %collective-permute-start.17 = (f16[200,256]{1,0:T(8,128)(2,1)S(1)}, f16[200,256]{1,0:T(8,128)(2,1)S(1)}, u32[]{:S(2)}, u32[]{:S(2)}) collective-permute-start(f16[200,256]{1,0:T(8,128)(2,1)S(1)} %convert_element_type.52), channel_id=1, source_target_pairs={{0,128},{1,129},{2,130},{3,131},{4,132},{5,133},{6,134},{7,135},{8... | collective-permute-start | bytes 307208 | tf_op jit(solution)/shard_map/ppermute | solution.py:32
  66.4 6.2 %collective-permute-start.16 = (f16[200,256]{1,0:T(8,128)(2,1)S(1)}, f16[200,256]{1,0:T(8,128)(2,1)S(1)}, u32[]{:S(2)}, u32[]{:S(2)}) collective-permute-start(f16[200,256]{1,0:T(8,128)(2,1)S(1)} %convert_element_type.51), channel_id=1, source_target_pairs={{0,64},{1,65},{2,66},{3,67},{4,68},{5,69},{6,70},{7,71},{8,72},{9,... | collective-permute-start | bytes 307208 | tf_op jit(solution)/shard_map/ppermute | solution.py:32
  66.4 7.4 %collective-permute-start.15 = (f16[200,256]{1,0:T(8,128)(2,1)S(1)}, f16[200,256]{1,0:T(8,128)(2,1)S(1)}, u32[]{:S(2)}, u32[]{:S(2)}) collective-permute-start(f16[200,256]{1,0:T(8,128)(2,1)S(1)} %convert_element_type.50), channel_id=1, source_target_pairs={{0,192},{1,193},{2,194},{3,195},{4,196},{5,197},{6,198},{7,199},{8... | collective-permute-start | bytes 307208 | tf_op jit(solution)/shard_map/ppermute | solution.py:32

commit v6 on v4

--- a/solution.py
+++ b/solution.py
@@ -19,9 +19,7 @@
     return x * 64 + (z >> 1) * 16 + core * 8 + (z & 1) * 4 + y
 
 
-Z_HI_GROUPS = [
-    [place(x, y, 2 * z + low, c) for z in range(4)] for x in range(4) for y in range(4) for low in range(2) for c in range(2)
-]
+YZ_GROUPS = [[place(x, y, z, c) for y in range(4) for z in range(8)] for x in range(4) for c in range(2)]
 
 
 def dot(left, right, dims):
@@ -93,13 +91,30 @@
 
 
 def attention_kernel(
-    q_ref, da_ref, k_ref, v_ref, d_query_ref, attended_ref, dkv_ref, scores_ref, d_probs_ref, probs_ref, d_scores_ref
+    q_hbm, da_hbm, kv_hbm, d_query_hbm, attended_hbm, dkv_ref,
+    q_ref, da_ref, k_ref, v_ref, d_query_ref, attended_ref, scores_ref, d_probs_ref, probs_ref, d_scores_ref,
+    in_sems, out_sems,
 ):
     bf = jnp.bfloat16
     blocks, _, tokens = dkv_ref.shape
     chunk = 16
     head_cols = lambda h: slice(h * HD, (h + 1) * HD)
     block_rows = lambda b: slice(b * tokens, (b + 1) * tokens)
+    arriving = [
+        pltpu.make_async_copy(source, ref, in_sems.at[i])
+        for i, (source, ref) in enumerate(
+            (
+                (kv_hbm.at[:, pl.ds(0, HD)], k_ref),
+                (q_hbm, q_ref),
+                (kv_hbm.at[:, pl.ds(HD, HD)], v_ref),
+                (da_hbm, da_ref),
+            )
+        )
+    ]
+    for copy in arriving:
+        copy.start()
+    for copy in arriving:
+        copy.wait()
 
     def ahead(h):
         def make(b, side_ref, other_ref, to_ref):
@@ -165,6 +180,12 @@
     for run in behind(HEADS - 1):
         run()
 
+    leaving = [
+        pltpu.make_async_copy(ref, target, out_sems.at[i])
+        for i, (ref, target) in enumerate(((d_query_ref, d_query_hbm), (attended_ref, attended_hbm)))
+    ]
+    for copy in leaving:
+        copy.start()
     for i, scale in enumerate((SCALE, 1.0)):
         rows = pl.ds(i * HD, HD)
         top = jnp.abs(dkv_ref[0, rows, :])
@@ -174,36 +195,36 @@
         factor = jnp.exp2(-power) * scale
         for b in range(blocks):
             dkv_ref[b, rows, :] = dkv_ref[b, rows, :] * factor
-            dkv_ref[b, pl.ds(2 * HD + 8 * i, 8), :] = jnp.broadcast_to(power, (8, tokens))
+            dkv_ref[b, pl.ds(2 * HD + 4 * i, 4), :] = jnp.broadcast_to(power, (4, tokens))
+    for copy in leaving:
+        copy.wait()
 
 
 def attention(queries, d_att, keys_values):
     tokens, inner = queries.shape
     length = keys_values.shape[0]
-    whole = pl.BlockSpec((tokens, inner), lambda i: (0, 0))
-    terms = (length // tokens, 2 * HD + 16, tokens)
+    blocks = length // tokens
+    anywhere = pl.BlockSpec(memory_space=pl.ANY)
+    small, large = pltpu.VMEM((tokens, inner), jnp.bfloat16), pltpu.VMEM((length, HD), jnp.bfloat16)
+    wide, half = pltpu.VMEM((2, tokens, length), jnp.float32), pltpu.VMEM((2, tokens, length), jnp.bfloat16)
+    operands = [pltpu.with_memory_space_constraint(v, pltpu.HBM) for v in (queries, d_att, keys_values)]
     return pl.pallas_call(
         attention_kernel,
-        grid=(1,),
-        in_specs=[
-            whole,
-            whole,
-            pl.BlockSpec((length, HD), lambda i: (0, 0)),
-            pl.BlockSpec((length, HD), lambda i: (0, 1)),
-        ],
-        out_specs=[whole, whole, pl.BlockSpec(terms, lambda i: (0, 0, 0))],
+        in_specs=[anywhere] * 3,
+        out_specs=[anywhere, anywhere, pl.BlockSpec(memory_space=pltpu.VMEM)],
         out_shape=[
             pltpu.HBM((tokens, inner), jnp.bfloat16),
             pltpu.HBM((tokens, inner), jnp.bfloat16),
-            jax.ShapeDtypeStruct(terms, jnp.float32),
+            jax.ShapeDtypeStruct((blocks, 2 * HD + 8, tokens), jnp.float32),
         ],
-        scratch_shapes=[pltpu.VMEM((2, tokens, length), jnp.float32)] * 2 + [pltpu.VMEM((2, tokens, length), jnp.bfloat16)] * 2,
+        scratch_shapes=[small, small, large, large, small, small, wide, wide, half, half]
+        + [pltpu.SemaphoreType.DMA((4,)), pltpu.SemaphoreType.DMA((2,))],
         compiler_params=pltpu.CompilerParams(vmem_limit_bytes=32 * MIB),
         cost_estimate=pl.CostEstimate(
             flops=12 * tokens * inner * length, bytes_accessed=4 << 20, transcendentals=tokens * HEADS * length
         ),
         name="attention",
-    )(queries, d_att, keys_values, keys_values)
+    )(*operands)
 
 
 def store_scaled(values, ref):
@@ -276,7 +297,7 @@
 
 def own_terms_kernel(terms_ref, out_ref):
     for i in range(2):
-        rows, powers = pl.ds(i * HD, HD), pl.ds(2 * HD + 8 * i, 1)
+        rows, powers = pl.ds(i * HD, HD), pl.ds(2 * HD + 4 * i, 1)
         total = unscaled(terms_ref, 0, rows, powers)
         for b in range(1, terms_ref.shape[0]):
             total = total + unscaled(terms_ref, b, rows, powers)
@@ -307,18 +328,17 @@
                 total = total + scaled(narrow_got_ref, m, here)
         top = exponent(total)
         total_ref[:, first : first + width] = total * jnp.exp2(-top)
-        out_ref[:, 240 + i, :] = jnp.broadcast_to(top, (out_ref.shape[0], HD))
-    out_ref[:, 244:, :] = jnp.zeros((out_ref.shape[0], 4, HD), jnp.float32)
+        out_ref[:, 60 + i, :] = jnp.broadcast_to(top, (out_ref.shape[0], HD))
     for k in range(out_ref.shape[0]):
+        y, z = k // 8, k % 8
+        start = 48 * (z // 2) + 6 * (4 * (z % 2) + y)
         for j in range(10):
-            for z_hi in range(4):
-                to, start = 24 * j + 6 * z_hi, 48 * z_hi + 6 * k
-                out_ref[k, to : to + 6, :] = total_ref[start : start + 6, j * HD : (j + 1) * HD]
+            out_ref[k, 6 * j : 6 * j + 6, :] = total_ref[start : start + 6, j * HD : (j + 1) * HD]
 
 
 def after_x(wide, wide_got, narrow, narrow_got):
     rows, cols = wide.shape
-    shape = (rows // 24, 248, HD)
+    shape = (rows // 6, 64, HD)
     return pl.pallas_call(
         after_x_kernel,
         out_shape=jax.ShapeDtypeStruct(shape, jnp.float32),
@@ -328,36 +348,17 @@
     )(wide, wide_got, narrow, narrow_got)
 
 
-def after_seq_kernel(got_ref, out_ref, total_ref):
-    for i, (first, count) in enumerate(((0, 96), (96, 96), (192, 24), (216, 24))):
-        rows = pl.ds(first, count)
-        total = unscaled(got_ref, 0, rows, pl.ds(240 + i, 1))
+def last_sum_kernel(got_ref, query_ref, out_ref, key_ref, value_ref):
+    first = 0
+    for i, ref in enumerate((query_ref, out_ref, key_ref, value_ref)):
+        tiles = ref.shape[1] // HD
+        rows = pl.ds(first, 6 * tiles)
+        total = unscaled(got_ref, 0, rows, pl.ds(60 + i, 1))
         for b in range(1, got_ref.shape[0]):
-            total = total + unscaled(got_ref, b, rows, pl.ds(240 + i, 1))
-        total_ref[rows, :] = total
-    for k in range(4):
-        for j in range(10):
-            out_ref[k, 6 * j : 6 * j + 6, :] = total_ref[24 * j + 6 * k : 24 * j + 6 * k + 6, :]
-        out_ref[k, 60:, :] = jnp.zeros((4, HD), jnp.float32)
-
-
-def after_seq(got):
-    return pl.pallas_call(
-        after_seq_kernel,
-        out_shape=jax.ShapeDtypeStruct((4, 64, HD), jnp.float32),
-        scratch_shapes=[pltpu.VMEM((240, HD), jnp.float32)],
-        compiler_params=pltpu.CompilerParams(vmem_limit_bytes=8 * MIB),
-        name="after_seq",
-    )(got)
-
-
-def last_sum_kernel(got_ref, query_ref, out_ref, key_ref, value_ref):
-    total = (got_ref[0] + got_ref[1]) + (got_ref[2] + got_ref[3])
-    first = 0
-    for ref in (query_ref, out_ref, key_ref, value_ref):
-        for j in range(ref.shape[1] // HD):
-            ref[:, j * HD : (j + 1) * HD] = total[first : first + 6]
-            first += 6
+            total = total + unscaled(got_ref, b, rows, pl.ds(60 + i, 1))
+        for j in range(tiles):
+            ref[:, j * HD : (j + 1) * HD] = total[6 * j : 6 * j + 6]
+        first += 6 * tiles
 
 
 def last_sum(got):
@@ -390,7 +391,6 @@
     g_from = [exchange(g_far[0], 3 << 6), exchange(g_far[1], (3 << 6) | 8)]
     h_core, g_core = from_other_core(h_core), from_other_core(g_core)
 
-    queries, d_att = (pltpu.with_memory_space_constraint(v, pltpu.HBM) for v in (queries, d_att))
     d_query, attended, terms = attention(queries, d_att, gathered.reshape(8 * tokens, 2 * HD))
     terms, d_query, attended, h_from, g_from, h_core, g_core = lax.optimization_barrier(
         (terms, d_query, attended, h_from, g_from, h_core, g_core)
@@ -415,9 +415,8 @@
     narrow_got = [exchange(block.astype(half), m << 6) for m, block in zip((3, 1, 2), sent)]
 
     part = after_x(keep, jnp.stack(wide_got).astype(f32), narrow, jnp.stack(narrow_got).astype(f32))
-    part = after_seq(lax.all_to_all(part.astype(half), "seq", 0, 0, tiled=True).astype(f32))
-    part = lax.all_to_all(part, AXES, 0, 0, axis_index_groups=Z_HI_GROUPS, tiled=True)
-    grad_query, grad_out, grad_key, grad_value = last_sum(part)
+    part = lax.all_to_all(part.astype(half), AXES, 0, 0, axis_index_groups=YZ_GROUPS, tiled=True)
+    grad_query, grad_out, grad_key, grad_value = last_sum(part.astype(f32))
     return branch[None], grad_query, grad_key, grad_value, grad_out
 
 

time: 103 us -> 101 us (0.981)
  blocking collectives: 29.8 us -> 28.1 us
    all_to_all x2 -> x1, blocking collectives: 29.8 us -> 28.1 us  [local(): lax.all_to_all(part.astype(half), AXES, 0, 0, axis_index_groups=YZ_GROUPS...]
    pallas_call x2 -> x1, Pallas kernels: 9.67 us -> 9.61 us  [attention(): pl.pallas_call(attention_kernel, in_specs=[anywhere] * 3, out_specs=[anyw...]
where the time goes in v6:
time: 101 us; the launch traced here: 100 us
  blocking collectives  28.1 us (28%)
  starting transfers between devices  27.2 us (27%)
  Pallas kernels  21.9 us (22%)
  waiting for transfers between devices  14.2 us (14%)
  matrix products  4.03 us (4%)
  other arithmetic  3.05 us (3%)
    all_to_all x1, blocking collectives, local(): lax.all_to_all(part.astype(half), AXES, 0, 0, axis_index_groups=YZ_GROUPS...  28.1 us
    ppermute x18, starting transfers between devices, exchange(): return lax.ppermute(value, AXES, [(i, i ^ mask) for i in range(256)])  16.2 us
    ppermute x18, waiting for transfers between devices, exchange(): return lax.ppermute(value, AXES, [(i, i ^ mask) for i in range(256)])  11.3 us
    pallas_call x1, Pallas kernels, attention(): pl.pallas_call(attention_kernel, in_specs=[anywhere] * 3, out_specs=[anyw...  9.61 us
    all_to_all x1, starting transfers between devices, local(): lax.all_to_all(project(hidden, w_key, w_value), 'seq', 0, 0, tiled=True)  6.1 us
    all_to_all x1, starting transfers between devices, local(): terms = lax.all_to_all(terms.astype(half), 'seq', 0, 0, tiled=True)  4.83 us
    dot_general x3, matrix products, dot(): lax.dot_general(left, right, (dims, ((), ())), preferred_element_type=jnp...  4.03 us
    pallas_call x1, Pallas kernels, wide_products(): pl.pallas_call(wide_kernel, out_shape=[pltpu.HBM((rows, 2 * cols), jnp.fl...  3.49 us
  transfers between devices with their start and end apart: 20, of which 8 were waited for; matrix products, arithmetic and copies ran while one was open for 4% of the time, Pallas kernels for 17%

profile of v6, /device:TPU:32, one launch (start us, length us, event | category | flops | bytes accessed | tf_op | source)
XLA Modules:
  0.0 100.4 jit_solution(1030971108321353876)
XLA Ops:
  0.6 0.0 copy-start
  0.6 3.0 %project.1 = bf16[8,256,256]{2,1,0:T(8,128)(2,1)} custom-call(bf16[256,1536]{1,0:T(8,128)(2,1)} %bitcast.19, bf16[1536,128]{1,0:T(8,128)(2,1)} %w_key_ref.1, bf16[1536,128]{1,0:T(8,128)(2,1)} %w_value_ref.1), custom_call_target="tpu_custom_call" | custom-call | tf_op jit(solution)/shard_map/project/pallas_call | solution.py:56
  3.7 6.1 %all-to-all-start = ((bf16[8,256,256]{2,1,0:T(8,128)(2,1)}), bf16[8,256,256]{2,1,0:T(8,128)(2,1)}, u32[]{:S(2)}, u32[]{:S(2)}) async-start(bf16[8,256,256]{2,1,0:T(8,128)(2,1)} %project.1), calls=%async_computation | async-start | bytes 2097152 | tf_op jit(solution)/shard_map/all_to_all | solution.py:383
  9.8 0.1 pad_add_fusion.place_ref
  9.8 1.6 %turn.3 = (bf16[384,256]{1,0:T(8,128)(2,1)S(1)}, bf16[384,256]{1,0:T(8,128)(2,1)}, bf16[384,256]{1,0:T(8,128)(2,1)S(1)}, bf16[384,256]{1,0:T(8,128)(2,1)}) custom-call(s32[2]{0:T(128)S(1)} %pad_add_fusion.place_ref, bf16[256,1536]{1,0:T(8,128)(2,1)S(1)} %bitcast.21), custom_call_target="tpu_custom_call" | custom-call | tf_op jit(solution)/shard_map/turn/pallas_call | solution.py:78
  11.4 2.7 %collective-permute-start.2 = (bf16[384,256]{1,0:T(8,128)(2,1)S(1)}, bf16[384,256]{1,0:T(8,128)(2,1)S(1)}, u32[]{:S(2)}, u32[]{:S(2)}) collective-permute-start(bf16[384,256]{1,0:T(8,128)(2,1)S(1)} %get-tuple-element.43), channel_id=1, source_target_pairs={{0,192},{1,193},{2,194},{3,195},{4,196},{5,197},{6,198},{7,199},{8... | collective-permute-start | bytes 589832 | tf_op jit(solution)/shard_map/ppermute | solution.py:30
  14.2 0.6 collective-permute-start.5
  14.8 1.7 %turn.2 = (bf16[768,256]{1,0:T(8,128)(2,1)S(1)}, bf16[768,256]{1,0:T(8,128)(2,1)}, bf16[384,256]{1,0:T(8,128)(2,1)}, bf16[384,256]{1,0:T(8,128)(2,1)}) custom-call(s32[2]{0:T(128)S(1)} %pad_add_fusion.place_ref, bf16[256,1536]{1,0:T(8,128)(2,1)S(1)} %bitcast.20), custom_call_target="tpu_custom_call" | custom-call | tf_op jit(solution)/shard_map/turn/pallas_call | solution.py:78
  16.5 0.2 collective-permute-start
  16.7 1.3 %convolution_convert_fusion.2.q_hbm = bf16[256,512]{1,0:T(8,128)(2,1)} fusion(bf16[1536,512]{1,0:T(8,128)(2,1)S(1)} %copy-done.14, bf16[1,256,1536]{2,1,0:T(8,128)(2,1)S(1)} %copy-done.1), kind=kOutput, calls=%fused_computation.2 | convolution fusion | flops 402784256 | bytes 2621440 | tf_op jit(solution)/shard_map/dot_general | solution.py:26
  18.0 1.3 %convolution_convert_fusion.1.da_hbm = bf16[256,512]{1,0:T(8,128)(2,1)} fusion(bf16[1536,512]{1,0:T(8,128)(2,1)S(1)} %copy-done, bf16[1,256,1536]{2,1,0:T(8,128)(2,1)S(1)} %copy-done.3), kind=kOutput, calls=%fused_computation.1 | convolution fusion | flops 402784256 | bytes 2621440 | tf_op jit(solution)/shard_map/dot_general | solution.py:26
  19.3 0.2 collective-permute-done.2.refs_10_
  19.5 1.7 %collective-permute-start.1 = (bf16[384,256]{1,0:T(8,128)(2,1)}, bf16[384,256]{1,0:T(8,128)(2,1)S(1)}, u32[]{:S(2)}, u32[]{:S(2)}) collective-permute-start(bf16[384,256]{1,0:T(8,128)(2,1)} %get-tuple-element.42), channel_id=1, source_target_pairs={{0,72},{1,73},{2,74},{3,75},{4,76},{5,77},{6,78},{7,79},{8,64},{9,... | collective-permute-start | bytes 589832 | tf_op jit(solution)/shard_map/ppermute | solution.py:30
  21.2 2.9 %all-to-all-done = bf16[8,256,256]{2,1,0:T(8,128)(2,1)} async-done(((bf16[8,256,256]{2,1,0:T(8,128)(2,1)}), bf16[8,256,256]{2,1,0:T(8,128)(2,1)}, u32[]{:S(2)}, u32[]{:S(2)}) %all-to-all-start) | async-done | bytes 1048608 | tf_op jit(solution)/shard_map/all_to_all | solution.py:383
  24.1 9.6 %attention.1 = (bf16[256,512]{1,0:T(8,128)(2,1)}, bf16[256,512]{1,0:T(8,128)(2,1)}, f32[8,264,256]{2,1,0:T(8,128)S(1)}) custom-call(bf16[256,512]{1,0:T(8,128)(2,1)} %convolution_convert_fusion.2.q_hbm, bf16[256,512]{1,0:T(8,128)(2,1)} %convolution_convert_fusion.1.da_hbm, bf16[2048,256]{1,0:T(8,128)(2,1)} %bitcast.2.kv_hbm), custom_call_target="tpu_custom_call" | custom-call | flops 3221225472 | bytes 4194304 | tf_op jit(solution)/shard_map/attention/pallas_call | solution.py:211
  33.7 1.2 %convert_element_type.44 = f16[8,264,256]{2,1,0:T(8,128)(2,1)} convert(f32[8,264,256]{2,1,0:T(8,128)S(1)} %get-tuple-element.47) | non-fusion elementwise | flops 540672 | bytes 3244032 | tf_op jit(solution)/shard_map/convert_element_type | solution.py:398
  34.9 4.8 %all-to-all-start.1 = ((f16[8,264,256]{2,1,0:T(8,128)(2,1)}), f16[8,264,256]{2,1,0:T(8,128)(2,1)}, u32[]{:S(2)}, u32[]{:S(2)}) async-start(f16[8,264,256]{2,1,0:T(8,128)(2,1)} %convert_element_type.44), calls=%async_computation.1 | async-start | bytes 2162688 | tf_op jit(solution)/shard_map/all_to_all | solution.py:398
  39.7 1.5 %collective-permute-start.7 = (bf16[256,512]{1,0:T(8,128)(2,1)S(1)}, bf16[256,512]{1,0:T(8,128)(2,1)S(1)}, u32[]{:S(2)}, u32[]{:S(2)}) collective-permute-start(bf16[256,512]{1,0:T(8,128)(2,1)S(1)} %copy-done.7), channel_id=1, source_target_pairs={{0,64},{1,65},{2,66},{3,67},{4,68},{5,69},{6,70},{7,71},{8,72},{9,... | collective-permute-start | bytes 786440 | tf_op jit(solution)/shard_map/ppermute | solution.py:30
  41.2 2.1 %collective-permute-start.10 = (bf16[256,512]{1,0:T(8,128)(2,1)S(1)}, bf16[256,512]{1,0:T(8,128)(2,1)S(1)}, u32[]{:S(2)}, u32[]{:S(2)}) collective-permute-start(bf16[256,512]{1,0:T(8,128)(2,1)S(1)} %copy-done.6), channel_id=1, source_target_pairs={{0,192},{1,193},{2,194},{3,195},{4,196},{5,197},{6,198},{7,199},{8... | collective-permute-start | bytes 786440 | tf_op jit(solution)/shard_map/ppermute | solution.py:30
  43.3 0.5 collective-permute-start.9
  43.8 3.4 %collective-permute-done.7.refs_6_ = bf16[256,512]{1,0:T(8,128)(2,1)S(1)} collective-permute-done((bf16[256,512]{1,0:T(8,128)(2,1)S(1)}, bf16[256,512]{1,0:T(8,128)(2,1)S(1)}, u32[]{:S(2)}, u32[]{:S(2)}) %collective-permute-start.7) | collective-permute-done | bytes 262176 | tf_op jit(solution)/shard_map/ppermute | solution.py:30
  47.2 2.5 %collective-permute-done.10.refs_14_ = bf16[256,512]{1,0:T(8,128)(2,1)S(1)} collective-permute-done((bf16[256,512]{1,0:T(8,128)(2,1)S(1)}, bf16[256,512]{1,0:T(8,128)(2,1)S(1)}, u32[]{:S(2)}, u32[]{:S(2)}) %collective-permute-start.10) | collective-permute-done | bytes 262176 | tf_op jit(solution)/shard_map/ppermute | solution.py:30
  49.8 1.5 %convolution_convert_fusion = bf16[256,1536]{1,0:T(8,128)(2,1)} fusion(bf16[256,512]{1,0:T(8,128)(2,1)S(1)} %copy-done.6, bf16[1536,512]{1,0:T(8,128)(2,1)S(1)} %copy-done), kind=kOutput, calls=%fused_computation | convolution fusion | flops 403046400 | bytes 2621440 | tf_op jit(solution)/shard_map/dot_general | solution.py:26
  51.3 0.0 collective-permute-done.11.refs_15_
  51.3 0.6 copy-done.10
  51.9 0.1 copy-done.11
  52.1 0.1 copy-done.12
  52.2 0.1 copy-done.13
  52.3 3.5 %wide.1 = (f32[192,1024]{1,0:T(8,128)}, f32[200,512]{1,0:T(8,128)S(1)}, f32[200,512]{1,0:T(8,128)S(1)}) custom-call(bf16[768,256]{1,0:T(8,128)(2,1)S(1)} %get-tuple-element.48.refs_0_.mine_ref, bf16[768,256]{1,0:T(8,128)(2,1)S(1)} %collective-permute-done.4.refs_1_.theirs_ref, bf16[384,256]{1,0:T(8,128)(2,1)} %collective-permute-done.refs_2_, ...), custom_call_target="tpu_custom_call" | custom-call | flops 1073741824 | bytes 5242880 | tf_op jit(solution)/shard_map/wide/pallas_call | solution.py:252
  55.8 1.4 %convert_element_type.49.terms_ref = f32[8,264,256]{2,1,0:T(8,128)S(1)} convert(f16[8,264,256]{2,1,0:T(8,128)(2,1)} %all-to-all-done.1) | non-fusion elementwise | flops 540672 | bytes 3244032 | tf_op jit(solution)/shard_map/convert_element_type | solution.py:413
  57.3 0.1 own_terms.1.own_ref
  57.4 0.6 collective-permute-start.14
  58.0 2.1 %collective-permute-start.12 = (f16[200,512]{1,0:T(8,128)(2,1)S(1)}, f16[200,512]{1,0:T(8,128)(2,1)S(1)}, u32[]{:S(2)}, u32[]{:S(2)}) collective-permute-start(f16[200,512]{1,0:T(8,128)(2,1)S(1)} %convert_element_type.45), channel_id=1, source_target_pairs={{0,192},{1,193},{2,194},{3,195},{4,196},{5,197},{6,198},{7,199},{8... | collective-permute-start | bytes 614408 | tf_op jit(solution)/shard_map/ppermute | solution.py:30
  60.1 1.2 %narrow.1 = (f32[192,256]{1,0:T(8,128)}, f32[200,256]{1,0:T(8,128)S(1)}, f32[200,256]{1,0:T(8,128)S(1)}, f32[200,256]{1,0:T(8,128)S(1)}) custom-call(bf16[768,256]{1,0:T(8,128)(2,1)S(1)} %get-tuple-element.48.refs_0_.mine_ref, bf16[768,256]{1,0:T(8,128)(2,1)S(1)} %collective-permute-done.4.refs_1_.theirs_ref, f32[256,256]{1,0:T(8,128)S(1)} %own_terms.1.own_ref, ...), custom_call_target="tpu_custom_call" | custom-call | flops 1 | bytes 1 | tf_op jit(solution)/shard_map/narrow/pallas_call | solution.py:289
  61.3 2.1 %collective-permute-start.17 = (f16[200,256]{1,0:T(8,128)(2,1)S(1)}, f16[200,256]{1,0:T(8,128)(2,1)S(1)}, u32[]{:S(2)}, u32[]{:S(2)}) collective-permute-start(f16[200,256]{1,0:T(8,128)(2,1)S(1)} %convert_element_type.52), channel_id=1, source_target_pairs={{0,128},{1,129},{2,130},{3,131},{4,132},{5,133},{6,134},{7,135},{8... | collective-permute-start | bytes 307208 | tf_op jit(solution)/shard_map/ppermute | solution.py:30
  63.4 0.0 collective-permute-start.16
  63.4 2.1 %collective-permute-start.15 = (f16[200,256]{1,0:T(8,128)(2,1)S(1)}, f16[200,256]{1,0:T(8,128)(2,1)S(1)}, u32[]{:S(2)}, u32[]{:S(2)}) collective-permute-start(f16[200,256]{1,0:T(8,128)(2,1)S(1)} %convert_element_type.50), channel_id=1, source_target_pairs={{0,192},{1,193},{2,194},{3,195},{4,196},{5,197},{6,198},{7,199},{8... | collective-permute-start | bytes 307208 | tf_op jit(solution)/shard_map/ppermute | solution.py:30
  65.5 0.2 collective-permute-done.13
  65.7 1.7 %collective-permute-done.12 = f16[200,512]{1,0:T(8,128)(2,1)S(1)} collective-permute-done((f16[200,512]{1,0:T(8,128)(2,1)S(1)}, f16[200,512]{1,0:T(8,128)(2,1)S(1)}, u32[]{:S(2)}, u32[]{:S(2)}) %collective-permute-start.12) | collective-permute-done | bytes 204832 | tf_op jit(solution)/shard_map/ppermute | solution.py:30
  67.4 0.1 maximum_convert_fusion.wide_got_ref
  67.5 2.1 %collective-permute-done.17 = f16[200,256]{1,0:T(8,128)(2,1)S(1)} collective-permute-done((f16[200,256]{1,0:T(8,128)(2,1)S(1)}, f16[200,256]{1,0:T(8,128)(2,1)S(1)}, u32[]{:S(2)}, u32[]{:S(2)}) %collective-permute-start.17) | collective-permute-done | bytes 102432 | tf_op jit(solution)/shard_map/ppermute | solution.py:30
  69.7 1.1 %collective-permute-done.15 = f16[200,256]{1,0:T(8,128)(2,1)S(1)} collective-permute-done((f16[200,256]{1,0:T(8,128)(2,1)S(1)}, f16[200,256]{1,0:T(8,128)(2,1)S(1)}, u32[]{:S(2)}, u32[]{:S(2)}) %collective-permute-start.15) | collective-permute-done | bytes 102432 | tf_op jit(solution)/shard_map/ppermute | solution.py:30
  70.8 0.1 maximum_convert_fusion.1.narrow_got_ref
  70.9 0.5 after_x.1
  71.4 0.1 convert_element_type.54
  71.5 28.1 %all_to_all.15 = f16[32,64,128]{2,1,0:T(8,128)(2,1)S(1)} all-to-all(f16[32,64,128]{2,1,0:T(8,128)(2,1)S(1)} %convert_element_type.54), channel_id=1, replica_groups={{0,4,16,20,32,36,48,52,1,5,17,21,33,37,49,53,2,6,18,22,34,38,50,54,3,7,..., dimensions={0} | all-to-all | bytes 1048576 | tf_op jit(solution)/shard_map/all_to_all | solution.py:418
  99.6 0.1 convert_element_type.55.got_ref
  99.7 0.7 last_sum.1
  (47 shorter events, 0.2 us)
Async XLA Ops:
  0.6 17.4 %copy-start = (bf16[1536,512]{1,0:T(8,128)(2,1)S(1)}, bf16[1536,512]{1,0:T(8,128)(2,1)}, u32[]{:S(2)}) copy-start(bf16[1536,512]{1,0:T(8,128)(2,1)} %param.10) | copy-start | bytes 4718596
  3.7 6.2 %copy-start.2 = (bf16[1,256,1536]{2,1,0:T(8,128)(2,1)S(1)}, bf16[1,256,1536]{2,1,0:T(8,128)(2,1)}, u32[]{:S(2)}) copy-start(bf16[1,256,1536]{2,1,0:T(8,128)(2,1)} %param.11) | copy-start | bytes 2359300
  3.7 11.1 %copy-start.1 = (bf16[1,256,1536]{2,1,0:T(8,128)(2,1)S(1)}, bf16[1,256,1536]{2,1,0:T(8,128)(2,1)}, u32[]{:S(2)}) copy-start(bf16[1,256,1536]{2,1,0:T(8,128)(2,1)} %param.6) | copy-start | bytes 2359300
  3.7 20.4 %all-to-all-start = ((bf16[8,256,256]{2,1,0:T(8,128)(2,1)}), bf16[8,256,256]{2,1,0:T(8,128)(2,1)}, u32[]{:S(2)}, u32[]{:S(2)}) async-start(bf16[8,256,256]{2,1,0:T(8,128)(2,1)} %project.1), calls=%async_computation | async-start | bytes 2097152 | tf_op jit(solution)/shard_map/all_to_all | solution.py:383
  9.8 7.0 %copy-start.14 = (bf16[1536,512]{1,0:T(8,128)(2,1)S(1)}, bf16[1536,512]{1,0:T(8,128)(2,1)}, u32[]{:S(2)}) copy-start(bf16[1536,512]{1,0:T(8,128)(2,1)} %param.7) | copy-start | bytes 4718596
  11.4 8.1 %collective-permute-start.2 = (bf16[384,256]{1,0:T(8,128)(2,1)S(1)}, bf16[384,256]{1,0:T(8,128)(2,1)S(1)}, u32[]{:S(2)}, u32[]{:S(2)}) collective-permute-start(bf16[384,256]{1,0:T(8,128)(2,1)S(1)} %get-tuple-element.43), channel_id=1, source_target_pairs={{0,192},{1,193},{2,194},{3,195},{4,196},{5,197},{6,198},{7,199},{8... | collective-permute-start | bytes 589832 | tf_op jit(solution)/shard_map/ppermute | solution.py:30
  14.1 19.5 %collective-permute-start.3 = (bf16[384,256]{1,0:T(8,128)(2,1)}, bf16[384,256]{1,0:T(8,128)(2,1)}, u32[]{:S(2)}, u32[]{:S(2)}) collective-permute-start(bf16[384,256]{1,0:T(8,128)(2,1)} %get-tuple-element.44), channel_id=1, source_target_pairs={{0,200},{1,201},{2,202},{3,203},{4,204},{5,205},{6,206},{7,207},{8... | collective-permute-start | bytes 589832 | tf_op jit(solution)/shard_map/ppermute | solution.py:30
  14.2 3.8 %copy-start.3 = (bf16[1,256,1536]{2,1,0:T(8,128)(2,1)S(1)}, bf16[1,256,1536]{2,1,0:T(8,128)(2,1)}, u32[]{:S(2)}) copy-start(bf16[1,256,1536]{2,1,0:T(8,128)(2,1)} %param.11) | copy-start | bytes 2359300
  14.2 19.6 %collective-permute-start.5 = (bf16[384,256]{1,0:T(8,128)(2,1)}, bf16[384,256]{1,0:T(8,128)(2,1)}, u32[]{:S(2)}, u32[]{:S(2)}) collective-permute-start(bf16[384,256]{1,0:T(8,128)(2,1)} %get-tuple-element.46), channel_id=1, source_target_pairs={{0,8},{1,9},{2,10},{3,11},{4,12},{5,13},{6,14},{7,15},{8,0},{9,1},... | collective-permute-start | bytes 589832 | tf_op jit(solution)/shard_map/ppermute | solution.py:30
  16.5 17.2 %collective-permute-start = (bf16[384,256]{1,0:T(8,128)(2,1)}, bf16[384,256]{1,0:T(8,128)(2,1)}, u32[]{:S(2)}, u32[]{:S(2)}) collective-permute-start(bf16[384,256]{1,0:T(8,128)(2,1)} %get-tuple-element.41), channel_id=1, source_target_pairs={{0,64},{1,65},{2,66},{3,67},{4,68},{5,69},{6,70},{7,71},{8,72},{9,... | collective-permute-start | bytes 589832 | tf_op jit(solution)/shard_map/ppermute | solution.py:30
  16.7 17.0 %collective-permute-start.4 = (bf16[768,256]{1,0:T(8,128)(2,1)}, bf16[768,256]{1,0:T(8,128)(2,1)S(1)}, u32[]{:S(2)}, u32[]{:S(2)}) collective-permute-start(bf16[768,256]{1,0:T(8,128)(2,1)} %get-tuple-element.45), channel_id=1, source_target_pairs={{0,8},{1,9},{2,10},{3,11},{4,12},{5,13},{6,14},{7,15},{8,0},{9,1},... | collective-permute-start | bytes 1179656 | tf_op jit(solution)/shard_map/ppermute | solution.py:30
  19.5 14.2 %collective-permute-start.1 = (bf16[384,256]{1,0:T(8,128)(2,1)}, bf16[384,256]{1,0:T(8,128)(2,1)S(1)}, u32[]{:S(2)}, u32[]{:S(2)}) collective-permute-start(bf16[384,256]{1,0:T(8,128)(2,1)} %get-tuple-element.42), channel_id=1, source_target_pairs={{0,72},{1,73},{2,74},{3,75},{4,76},{5,77},{6,78},{7,79},{8,64},{9,... | collective-permute-start | bytes 589832 | tf_op jit(solution)/shard_map/ppermute | solution.py:30
  34.9 4.8 %copy-start.7 = (bf16[256,512]{1,0:T(8,128)(2,1)S(1)}, bf16[256,512]{1,0:T(8,128)(2,1)}, u32[]{:S(2)}) copy-start(bf16[256,512]{1,0:T(8,128)(2,1)} %get-tuple-element.52.refs_4_) | copy-start | bytes 786436
  34.9 6.3 %copy-start.6 = (bf16[256,512]{1,0:T(8,128)(2,1)S(1)}, bf16[256,512]{1,0:T(8,128)(2,1)}, u32[]{:S(2)}) copy-start(bf16[256,512]{1,0:T(8,128)(2,1)} %get-tuple-element.57.refs_12_) | copy-start | bytes 786436
  34.9 20.9 %all-to-all-start.1 = ((f16[8,264,256]{2,1,0:T(8,128)(2,1)}), f16[8,264,256]{2,1,0:T(8,128)(2,1)}, u32[]{:S(2)}, u32[]{:S(2)}) async-start(f16[8,264,256]{2,1,0:T(8,128)(2,1)} %convert_element_type.44), calls=%async_computation.1 | async-start | bytes 2162688 | tf_op jit(solution)/shard_map/all_to_all | solution.py:398
  39.7 7.5 %collective-permute-start.7 = (bf16[256,512]{1,0:T(8,128)(2,1)S(1)}, bf16[256,512]{1,0:T(8,128)(2,1)S(1)}, u32[]{:S(2)}, u32[]{:S(2)}) collective-permute-start(bf16[256,512]{1,0:T(8,128)(2,1)S(1)} %copy-done.7), channel_id=1, source_target_pairs={{0,64},{1,65},{2,66},{3,67},{4,68},{5,69},{6,70},{7,71},{8,72},{9,... | collective-permute-start | bytes 786440 | tf_op jit(solution)/shard_map/ppermute | solution.py:30
  41.2 8.5 %collective-permute-start.10 = (bf16[256,512]{1,0:T(8,128)(2,1)S(1)}, bf16[256,512]{1,0:T(8,128)(2,1)S(1)}, u32[]{:S(2)}, u32[]{:S(2)}) collective-permute-start(bf16[256,512]{1,0:T(8,128)(2,1)S(1)} %copy-done.6), channel_id=1, source_target_pairs={{0,192},{1,193},{2,194},{3,195},{4,196},{5,197},{6,198},{7,199},{8... | collective-permute-start | bytes 786440 | tf_op jit(solution)/shard_map/ppermute | solution.py:30
  43.3 7.9 %collective-permute-start.6 = (bf16[256,512]{1,0:T(8,128)(2,1)S(1)}, bf16[256,512]{1,0:T(8,128)(2,1)S(1)}, u32[]{:S(2)}, u32[]{:S(2)}) collective-permute-start(bf16[256,512]{1,0:T(8,128)(2,1)S(1)} %copy-done.7), channel_id=1, source_target_pairs={{0,8},{1,9},{2,10},{3,11},{4,12},{5,13},{6,14},{7,15},{8,0},{9,1},... | collective-permute-start | bytes 786440 | tf_op jit(solution)/shard_map/ppermute | solution.py:30
  43.3 7.9 %collective-permute-start.9 = (bf16[256,512]{1,0:T(8,128)(2,1)S(1)}, bf16[256,512]{1,0:T(8,128)(2,1)S(1)}, u32[]{:S(2)}, u32[]{:S(2)}) collective-permute-start(bf16[256,512]{1,0:T(8,128)(2,1)S(1)} %copy-done.6), channel_id=1, source_target_pairs={{0,8},{1,9},{2,10},{3,11},{4,12},{5,13},{6,14},{7,15},{8,0},{9,1},... | collective-permute-start | bytes 786440 | tf_op jit(solution)/shard_map/ppermute | solution.py:30
  47.2 4.1 %copy-start.8 = (bf16[256,512]{1,0:T(8,128)(2,1)}, bf16[256,512]{1,0:T(8,128)(2,1)S(1)}, u32[]{:S(2)}) copy-start(bf16[256,512]{1,0:T(8,128)(2,1)S(1)} %collective-permute-done.7.refs_6_) | copy-start | bytes 786436
  47.2 4.0 %collective-permute-start.8 = (bf16[256,512]{1,0:T(8,128)(2,1)S(1)}, bf16[256,512]{1,0:T(8,128)(2,1)S(1)}, u32[]{:S(2)}, u32[]{:S(2)}) collective-permute-start(bf16[256,512]{1,0:T(8,128)(2,1)S(1)} %collective-permute-done.7.refs_6_), channel_id=1, source_target_pairs={{0,8},{1,9},{2,10},{3,11},{4,12},{5,13},{6,14},{7,15},{8,0},{9,1},... | collective-permute-start | bytes 786440 | tf_op jit(solution)/shard_map/ppermute | solution.py:30
  49.8 1.6 %copy-start.9 = (bf16[256,512]{1,0:T(8,128)(2,1)}, bf16[256,512]{1,0:T(8,128)(2,1)S(1)}, u32[]{:S(2)}) copy-start(bf16[256,512]{1,0:T(8,128)(2,1)S(1)} %collective-permute-done.10.refs_14_) | copy-start | bytes 786436
  49.8 1.5 %collective-permute-start.11 = (bf16[256,512]{1,0:T(8,128)(2,1)S(1)}, bf16[256,512]{1,0:T(8,128)(2,1)S(1)}, u32[]{:S(2)}, u32[]{:S(2)}) collective-permute-start(bf16[256,512]{1,0:T(8,128)(2,1)S(1)} %collective-permute-done.10.refs_14_), channel_id=1, source_target_pairs={{0,8},{1,9},{2,10},{3,11},{4,12},{5,13},{6,14},{7,15},{8,0},{9,1},... | collective-permute-start | bytes 786440 | tf_op jit(solution)/shard_map/ppermute | solution.py:30
  51.3 0.7 copy-start.10
  51.3 0.8 copy-start.11
  51.3 0.9 copy-start.12
  51.3 1.0 copy-start.13
  57.4 2.7 %collective-permute-start.14 = (f32[256,256]{1,0:T(8,128)S(1)}, f32[256,256]{1,0:T(8,128)S(1)}, u32[]{:S(2)}, u32[]{:S(2)}) collective-permute-start(f32[256,256]{1,0:T(8,128)S(1)} %own_terms.1.own_ref), channel_id=1, source_target_pairs={{0,8},{1,9},{2,10},{3,11},{4,12},{5,13},{6,14},{7,15},{8,0},{9,1},... | collective-permute-start | bytes 786440 | tf_op jit(solution)/shard_map/ppermute | solution.py:30
  58.0 7.7 %collective-permute-start.13 = (f16[200,512]{1,0:T(8,128)(2,1)S(1)}, f16[200,512]{1,0:T(8,128)(2,1)S(1)}, u32[]{:S(2)}, u32[]{:S(2)}) collective-permute-start(f16[200,512]{1,0:T(8,128)(2,1)S(1)} %convert_element_type.46), channel_id=1, source_target_pairs={{0,64},{1,65},{2,66},{3,67},{4,68},{5,69},{6,70},{7,71},{8,72},{9,... | collective-permute-start | bytes 614408 | tf_op jit(solution)/shard_map/ppermute | solution.py:30
  58.0 9.4 %collective-permute-start.12 = (f16[200,512]{1,0:T(8,128)(2,1)S(1)}, f16[200,512]{1,0:T(8,128)(2,1)S(1)}, u32[]{:S(2)}, u32[]{:S(2)}) collective-permute-start(f16[200,512]{1,0:T(8,128)(2,1)S(1)} %convert_element_type.45), channel_id=1, source_target_pairs={{0,192},{1,193},{2,194},{3,195},{4,196},{5,197},{6,198},{7,199},{8... | collective-permute-start | bytes 614408 | tf_op jit(solution)/shard_map/ppermute | solution.py:30
  61.3 9.6 %copy-start.4 = (f32[192,1024]{1,0:T(8,128)S(1)}, f32[192,1024]{1,0:T(8,128)}, u32[]{:S(2)}) copy-start(f32[192,1024]{1,0:T(8,128)} %get-tuple-element.61.wide_ref) | copy-start | bytes 2359300
  61.3 9.6 %copy-start.5 = (f32[192,256]{1,0:T(8,128)S(1)}, f32[192,256]{1,0:T(8,128)}, u32[]{:S(2)}) copy-start(f32[192,256]{1,0:T(8,128)} %get-tuple-element.63.narrow_ref) | copy-start | bytes 589828
  61.3 8.3 %collective-permute-start.17 = (f16[200,256]{1,0:T(8,128)(2,1)S(1)}, f16[200,256]{1,0:T(8,128)(2,1)S(1)}, u32[]{:S(2)}, u32[]{:S(2)}) collective-permute-start(f16[200,256]{1,0:T(8,128)(2,1)S(1)} %convert_element_type.52), channel_id=1, source_target_pairs={{0,128},{1,129},{2,130},{3,131},{4,132},{5,133},{6,134},{7,135},{8... | collective-permute-start | bytes 307208 | tf_op jit(solution)/shard_map/ppermute | solution.py:30
  63.4 6.2 %collective-permute-start.16 = (f16[200,256]{1,0:T(8,128)(2,1)S(1)}, f16[200,256]{1,0:T(8,128)(2,1)S(1)}, u32[]{:S(2)}, u32[]{:S(2)}) collective-permute-start(f16[200,256]{1,0:T(8,128)(2,1)S(1)} %convert_element_type.51), channel_id=1, source_target_pairs={{0,64},{1,65},{2,66},{3,67},{4,68},{5,69},{6,70},{7,71},{8,72},{9,... | collective-permute-start | bytes 307208 | tf_op jit(solution)/shard_map/ppermute | solution.py:30
  63.4 7.4 %collective-permute-start.15 = (f16[200,256]{1,0:T(8,128)(2,1)S(1)}, f16[200,256]{1,0:T(8,128)(2,1)S(1)}, u32[]{:S(2)}, u32[]{:S(2)}) collective-permute-start(f16[200,256]{1,0:T(8,128)(2,1)S(1)} %convert_element_type.50), channel_id=1, source_target_pairs={{0,192},{1,193},{2,194},{3,195},{4,196},{5,197},{6,198},{7,199},{8... | collective-permute-start | bytes 307208 | tf_op jit(solution)/shard_map/ppermute | solution.py:30

commit v7 on v6

--- a/solution.py
+++ b/solution.py
@@ -19,6 +19,9 @@
     return x * 64 + (z >> 1) * 16 + core * 8 + (z & 1) * 4 + y
 
 
+SEQ_GROUPS = [
+    [place(x, y, 2 * z + low, c) for y in range(4) for low in range(2)] for x in range(4) for z in range(4) for c in range(2)
+]
 YZ_GROUPS = [[place(x, y, z, c) for y in range(4) for z in range(8)] for x in range(4) for c in range(2)]
 
 
@@ -234,27 +237,57 @@
 
 
 def wide_kernel(*refs):
-    keep_ref, *send_refs = refs[16:]
+    keep_hbm, *send_refs = refs[16:19]
+    sides_ref, factors_ref, keep_ref, in_sems, out_sems = refs[19:]
     rows, cols = keep_ref.shape[0], send_refs[0].shape[1]
+    arriving = []
     for i in range(2):
+        arriving.append([])
+        for n in range(4):
+            side, factor = refs[8 * i + n], refs[8 * i + 4 + n]
+            copies = (
+                pltpu.make_async_copy(side.at[pl.ds(0, 2 * rows), :], sides_ref.at[i, n], in_sems.at[i, n, 0]),
+                pltpu.make_async_copy(factor, factors_ref.at[i, n], in_sems.at[i, n, 1]),
+            )
+            for copy in copies:
+                copy.start()
+            arriving[i].extend(copies)
+    leaving = []
+    for i in range(2):
+        for copy in arriving[i]:
+            copy.wait()
         product = None
-        for side_ref, factor_ref in zip(refs[8 * i : 8 * i + 4], refs[8 * i + 4 : 8 * i + 8]):
-            term = dot(side_ref[: 2 * rows], factor_ref[...], ((1,), (0,)))
+        for n in range(4):
+            term = dot(sides_ref[i, n], factors_ref[i, n], ((1,), (0,)))
             product = term if product is None else product + term
+        here = (slice(None), pl.ds(i * cols, cols))
         keep_ref[:, i * cols : (i + 1) * cols] = product[:rows]
+        leaving.append(pltpu.make_async_copy(keep_ref.at[here], keep_hbm.at[here], out_sems.at[i]))
+        leaving[i].start()
         store_scaled(product[rows:], send_refs[i])
+    for copy in leaving:
+        copy.wait()
 
 
 def wide_products(query, out):
-    rows = out[0].shape[0] // 2
+    rows, tokens = out[0].shape[0] // 2, out[0].shape[1]
     cols = out[4].shape[1]
-    query, out = (v[:4] + [pltpu.with_memory_space_constraint(f, pltpu.HBM) for f in v[4:]] for v in (query, out))
+    anywhere, fast = pl.BlockSpec(memory_space=pl.ANY), pl.BlockSpec(memory_space=pltpu.VMEM)
     return pl.pallas_call(
         wide_kernel,
+        in_specs=[anywhere] * 16,
+        out_specs=[anywhere, fast, fast],
         out_shape=[
             pltpu.HBM((rows, 2 * cols), jnp.float32),
             jax.ShapeDtypeStruct((rows + 8, cols), jnp.float32),
             jax.ShapeDtypeStruct((rows + 8, cols), jnp.float32),
+        ],
+        scratch_shapes=[
+            pltpu.VMEM((2, 4, 2 * rows, tokens), jnp.bfloat16),
+            pltpu.VMEM((2, 4, tokens, cols), jnp.bfloat16),
+            pltpu.VMEM((rows, 2 * cols), jnp.float32),
+            pltpu.SemaphoreType.DMA((2, 4, 2)),
+            pltpu.SemaphoreType.DMA((2,)),
         ],
         compiler_params=pltpu.CompilerParams(vmem_limit_bytes=20 * MIB),
         cost_estimate=pl.CostEstimate(flops=1 << 30, bytes_accessed=5 << 20, transcendentals=0),
@@ -380,7 +413,7 @@
     x, core = dp >> 3, dp & 1
     f32 = jnp.float32
 
-    gathered = lax.all_to_all(project(hidden, w_key, w_value), "seq", 0, 0, tiled=True)
+    gathered = lax.all_to_all(project(hidden, w_key, w_value), AXES, 0, 0, axis_index_groups=SEQ_GROUPS, tiled=True)
 
     queries = dot(hidden, w_query, ((1,), (0,))).astype(bf)
     d_att = dot(grads_in, w_out, ((1,), (0,))).astype(bf)
@@ -395,11 +428,12 @@
     terms, d_query, attended, h_from, g_from, h_core, g_core = lax.optimization_barrier(
         (terms, d_query, attended, h_from, g_from, h_core, g_core)
     )
-    terms = lax.all_to_all(terms.astype(half), "seq", 0, 0, tiled=True)
+    terms = lax.all_to_all(terms.astype(half), AXES, 0, 0, axis_index_groups=SEQ_GROUPS, tiled=True)
 
     def factors(own, first):
         beside = exchange(own, first << 6)
-        return [own, from_other_core(own), beside, from_other_core(beside)]
+        here = pltpu.with_memory_space_constraint(own, pltpu.HBM)
+        return [here, from_other_core(own), beside, from_other_core(beside)]
 
     keep, *sent = wide_products(
         [h, h_core, *h_from] + factors(d_query, 1),

time: 101 us -> 100 us (0.990)
  transfers between devices with their start and end apart: 20 -> 20, of which waited for: 8 -> 8; matrix products, arithmetic and copies ran while one was open for 4% -> 4% of each run, Pallas kernels for 17% -> 18%
where the time goes in v7:
time: 100 us; the launch traced here: 99.9 us
  starting transfers between devices  28 us (28%)
  blocking collectives  28 us (28%)
  Pallas kernels  22.4 us (22%)
  waiting for transfers between devices  13.5 us (14%)
  matrix products  4.06 us (4%)
  other arithmetic  3.07 us (3%)
    all_to_all x1, blocking collectives, local(): lax.all_to_all(part.astype(half), AXES, 0, 0, axis_index_groups=YZ_GROUPS...  28 us
    ppermute x18, starting transfers between devices, exchange(): return lax.ppermute(value, AXES, [(i, i ^ mask) for i in range(256)])  16.5 us
    ppermute x18, waiting for transfers between devices, exchange(): return lax.ppermute(value, AXES, [(i, i ^ mask) for i in range(256)])  10.4 us
    pallas_call x1, Pallas kernels, attention(): pl.pallas_call(attention_kernel, in_specs=[anywhere] * 3, out_specs=[anyw...  9.63 us
    all_to_all x1, starting transfers between devices, local(): lax.all_to_all(project(hidden, w_key, w_value), AXES, 0, 0, axis_index_gr...  6.11 us
    all_to_all x1, starting transfers between devices, local(): lax.all_to_all(terms.astype(half), AXES, 0, 0, axis_index_groups=SEQ_GROU...  5.42 us
    dot_general x3, matrix products, dot(): lax.dot_general(left, right, (dims, ((), ())), preferred_element_type=jnp...  4.06 us
    pallas_call x1, Pallas kernels, wide_products(): pl.pallas_call(wide_kernel, in_specs=[anywhere] * 16, out_specs=[anywhere...  3.95 us
  transfers between devices with their start and end apart: 20, of which 8 were waited for; matrix products, arithmetic and copies ran while one was open for 4% of the time, Pallas kernels for 18%

profile of v7, /device:TPU:32, one launch (start us, length us, event | category | flops | bytes accessed | tf_op | source)
XLA Modules:
  0.0 99.9 jit_solution(7290222440609541898)
XLA Ops:
  0.6 0.0 copy-start
  0.6 3.0 %project.1 = bf16[8,256,256]{2,1,0:T(8,128)(2,1)} custom-call(bf16[256,1536]{1,0:T(8,128)(2,1)} %bitcast.19, bf16[1536,128]{1,0:T(8,128)(2,1)} %w_key_ref.1, bf16[1536,128]{1,0:T(8,128)(2,1)} %w_value_ref.1), custom_call_target="tpu_custom_call" | custom-call | tf_op jit(solution)/shard_map/project/pallas_call | solution.py:59
  3.6 6.1 %all-to-all-start = ((bf16[8,256,256]{2,1,0:T(8,128)(2,1)}), bf16[8,256,256]{2,1,0:T(8,128)(2,1)}, u32[]{:S(2)}, u32[]{:S(2)}) async-start(bf16[8,256,256]{2,1,0:T(8,128)(2,1)} %project.1), calls=%async_computation | async-start | bytes 2097152 | tf_op jit(solution)/shard_map/all_to_all | solution.py:416
  9.8 0.1 pad_add_fusion.place_ref
  9.8 1.6 %turn.3 = (bf16[384,256]{1,0:T(8,128)(2,1)S(1)}, bf16[384,256]{1,0:T(8,128)(2,1)}, bf16[384,256]{1,0:T(8,128)(2,1)S(1)}, bf16[384,256]{1,0:T(8,128)(2,1)}) custom-call(s32[2]{0:T(128)S(1)} %pad_add_fusion.place_ref, bf16[256,1536]{1,0:T(8,128)(2,1)S(1)} %bitcast.21), custom_call_target="tpu_custom_call" | custom-call | tf_op jit(solution)/shard_map/turn/pallas_call | solution.py:81
  11.4 2.7 %collective-permute-start.2 = (bf16[384,256]{1,0:T(8,128)(2,1)S(1)}, bf16[384,256]{1,0:T(8,128)(2,1)S(1)}, u32[]{:S(2)}, u32[]{:S(2)}) collective-permute-start(bf16[384,256]{1,0:T(8,128)(2,1)S(1)} %get-tuple-element.43), channel_id=1, source_target_pairs={{0,192},{1,193},{2,194},{3,195},{4,196},{5,197},{6,198},{7,199},{8... | collective-permute-start | bytes 589832 | tf_op jit(solution)/shard_map/ppermute | solution.py:33
  14.1 0.6 collective-permute-start.5
  14.8 1.7 %turn.2 = (bf16[768,256]{1,0:T(8,128)(2,1)S(1)}, bf16[768,256]{1,0:T(8,128)(2,1)}, bf16[384,256]{1,0:T(8,128)(2,1)}, bf16[384,256]{1,0:T(8,128)(2,1)}) custom-call(s32[2]{0:T(128)S(1)} %pad_add_fusion.place_ref, bf16[256,1536]{1,0:T(8,128)(2,1)S(1)} %bitcast.20), custom_call_target="tpu_custom_call" | custom-call | tf_op jit(solution)/shard_map/turn/pallas_call | solution.py:81
  16.5 0.2 collective-permute-start
  16.7 1.3 %convolution_convert_fusion.2.q_hbm = bf16[256,512]{1,0:T(8,128)(2,1)} fusion(bf16[1536,512]{1,0:T(8,128)(2,1)S(1)} %copy-done.10, bf16[1,256,1536]{2,1,0:T(8,128)(2,1)S(1)} %copy-done.1), kind=kOutput, calls=%fused_computation.2 | convolution fusion | flops 402784256 | bytes 2621440 | tf_op jit(solution)/shard_map/dot_general | solution.py:29
  18.0 1.3 %convolution_convert_fusion.1.da_hbm = bf16[256,512]{1,0:T(8,128)(2,1)} fusion(bf16[1536,512]{1,0:T(8,128)(2,1)S(1)} %copy-done, bf16[1,256,1536]{2,1,0:T(8,128)(2,1)S(1)} %copy-done.3), kind=kOutput, calls=%fused_computation.1 | convolution fusion | flops 402784256 | bytes 2621440 | tf_op jit(solution)/shard_map/dot_general | solution.py:29
  19.3 0.2 collective-permute-done.2.refs_10_
  19.5 1.7 %collective-permute-start.1 = (bf16[384,256]{1,0:T(8,128)(2,1)}, bf16[384,256]{1,0:T(8,128)(2,1)S(1)}, u32[]{:S(2)}, u32[]{:S(2)}) collective-permute-start(bf16[384,256]{1,0:T(8,128)(2,1)} %get-tuple-element.42), channel_id=1, source_target_pairs={{0,72},{1,73},{2,74},{3,75},{4,76},{5,77},{6,78},{7,79},{8,64},{9,... | collective-permute-start | bytes 589832 | tf_op jit(solution)/shard_map/ppermute | solution.py:33
  21.2 3.2 %all-to-all-done = bf16[8,256,256]{2,1,0:T(8,128)(2,1)} async-done(((bf16[8,256,256]{2,1,0:T(8,128)(2,1)}), bf16[8,256,256]{2,1,0:T(8,128)(2,1)}, u32[]{:S(2)}, u32[]{:S(2)}) %all-to-all-start) | async-done | bytes 1048608 | tf_op jit(solution)/shard_map/all_to_all | solution.py:416
  24.3 9.6 %attention.1 = (bf16[256,512]{1,0:T(8,128)(2,1)}, bf16[256,512]{1,0:T(8,128)(2,1)}, f32[8,264,256]{2,1,0:T(8,128)S(1)}) custom-call(bf16[256,512]{1,0:T(8,128)(2,1)} %convolution_convert_fusion.2.q_hbm, bf16[256,512]{1,0:T(8,128)(2,1)} %convolution_convert_fusion.1.da_hbm, bf16[2048,256]{1,0:T(8,128)(2,1)} %bitcast.2.kv_hbm), custom_call_target="tpu_custom_call" | custom-call | flops 3221225472 | bytes 4194304 | tf_op jit(solution)/shard_map/attention/pallas_call | solution.py:214
  34.0 0.0 collective-permute-done.3.refs_11_
  34.0 0.0 collective-permute-done.5.refs_9_
  34.0 1.2 %convert_element_type.44 = f16[8,264,256]{2,1,0:T(8,128)(2,1)} convert(f32[8,264,256]{2,1,0:T(8,128)S(1)} %get-tuple-element.47) | non-fusion elementwise | flops 540672 | bytes 3244032 | tf_op jit(solution)/shard_map/convert_element_type | solution.py:431
  35.2 5.4 %all-to-all-start.1 = ((f16[8,264,256]{2,1,0:T(8,128)(2,1)}), f16[8,264,256]{2,1,0:T(8,128)(2,1)}, u32[]{:S(2)}, u32[]{:S(2)}) async-start(f16[8,264,256]{2,1,0:T(8,128)(2,1)} %convert_element_type.44), calls=%async_computation.1 | async-start | bytes 2162688 | tf_op jit(solution)/shard_map/all_to_all | solution.py:431
  40.6 1.6 %collective-permute-start.7 = (bf16[256,512]{1,0:T(8,128)(2,1)S(1)}, bf16[256,512]{1,0:T(8,128)(2,1)S(1)}, u32[]{:S(2)}, u32[]{:S(2)}) collective-permute-start(bf16[256,512]{1,0:T(8,128)(2,1)S(1)} %copy-done.9), channel_id=1, source_target_pairs={{0,64},{1,65},{2,66},{3,67},{4,68},{5,69},{6,70},{7,71},{8,72},{9,... | collective-permute-start | bytes 786440 | tf_op jit(solution)/shard_map/ppermute | solution.py:33
  42.2 2.1 %collective-permute-start.10 = (bf16[256,512]{1,0:T(8,128)(2,1)S(1)}, bf16[256,512]{1,0:T(8,128)(2,1)S(1)}, u32[]{:S(2)}, u32[]{:S(2)}) collective-permute-start(bf16[256,512]{1,0:T(8,128)(2,1)S(1)} %copy-done.8), channel_id=1, source_target_pairs={{0,192},{1,193},{2,194},{3,195},{4,196},{5,197},{6,198},{7,199},{8... | collective-permute-start | bytes 786440 | tf_op jit(solution)/shard_map/ppermute | solution.py:33
  44.3 0.5 collective-permute-start.9
  44.8 2.3 %collective-permute-done.7.refs_6_ = bf16[256,512]{1,0:T(8,128)(2,1)S(1)} collective-permute-done((bf16[256,512]{1,0:T(8,128)(2,1)S(1)}, bf16[256,512]{1,0:T(8,128)(2,1)S(1)}, u32[]{:S(2)}, u32[]{:S(2)}) %collective-permute-start.7) | collective-permute-done | bytes 262176 | tf_op jit(solution)/shard_map/ppermute | solution.py:33
  47.1 2.7 %collective-permute-done.10.refs_14_ = bf16[256,512]{1,0:T(8,128)(2,1)S(1)} collective-permute-done((bf16[256,512]{1,0:T(8,128)(2,1)S(1)}, bf16[256,512]{1,0:T(8,128)(2,1)S(1)}, u32[]{:S(2)}, u32[]{:S(2)}) %collective-permute-start.10) | collective-permute-done | bytes 262176 | tf_op jit(solution)/shard_map/ppermute | solution.py:33
  49.8 0.0 collective-permute-start.11
  49.8 1.5 %convolution_convert_fusion = bf16[256,1536]{1,0:T(8,128)(2,1)} fusion(bf16[256,512]{1,0:T(8,128)(2,1)S(1)} %copy-done.8, bf16[1536,512]{1,0:T(8,128)(2,1)S(1)} %copy-done), kind=kOutput, calls=%fused_computation | convolution fusion | flops 403046400 | bytes 2621440 | tf_op jit(solution)/shard_map/dot_general | solution.py:29
  51.3 0.0 collective-permute-done.11.refs_15_
  51.4 3.9 %wide.1 = (f32[192,1024]{1,0:T(8,128)}, f32[200,512]{1,0:T(8,128)S(1)}, f32[200,512]{1,0:T(8,128)S(1)}) custom-call(bf16[768,256]{1,0:T(8,128)(2,1)S(1)} %get-tuple-element.48.refs_0_.mine_ref, bf16[768,256]{1,0:T(8,128)(2,1)S(1)} %collective-permute-done.4.refs_1_.theirs_ref, bf16[384,256]{1,0:T(8,128)(2,1)} %collective-permute-done.refs_2_, ...), custom_call_target="tpu_custom_call" | custom-call | flops 1073741824 | bytes 5242880 | tf_op jit(solution)/shard_map/wide/pallas_call | solution.py:276
  55.4 1.4 %convert_element_type.49.terms_ref = f32[8,264,256]{2,1,0:T(8,128)S(1)} convert(f16[8,264,256]{2,1,0:T(8,128)(2,1)} %all-to-all-done.1) | non-fusion elementwise | flops 540672 | bytes 3244032 | tf_op jit(solution)/shard_map/convert_element_type | solution.py:447
  56.8 0.1 own_terms.1.own_ref
  57.0 0.6 collective-permute-start.14
  57.5 0.1 collective-permute-start.13
  57.7 2.1 %collective-permute-start.12 = (f16[200,512]{1,0:T(8,128)(2,1)S(1)}, f16[200,512]{1,0:T(8,128)(2,1)S(1)}, u32[]{:S(2)}, u32[]{:S(2)}) collective-permute-start(f16[200,512]{1,0:T(8,128)(2,1)S(1)} %convert_element_type.45), channel_id=1, source_target_pairs={{0,192},{1,193},{2,194},{3,195},{4,196},{5,197},{6,198},{7,199},{8... | collective-permute-start | bytes 614408 | tf_op jit(solution)/shard_map/ppermute | solution.py:33
  59.8 1.2 %narrow.1 = (f32[192,256]{1,0:T(8,128)}, f32[200,256]{1,0:T(8,128)S(1)}, f32[200,256]{1,0:T(8,128)S(1)}, f32[200,256]{1,0:T(8,128)S(1)}) custom-call(bf16[768,256]{1,0:T(8,128)(2,1)S(1)} %get-tuple-element.48.refs_0_.mine_ref, bf16[768,256]{1,0:T(8,128)(2,1)S(1)} %collective-permute-done.4.refs_1_.theirs_ref, f32[256,256]{1,0:T(8,128)S(1)} %own_terms.1.own_ref, ...), custom_call_target="tpu_custom_call" | custom-call | flops 1 | bytes 1 | tf_op jit(solution)/shard_map/narrow/pallas_call | solution.py:322
  61.0 1.9 %collective-permute-start.17 = (f16[200,256]{1,0:T(8,128)(2,1)S(1)}, f16[200,256]{1,0:T(8,128)(2,1)S(1)}, u32[]{:S(2)}, u32[]{:S(2)}) collective-permute-start(f16[200,256]{1,0:T(8,128)(2,1)S(1)} %convert_element_type.52), channel_id=1, source_target_pairs={{0,128},{1,129},{2,130},{3,131},{4,132},{5,133},{6,134},{7,135},{8... | collective-permute-start | bytes 307208 | tf_op jit(solution)/shard_map/ppermute | solution.py:33
  62.9 0.2 collective-permute-start.16
  63.1 2.1 %collective-permute-start.15 = (f16[200,256]{1,0:T(8,128)(2,1)S(1)}, f16[200,256]{1,0:T(8,128)(2,1)S(1)}, u32[]{:S(2)}, u32[]{:S(2)}) collective-permute-start(f16[200,256]{1,0:T(8,128)(2,1)S(1)} %convert_element_type.50), channel_id=1, source_target_pairs={{0,192},{1,193},{2,194},{3,195},{4,196},{5,197},{6,198},{7,199},{8... | collective-permute-start | bytes 307208 | tf_op jit(solution)/shard_map/ppermute | solution.py:33
  65.2 0.1 collective-permute-done.13
  65.3 1.9 %collective-permute-done.12 = f16[200,512]{1,0:T(8,128)(2,1)S(1)} collective-permute-done((f16[200,512]{1,0:T(8,128)(2,1)S(1)}, f16[200,512]{1,0:T(8,128)(2,1)S(1)}, u32[]{:S(2)}, u32[]{:S(2)}) %collective-permute-start.12) | collective-permute-done | bytes 204832 | tf_op jit(solution)/shard_map/ppermute | solution.py:33
  67.2 0.1 maximum_convert_fusion.wide_got_ref
  67.3 1.9 %collective-permute-done.17 = f16[200,256]{1,0:T(8,128)(2,1)S(1)} collective-permute-done((f16[200,256]{1,0:T(8,128)(2,1)S(1)}, f16[200,256]{1,0:T(8,128)(2,1)S(1)}, u32[]{:S(2)}, u32[]{:S(2)}) %collective-permute-start.17) | collective-permute-done | bytes 102432 | tf_op jit(solution)/shard_map/ppermute | solution.py:33
  69.2 1.2 %collective-permute-done.15 = f16[200,256]{1,0:T(8,128)(2,1)S(1)} collective-permute-done((f16[200,256]{1,0:T(8,128)(2,1)S(1)}, f16[200,256]{1,0:T(8,128)(2,1)S(1)}, u32[]{:S(2)}, u32[]{:S(2)}) %collective-permute-start.15) | collective-permute-done | bytes 102432 | tf_op jit(solution)/shard_map/ppermute | solution.py:33
  70.4 0.1 maximum_convert_fusion.1.narrow_got_ref
  70.5 0.5 after_x.1
  71.0 0.1 convert_element_type.54
  71.1 28.0 %all_to_all.15 = f16[32,64,128]{2,1,0:T(8,128)(2,1)S(1)} all-to-all(f16[32,64,128]{2,1,0:T(8,128)(2,1)S(1)} %convert_element_type.54), channel_id=1, replica_groups={{0,4,16,20,32,36,48,52,1,5,17,21,33,37,49,53,2,6,18,22,34,38,50,54,3,7,..., dimensions={0} | all-to-all | bytes 1048576 | tf_op jit(solution)/shard_map/all_to_all | solution.py:452
  99.1 0.1 convert_element_type.55.got_ref
  99.2 0.7 last_sum.1
  (39 shorter events, 0.2 us)
Async XLA Ops:
  0.6 17.3 %copy-start = (bf16[1536,512]{1,0:T(8,128)(2,1)S(1)}, bf16[1536,512]{1,0:T(8,128)(2,1)}, u32[]{:S(2)}) copy-start(bf16[1536,512]{1,0:T(8,128)(2,1)} %param.10) | copy-start | bytes 4718596
  3.6 6.2 %copy-start.2 = (bf16[1,256,1536]{2,1,0:T(8,128)(2,1)S(1)}, bf16[1,256,1536]{2,1,0:T(8,128)(2,1)}, u32[]{:S(2)}) copy-start(bf16[1,256,1536]{2,1,0:T(8,128)(2,1)} %param.11) | copy-start | bytes 2359300
  3.6 11.1 %copy-start.1 = (bf16[1,256,1536]{2,1,0:T(8,128)(2,1)S(1)}, bf16[1,256,1536]{2,1,0:T(8,128)(2,1)}, u32[]{:S(2)}) copy-start(bf16[1,256,1536]{2,1,0:T(8,128)(2,1)} %param.6) | copy-start | bytes 2359300
  3.6 20.7 %all-to-all-start = ((bf16[8,256,256]{2,1,0:T(8,128)(2,1)}), bf16[8,256,256]{2,1,0:T(8,128)(2,1)}, u32[]{:S(2)}, u32[]{:S(2)}) async-start(bf16[8,256,256]{2,1,0:T(8,128)(2,1)} %project.1), calls=%async_computation | async-start | bytes 2097152 | tf_op jit(solution)/shard_map/all_to_all | solution.py:416
  9.8 6.9 %copy-start.10 = (bf16[1536,512]{1,0:T(8,128)(2,1)S(1)}, bf16[1536,512]{1,0:T(8,128)(2,1)}, u32[]{:S(2)}) copy-start(bf16[1536,512]{1,0:T(8,128)(2,1)} %param.7) | copy-start | bytes 4718596
  11.4 8.1 %collective-permute-start.2 = (bf16[384,256]{1,0:T(8,128)(2,1)S(1)}, bf16[384,256]{1,0:T(8,128)(2,1)S(1)}, u32[]{:S(2)}, u32[]{:S(2)}) collective-permute-start(bf16[384,256]{1,0:T(8,128)(2,1)S(1)} %get-tuple-element.43), channel_id=1, source_target_pairs={{0,192},{1,193},{2,194},{3,195},{4,196},{5,197},{6,198},{7,199},{8... | collective-permute-start | bytes 589832 | tf_op jit(solution)/shard_map/ppermute | solution.py:33
  14.1 19.9 %collective-permute-start.3 = (bf16[384,256]{1,0:T(8,128)(2,1)}, bf16[384,256]{1,0:T(8,128)(2,1)}, u32[]{:S(2)}, u32[]{:S(2)}) collective-permute-start(bf16[384,256]{1,0:T(8,128)(2,1)} %get-tuple-element.44), channel_id=1, source_target_pairs={{0,200},{1,201},{2,202},{3,203},{4,204},{5,205},{6,206},{7,207},{8... | collective-permute-start | bytes 589832 | tf_op jit(solution)/shard_map/ppermute | solution.py:33
  14.1 3.9 %copy-start.3 = (bf16[1,256,1536]{2,1,0:T(8,128)(2,1)S(1)}, bf16[1,256,1536]{2,1,0:T(8,128)(2,1)}, u32[]{:S(2)}) copy-start(bf16[1,256,1536]{2,1,0:T(8,128)(2,1)} %param.11) | copy-start | bytes 2359300
  14.1 19.9 %collective-permute-start.5 = (bf16[384,256]{1,0:T(8,128)(2,1)}, bf16[384,256]{1,0:T(8,128)(2,1)}, u32[]{:S(2)}, u32[]{:S(2)}) collective-permute-start(bf16[384,256]{1,0:T(8,128)(2,1)} %get-tuple-element.46), channel_id=1, source_target_pairs={{0,8},{1,9},{2,10},{3,11},{4,12},{5,13},{6,14},{7,15},{8,0},{9,1},... | collective-permute-start | bytes 589832 | tf_op jit(solution)/shard_map/ppermute | solution.py:33
  16.5 17.6 %collective-permute-start = (bf16[384,256]{1,0:T(8,128)(2,1)}, bf16[384,256]{1,0:T(8,128)(2,1)}, u32[]{:S(2)}, u32[]{:S(2)}) collective-permute-start(bf16[384,256]{1,0:T(8,128)(2,1)} %get-tuple-element.41), channel_id=1, source_target_pairs={{0,64},{1,65},{2,66},{3,67},{4,68},{5,69},{6,70},{7,71},{8,72},{9,... | collective-permute-start | bytes 589832 | tf_op jit(solution)/shard_map/ppermute | solution.py:33
  16.7 17.4 %collective-permute-start.4 = (bf16[768,256]{1,0:T(8,128)(2,1)}, bf16[768,256]{1,0:T(8,128)(2,1)S(1)}, u32[]{:S(2)}, u32[]{:S(2)}) collective-permute-start(bf16[768,256]{1,0:T(8,128)(2,1)} %get-tuple-element.45), channel_id=1, source_target_pairs={{0,8},{1,9},{2,10},{3,11},{4,12},{5,13},{6,14},{7,15},{8,0},{9,1},... | collective-permute-start | bytes 1179656 | tf_op jit(solution)/shard_map/ppermute | solution.py:33
  19.5 14.5 %collective-permute-start.1 = (bf16[384,256]{1,0:T(8,128)(2,1)}, bf16[384,256]{1,0:T(8,128)(2,1)S(1)}, u32[]{:S(2)}, u32[]{:S(2)}) collective-permute-start(bf16[384,256]{1,0:T(8,128)(2,1)} %get-tuple-element.42), channel_id=1, source_target_pairs={{0,72},{1,73},{2,74},{3,75},{4,76},{5,77},{6,78},{7,79},{8,64},{9,... | collective-permute-start | bytes 589832 | tf_op jit(solution)/shard_map/ppermute | solution.py:33
  34.0 1.2 %copy-start.5 = (bf16[384,256]{1,0:T(8,128)(2,1)}, bf16[384,256]{1,0:T(8,128)(2,1)S(1)}, u32[]{:S(2)}) copy-start(bf16[384,256]{1,0:T(8,128)(2,1)S(1)} %collective-permute-done.1.refs_3_) | copy-start | bytes 589828
  35.2 5.4 %copy-start.9 = (bf16[256,512]{1,0:T(8,128)(2,1)S(1)}, bf16[256,512]{1,0:T(8,128)(2,1)}, u32[]{:S(2)}) copy-start(bf16[256,512]{1,0:T(8,128)(2,1)} %get-tuple-element.52.refs_4_) | copy-start | bytes 786436
  35.2 7.0 %copy-start.8 = (bf16[256,512]{1,0:T(8,128)(2,1)S(1)}, bf16[256,512]{1,0:T(8,128)(2,1)}, u32[]{:S(2)}) copy-start(bf16[256,512]{1,0:T(8,128)(2,1)} %get-tuple-element.57.refs_12_) | copy-start | bytes 786436
  35.2 20.2 %all-to-all-start.1 = ((f16[8,264,256]{2,1,0:T(8,128)(2,1)}), f16[8,264,256]{2,1,0:T(8,128)(2,1)}, u32[]{:S(2)}, u32[]{:S(2)}) async-start(f16[8,264,256]{2,1,0:T(8,128)(2,1)} %convert_element_type.44), calls=%async_computation.1 | async-start | bytes 2162688 | tf_op jit(solution)/shard_map/all_to_all | solution.py:431
  40.6 10.7 %copy-start.6 = (bf16[384,256]{1,0:T(8,128)(2,1)S(1)}, bf16[384,256]{1,0:T(8,128)(2,1)}, u32[]{:S(2)}) copy-start(bf16[384,256]{1,0:T(8,128)(2,1)} %copy-done.5) | copy-start | bytes 589828
  40.6 6.5 %collective-permute-start.7 = (bf16[256,512]{1,0:T(8,128)(2,1)S(1)}, bf16[256,512]{1,0:T(8,128)(2,1)S(1)}, u32[]{:S(2)}, u32[]{:S(2)}) collective-permute-start(bf16[256,512]{1,0:T(8,128)(2,1)S(1)} %copy-done.9), channel_id=1, source_target_pairs={{0,64},{1,65},{2,66},{3,67},{4,68},{5,69},{6,70},{7,71},{8,72},{9,... | collective-permute-start | bytes 786440 | tf_op jit(solution)/shard_map/ppermute | solution.py:33
  42.2 7.6 %collective-permute-start.10 = (bf16[256,512]{1,0:T(8,128)(2,1)S(1)}, bf16[256,512]{1,0:T(8,128)(2,1)S(1)}, u32[]{:S(2)}, u32[]{:S(2)}) collective-permute-start(bf16[256,512]{1,0:T(8,128)(2,1)S(1)} %copy-done.8), channel_id=1, source_target_pairs={{0,192},{1,193},{2,194},{3,195},{4,196},{5,197},{6,198},{7,199},{8... | collective-permute-start | bytes 786440 | tf_op jit(solution)/shard_map/ppermute | solution.py:33
  44.3 7.0 %collective-permute-start.6 = (bf16[256,512]{1,0:T(8,128)(2,1)S(1)}, bf16[256,512]{1,0:T(8,128)(2,1)S(1)}, u32[]{:S(2)}, u32[]{:S(2)}) collective-permute-start(bf16[256,512]{1,0:T(8,128)(2,1)S(1)} %copy-done.9), channel_id=1, source_target_pairs={{0,8},{1,9},{2,10},{3,11},{4,12},{5,13},{6,14},{7,15},{8,0},{9,1},... | collective-permute-start | bytes 786440 | tf_op jit(solution)/shard_map/ppermute | solution.py:33
  44.3 7.0 %collective-permute-start.9 = (bf16[256,512]{1,0:T(8,128)(2,1)S(1)}, bf16[256,512]{1,0:T(8,128)(2,1)S(1)}, u32[]{:S(2)}, u32[]{:S(2)}) collective-permute-start(bf16[256,512]{1,0:T(8,128)(2,1)S(1)} %copy-done.8), channel_id=1, source_target_pairs={{0,8},{1,9},{2,10},{3,11},{4,12},{5,13},{6,14},{7,15},{8,0},{9,1},... | collective-permute-start | bytes 786440 | tf_op jit(solution)/shard_map/ppermute | solution.py:33
  47.1 4.2 %collective-permute-start.8 = (bf16[256,512]{1,0:T(8,128)(2,1)S(1)}, bf16[256,512]{1,0:T(8,128)(2,1)S(1)}, u32[]{:S(2)}, u32[]{:S(2)}) collective-permute-start(bf16[256,512]{1,0:T(8,128)(2,1)S(1)} %collective-permute-done.7.refs_6_), channel_id=1, source_target_pairs={{0,8},{1,9},{2,10},{3,11},{4,12},{5,13},{6,14},{7,15},{8,0},{9,1},... | collective-permute-start | bytes 786440 | tf_op jit(solution)/shard_map/ppermute | solution.py:33
  49.8 1.5 %collective-permute-start.11 = (bf16[256,512]{1,0:T(8,128)(2,1)S(1)}, bf16[256,512]{1,0:T(8,128)(2,1)S(1)}, u32[]{:S(2)}, u32[]{:S(2)}) collective-permute-start(bf16[256,512]{1,0:T(8,128)(2,1)S(1)} %collective-permute-done.10.refs_14_), channel_id=1, source_target_pairs={{0,8},{1,9},{2,10},{3,11},{4,12},{5,13},{6,14},{7,15},{8,0},{9,1},... | collective-permute-start | bytes 786440 | tf_op jit(solution)/shard_map/ppermute | solution.py:33
  57.0 2.8 %collective-permute-start.14 = (f32[256,256]{1,0:T(8,128)S(1)}, f32[256,256]{1,0:T(8,128)S(1)}, u32[]{:S(2)}, u32[]{:S(2)}) collective-permute-start(f32[256,256]{1,0:T(8,128)S(1)} %own_terms.1.own_ref), channel_id=1, source_target_pairs={{0,8},{1,9},{2,10},{3,11},{4,12},{5,13},{6,14},{7,15},{8,0},{9,1},... | collective-permute-start | bytes 786440 | tf_op jit(solution)/shard_map/ppermute | solution.py:33
  57.5 7.7 %collective-permute-start.13 = (f16[200,512]{1,0:T(8,128)(2,1)S(1)}, f16[200,512]{1,0:T(8,128)(2,1)S(1)}, u32[]{:S(2)}, u32[]{:S(2)}) collective-permute-start(f16[200,512]{1,0:T(8,128)(2,1)S(1)} %convert_element_type.46), channel_id=1, source_target_pairs={{0,64},{1,65},{2,66},{3,67},{4,68},{5,69},{6,70},{7,71},{8,72},{9,... | collective-permute-start | bytes 614408 | tf_op jit(solution)/shard_map/ppermute | solution.py:33
  57.7 9.5 %collective-permute-start.12 = (f16[200,512]{1,0:T(8,128)(2,1)S(1)}, f16[200,512]{1,0:T(8,128)(2,1)S(1)}, u32[]{:S(2)}, u32[]{:S(2)}) collective-permute-start(f16[200,512]{1,0:T(8,128)(2,1)S(1)} %convert_element_type.45), channel_id=1, source_target_pairs={{0,192},{1,193},{2,194},{3,195},{4,196},{5,197},{6,198},{7,199},{8... | collective-permute-start | bytes 614408 | tf_op jit(solution)/shard_map/ppermute | solution.py:33
  61.0 9.5 %copy-start.4 = (f32[192,1024]{1,0:T(8,128)S(1)}, f32[192,1024]{1,0:T(8,128)}, u32[]{:S(2)}) copy-start(f32[192,1024]{1,0:T(8,128)} %get-tuple-element.61.wide_ref) | copy-start | bytes 2359300
  61.0 9.5 %copy-start.7 = (f32[192,256]{1,0:T(8,128)S(1)}, f32[192,256]{1,0:T(8,128)}, u32[]{:S(2)}) copy-start(f32[192,256]{1,0:T(8,128)} %get-tuple-element.63.narrow_ref) | copy-start | bytes 589828
  61.0 8.2 %collective-permute-start.17 = (f16[200,256]{1,0:T(8,128)(2,1)S(1)}, f16[200,256]{1,0:T(8,128)(2,1)S(1)}, u32[]{:S(2)}, u32[]{:S(2)}) collective-permute-start(f16[200,256]{1,0:T(8,128)(2,1)S(1)} %convert_element_type.52), channel_id=1, source_target_pairs={{0,128},{1,129},{2,130},{3,131},{4,132},{5,133},{6,134},{7,135},{8... | collective-permute-start | bytes 307208 | tf_op jit(solution)/shard_map/ppermute | solution.py:33
  62.9 6.3 %collective-permute-start.16 = (f16[200,256]{1,0:T(8,128)(2,1)S(1)}, f16[200,256]{1,0:T(8,128)(2,1)S(1)}, u32[]{:S(2)}, u32[]{:S(2)}) collective-permute-start(f16[200,256]{1,0:T(8,128)(2,1)S(1)} %convert_element_type.51), channel_id=1, source_target_pairs={{0,64},{1,65},{2,66},{3,67},{4,68},{5,69},{6,70},{7,71},{8,72},{9,... | collective-permute-start | bytes 307208 | tf_op jit(solution)/shard_map/ppermute | solution.py:33
  63.1 7.3 %collective-permute-start.15 = (f16[200,256]{1,0:T(8,128)(2,1)S(1)}, f16[200,256]{1,0:T(8,128)(2,1)S(1)}, u32[]{:S(2)}, u32[]{:S(2)}) collective-permute-start(f16[200,256]{1,0:T(8,128)(2,1)S(1)} %convert_element_type.50), channel_id=1, source_target_pairs={{0,192},{1,193},{2,194},{3,195},{4,196},{5,197},{6,198},{7,199},{8... | collective-permute-start | bytes 307208 | tf_op jit(solution)/shard_map/ppermute | solution.py:33

commit v8 on v7

--- a/solution.py
+++ b/solution.py
@@ -22,7 +22,8 @@
 SEQ_GROUPS = [
     [place(x, y, 2 * z + low, c) for y in range(4) for low in range(2)] for x in range(4) for z in range(4) for c in range(2)
 ]
-YZ_GROUPS = [[place(x, y, z, c) for y in range(4) for z in range(8)] for x in range(4) for c in range(2)]
+YZ_ORDER = [(y, (i + 2 * y) % 8) for i in range(8) for y in range(4)]
+YZ_GROUPS = [[place(x, y, z, c) for y, z in YZ_ORDER] for x in range(4) for c in range(2)]
 
 
 def dot(left, right, dims):
@@ -362,8 +363,7 @@
         top = exponent(total)
         total_ref[:, first : first + width] = total * jnp.exp2(-top)
         out_ref[:, 60 + i, :] = jnp.broadcast_to(top, (out_ref.shape[0], HD))
-    for k in range(out_ref.shape[0]):
-        y, z = k // 8, k % 8
+    for k, (y, z) in enumerate(YZ_ORDER):
         start = 48 * (z // 2) + 6 * (4 * (z % 2) + y)
         for j in range(10):
             out_ref[k, 6 * j : 6 * j + 6, :] = total_ref[start : start + 6, j * HD : (j + 1) * HD]
@@ -443,7 +443,7 @@
     wide_got = [exchange(block, m << 6) for m, block in zip((3, 1), sent)]
     branch = dot(attended, w_out, ((1,), (1,))).astype(bf)
 
-    terms, _, branch = lax.optimization_barrier((terms, sent, branch))
+    terms, _ = lax.optimization_barrier((terms, sent))
     d_kv = own_terms(terms.astype(f32))
     narrow, *sent = narrow_products(h, h_core, d_kv, from_other_core(d_kv))
     narrow_got = [exchange(block.astype(half), m << 6) for m, block in zip((3, 1, 2), sent)]

time: 100 us -> 102 us (1.020)
  blocking collectives: 28 us -> 0 us
  waiting for transfers between devices: 13.5 us -> 31 us
  starting transfers between devices: 28 us -> 38.2 us
    all_to_all x1 -> x0, blocking collectives: 28 us -> none  [local(): lax.all_to_all(part.astype(half), AXES, 0, 0, axis_index_groups=YZ_GROUPS...]
    all_to_all x0 -> x1, waiting for transfers between devices: none -> 15.7 us  [local(): lax.all_to_all(part.astype(half), AXES, 0, 0, axis_index_groups=YZ_GROUPS...]
    all_to_all x0 -> x1, starting transfers between devices: none -> 10.7 us  [local(): lax.all_to_all(part.astype(half), AXES, 0, 0, axis_index_groups=YZ_GROUPS...]
    ppermute x18, waiting for transfers between devices: 10.4 us -> 12.1 us  [exchange(): return lax.ppermute(value, AXES, [(i, i ^ mask) for i in range(256)])]
  transfers between devices with their start and end apart: 20 -> 21, of which waited for: 8 -> 11; matrix products, arithmetic and copies ran while one was open for 4% -> 4% of each run, Pallas kernels for 18% -> 18%
where the time goes in v8:
time: 102 us; the launch traced here: 101 us
  starting transfers between devices  38.2 us (37%)
  waiting for transfers between devices  31 us (30%)
  Pallas kernels  22.3 us (22%)
  matrix products  4.04 us (4%)
  other arithmetic  3.85 us (4%)
    ppermute x18, starting transfers between devices, exchange(): return lax.ppermute(value, AXES, [(i, i ^ mask) for i in range(256)])  15.9 us
    all_to_all x1, waiting for transfers between devices, local(): lax.all_to_all(part.astype(half), AXES, 0, 0, axis_index_groups=YZ_GROUPS...  15.7 us
    ppermute x18, waiting for transfers between devices, exchange(): return lax.ppermute(value, AXES, [(i, i ^ mask) for i in range(256)])  12.1 us
    all_to_all x1, starting transfers between devices, local(): lax.all_to_all(part.astype(half), AXES, 0, 0, axis_index_groups=YZ_GROUPS...  10.7 us
    pallas_call x1, Pallas kernels, attention(): pl.pallas_call(attention_kernel, in_specs=[anywhere] * 3, out_specs=[anyw...  9.58 us
    all_to_all x1, starting transfers between devices, local(): lax.all_to_all(project(hidden, w_key, w_value), AXES, 0, 0, axis_index_gr...  6.09 us
    all_to_all x1, starting transfers between devices, local(): lax.all_to_all(terms.astype(half), AXES, 0, 0, axis_index_groups=SEQ_GROU...  5.41 us
    dot_general x3, matrix products, dot(): lax.dot_general(left, right, (dims, ((), ())), preferred_element_type=jnp...  4.04 us
  transfers between devices with their start and end apart: 21, of which 11 were waited for; matrix products, arithmetic and copies ran while one was open for 4% of the time, Pallas kernels for 18%

profile of v8, /device:TPU:32, one launch (start us, length us, event | category | flops | bytes accessed | tf_op | source)
XLA Modules:
  0.0 101.2 jit_solution(18269585022400369247)
XLA Ops:
  0.6 0.0 copy-start
  0.6 3.0 %project.1 = bf16[8,256,256]{2,1,0:T(8,128)(2,1)} custom-call(bf16[256,1536]{1,0:T(8,128)(2,1)} %bitcast.20, bf16[1536,128]{1,0:T(8,128)(2,1)} %w_key_ref.1, bf16[1536,128]{1,0:T(8,128)(2,1)} %w_value_ref.1), custom_call_target="tpu_custom_call" | custom-call | tf_op jit(solution)/shard_map/project/pallas_call | solution.py:60
  3.6 6.1 %all-to-all-start = ((bf16[8,256,256]{2,1,0:T(8,128)(2,1)}), bf16[8,256,256]{2,1,0:T(8,128)(2,1)}, u32[]{:S(2)}, u32[]{:S(2)}) async-start(bf16[8,256,256]{2,1,0:T(8,128)(2,1)} %project.1), calls=%async_computation | async-start | bytes 2097152 | tf_op jit(solution)/shard_map/all_to_all | solution.py:416
  9.7 0.1 pad_add_fusion.place_ref
  9.8 1.6 %turn.3 = (bf16[384,256]{1,0:T(8,128)(2,1)S(1)}, bf16[384,256]{1,0:T(8,128)(2,1)}, bf16[384,256]{1,0:T(8,128)(2,1)S(1)}, bf16[384,256]{1,0:T(8,128)(2,1)}) custom-call(s32[2]{0:T(128)S(1)} %pad_add_fusion.place_ref, bf16[256,1536]{1,0:T(8,128)(2,1)S(1)} %bitcast.22), custom_call_target="tpu_custom_call" | custom-call | tf_op jit(solution)/shard_map/turn/pallas_call | solution.py:82
  11.4 2.7 %collective-permute-start.2 = (bf16[384,256]{1,0:T(8,128)(2,1)S(1)}, bf16[384,256]{1,0:T(8,128)(2,1)S(1)}, u32[]{:S(2)}, u32[]{:S(2)}) collective-permute-start(bf16[384,256]{1,0:T(8,128)(2,1)S(1)} %get-tuple-element.42), channel_id=1, source_target_pairs={{0,192},{1,193},{2,194},{3,195},{4,196},{5,197},{6,198},{7,199},{8... | collective-permute-start | bytes 589832 | tf_op jit(solution)/shard_map/ppermute | solution.py:34
  14.1 0.6 collective-permute-start.5
  14.7 1.7 %turn.2 = (bf16[768,256]{1,0:T(8,128)(2,1)S(1)}, bf16[768,256]{1,0:T(8,128)(2,1)}, bf16[384,256]{1,0:T(8,128)(2,1)}, bf16[384,256]{1,0:T(8,128)(2,1)}) custom-call(s32[2]{0:T(128)S(1)} %pad_add_fusion.place_ref, bf16[256,1536]{1,0:T(8,128)(2,1)S(1)} %bitcast.21), custom_call_target="tpu_custom_call" | custom-call | tf_op jit(solution)/shard_map/turn/pallas_call | solution.py:82
  16.4 0.2 collective-permute-start
  16.7 1.3 %convolution_convert_fusion.2.q_hbm = bf16[256,512]{1,0:T(8,128)(2,1)} fusion(bf16[1536,512]{1,0:T(8,128)(2,1)S(1)} %copy-done.11, bf16[1,256,1536]{2,1,0:T(8,128)(2,1)S(1)} %copy-done.1), kind=kOutput, calls=%fused_computation.3 | convolution fusion | flops 402784256 | bytes 2621440 | tf_op jit(solution)/shard_map/dot_general | solution.py:30
  18.0 1.3 %convolution_convert_fusion.1.da_hbm = bf16[256,512]{1,0:T(8,128)(2,1)} fusion(bf16[1536,512]{1,0:T(8,128)(2,1)S(1)} %copy-done, bf16[1,256,1536]{2,1,0:T(8,128)(2,1)S(1)} %copy-done.3), kind=kOutput, calls=%fused_computation.2 | convolution fusion | flops 402784256 | bytes 2621440 | tf_op jit(solution)/shard_map/dot_general | solution.py:30
  19.3 0.2 collective-permute-done.2.refs_10_
  19.5 1.7 %collective-permute-start.1 = (bf16[384,256]{1,0:T(8,128)(2,1)}, bf16[384,256]{1,0:T(8,128)(2,1)S(1)}, u32[]{:S(2)}, u32[]{:S(2)}) collective-permute-start(bf16[384,256]{1,0:T(8,128)(2,1)} %get-tuple-element.41), channel_id=1, source_target_pairs={{0,72},{1,73},{2,74},{3,75},{4,76},{5,77},{6,78},{7,79},{8,64},{9,... | collective-permute-start | bytes 589832 | tf_op jit(solution)/shard_map/ppermute | solution.py:34
  21.1 3.2 %all-to-all-done = bf16[8,256,256]{2,1,0:T(8,128)(2,1)} async-done(((bf16[8,256,256]{2,1,0:T(8,128)(2,1)}), bf16[8,256,256]{2,1,0:T(8,128)(2,1)}, u32[]{:S(2)}, u32[]{:S(2)}) %all-to-all-start) | async-done | bytes 1048608 | tf_op jit(solution)/shard_map/all_to_all | solution.py:416
  24.3 9.6 %attention.1 = (bf16[256,512]{1,0:T(8,128)(2,1)}, bf16[256,512]{1,0:T(8,128)(2,1)}, f32[8,264,256]{2,1,0:T(8,128)S(1)}) custom-call(bf16[256,512]{1,0:T(8,128)(2,1)} %convolution_convert_fusion.2.q_hbm, bf16[256,512]{1,0:T(8,128)(2,1)} %convolution_convert_fusion.1.da_hbm, bf16[2048,256]{1,0:T(8,128)(2,1)} %bitcast.2.kv_hbm), custom_call_target="tpu_custom_call" | custom-call | flops 3221225472 | bytes 4194304 | tf_op jit(solution)/shard_map/attention/pallas_call | solution.py:215
  34.0 1.1 %convert_element_type.48 = f16[8,264,256]{2,1,0:T(8,128)(2,1)} convert(f32[8,264,256]{2,1,0:T(8,128)S(1)} %get-tuple-element.59) | non-fusion elementwise | flops 540672 | bytes 3244032 | tf_op jit(solution)/shard_map/convert_element_type | solution.py:431
  35.2 5.4 %all-to-all-start.1 = ((f16[8,264,256]{2,1,0:T(8,128)(2,1)}), f16[8,264,256]{2,1,0:T(8,128)(2,1)}, u32[]{:S(2)}, u32[]{:S(2)}) async-start(f16[8,264,256]{2,1,0:T(8,128)(2,1)} %convert_element_type.48), calls=%async_computation.1 | async-start | bytes 2162688 | tf_op jit(solution)/shard_map/all_to_all | solution.py:431
  40.6 1.5 %collective-permute-start.7 = (bf16[256,512]{1,0:T(8,128)(2,1)S(1)}, bf16[256,512]{1,0:T(8,128)(2,1)S(1)}, u32[]{:S(2)}, u32[]{:S(2)}) collective-permute-start(bf16[256,512]{1,0:T(8,128)(2,1)S(1)} %copy-done.10), channel_id=1, source_target_pairs={{0,64},{1,65},{2,66},{3,67},{4,68},{5,69},{6,70},{7,71},{8,72},{9,... | collective-permute-start | bytes 786440 | tf_op jit(solution)/shard_map/ppermute | solution.py:34
  42.1 2.1 %collective-permute-start.10 = (bf16[256,512]{1,0:T(8,128)(2,1)S(1)}, bf16[256,512]{1,0:T(8,128)(2,1)S(1)}, u32[]{:S(2)}, u32[]{:S(2)}) collective-permute-start(bf16[256,512]{1,0:T(8,128)(2,1)S(1)} %copy-done.8), channel_id=1, source_target_pairs={{0,192},{1,193},{2,194},{3,195},{4,196},{5,197},{6,198},{7,199},{8... | collective-permute-start | bytes 786440 | tf_op jit(solution)/shard_map/ppermute | solution.py:34
  44.2 0.5 collective-permute-start.9
  44.7 2.3 %collective-permute-done.7.refs_6_ = bf16[256,512]{1,0:T(8,128)(2,1)S(1)} collective-permute-done((bf16[256,512]{1,0:T(8,128)(2,1)S(1)}, bf16[256,512]{1,0:T(8,128)(2,1)S(1)}, u32[]{:S(2)}, u32[]{:S(2)}) %collective-permute-start.7) | collective-permute-done | bytes 262176 | tf_op jit(solution)/shard_map/ppermute | solution.py:34
  46.9 2.7 %collective-permute-done.10.refs_14_ = bf16[256,512]{1,0:T(8,128)(2,1)S(1)} collective-permute-done((bf16[256,512]{1,0:T(8,128)(2,1)S(1)}, bf16[256,512]{1,0:T(8,128)(2,1)S(1)}, u32[]{:S(2)}, u32[]{:S(2)}) %collective-permute-start.10) | collective-permute-done | bytes 262176 | tf_op jit(solution)/shard_map/ppermute | solution.py:34
  49.6 0.0 collective-permute-start.11
  49.7 1.5 %collective-permute-done.11.refs_15_ = bf16[256,512]{1,0:T(8,128)(2,1)S(1)} collective-permute-done((bf16[256,512]{1,0:T(8,128)(2,1)S(1)}, bf16[256,512]{1,0:T(8,128)(2,1)S(1)}, u32[]{:S(2)}, u32[]{:S(2)}) %collective-permute-start.11) | collective-permute-done | bytes 262176 | tf_op jit(solution)/shard_map/ppermute | solution.py:34
  51.2 0.9 copy-done.6
  52.1 3.9 %wide.1 = (f32[192,1024]{1,0:T(8,128)}, f32[200,512]{1,0:T(8,128)S(1)}, f32[200,512]{1,0:T(8,128)S(1)}) custom-call(bf16[768,256]{1,0:T(8,128)(2,1)S(1)} %get-tuple-element.47.refs_0_.mine_ref, bf16[768,256]{1,0:T(8,128)(2,1)S(1)} %collective-permute-done.4.refs_1_.theirs_ref, bf16[384,256]{1,0:T(8,128)(2,1)} %collective-permute-done.refs_2_, ...), custom_call_target="tpu_custom_call" | custom-call | flops 1073741824 | bytes 5242880 | tf_op jit(solution)/shard_map/wide/pallas_call | solution.py:277
  56.1 1.4 %convert_element_type.49.terms_ref = f32[8,264,256]{2,1,0:T(8,128)S(1)} convert(f16[8,264,256]{2,1,0:T(8,128)(2,1)} %all-to-all-done.1) | non-fusion elementwise | flops 540672 | bytes 3244032 | tf_op jit(solution)/shard_map/convert_element_type | solution.py:447
  57.5 0.1 own_terms.1.own_ref
  57.6 0.2 collective-permute-start.14
  57.9 2.2 %collective-permute-start.12 = (f16[200,512]{1,0:T(8,128)(2,1)S(1)}, f16[200,512]{1,0:T(8,128)(2,1)S(1)}, u32[]{:S(2)}, u32[]{:S(2)}) collective-permute-start(f16[200,512]{1,0:T(8,128)(2,1)S(1)} %convert_element_type.45), channel_id=1, source_target_pairs={{0,192},{1,193},{2,194},{3,195},{4,196},{5,197},{6,198},{7,199},{8... | collective-permute-start | bytes 614408 | tf_op jit(solution)/shard_map/ppermute | solution.py:34
  60.0 1.2 %narrow.1 = (f32[192,256]{1,0:T(8,128)}, f32[200,256]{1,0:T(8,128)S(1)}, f32[200,256]{1,0:T(8,128)S(1)}, f32[200,256]{1,0:T(8,128)S(1)}) custom-call(bf16[768,256]{1,0:T(8,128)(2,1)S(1)} %get-tuple-element.47.refs_0_.mine_ref, bf16[768,256]{1,0:T(8,128)(2,1)S(1)} %collective-permute-done.4.refs_1_.theirs_ref, f32[256,256]{1,0:T(8,128)S(1)} %own_terms.1.own_ref, ...), custom_call_target="tpu_custom_call" | custom-call | flops 1 | bytes 1 | tf_op jit(solution)/shard_map/narrow/pallas_call | solution.py:323
  61.3 2.0 %collective-permute-start.17 = (f16[200,256]{1,0:T(8,128)(2,1)S(1)}, f16[200,256]{1,0:T(8,128)(2,1)S(1)}, u32[]{:S(2)}, u32[]{:S(2)}) collective-permute-start(f16[200,256]{1,0:T(8,128)(2,1)S(1)} %convert_element_type.52), channel_id=1, source_target_pairs={{0,128},{1,129},{2,130},{3,131},{4,132},{5,133},{6,134},{7,135},{8... | collective-permute-start | bytes 307208 | tf_op jit(solution)/shard_map/ppermute | solution.py:34
  63.3 0.2 collective-permute-start.16
  63.5 1.9 %collective-permute-start.15 = (f16[200,256]{1,0:T(8,128)(2,1)S(1)}, f16[200,256]{1,0:T(8,128)(2,1)S(1)}, u32[]{:S(2)}, u32[]{:S(2)}) collective-permute-start(f16[200,256]{1,0:T(8,128)(2,1)S(1)} %convert_element_type.50), channel_id=1, source_target_pairs={{0,192},{1,193},{2,194},{3,195},{4,196},{5,197},{6,198},{7,199},{8... | collective-permute-start | bytes 307208 | tf_op jit(solution)/shard_map/ppermute | solution.py:34
  65.4 0.3 collective-permute-done.13
  65.8 1.6 %collective-permute-done.12 = f16[200,512]{1,0:T(8,128)(2,1)S(1)} collective-permute-done((f16[200,512]{1,0:T(8,128)(2,1)S(1)}, f16[200,512]{1,0:T(8,128)(2,1)S(1)}, u32[]{:S(2)}, u32[]{:S(2)}) %collective-permute-start.12) | collective-permute-done | bytes 204832 | tf_op jit(solution)/shard_map/ppermute | solution.py:34
  67.4 0.1 maximum_convert_fusion.wide_got_ref
  67.5 2.1 %collective-permute-done.17 = f16[200,256]{1,0:T(8,128)(2,1)S(1)} collective-permute-done((f16[200,256]{1,0:T(8,128)(2,1)S(1)}, f16[200,256]{1,0:T(8,128)(2,1)S(1)}, u32[]{:S(2)}, u32[]{:S(2)}) %collective-permute-start.17) | collective-permute-done | bytes 102432 | tf_op jit(solution)/shard_map/ppermute | solution.py:34
  69.5 0.1 collective-permute-done.16
  69.7 1.3 %collective-permute-done.15 = f16[200,256]{1,0:T(8,128)(2,1)S(1)} collective-permute-done((f16[200,256]{1,0:T(8,128)(2,1)S(1)}, f16[200,256]{1,0:T(8,128)(2,1)S(1)}, u32[]{:S(2)}, u32[]{:S(2)}) %collective-permute-start.15) | collective-permute-done | bytes 102432 | tf_op jit(solution)/shard_map/ppermute | solution.py:34
  70.9 0.1 maximum_convert_fusion.1.narrow_got_ref
  71.0 0.5 after_x.1
  71.5 0.9 convert_element_type.54
  72.5 10.7 %all-to-all-start.2 = ((f16[32,64,128]{2,1,0:T(8,128)(2,1)}), f16[32,64,128]{2,1,0:T(8,128)(2,1)S(1)}, u32[]{:S(2)}, u32[]{:S(2)}) async-start(f16[32,64,128]{2,1,0:T(8,128)(2,1)} %convert_element_type.54), calls=%async_computation.2 | async-start | bytes 1048576 | tf_op jit(solution)/shard_map/all_to_all | solution.py:452
  83.2 1.5 %fusion = bf16[1,256,1536]{2,1,0:T(8,128)(2,1)} fusion(bf16[256,512]{1,0:T(8,128)(2,1)S(1)} %copy-done.9, bf16[1536,512]{1,0:T(8,128)(2,1)S(1)} %copy-done), kind=kOutput, calls=%fused_computation.1 | convolution fusion | flops 403046400 | bytes 2621440 | tf_op jit(solution)/shard_map/dot_general | solution.py:30
  84.7 15.7 %all-to-all-done.2 = f16[32,64,128]{2,1,0:T(8,128)(2,1)S(1)} async-done(((f16[32,64,128]{2,1,0:T(8,128)(2,1)}), f16[32,64,128]{2,1,0:T(8,128)(2,1)S(1)}, u32[]{:S(2)}, u32[]{:S(2)}) %all-to-all-start.2) | async-done | bytes 524320 | tf_op jit(solution)/shard_map/all_to_all | solution.py:452
  100.3 0.1 convert_element_type.55.got_ref
  100.4 0.7 last_sum.1
  (42 shorter events, 0.2 us)
Async XLA Ops:
  0.6 17.3 %copy-start = (bf16[1536,512]{1,0:T(8,128)(2,1)S(1)}, bf16[1536,512]{1,0:T(8,128)(2,1)}, u32[]{:S(2)}) copy-start(bf16[1536,512]{1,0:T(8,128)(2,1)} %param.10) | copy-start | bytes 4718596
  3.6 6.2 %copy-start.2 = (bf16[1,256,1536]{2,1,0:T(8,128)(2,1)S(1)}, bf16[1,256,1536]{2,1,0:T(8,128)(2,1)}, u32[]{:S(2)}) copy-start(bf16[1,256,1536]{2,1,0:T(8,128)(2,1)} %param.11) | copy-start | bytes 2359300
  3.6 11.1 %copy-start.1 = (bf16[1,256,1536]{2,1,0:T(8,128)(2,1)S(1)}, bf16[1,256,1536]{2,1,0:T(8,128)(2,1)}, u32[]{:S(2)}) copy-start(bf16[1,256,1536]{2,1,0:T(8,128)(2,1)} %param.6) | copy-start | bytes 2359300
  3.6 20.7 %all-to-all-start = ((bf16[8,256,256]{2,1,0:T(8,128)(2,1)}), bf16[8,256,256]{2,1,0:T(8,128)(2,1)}, u32[]{:S(2)}, u32[]{:S(2)}) async-start(bf16[8,256,256]{2,1,0:T(8,128)(2,1)} %project.1), calls=%async_computation | async-start | bytes 2097152 | tf_op jit(solution)/shard_map/all_to_all | solution.py:416
  9.7 7.0 %copy-start.11 = (bf16[1536,512]{1,0:T(8,128)(2,1)S(1)}, bf16[1536,512]{1,0:T(8,128)(2,1)}, u32[]{:S(2)}) copy-start(bf16[1536,512]{1,0:T(8,128)(2,1)} %param.7) | copy-start | bytes 4718596
  11.4 8.1 %collective-permute-start.2 = (bf16[384,256]{1,0:T(8,128)(2,1)S(1)}, bf16[384,256]{1,0:T(8,128)(2,1)S(1)}, u32[]{:S(2)}, u32[]{:S(2)}) collective-permute-start(bf16[384,256]{1,0:T(8,128)(2,1)S(1)} %get-tuple-element.42), channel_id=1, source_target_pairs={{0,192},{1,193},{2,194},{3,195},{4,196},{5,197},{6,198},{7,199},{8... | collective-permute-start | bytes 589832 | tf_op jit(solution)/shard_map/ppermute | solution.py:34
  14.1 19.8 %collective-permute-start.3 = (bf16[384,256]{1,0:T(8,128)(2,1)}, bf16[384,256]{1,0:T(8,128)(2,1)}, u32[]{:S(2)}, u32[]{:S(2)}) collective-permute-start(bf16[384,256]{1,0:T(8,128)(2,1)} %get-tuple-element.43), channel_id=1, source_target_pairs={{0,200},{1,201},{2,202},{3,203},{4,204},{5,205},{6,206},{7,207},{8... | collective-permute-start | bytes 589832 | tf_op jit(solution)/shard_map/ppermute | solution.py:34
  14.1 3.8 %copy-start.3 = (bf16[1,256,1536]{2,1,0:T(8,128)(2,1)S(1)}, bf16[1,256,1536]{2,1,0:T(8,128)(2,1)}, u32[]{:S(2)}) copy-start(bf16[1,256,1536]{2,1,0:T(8,128)(2,1)} %param.11) | copy-start | bytes 2359300
  14.1 19.8 %collective-permute-start.5 = (bf16[384,256]{1,0:T(8,128)(2,1)}, bf16[384,256]{1,0:T(8,128)(2,1)}, u32[]{:S(2)}, u32[]{:S(2)}) collective-permute-start(bf16[384,256]{1,0:T(8,128)(2,1)} %get-tuple-element.45), channel_id=1, source_target_pairs={{0,8},{1,9},{2,10},{3,11},{4,12},{5,13},{6,14},{7,15},{8,0},{9,1},... | collective-permute-start | bytes 589832 | tf_op jit(solution)/shard_map/ppermute | solution.py:34
  16.4 17.5 %collective-permute-start = (bf16[384,256]{1,0:T(8,128)(2,1)}, bf16[384,256]{1,0:T(8,128)(2,1)}, u32[]{:S(2)}, u32[]{:S(2)}) collective-permute-start(bf16[384,256]{1,0:T(8,128)(2,1)} %get-tuple-element.40), channel_id=1, source_target_pairs={{0,64},{1,65},{2,66},{3,67},{4,68},{5,69},{6,70},{7,71},{8,72},{9,... | collective-permute-start | bytes 589832 | tf_op jit(solution)/shard_map/ppermute | solution.py:34
  16.7 17.3 %collective-permute-start.4 = (bf16[768,256]{1,0:T(8,128)(2,1)}, bf16[768,256]{1,0:T(8,128)(2,1)S(1)}, u32[]{:S(2)}, u32[]{:S(2)}) collective-permute-start(bf16[768,256]{1,0:T(8,128)(2,1)} %get-tuple-element.44), channel_id=1, source_target_pairs={{0,8},{1,9},{2,10},{3,11},{4,12},{5,13},{6,14},{7,15},{8,0},{9,1},... | collective-permute-start | bytes 1179656 | tf_op jit(solution)/shard_map/ppermute | solution.py:34
  19.5 14.5 %collective-permute-start.1 = (bf16[384,256]{1,0:T(8,128)(2,1)}, bf16[384,256]{1,0:T(8,128)(2,1)S(1)}, u32[]{:S(2)}, u32[]{:S(2)}) collective-permute-start(bf16[384,256]{1,0:T(8,128)(2,1)} %get-tuple-element.41), channel_id=1, source_target_pairs={{0,72},{1,73},{2,74},{3,75},{4,76},{5,77},{6,78},{7,79},{8,64},{9,... | collective-permute-start | bytes 589832 | tf_op jit(solution)/shard_map/ppermute | solution.py:34
  34.0 1.2 %copy-start.5 = (bf16[384,256]{1,0:T(8,128)(2,1)}, bf16[384,256]{1,0:T(8,128)(2,1)S(1)}, u32[]{:S(2)}) copy-start(bf16[384,256]{1,0:T(8,128)(2,1)S(1)} %collective-permute-done.1.refs_3_) | copy-start | bytes 589828
  35.1 5.4 %copy-start.10 = (bf16[256,512]{1,0:T(8,128)(2,1)S(1)}, bf16[256,512]{1,0:T(8,128)(2,1)}, u32[]{:S(2)}) copy-start(bf16[256,512]{1,0:T(8,128)(2,1)} %get-tuple-element.51.refs_4_) | copy-start | bytes 786436
  35.1 6.9 %copy-start.8 = (bf16[256,512]{1,0:T(8,128)(2,1)S(1)}, bf16[256,512]{1,0:T(8,128)(2,1)}, u32[]{:S(2)}) copy-start(bf16[256,512]{1,0:T(8,128)(2,1)} %get-tuple-element.46.refs_12_) | copy-start | bytes 786436
  35.2 20.9 %all-to-all-start.1 = ((f16[8,264,256]{2,1,0:T(8,128)(2,1)}), f16[8,264,256]{2,1,0:T(8,128)(2,1)}, u32[]{:S(2)}, u32[]{:S(2)}) async-start(f16[8,264,256]{2,1,0:T(8,128)(2,1)} %convert_element_type.48), calls=%async_computation.1 | async-start | bytes 2162688 | tf_op jit(solution)/shard_map/all_to_all | solution.py:431
  40.6 6.4 %collective-permute-start.7 = (bf16[256,512]{1,0:T(8,128)(2,1)S(1)}, bf16[256,512]{1,0:T(8,128)(2,1)S(1)}, u32[]{:S(2)}, u32[]{:S(2)}) collective-permute-start(bf16[256,512]{1,0:T(8,128)(2,1)S(1)} %copy-done.10), channel_id=1, source_target_pairs={{0,64},{1,65},{2,66},{3,67},{4,68},{5,69},{6,70},{7,71},{8,72},{9,... | collective-permute-start | bytes 786440 | tf_op jit(solution)/shard_map/ppermute | solution.py:34
  42.1 7.6 %collective-permute-start.10 = (bf16[256,512]{1,0:T(8,128)(2,1)S(1)}, bf16[256,512]{1,0:T(8,128)(2,1)S(1)}, u32[]{:S(2)}, u32[]{:S(2)}) collective-permute-start(bf16[256,512]{1,0:T(8,128)(2,1)S(1)} %copy-done.8), channel_id=1, source_target_pairs={{0,192},{1,193},{2,194},{3,195},{4,196},{5,197},{6,198},{7,199},{8... | collective-permute-start | bytes 786440 | tf_op jit(solution)/shard_map/ppermute | solution.py:34
  44.2 5.5 %collective-permute-start.6 = (bf16[256,512]{1,0:T(8,128)(2,1)S(1)}, bf16[256,512]{1,0:T(8,128)(2,1)S(1)}, u32[]{:S(2)}, u32[]{:S(2)}) collective-permute-start(bf16[256,512]{1,0:T(8,128)(2,1)S(1)} %copy-done.10), channel_id=1, source_target_pairs={{0,8},{1,9},{2,10},{3,11},{4,12},{5,13},{6,14},{7,15},{8,0},{9,1},... | collective-permute-start | bytes 786440 | tf_op jit(solution)/shard_map/ppermute | solution.py:34
  44.2 5.5 %collective-permute-start.9 = (bf16[256,512]{1,0:T(8,128)(2,1)S(1)}, bf16[256,512]{1,0:T(8,128)(2,1)S(1)}, u32[]{:S(2)}, u32[]{:S(2)}) collective-permute-start(bf16[256,512]{1,0:T(8,128)(2,1)S(1)} %copy-done.8), channel_id=1, source_target_pairs={{0,8},{1,9},{2,10},{3,11},{4,12},{5,13},{6,14},{7,15},{8,0},{9,1},... | collective-permute-start | bytes 786440 | tf_op jit(solution)/shard_map/ppermute | solution.py:34
  46.9 2.7 %collective-permute-start.8 = (bf16[256,512]{1,0:T(8,128)(2,1)S(1)}, bf16[256,512]{1,0:T(8,128)(2,1)S(1)}, u32[]{:S(2)}, u32[]{:S(2)}) collective-permute-start(bf16[256,512]{1,0:T(8,128)(2,1)S(1)} %collective-permute-done.7.refs_6_), channel_id=1, source_target_pairs={{0,8},{1,9},{2,10},{3,11},{4,12},{5,13},{6,14},{7,15},{8,0},{9,1},... | collective-permute-start | bytes 786440 | tf_op jit(solution)/shard_map/ppermute | solution.py:34
  49.6 1.5 %collective-permute-start.11 = (bf16[256,512]{1,0:T(8,128)(2,1)S(1)}, bf16[256,512]{1,0:T(8,128)(2,1)S(1)}, u32[]{:S(2)}, u32[]{:S(2)}) collective-permute-start(bf16[256,512]{1,0:T(8,128)(2,1)S(1)} %collective-permute-done.10.refs_14_), channel_id=1, source_target_pairs={{0,8},{1,9},{2,10},{3,11},{4,12},{5,13},{6,14},{7,15},{8,0},{9,1},... | collective-permute-start | bytes 786440 | tf_op jit(solution)/shard_map/ppermute | solution.py:34
  51.2 0.9 copy-start.6
  57.6 2.4 %collective-permute-start.14 = (f32[256,256]{1,0:T(8,128)S(1)}, f32[256,256]{1,0:T(8,128)S(1)}, u32[]{:S(2)}, u32[]{:S(2)}) collective-permute-start(f32[256,256]{1,0:T(8,128)S(1)} %own_terms.1.own_ref), channel_id=1, source_target_pairs={{0,8},{1,9},{2,10},{3,11},{4,12},{5,13},{6,14},{7,15},{8,0},{9,1},... | collective-permute-start | bytes 786440 | tf_op jit(solution)/shard_map/ppermute | solution.py:34
  57.9 7.9 %collective-permute-start.13 = (f16[200,512]{1,0:T(8,128)(2,1)S(1)}, f16[200,512]{1,0:T(8,128)(2,1)S(1)}, u32[]{:S(2)}, u32[]{:S(2)}) collective-permute-start(f16[200,512]{1,0:T(8,128)(2,1)S(1)} %convert_element_type.46), channel_id=1, source_target_pairs={{0,64},{1,65},{2,66},{3,67},{4,68},{5,69},{6,70},{7,71},{8,72},{9,... | collective-permute-start | bytes 614408 | tf_op jit(solution)/shard_map/ppermute | solution.py:34
  57.9 9.5 %collective-permute-start.12 = (f16[200,512]{1,0:T(8,128)(2,1)S(1)}, f16[200,512]{1,0:T(8,128)(2,1)S(1)}, u32[]{:S(2)}, u32[]{:S(2)}) collective-permute-start(f16[200,512]{1,0:T(8,128)(2,1)S(1)} %convert_element_type.45), channel_id=1, source_target_pairs={{0,192},{1,193},{2,194},{3,195},{4,196},{5,197},{6,198},{7,199},{8... | collective-permute-start | bytes 614408 | tf_op jit(solution)/shard_map/ppermute | solution.py:34
  61.2 9.8 %copy-start.4 = (f32[192,1024]{1,0:T(8,128)S(1)}, f32[192,1024]{1,0:T(8,128)}, u32[]{:S(2)}) copy-start(f32[192,1024]{1,0:T(8,128)} %get-tuple-element.56.wide_ref) | copy-start | bytes 2359300
  61.2 9.8 %copy-start.7 = (f32[192,256]{1,0:T(8,128)S(1)}, f32[192,256]{1,0:T(8,128)}, u32[]{:S(2)}) copy-start(f32[192,256]{1,0:T(8,128)} %get-tuple-element.61.narrow_ref) | copy-start | bytes 589828
  61.3 8.3 %collective-permute-start.17 = (f16[200,256]{1,0:T(8,128)(2,1)S(1)}, f16[200,256]{1,0:T(8,128)(2,1)S(1)}, u32[]{:S(2)}, u32[]{:S(2)}) collective-permute-start(f16[200,256]{1,0:T(8,128)(2,1)S(1)} %convert_element_type.52), channel_id=1, source_target_pairs={{0,128},{1,129},{2,130},{3,131},{4,132},{5,133},{6,134},{7,135},{8... | collective-permute-start | bytes 307208 | tf_op jit(solution)/shard_map/ppermute | solution.py:34
  63.3 6.4 %collective-permute-start.16 = (f16[200,256]{1,0:T(8,128)(2,1)S(1)}, f16[200,256]{1,0:T(8,128)(2,1)S(1)}, u32[]{:S(2)}, u32[]{:S(2)}) collective-permute-start(f16[200,256]{1,0:T(8,128)(2,1)S(1)} %convert_element_type.51), channel_id=1, source_target_pairs={{0,64},{1,65},{2,66},{3,67},{4,68},{5,69},{6,70},{7,71},{8,72},{9,... | collective-permute-start | bytes 307208 | tf_op jit(solution)/shard_map/ppermute | solution.py:34
  63.5 7.4 %collective-permute-start.15 = (f16[200,256]{1,0:T(8,128)(2,1)S(1)}, f16[200,256]{1,0:T(8,128)(2,1)S(1)}, u32[]{:S(2)}, u32[]{:S(2)}) collective-permute-start(f16[200,256]{1,0:T(8,128)(2,1)S(1)} %convert_element_type.50), channel_id=1, source_target_pairs={{0,192},{1,193},{2,194},{3,195},{4,196},{5,197},{6,198},{7,199},{8... | collective-permute-start | bytes 307208 | tf_op jit(solution)/shard_map/ppermute | solution.py:34
  71.5 11.6 %copy-start.9 = (bf16[256,512]{1,0:T(8,128)(2,1)S(1)}, bf16[256,512]{1,0:T(8,128)(2,1)}, u32[]{:S(2)}) copy-start(bf16[256,512]{1,0:T(8,128)(2,1)} %get-tuple-element.46.refs_12_) | copy-start | bytes 786436
  72.5 27.9 %all-to-all-start.2 = ((f16[32,64,128]{2,1,0:T(8,128)(2,1)}), f16[32,64,128]{2,1,0:T(8,128)(2,1)S(1)}, u32[]{:S(2)}, u32[]{:S(2)}) async-start(f16[32,64,128]{2,1,0:T(8,128)(2,1)} %convert_element_type.54), calls=%async_computation.2 | async-start | bytes 1048576 | tf_op jit(solution)/shard_map/all_to_all | solution.py:452

commit v9 on v8

--- a/solution.py
+++ b/solution.py
@@ -443,7 +443,7 @@
     wide_got = [exchange(block, m << 6) for m, block in zip((3, 1), sent)]
     branch = dot(attended, w_out, ((1,), (1,))).astype(bf)
 
-    terms, _ = lax.optimization_barrier((terms, sent))
+    terms, _, branch = lax.optimization_barrier((terms, sent, branch))
     d_kv = own_terms(terms.astype(f32))
     narrow, *sent = narrow_products(h, h_core, d_kv, from_other_core(d_kv))
     narrow_got = [exchange(block.astype(half), m << 6) for m, block in zip((3, 1, 2), sent)]

time: 102 us -> 99.8 us (0.978)
  blocking collectives: 0 us -> 27.5 us
  waiting for transfers between devices: 31 us -> 13.5 us
  starting transfers between devices: 38.2 us -> 28 us
    all_to_all x0 -> x1, blocking collectives: none -> 27.5 us  [local(): lax.all_to_all(part.astype(half), AXES, 0, 0, axis_index_groups=YZ_GROUPS...]
    all_to_all x1 -> x0, waiting for transfers between devices: 15.7 us -> none  [local(): lax.all_to_all(part.astype(half), AXES, 0, 0, axis_index_groups=YZ_GROUPS...]
    all_to_all x1 -> x0, starting transfers between devices: 10.7 us -> none  [local(): lax.all_to_all(part.astype(half), AXES, 0, 0, axis_index_groups=YZ_GROUPS...]
    ppermute x18, waiting for transfers between devices: 12.1 us -> 10.4 us  [exchange(): return lax.ppermute(value, AXES, [(i, i ^ mask) for i in range(256)])]
  transfers between devices with their start and end apart: 21 -> 20, of which waited for: 11 -> 8; matrix products, arithmetic and copies ran while one was open for 4% -> 4% of each run, Pallas kernels for 18% -> 18%
where the time goes in v9:
time: 99.8 us; the launch traced here: 99.5 us
  starting transfers between devices  28 us (28%)
  blocking collectives  27.5 us (28%)
  Pallas kernels  22.4 us (22%)
  waiting for transfers between devices  13.5 us (14%)
  matrix products  4.06 us (4%)
  other arithmetic  3.07 us (3%)
    all_to_all x1, blocking collectives, local(): lax.all_to_all(part.astype(half), AXES, 0, 0, axis_index_groups=YZ_GROUPS...  27.5 us
    ppermute x18, starting transfers between devices, exchange(): return lax.ppermute(value, AXES, [(i, i ^ mask) for i in range(256)])  16.5 us
    ppermute x18, waiting for transfers between devices, exchange(): return lax.ppermute(value, AXES, [(i, i ^ mask) for i in range(256)])  10.4 us
    pallas_call x1, Pallas kernels, attention(): pl.pallas_call(attention_kernel, in_specs=[anywhere] * 3, out_specs=[anyw...  9.63 us
    all_to_all x1, starting transfers between devices, local(): lax.all_to_all(project(hidden, w_key, w_value), AXES, 0, 0, axis_index_gr...  6.11 us
    all_to_all x1, starting transfers between devices, local(): lax.all_to_all(terms.astype(half), AXES, 0, 0, axis_index_groups=SEQ_GROU...  5.42 us
    dot_general x3, matrix products, dot(): lax.dot_general(left, right, (dims, ((), ())), preferred_element_type=jnp...  4.06 us
    pallas_call x1, Pallas kernels, wide_products(): pl.pallas_call(wide_kernel, in_specs=[anywhere] * 16, out_specs=[anywhere...  3.95 us
  transfers between devices with their start and end apart: 20, of which 8 were waited for; matrix products, arithmetic and copies ran while one was open for 4% of the time, Pallas kernels for 18%

profile of v9, /device:TPU:32, one launch (start us, length us, event | category | flops | bytes accessed | tf_op | source)
XLA Modules:
  0.0 99.5 jit_solution(15941430657526008136)
XLA Ops:
  0.6 0.0 copy-start
  0.6 3.0 %project.1 = bf16[8,256,256]{2,1,0:T(8,128)(2,1)} custom-call(bf16[256,1536]{1,0:T(8,128)(2,1)} %bitcast.19, bf16[1536,128]{1,0:T(8,128)(2,1)} %w_key_ref.1, bf16[1536,128]{1,0:T(8,128)(2,1)} %w_value_ref.1), custom_call_target="tpu_custom_call" | custom-call | tf_op jit(solution)/shard_map/project/pallas_call | solution.py:60
  3.6 6.1 %all-to-all-start = ((bf16[8,256,256]{2,1,0:T(8,128)(2,1)}), bf16[8,256,256]{2,1,0:T(8,128)(2,1)}, u32[]{:S(2)}, u32[]{:S(2)}) async-start(bf16[8,256,256]{2,1,0:T(8,128)(2,1)} %project.1), calls=%async_computation | async-start | bytes 2097152 | tf_op jit(solution)/shard_map/all_to_all | solution.py:416
  9.8 0.1 pad_add_fusion.place_ref
  9.8 1.6 %turn.3 = (bf16[384,256]{1,0:T(8,128)(2,1)S(1)}, bf16[384,256]{1,0:T(8,128)(2,1)}, bf16[384,256]{1,0:T(8,128)(2,1)S(1)}, bf16[384,256]{1,0:T(8,128)(2,1)}) custom-call(s32[2]{0:T(128)S(1)} %pad_add_fusion.place_ref, bf16[256,1536]{1,0:T(8,128)(2,1)S(1)} %bitcast.21), custom_call_target="tpu_custom_call" | custom-call | tf_op jit(solution)/shard_map/turn/pallas_call | solution.py:82
  11.4 2.7 %collective-permute-start.2 = (bf16[384,256]{1,0:T(8,128)(2,1)S(1)}, bf16[384,256]{1,0:T(8,128)(2,1)S(1)}, u32[]{:S(2)}, u32[]{:S(2)}) collective-permute-start(bf16[384,256]{1,0:T(8,128)(2,1)S(1)} %get-tuple-element.43), channel_id=1, source_target_pairs={{0,192},{1,193},{2,194},{3,195},{4,196},{5,197},{6,198},{7,199},{8... | collective-permute-start | bytes 589832 | tf_op jit(solution)/shard_map/ppermute | solution.py:34
  14.1 0.6 collective-permute-start.5
  14.8 1.7 %turn.2 = (bf16[768,256]{1,0:T(8,128)(2,1)S(1)}, bf16[768,256]{1,0:T(8,128)(2,1)}, bf16[384,256]{1,0:T(8,128)(2,1)}, bf16[384,256]{1,0:T(8,128)(2,1)}) custom-call(s32[2]{0:T(128)S(1)} %pad_add_fusion.place_ref, bf16[256,1536]{1,0:T(8,128)(2,1)S(1)} %bitcast.20), custom_call_target="tpu_custom_call" | custom-call | tf_op jit(solution)/shard_map/turn/pallas_call | solution.py:82
  16.5 0.2 collective-permute-start
  16.7 1.3 %convolution_convert_fusion.2.q_hbm = bf16[256,512]{1,0:T(8,128)(2,1)} fusion(bf16[1536,512]{1,0:T(8,128)(2,1)S(1)} %copy-done.10, bf16[1,256,1536]{2,1,0:T(8,128)(2,1)S(1)} %copy-done.1), kind=kOutput, calls=%fused_computation.2 | convolution fusion | flops 402784256 | bytes 2621440 | tf_op jit(solution)/shard_map/dot_general | solution.py:30
  18.0 1.3 %convolution_convert_fusion.1.da_hbm = bf16[256,512]{1,0:T(8,128)(2,1)} fusion(bf16[1536,512]{1,0:T(8,128)(2,1)S(1)} %copy-done, bf16[1,256,1536]{2,1,0:T(8,128)(2,1)S(1)} %copy-done.3), kind=kOutput, calls=%fused_computation.1 | convolution fusion | flops 402784256 | bytes 2621440 | tf_op jit(solution)/shard_map/dot_general | solution.py:30
  19.3 0.2 collective-permute-done.2.refs_10_
  19.5 1.7 %collective-permute-start.1 = (bf16[384,256]{1,0:T(8,128)(2,1)}, bf16[384,256]{1,0:T(8,128)(2,1)S(1)}, u32[]{:S(2)}, u32[]{:S(2)}) collective-permute-start(bf16[384,256]{1,0:T(8,128)(2,1)} %get-tuple-element.42), channel_id=1, source_target_pairs={{0,72},{1,73},{2,74},{3,75},{4,76},{5,77},{6,78},{7,79},{8,64},{9,... | collective-permute-start | bytes 589832 | tf_op jit(solution)/shard_map/ppermute | solution.py:34
  21.2 3.2 %all-to-all-done = bf16[8,256,256]{2,1,0:T(8,128)(2,1)} async-done(((bf16[8,256,256]{2,1,0:T(8,128)(2,1)}), bf16[8,256,256]{2,1,0:T(8,128)(2,1)}, u32[]{:S(2)}, u32[]{:S(2)}) %all-to-all-start) | async-done | bytes 1048608 | tf_op jit(solution)/shard_map/all_to_all | solution.py:416
  24.3 9.6 %attention.1 = (bf16[256,512]{1,0:T(8,128)(2,1)}, bf16[256,512]{1,0:T(8,128)(2,1)}, f32[8,264,256]{2,1,0:T(8,128)S(1)}) custom-call(bf16[256,512]{1,0:T(8,128)(2,1)} %convolution_convert_fusion.2.q_hbm, bf16[256,512]{1,0:T(8,128)(2,1)} %convolution_convert_fusion.1.da_hbm, bf16[2048,256]{1,0:T(8,128)(2,1)} %bitcast.2.kv_hbm), custom_call_target="tpu_custom_call" | custom-call | flops 3221225472 | bytes 4194304 | tf_op jit(solution)/shard_map/attention/pallas_call | solution.py:215
  34.0 0.0 collective-permute-done.3.refs_11_
  34.0 0.0 collective-permute-done.5.refs_9_
  34.0 1.2 %convert_element_type.44 = f16[8,264,256]{2,1,0:T(8,128)(2,1)} convert(f32[8,264,256]{2,1,0:T(8,128)S(1)} %get-tuple-element.47) | non-fusion elementwise | flops 540672 | bytes 3244032 | tf_op jit(solution)/shard_map/convert_element_type | solution.py:431
  35.2 5.4 %all-to-all-start.1 = ((f16[8,264,256]{2,1,0:T(8,128)(2,1)}), f16[8,264,256]{2,1,0:T(8,128)(2,1)}, u32[]{:S(2)}, u32[]{:S(2)}) async-start(f16[8,264,256]{2,1,0:T(8,128)(2,1)} %convert_element_type.44), calls=%async_computation.1 | async-start | bytes 2162688 | tf_op jit(solution)/shard_map/all_to_all | solution.py:431
  40.6 1.6 %collective-permute-start.7 = (bf16[256,512]{1,0:T(8,128)(2,1)S(1)}, bf16[256,512]{1,0:T(8,128)(2,1)S(1)}, u32[]{:S(2)}, u32[]{:S(2)}) collective-permute-start(bf16[256,512]{1,0:T(8,128)(2,1)S(1)} %copy-done.9), channel_id=1, source_target_pairs={{0,64},{1,65},{2,66},{3,67},{4,68},{5,69},{6,70},{7,71},{8,72},{9,... | collective-permute-start | bytes 786440 | tf_op jit(solution)/shard_map/ppermute | solution.py:34
  42.2 2.1 %collective-permute-start.10 = (bf16[256,512]{1,0:T(8,128)(2,1)S(1)}, bf16[256,512]{1,0:T(8,128)(2,1)S(1)}, u32[]{:S(2)}, u32[]{:S(2)}) collective-permute-start(bf16[256,512]{1,0:T(8,128)(2,1)S(1)} %copy-done.8), channel_id=1, source_target_pairs={{0,192},{1,193},{2,194},{3,195},{4,196},{5,197},{6,198},{7,199},{8... | collective-permute-start | bytes 786440 | tf_op jit(solution)/shard_map/ppermute | solution.py:34
  44.3 0.5 collective-permute-start.9
  44.8 2.3 %collective-permute-done.7.refs_6_ = bf16[256,512]{1,0:T(8,128)(2,1)S(1)} collective-permute-done((bf16[256,512]{1,0:T(8,128)(2,1)S(1)}, bf16[256,512]{1,0:T(8,128)(2,1)S(1)}, u32[]{:S(2)}, u32[]{:S(2)}) %collective-permute-start.7) | collective-permute-done | bytes 262176 | tf_op jit(solution)/shard_map/ppermute | solution.py:34
  47.1 2.7 %collective-permute-done.10.refs_14_ = bf16[256,512]{1,0:T(8,128)(2,1)S(1)} collective-permute-done((bf16[256,512]{1,0:T(8,128)(2,1)S(1)}, bf16[256,512]{1,0:T(8,128)(2,1)S(1)}, u32[]{:S(2)}, u32[]{:S(2)}) %collective-permute-start.10) | collective-permute-done | bytes 262176 | tf_op jit(solution)/shard_map/ppermute | solution.py:34
  49.8 0.0 collective-permute-start.11
  49.8 1.5 %convolution_convert_fusion = bf16[256,1536]{1,0:T(8,128)(2,1)} fusion(bf16[256,512]{1,0:T(8,128)(2,1)S(1)} %copy-done.8, bf16[1536,512]{1,0:T(8,128)(2,1)S(1)} %copy-done), kind=kOutput, calls=%fused_computation | convolution fusion | flops 403046400 | bytes 2621440 | tf_op jit(solution)/shard_map/dot_general | solution.py:30
  51.3 0.0 collective-permute-done.11.refs_15_
  51.4 3.9 %wide.1 = (f32[192,1024]{1,0:T(8,128)}, f32[200,512]{1,0:T(8,128)S(1)}, f32[200,512]{1,0:T(8,128)S(1)}) custom-call(bf16[768,256]{1,0:T(8,128)(2,1)S(1)} %get-tuple-element.48.refs_0_.mine_ref, bf16[768,256]{1,0:T(8,128)(2,1)S(1)} %collective-permute-done.4.refs_1_.theirs_ref, bf16[384,256]{1,0:T(8,128)(2,1)} %collective-permute-done.refs_2_, ...), custom_call_target="tpu_custom_call" | custom-call | flops 1073741824 | bytes 5242880 | tf_op jit(solution)/shard_map/wide/pallas_call | solution.py:277
  55.4 1.4 %convert_element_type.49.terms_ref = f32[8,264,256]{2,1,0:T(8,128)S(1)} convert(f16[8,264,256]{2,1,0:T(8,128)(2,1)} %all-to-all-done.1) | non-fusion elementwise | flops 540672 | bytes 3244032 | tf_op jit(solution)/shard_map/convert_element_type | solution.py:447
  56.8 0.1 own_terms.1.own_ref
  57.0 0.6 collective-permute-start.14
  57.5 0.1 collective-permute-start.13
  57.7 2.1 %collective-permute-start.12 = (f16[200,512]{1,0:T(8,128)(2,1)S(1)}, f16[200,512]{1,0:T(8,128)(2,1)S(1)}, u32[]{:S(2)}, u32[]{:S(2)}) collective-permute-start(f16[200,512]{1,0:T(8,128)(2,1)S(1)} %convert_element_type.45), channel_id=1, source_target_pairs={{0,192},{1,193},{2,194},{3,195},{4,196},{5,197},{6,198},{7,199},{8... | collective-permute-start | bytes 614408 | tf_op jit(solution)/shard_map/ppermute | solution.py:34
  59.8 1.2 %narrow.1 = (f32[192,256]{1,0:T(8,128)}, f32[200,256]{1,0:T(8,128)S(1)}, f32[200,256]{1,0:T(8,128)S(1)}, f32[200,256]{1,0:T(8,128)S(1)}) custom-call(bf16[768,256]{1,0:T(8,128)(2,1)S(1)} %get-tuple-element.48.refs_0_.mine_ref, bf16[768,256]{1,0:T(8,128)(2,1)S(1)} %collective-permute-done.4.refs_1_.theirs_ref, f32[256,256]{1,0:T(8,128)S(1)} %own_terms.1.own_ref, ...), custom_call_target="tpu_custom_call" | custom-call | flops 1 | bytes 1 | tf_op jit(solution)/shard_map/narrow/pallas_call | solution.py:323
  61.0 1.9 %collective-permute-start.17 = (f16[200,256]{1,0:T(8,128)(2,1)S(1)}, f16[200,256]{1,0:T(8,128)(2,1)S(1)}, u32[]{:S(2)}, u32[]{:S(2)}) collective-permute-start(f16[200,256]{1,0:T(8,128)(2,1)S(1)} %convert_element_type.52), channel_id=1, source_target_pairs={{0,128},{1,129},{2,130},{3,131},{4,132},{5,133},{6,134},{7,135},{8... | collective-permute-start | bytes 307208 | tf_op jit(solution)/shard_map/ppermute | solution.py:34
  62.9 0.2 collective-permute-start.16
  63.1 2.1 %collective-permute-start.15 = (f16[200,256]{1,0:T(8,128)(2,1)S(1)}, f16[200,256]{1,0:T(8,128)(2,1)S(1)}, u32[]{:S(2)}, u32[]{:S(2)}) collective-permute-start(f16[200,256]{1,0:T(8,128)(2,1)S(1)} %convert_element_type.50), channel_id=1, source_target_pairs={{0,192},{1,193},{2,194},{3,195},{4,196},{5,197},{6,198},{7,199},{8... | collective-permute-start | bytes 307208 | tf_op jit(solution)/shard_map/ppermute | solution.py:34
  65.2 0.1 collective-permute-done.13
  65.3 1.9 %collective-permute-done.12 = f16[200,512]{1,0:T(8,128)(2,1)S(1)} collective-permute-done((f16[200,512]{1,0:T(8,128)(2,1)S(1)}, f16[200,512]{1,0:T(8,128)(2,1)S(1)}, u32[]{:S(2)}, u32[]{:S(2)}) %collective-permute-start.12) | collective-permute-done | bytes 204832 | tf_op jit(solution)/shard_map/ppermute | solution.py:34
  67.2 0.1 maximum_convert_fusion.wide_got_ref
  67.3 1.9 %collective-permute-done.17 = f16[200,256]{1,0:T(8,128)(2,1)S(1)} collective-permute-done((f16[200,256]{1,0:T(8,128)(2,1)S(1)}, f16[200,256]{1,0:T(8,128)(2,1)S(1)}, u32[]{:S(2)}, u32[]{:S(2)}) %collective-permute-start.17) | collective-permute-done | bytes 102432 | tf_op jit(solution)/shard_map/ppermute | solution.py:34
  69.2 1.2 %collective-permute-done.15 = f16[200,256]{1,0:T(8,128)(2,1)S(1)} collective-permute-done((f16[200,256]{1,0:T(8,128)(2,1)S(1)}, f16[200,256]{1,0:T(8,128)(2,1)S(1)}, u32[]{:S(2)}, u32[]{:S(2)}) %collective-permute-start.15) | collective-permute-done | bytes 102432 | tf_op jit(solution)/shard_map/ppermute | solution.py:34
  70.4 0.1 maximum_convert_fusion.1.narrow_got_ref
  70.5 0.5 after_x.1
  71.0 0.1 convert_element_type.54
  71.1 27.5 %all_to_all.15 = f16[32,64,128]{2,1,0:T(8,128)(2,1)S(1)} all-to-all(f16[32,64,128]{2,1,0:T(8,128)(2,1)S(1)} %convert_element_type.54), channel_id=1, replica_groups={{0,17,34,51,4,21,38,55,16,33,50,3,20,37,54,7,32,49,2,19,36,53,6,23,48,1..., dimensions={0} | all-to-all | bytes 1048576 | tf_op jit(solution)/shard_map/all_to_all | solution.py:452
  98.7 0.1 convert_element_type.55.got_ref
  98.8 0.7 last_sum.1
  (39 shorter events, 0.2 us)
Async XLA Ops:
  0.6 17.3 %copy-start = (bf16[1536,512]{1,0:T(8,128)(2,1)S(1)}, bf16[1536,512]{1,0:T(8,128)(2,1)}, u32[]{:S(2)}) copy-start(bf16[1536,512]{1,0:T(8,128)(2,1)} %param.10) | copy-start | bytes 4718596
  3.6 6.2 %copy-start.2 = (bf16[1,256,1536]{2,1,0:T(8,128)(2,1)S(1)}, bf16[1,256,1536]{2,1,0:T(8,128)(2,1)}, u32[]{:S(2)}) copy-start(bf16[1,256,1536]{2,1,0:T(8,128)(2,1)} %param.11) | copy-start | bytes 2359300
  3.6 11.1 %copy-start.1 = (bf16[1,256,1536]{2,1,0:T(8,128)(2,1)S(1)}, bf16[1,256,1536]{2,1,0:T(8,128)(2,1)}, u32[]{:S(2)}) copy-start(bf16[1,256,1536]{2,1,0:T(8,128)(2,1)} %param.6) | copy-start | bytes 2359300
  3.6 20.7 %all-to-all-start = ((bf16[8,256,256]{2,1,0:T(8,128)(2,1)}), bf16[8,256,256]{2,1,0:T(8,128)(2,1)}, u32[]{:S(2)}, u32[]{:S(2)}) async-start(bf16[8,256,256]{2,1,0:T(8,128)(2,1)} %project.1), calls=%async_computation | async-start | bytes 2097152 | tf_op jit(solution)/shard_map/all_to_all | solution.py:416
  9.8 6.9 %copy-start.10 = (bf16[1536,512]{1,0:T(8,128)(2,1)S(1)}, bf16[1536,512]{1,0:T(8,128)(2,1)}, u32[]{:S(2)}) copy-start(bf16[1536,512]{1,0:T(8,128)(2,1)} %param.7) | copy-start | bytes 4718596
  11.4 8.1 %collective-permute-start.2 = (bf16[384,256]{1,0:T(8,128)(2,1)S(1)}, bf16[384,256]{1,0:T(8,128)(2,1)S(1)}, u32[]{:S(2)}, u32[]{:S(2)}) collective-permute-start(bf16[384,256]{1,0:T(8,128)(2,1)S(1)} %get-tuple-element.43), channel_id=1, source_target_pairs={{0,192},{1,193},{2,194},{3,195},{4,196},{5,197},{6,198},{7,199},{8... | collective-permute-start | bytes 589832 | tf_op jit(solution)/shard_map/ppermute | solution.py:34
  14.1 19.9 %collective-permute-start.3 = (bf16[384,256]{1,0:T(8,128)(2,1)}, bf16[384,256]{1,0:T(8,128)(2,1)}, u32[]{:S(2)}, u32[]{:S(2)}) collective-permute-start(bf16[384,256]{1,0:T(8,128)(2,1)} %get-tuple-element.44), channel_id=1, source_target_pairs={{0,200},{1,201},{2,202},{3,203},{4,204},{5,205},{6,206},{7,207},{8... | collective-permute-start | bytes 589832 | tf_op jit(solution)/shard_map/ppermute | solution.py:34
  14.1 3.9 %copy-start.3 = (bf16[1,256,1536]{2,1,0:T(8,128)(2,1)S(1)}, bf16[1,256,1536]{2,1,0:T(8,128)(2,1)}, u32[]{:S(2)}) copy-start(bf16[1,256,1536]{2,1,0:T(8,128)(2,1)} %param.11) | copy-start | bytes 2359300
  14.1 19.9 %collective-permute-start.5 = (bf16[384,256]{1,0:T(8,128)(2,1)}, bf16[384,256]{1,0:T(8,128)(2,1)}, u32[]{:S(2)}, u32[]{:S(2)}) collective-permute-start(bf16[384,256]{1,0:T(8,128)(2,1)} %get-tuple-element.46), channel_id=1, source_target_pairs={{0,8},{1,9},{2,10},{3,11},{4,12},{5,13},{6,14},{7,15},{8,0},{9,1},... | collective-permute-start | bytes 589832 | tf_op jit(solution)/shard_map/ppermute | solution.py:34
  16.5 17.6 %collective-permute-start = (bf16[384,256]{1,0:T(8,128)(2,1)}, bf16[384,256]{1,0:T(8,128)(2,1)}, u32[]{:S(2)}, u32[]{:S(2)}) collective-permute-start(bf16[384,256]{1,0:T(8,128)(2,1)} %get-tuple-element.41), channel_id=1, source_target_pairs={{0,64},{1,65},{2,66},{3,67},{4,68},{5,69},{6,70},{7,71},{8,72},{9,... | collective-permute-start | bytes 589832 | tf_op jit(solution)/shard_map/ppermute | solution.py:34
  16.7 17.4 %collective-permute-start.4 = (bf16[768,256]{1,0:T(8,128)(2,1)}, bf16[768,256]{1,0:T(8,128)(2,1)S(1)}, u32[]{:S(2)}, u32[]{:S(2)}) collective-permute-start(bf16[768,256]{1,0:T(8,128)(2,1)} %get-tuple-element.45), channel_id=1, source_target_pairs={{0,8},{1,9},{2,10},{3,11},{4,12},{5,13},{6,14},{7,15},{8,0},{9,1},... | collective-permute-start | bytes 1179656 | tf_op jit(solution)/shard_map/ppermute | solution.py:34
  19.5 14.5 %collective-permute-start.1 = (bf16[384,256]{1,0:T(8,128)(2,1)}, bf16[384,256]{1,0:T(8,128)(2,1)S(1)}, u32[]{:S(2)}, u32[]{:S(2)}) collective-permute-start(bf16[384,256]{1,0:T(8,128)(2,1)} %get-tuple-element.42), channel_id=1, source_target_pairs={{0,72},{1,73},{2,74},{3,75},{4,76},{5,77},{6,78},{7,79},{8,64},{9,... | collective-permute-start | bytes 589832 | tf_op jit(solution)/shard_map/ppermute | solution.py:34
  34.0 1.2 %copy-start.5 = (bf16[384,256]{1,0:T(8,128)(2,1)}, bf16[384,256]{1,0:T(8,128)(2,1)S(1)}, u32[]{:S(2)}) copy-start(bf16[384,256]{1,0:T(8,128)(2,1)S(1)} %collective-permute-done.1.refs_3_) | copy-start | bytes 589828
  35.2 5.4 %copy-start.9 = (bf16[256,512]{1,0:T(8,128)(2,1)S(1)}, bf16[256,512]{1,0:T(8,128)(2,1)}, u32[]{:S(2)}) copy-start(bf16[256,512]{1,0:T(8,128)(2,1)} %get-tuple-element.52.refs_4_) | copy-start | bytes 786436
  35.2 7.0 %copy-start.8 = (bf16[256,512]{1,0:T(8,128)(2,1)S(1)}, bf16[256,512]{1,0:T(8,128)(2,1)}, u32[]{:S(2)}) copy-start(bf16[256,512]{1,0:T(8,128)(2,1)} %get-tuple-element.57.refs_12_) | copy-start | bytes 786436
  35.2 20.2 %all-to-all-start.1 = ((f16[8,264,256]{2,1,0:T(8,128)(2,1)}), f16[8,264,256]{2,1,0:T(8,128)(2,1)}, u32[]{:S(2)}, u32[]{:S(2)}) async-start(f16[8,264,256]{2,1,0:T(8,128)(2,1)} %convert_element_type.44), calls=%async_computation.1 | async-start | bytes 2162688 | tf_op jit(solution)/shard_map/all_to_all | solution.py:431
  40.6 10.7 %copy-start.6 = (bf16[384,256]{1,0:T(8,128)(2,1)S(1)}, bf16[384,256]{1,0:T(8,128)(2,1)}, u32[]{:S(2)}) copy-start(bf16[384,256]{1,0:T(8,128)(2,1)} %copy-done.5) | copy-start | bytes 589828
  40.6 6.5 %collective-permute-start.7 = (bf16[256,512]{1,0:T(8,128)(2,1)S(1)}, bf16[256,512]{1,0:T(8,128)(2,1)S(1)}, u32[]{:S(2)}, u32[]{:S(2)}) collective-permute-start(bf16[256,512]{1,0:T(8,128)(2,1)S(1)} %copy-done.9), channel_id=1, source_target_pairs={{0,64},{1,65},{2,66},{3,67},{4,68},{5,69},{6,70},{7,71},{8,72},{9,... | collective-permute-start | bytes 786440 | tf_op jit(solution)/shard_map/ppermute | solution.py:34
  42.2 7.6 %collective-permute-start.10 = (bf16[256,512]{1,0:T(8,128)(2,1)S(1)}, bf16[256,512]{1,0:T(8,128)(2,1)S(1)}, u32[]{:S(2)}, u32[]{:S(2)}) collective-permute-start(bf16[256,512]{1,0:T(8,128)(2,1)S(1)} %copy-done.8), channel_id=1, source_target_pairs={{0,192},{1,193},{2,194},{3,195},{4,196},{5,197},{6,198},{7,199},{8... | collective-permute-start | bytes 786440 | tf_op jit(solution)/shard_map/ppermute | solution.py:34
  44.3 7.0 %collective-permute-start.6 = (bf16[256,512]{1,0:T(8,128)(2,1)S(1)}, bf16[256,512]{1,0:T(8,128)(2,1)S(1)}, u32[]{:S(2)}, u32[]{:S(2)}) collective-permute-start(bf16[256,512]{1,0:T(8,128)(2,1)S(1)} %copy-done.9), channel_id=1, source_target_pairs={{0,8},{1,9},{2,10},{3,11},{4,12},{5,13},{6,14},{7,15},{8,0},{9,1},... | collective-permute-start | bytes 786440 | tf_op jit(solution)/shard_map/ppermute | solution.py:34
  44.3 7.0 %collective-permute-start.9 = (bf16[256,512]{1,0:T(8,128)(2,1)S(1)}, bf16[256,512]{1,0:T(8,128)(2,1)S(1)}, u32[]{:S(2)}, u32[]{:S(2)}) collective-permute-start(bf16[256,512]{1,0:T(8,128)(2,1)S(1)} %copy-done.8), channel_id=1, source_target_pairs={{0,8},{1,9},{2,10},{3,11},{4,12},{5,13},{6,14},{7,15},{8,0},{9,1},... | collective-permute-start | bytes 786440 | tf_op jit(solution)/shard_map/ppermute | solution.py:34
  47.1 4.2 %collective-permute-start.8 = (bf16[256,512]{1,0:T(8,128)(2,1)S(1)}, bf16[256,512]{1,0:T(8,128)(2,1)S(1)}, u32[]{:S(2)}, u32[]{:S(2)}) collective-permute-start(bf16[256,512]{1,0:T(8,128)(2,1)S(1)} %collective-permute-done.7.refs_6_), channel_id=1, source_target_pairs={{0,8},{1,9},{2,10},{3,11},{4,12},{5,13},{6,14},{7,15},{8,0},{9,1},... | collective-permute-start | bytes 786440 | tf_op jit(solution)/shard_map/ppermute | solution.py:34
  49.8 1.5 %collective-permute-start.11 = (bf16[256,512]{1,0:T(8,128)(2,1)S(1)}, bf16[256,512]{1,0:T(8,128)(2,1)S(1)}, u32[]{:S(2)}, u32[]{:S(2)}) collective-permute-start(bf16[256,512]{1,0:T(8,128)(2,1)S(1)} %collective-permute-done.10.refs_14_), channel_id=1, source_target_pairs={{0,8},{1,9},{2,10},{3,11},{4,12},{5,13},{6,14},{7,15},{8,0},{9,1},... | collective-permute-start | bytes 786440 | tf_op jit(solution)/shard_map/ppermute | solution.py:34
  57.0 2.8 %collective-permute-start.14 = (f32[256,256]{1,0:T(8,128)S(1)}, f32[256,256]{1,0:T(8,128)S(1)}, u32[]{:S(2)}, u32[]{:S(2)}) collective-permute-start(f32[256,256]{1,0:T(8,128)S(1)} %own_terms.1.own_ref), channel_id=1, source_target_pairs={{0,8},{1,9},{2,10},{3,11},{4,12},{5,13},{6,14},{7,15},{8,0},{9,1},... | collective-permute-start | bytes 786440 | tf_op jit(solution)/shard_map/ppermute | solution.py:34
  57.5 7.7 %collective-permute-start.13 = (f16[200,512]{1,0:T(8,128)(2,1)S(1)}, f16[200,512]{1,0:T(8,128)(2,1)S(1)}, u32[]{:S(2)}, u32[]{:S(2)}) collective-permute-start(f16[200,512]{1,0:T(8,128)(2,1)S(1)} %convert_element_type.46), channel_id=1, source_target_pairs={{0,64},{1,65},{2,66},{3,67},{4,68},{5,69},{6,70},{7,71},{8,72},{9,... | collective-permute-start | bytes 614408 | tf_op jit(solution)/shard_map/ppermute | solution.py:34
  57.7 9.5 %collective-permute-start.12 = (f16[200,512]{1,0:T(8,128)(2,1)S(1)}, f16[200,512]{1,0:T(8,128)(2,1)S(1)}, u32[]{:S(2)}, u32[]{:S(2)}) collective-permute-start(f16[200,512]{1,0:T(8,128)(2,1)S(1)} %convert_element_type.45), channel_id=1, source_target_pairs={{0,192},{1,193},{2,194},{3,195},{4,196},{5,197},{6,198},{7,199},{8... | collective-permute-start | bytes 614408 | tf_op jit(solution)/shard_map/ppermute | solution.py:34
  61.0 9.5 %copy-start.4 = (f32[192,1024]{1,0:T(8,128)S(1)}, f32[192,1024]{1,0:T(8,128)}, u32[]{:S(2)}) copy-start(f32[192,1024]{1,0:T(8,128)} %get-tuple-element.61.wide_ref) | copy-start | bytes 2359300
  61.0 9.5 %copy-start.7 = (f32[192,256]{1,0:T(8,128)S(1)}, f32[192,256]{1,0:T(8,128)}, u32[]{:S(2)}) copy-start(f32[192,256]{1,0:T(8,128)} %get-tuple-element.63.narrow_ref) | copy-start | bytes 589828
  61.0 8.2 %collective-permute-start.17 = (f16[200,256]{1,0:T(8,128)(2,1)S(1)}, f16[200,256]{1,0:T(8,128)(2,1)S(1)}, u32[]{:S(2)}, u32[]{:S(2)}) collective-permute-start(f16[200,256]{1,0:T(8,128)(2,1)S(1)} %convert_element_type.52), channel_id=1, source_target_pairs={{0,128},{1,129},{2,130},{3,131},{4,132},{5,133},{6,134},{7,135},{8... | collective-permute-start | bytes 307208 | tf_op jit(solution)/shard_map/ppermute | solution.py:34
  62.9 6.3 %collective-permute-start.16 = (f16[200,256]{1,0:T(8,128)(2,1)S(1)}, f16[200,256]{1,0:T(8,128)(2,1)S(1)}, u32[]{:S(2)}, u32[]{:S(2)}) collective-permute-start(f16[200,256]{1,0:T(8,128)(2,1)S(1)} %convert_element_type.51), channel_id=1, source_target_pairs={{0,64},{1,65},{2,66},{3,67},{4,68},{5,69},{6,70},{7,71},{8,72},{9,... | collective-permute-start | bytes 307208 | tf_op jit(solution)/shard_map/ppermute | solution.py:34
  63.1 7.3 %collective-permute-start.15 = (f16[200,256]{1,0:T(8,128)(2,1)S(1)}, f16[200,256]{1,0:T(8,128)(2,1)S(1)}, u32[]{:S(2)}, u32[]{:S(2)}) collective-permute-start(f16[200,256]{1,0:T(8,128)(2,1)S(1)} %convert_element_type.50), channel_id=1, source_target_pairs={{0,192},{1,193},{2,194},{3,195},{4,196},{5,197},{6,198},{7,199},{8... | collective-permute-start | bytes 307208 | tf_op jit(solution)/shard_map/ppermute | solution.py:34

commit v10 on v9

--- a/solution.py
+++ b/solution.py
@@ -150,7 +150,13 @@
             def run():
                 term = dot(sides[i], from_ref[h % 2, :, block_rows(b)], ((1,), (0,)))
                 rows = slice(i * HD, (i + 1) * HD)
-                dkv_ref[b, rows, :] = term if h == 0 else dkv_ref[b, rows, :] + term
+                total = term if h == 0 else dkv_ref[b, rows, :] + term
+                if h == HEADS - 1:
+                    total = total * (SCALE, 1.0)[i]
+                    power = exponent(total)
+                    total = total * jnp.exp2(-power)
+                    dkv_ref[b, pl.ds(2 * HD + 4 * i, 4), :] = jnp.broadcast_to(power, (4, tokens))
+                dkv_ref[b, rows, :] = total
 
             return run
 
@@ -162,10 +168,17 @@
             return run
 
         work = [terms(b, i, ref) for b in range(blocks) for i, ref in enumerate((d_scores_ref, probs_ref))]
-        work.insert(4, rows_of(probs_ref, v_ref, attended_ref, None))
-        work.insert(13, rows_of(d_scores_ref, k_ref, d_query_ref, SCALE))
+        rows = [rows_of(probs_ref, v_ref, attended_ref, None), rows_of(d_scores_ref, k_ref, d_query_ref, SCALE)]
+        if h == HEADS - 1:
+            return rows + [copy.start for copy in leaving] + work
+        work.insert(4, rows[0])
+        work.insert(13, rows[1])
         return work
 
+    leaving = [
+        pltpu.make_async_copy(ref, target, out_sems.at[i])
+        for i, (ref, target) in enumerate(((d_query_ref, d_query_hbm), (attended_ref, attended_hbm)))
+    ]
     for run in ahead(0):
         run()
     for h in range(HEADS):
@@ -184,22 +197,6 @@
     for run in behind(HEADS - 1):
         run()
 
-    leaving = [
-        pltpu.make_async_copy(ref, target, out_sems.at[i])
-        for i, (ref, target) in enumerate(((d_query_ref, d_query_hbm), (attended_ref, attended_hbm)))
-    ]
-    for copy in leaving:
-        copy.start()
-    for i, scale in enumerate((SCALE, 1.0)):
-        rows = pl.ds(i * HD, HD)
-        top = jnp.abs(dkv_ref[0, rows, :])
-        for b in range(1, blocks):
-            top = jnp.maximum(top, jnp.abs(dkv_ref[b, rows, :]))
-        power = exponent(top * scale)
-        factor = jnp.exp2(-power) * scale
-        for b in range(blocks):
-            dkv_ref[b, rows, :] = dkv_ref[b, rows, :] * factor
-            dkv_ref[b, pl.ds(2 * HD + 4 * i, 4), :] = jnp.broadcast_to(power, (4, tokens))
     for copy in leaving:
         copy.wait()
 

time: 99.8 us -> 99.7 us (level)
  no operation moved by 1% of the time
where the time goes in v10:
time: 99.7 us; the launch traced here: 99.3 us
  starting transfers between devices  28 us (28%)
  blocking collectives  27.5 us (28%)
  Pallas kernels  22.2 us (22%)
  waiting for transfers between devices  13.5 us (14%)
  matrix products  4.05 us (4%)
  other arithmetic  3.07 us (3%)
    all_to_all x1, blocking collectives, local(): lax.all_to_all(part.astype(half), AXES, 0, 0, axis_index_groups=YZ_GROUPS...  27.5 us
    ppermute x18, starting transfers between devices, exchange(): return lax.ppermute(value, AXES, [(i, i ^ mask) for i in range(256)])  16.5 us
    ppermute x18, waiting for transfers between devices, exchange(): return lax.ppermute(value, AXES, [(i, i ^ mask) for i in range(256)])  10.4 us
    pallas_call x1, Pallas kernels, attention(): pl.pallas_call(attention_kernel, in_specs=[anywhere] * 3, out_specs=[anyw...  9.49 us
    all_to_all x1, starting transfers between devices, local(): lax.all_to_all(project(hidden, w_key, w_value), AXES, 0, 0, axis_index_gr...  6.11 us
    all_to_all x1, starting transfers between devices, local(): lax.all_to_all(terms.astype(half), AXES, 0, 0, axis_index_groups=SEQ_GROU...  5.41 us
    dot_general x3, matrix products, dot(): lax.dot_general(left, right, (dims, ((), ())), preferred_element_type=jnp...  4.05 us
    pallas_call x1, Pallas kernels, wide_products(): pl.pallas_call(wide_kernel, in_specs=[anywhere] * 16, out_specs=[anywhere...  3.94 us
  transfers between devices with their start and end apart: 20, of which 8 were waited for; matrix products, arithmetic and copies ran while one was open for 4% of the time, Pallas kernels for 18%

profile of v10, /device:TPU:32, one launch (start us, length us, event | category | flops | bytes accessed | tf_op | source)
XLA Modules:
  0.0 99.3 jit_solution(14098218585406482506)
XLA Ops:
  0.6 0.0 copy-start
  0.6 3.0 %project.1 = bf16[8,256,256]{2,1,0:T(8,128)(2,1)} custom-call(bf16[256,1536]{1,0:T(8,128)(2,1)} %bitcast.19, bf16[1536,128]{1,0:T(8,128)(2,1)} %w_key_ref.1, bf16[1536,128]{1,0:T(8,128)(2,1)} %w_value_ref.1), custom_call_target="tpu_custom_call" | custom-call | tf_op jit(solution)/shard_map/project/pallas_call | solution.py:60
  3.6 6.1 %all-to-all-start = ((bf16[8,256,256]{2,1,0:T(8,128)(2,1)}), bf16[8,256,256]{2,1,0:T(8,128)(2,1)}, u32[]{:S(2)}, u32[]{:S(2)}) async-start(bf16[8,256,256]{2,1,0:T(8,128)(2,1)} %project.1), calls=%async_computation | async-start | bytes 2097152 | tf_op jit(solution)/shard_map/all_to_all | solution.py:413
  9.8 0.1 pad_add_fusion.place_ref
  9.8 1.6 %turn.3 = (bf16[384,256]{1,0:T(8,128)(2,1)S(1)}, bf16[384,256]{1,0:T(8,128)(2,1)}, bf16[384,256]{1,0:T(8,128)(2,1)S(1)}, bf16[384,256]{1,0:T(8,128)(2,1)}) custom-call(s32[2]{0:T(128)S(1)} %pad_add_fusion.place_ref, bf16[256,1536]{1,0:T(8,128)(2,1)S(1)} %bitcast.21), custom_call_target="tpu_custom_call" | custom-call | tf_op jit(solution)/shard_map/turn/pallas_call | solution.py:82
  11.4 2.7 %collective-permute-start.2 = (bf16[384,256]{1,0:T(8,128)(2,1)S(1)}, bf16[384,256]{1,0:T(8,128)(2,1)S(1)}, u32[]{:S(2)}, u32[]{:S(2)}) collective-permute-start(bf16[384,256]{1,0:T(8,128)(2,1)S(1)} %get-tuple-element.43), channel_id=1, source_target_pairs={{0,192},{1,193},{2,194},{3,195},{4,196},{5,197},{6,198},{7,199},{8... | collective-permute-start | bytes 589832 | tf_op jit(solution)/shard_map/ppermute | solution.py:34
  14.1 0.0 collective-permute-start.3
  14.1 0.6 collective-permute-start.5
  14.8 1.7 %turn.2 = (bf16[768,256]{1,0:T(8,128)(2,1)S(1)}, bf16[768,256]{1,0:T(8,128)(2,1)}, bf16[384,256]{1,0:T(8,128)(2,1)}, bf16[384,256]{1,0:T(8,128)(2,1)}) custom-call(s32[2]{0:T(128)S(1)} %pad_add_fusion.place_ref, bf16[256,1536]{1,0:T(8,128)(2,1)S(1)} %bitcast.20), custom_call_target="tpu_custom_call" | custom-call | tf_op jit(solution)/shard_map/turn/pallas_call | solution.py:82
  16.5 0.2 collective-permute-start
  16.7 0.0 collective-permute-start.4
  16.7 1.3 %convolution_convert_fusion.2.q_hbm = bf16[256,512]{1,0:T(8,128)(2,1)} fusion(bf16[1536,512]{1,0:T(8,128)(2,1)S(1)} %copy-done.10, bf16[1,256,1536]{2,1,0:T(8,128)(2,1)S(1)} %copy-done.1), kind=kOutput, calls=%fused_computation.2 | convolution fusion | flops 402784256 | bytes 2621440 | tf_op jit(solution)/shard_map/dot_general | solution.py:30
  18.0 1.3 %convolution_convert_fusion.1.da_hbm = bf16[256,512]{1,0:T(8,128)(2,1)} fusion(bf16[1536,512]{1,0:T(8,128)(2,1)S(1)} %copy-done, bf16[1,256,1536]{2,1,0:T(8,128)(2,1)S(1)} %copy-done.3), kind=kOutput, calls=%fused_computation.1 | convolution fusion | flops 402784256 | bytes 2621440 | tf_op jit(solution)/shard_map/dot_general | solution.py:30
  19.3 0.2 collective-permute-done.2.refs_10_
  19.5 1.7 %collective-permute-start.1 = (bf16[384,256]{1,0:T(8,128)(2,1)}, bf16[384,256]{1,0:T(8,128)(2,1)S(1)}, u32[]{:S(2)}, u32[]{:S(2)}) collective-permute-start(bf16[384,256]{1,0:T(8,128)(2,1)} %get-tuple-element.42), channel_id=1, source_target_pairs={{0,72},{1,73},{2,74},{3,75},{4,76},{5,77},{6,78},{7,79},{8,64},{9,... | collective-permute-start | bytes 589832 | tf_op jit(solution)/shard_map/ppermute | solution.py:34
  21.2 3.2 %all-to-all-done = bf16[8,256,256]{2,1,0:T(8,128)(2,1)} async-done(((bf16[8,256,256]{2,1,0:T(8,128)(2,1)}), bf16[8,256,256]{2,1,0:T(8,128)(2,1)}, u32[]{:S(2)}, u32[]{:S(2)}) %all-to-all-start) | async-done | bytes 1048608 | tf_op jit(solution)/shard_map/all_to_all | solution.py:413
  24.3 9.5 %attention.1 = (bf16[256,512]{1,0:T(8,128)(2,1)}, bf16[256,512]{1,0:T(8,128)(2,1)}, f32[8,264,256]{2,1,0:T(8,128)S(1)}) custom-call(bf16[256,512]{1,0:T(8,128)(2,1)} %convolution_convert_fusion.2.q_hbm, bf16[256,512]{1,0:T(8,128)(2,1)} %convolution_convert_fusion.1.da_hbm, bf16[2048,256]{1,0:T(8,128)(2,1)} %bitcast.2.kv_hbm), custom_call_target="tpu_custom_call" | custom-call | flops 3221225472 | bytes 4194304 | tf_op jit(solution)/shard_map/attention/pallas_call | solution.py:212
  33.9 1.2 %convert_element_type.44 = f16[8,264,256]{2,1,0:T(8,128)(2,1)} convert(f32[8,264,256]{2,1,0:T(8,128)S(1)} %get-tuple-element.47) | non-fusion elementwise | flops 540672 | bytes 3244032 | tf_op jit(solution)/shard_map/convert_element_type | solution.py:428
  35.1 5.4 %all-to-all-start.1 = ((f16[8,264,256]{2,1,0:T(8,128)(2,1)}), f16[8,264,256]{2,1,0:T(8,128)(2,1)}, u32[]{:S(2)}, u32[]{:S(2)}) async-start(f16[8,264,256]{2,1,0:T(8,128)(2,1)} %convert_element_type.44), calls=%async_computation.1 | async-start | bytes 2162688 | tf_op jit(solution)/shard_map/all_to_all | solution.py:428
  40.5 1.6 %collective-permute-start.7 = (bf16[256,512]{1,0:T(8,128)(2,1)S(1)}, bf16[256,512]{1,0:T(8,128)(2,1)S(1)}, u32[]{:S(2)}, u32[]{:S(2)}) collective-permute-start(bf16[256,512]{1,0:T(8,128)(2,1)S(1)} %copy-done.9), channel_id=1, source_target_pairs={{0,64},{1,65},{2,66},{3,67},{4,68},{5,69},{6,70},{7,71},{8,72},{9,... | collective-permute-start | bytes 786440 | tf_op jit(solution)/shard_map/ppermute | solution.py:34
  42.1 2.1 %collective-permute-start.10 = (bf16[256,512]{1,0:T(8,128)(2,1)S(1)}, bf16[256,512]{1,0:T(8,128)(2,1)S(1)}, u32[]{:S(2)}, u32[]{:S(2)}) collective-permute-start(bf16[256,512]{1,0:T(8,128)(2,1)S(1)} %copy-done.8), channel_id=1, source_target_pairs={{0,192},{1,193},{2,194},{3,195},{4,196},{5,197},{6,198},{7,199},{8... | collective-permute-start | bytes 786440 | tf_op jit(solution)/shard_map/ppermute | solution.py:34
  44.2 0.5 collective-permute-start.9
  44.7 2.3 %collective-permute-done.7.refs_6_ = bf16[256,512]{1,0:T(8,128)(2,1)S(1)} collective-permute-done((bf16[256,512]{1,0:T(8,128)(2,1)S(1)}, bf16[256,512]{1,0:T(8,128)(2,1)S(1)}, u32[]{:S(2)}, u32[]{:S(2)}) %collective-permute-start.7) | collective-permute-done | bytes 262176 | tf_op jit(solution)/shard_map/ppermute | solution.py:34
  47.0 2.7 %collective-permute-done.10.refs_14_ = bf16[256,512]{1,0:T(8,128)(2,1)S(1)} collective-permute-done((bf16[256,512]{1,0:T(8,128)(2,1)S(1)}, bf16[256,512]{1,0:T(8,128)(2,1)S(1)}, u32[]{:S(2)}, u32[]{:S(2)}) %collective-permute-start.10) | collective-permute-done | bytes 262176 | tf_op jit(solution)/shard_map/ppermute | solution.py:34
  49.7 0.0 collective-permute-start.11
  49.7 1.5 %convolution_convert_fusion = bf16[256,1536]{1,0:T(8,128)(2,1)} fusion(bf16[256,512]{1,0:T(8,128)(2,1)S(1)} %copy-done.8, bf16[1536,512]{1,0:T(8,128)(2,1)S(1)} %copy-done), kind=kOutput, calls=%fused_computation | convolution fusion | flops 403046400 | bytes 2621440 | tf_op jit(solution)/shard_map/dot_general | solution.py:30
  51.2 0.0 collective-permute-done.11.refs_15_
  51.2 3.9 %wide.1 = (f32[192,1024]{1,0:T(8,128)}, f32[200,512]{1,0:T(8,128)S(1)}, f32[200,512]{1,0:T(8,128)S(1)}) custom-call(bf16[768,256]{1,0:T(8,128)(2,1)S(1)} %get-tuple-element.48.refs_0_.mine_ref, bf16[768,256]{1,0:T(8,128)(2,1)S(1)} %collective-permute-done.4.refs_1_.theirs_ref, bf16[384,256]{1,0:T(8,128)(2,1)} %collective-permute-done.refs_2_, ...), custom_call_target="tpu_custom_call" | custom-call | flops 1073741824 | bytes 5242880 | tf_op jit(solution)/shard_map/wide/pallas_call | solution.py:274
  55.3 1.4 %convert_element_type.49.terms_ref = f32[8,264,256]{2,1,0:T(8,128)S(1)} convert(f16[8,264,256]{2,1,0:T(8,128)(2,1)} %all-to-all-done.1) | non-fusion elementwise | flops 540672 | bytes 3244032 | tf_op jit(solution)/shard_map/convert_element_type | solution.py:444
  56.7 0.1 own_terms.1.own_ref
  56.8 0.6 collective-permute-start.14
  57.4 0.2 collective-permute-start.13
  57.6 2.1 %collective-permute-start.12 = (f16[200,512]{1,0:T(8,128)(2,1)S(1)}, f16[200,512]{1,0:T(8,128)(2,1)S(1)}, u32[]{:S(2)}, u32[]{:S(2)}) collective-permute-start(f16[200,512]{1,0:T(8,128)(2,1)S(1)} %convert_element_type.45), channel_id=1, source_target_pairs={{0,192},{1,193},{2,194},{3,195},{4,196},{5,197},{6,198},{7,199},{8... | collective-permute-start | bytes 614408 | tf_op jit(solution)/shard_map/ppermute | solution.py:34
  59.7 1.2 %narrow.1 = (f32[192,256]{1,0:T(8,128)}, f32[200,256]{1,0:T(8,128)S(1)}, f32[200,256]{1,0:T(8,128)S(1)}, f32[200,256]{1,0:T(8,128)S(1)}) custom-call(bf16[768,256]{1,0:T(8,128)(2,1)S(1)} %get-tuple-element.48.refs_0_.mine_ref, bf16[768,256]{1,0:T(8,128)(2,1)S(1)} %collective-permute-done.4.refs_1_.theirs_ref, f32[256,256]{1,0:T(8,128)S(1)} %own_terms.1.own_ref, ...), custom_call_target="tpu_custom_call" | custom-call | flops 1 | bytes 1 | tf_op jit(solution)/shard_map/narrow/pallas_call | solution.py:320
  60.9 1.9 %collective-permute-start.17 = (f16[200,256]{1,0:T(8,128)(2,1)S(1)}, f16[200,256]{1,0:T(8,128)(2,1)S(1)}, u32[]{:S(2)}, u32[]{:S(2)}) collective-permute-start(f16[200,256]{1,0:T(8,128)(2,1)S(1)} %convert_element_type.52), channel_id=1, source_target_pairs={{0,128},{1,129},{2,130},{3,131},{4,132},{5,133},{6,134},{7,135},{8... | collective-permute-start | bytes 307208 | tf_op jit(solution)/shard_map/ppermute | solution.py:34
  62.8 0.2 collective-permute-start.16
  63.0 2.1 %collective-permute-start.15 = (f16[200,256]{1,0:T(8,128)(2,1)S(1)}, f16[200,256]{1,0:T(8,128)(2,1)S(1)}, u32[]{:S(2)}, u32[]{:S(2)}) collective-permute-start(f16[200,256]{1,0:T(8,128)(2,1)S(1)} %convert_element_type.50), channel_id=1, source_target_pairs={{0,192},{1,193},{2,194},{3,195},{4,196},{5,197},{6,198},{7,199},{8... | collective-permute-start | bytes 307208 | tf_op jit(solution)/shard_map/ppermute | solution.py:34
  65.1 0.1 collective-permute-done.13
  65.1 1.9 %collective-permute-done.12 = f16[200,512]{1,0:T(8,128)(2,1)S(1)} collective-permute-done((f16[200,512]{1,0:T(8,128)(2,1)S(1)}, f16[200,512]{1,0:T(8,128)(2,1)S(1)}, u32[]{:S(2)}, u32[]{:S(2)}) %collective-permute-start.12) | collective-permute-done | bytes 204832 | tf_op jit(solution)/shard_map/ppermute | solution.py:34
  67.0 0.1 maximum_convert_fusion.wide_got_ref
  67.1 1.9 %collective-permute-done.17 = f16[200,256]{1,0:T(8,128)(2,1)S(1)} collective-permute-done((f16[200,256]{1,0:T(8,128)(2,1)S(1)}, f16[200,256]{1,0:T(8,128)(2,1)S(1)}, u32[]{:S(2)}, u32[]{:S(2)}) %collective-permute-start.17) | collective-permute-done | bytes 102432 | tf_op jit(solution)/shard_map/ppermute | solution.py:34
  69.1 1.2 %collective-permute-done.15 = f16[200,256]{1,0:T(8,128)(2,1)S(1)} collective-permute-done((f16[200,256]{1,0:T(8,128)(2,1)S(1)}, f16[200,256]{1,0:T(8,128)(2,1)S(1)}, u32[]{:S(2)}, u32[]{:S(2)}) %collective-permute-start.15) | collective-permute-done | bytes 102432 | tf_op jit(solution)/shard_map/ppermute | solution.py:34
  70.3 0.1 maximum_convert_fusion.1.narrow_got_ref
  70.4 0.5 after_x.1
  70.9 0.1 convert_element_type.54
  71.0 27.5 %all_to_all.15 = f16[32,64,128]{2,1,0:T(8,128)(2,1)S(1)} all-to-all(f16[32,64,128]{2,1,0:T(8,128)(2,1)S(1)} %convert_element_type.54), channel_id=1, replica_groups={{0,17,34,51,4,21,38,55,16,33,50,3,20,37,54,7,32,49,2,19,36,53,6,23,48,1..., dimensions={0} | all-to-all | bytes 1048576 | tf_op jit(solution)/shard_map/all_to_all | solution.py:449
  98.5 0.1 convert_element_type.55.got_ref
  98.6 0.7 last_sum.1
  (39 shorter events, 0.2 us)
Async XLA Ops:
  0.6 17.3 %copy-start = (bf16[1536,512]{1,0:T(8,128)(2,1)S(1)}, bf16[1536,512]{1,0:T(8,128)(2,1)}, u32[]{:S(2)}) copy-start(bf16[1536,512]{1,0:T(8,128)(2,1)} %param.10) | copy-start | bytes 4718596
  3.6 6.2 %copy-start.2 = (bf16[1,256,1536]{2,1,0:T(8,128)(2,1)S(1)}, bf16[1,256,1536]{2,1,0:T(8,128)(2,1)}, u32[]{:S(2)}) copy-start(bf16[1,256,1536]{2,1,0:T(8,128)(2,1)} %param.11) | copy-start | bytes 2359300
  3.6 11.1 %copy-start.1 = (bf16[1,256,1536]{2,1,0:T(8,128)(2,1)S(1)}, bf16[1,256,1536]{2,1,0:T(8,128)(2,1)}, u32[]{:S(2)}) copy-start(bf16[1,256,1536]{2,1,0:T(8,128)(2,1)} %param.6) | copy-start | bytes 2359300
  3.6 20.7 %all-to-all-start = ((bf16[8,256,256]{2,1,0:T(8,128)(2,1)}), bf16[8,256,256]{2,1,0:T(8,128)(2,1)}, u32[]{:S(2)}, u32[]{:S(2)}) async-start(bf16[8,256,256]{2,1,0:T(8,128)(2,1)} %project.1), calls=%async_computation | async-start | bytes 2097152 | tf_op jit(solution)/shard_map/all_to_all | solution.py:413
  9.8 6.9 %copy-start.10 = (bf16[1536,512]{1,0:T(8,128)(2,1)S(1)}, bf16[1536,512]{1,0:T(8,128)(2,1)}, u32[]{:S(2)}) copy-start(bf16[1536,512]{1,0:T(8,128)(2,1)} %param.7) | copy-start | bytes 4718596
  11.4 8.1 %collective-permute-start.2 = (bf16[384,256]{1,0:T(8,128)(2,1)S(1)}, bf16[384,256]{1,0:T(8,128)(2,1)S(1)}, u32[]{:S(2)}, u32[]{:S(2)}) collective-permute-start(bf16[384,256]{1,0:T(8,128)(2,1)S(1)} %get-tuple-element.43), channel_id=1, source_target_pairs={{0,192},{1,193},{2,194},{3,195},{4,196},{5,197},{6,198},{7,199},{8... | collective-permute-start | bytes 589832 | tf_op jit(solution)/shard_map/ppermute | solution.py:34
  14.1 19.7 %collective-permute-start.3 = (bf16[384,256]{1,0:T(8,128)(2,1)}, bf16[384,256]{1,0:T(8,128)(2,1)}, u32[]{:S(2)}, u32[]{:S(2)}) collective-permute-start(bf16[384,256]{1,0:T(8,128)(2,1)} %get-tuple-element.44), channel_id=1, source_target_pairs={{0,200},{1,201},{2,202},{3,203},{4,204},{5,205},{6,206},{7,207},{8... | collective-permute-start | bytes 589832 | tf_op jit(solution)/shard_map/ppermute | solution.py:34
  14.1 3.9 %copy-start.3 = (bf16[1,256,1536]{2,1,0:T(8,128)(2,1)S(1)}, bf16[1,256,1536]{2,1,0:T(8,128)(2,1)}, u32[]{:S(2)}) copy-start(bf16[1,256,1536]{2,1,0:T(8,128)(2,1)} %param.11) | copy-start | bytes 2359300
  14.1 19.7 %collective-permute-start.5 = (bf16[384,256]{1,0:T(8,128)(2,1)}, bf16[384,256]{1,0:T(8,128)(2,1)}, u32[]{:S(2)}, u32[]{:S(2)}) collective-permute-start(bf16[384,256]{1,0:T(8,128)(2,1)} %get-tuple-element.46), channel_id=1, source_target_pairs={{0,8},{1,9},{2,10},{3,11},{4,12},{5,13},{6,14},{7,15},{8,0},{9,1},... | collective-permute-start | bytes 589832 | tf_op jit(solution)/shard_map/ppermute | solution.py:34
  16.5 17.4 %collective-permute-start = (bf16[384,256]{1,0:T(8,128)(2,1)}, bf16[384,256]{1,0:T(8,128)(2,1)}, u32[]{:S(2)}, u32[]{:S(2)}) collective-permute-start(bf16[384,256]{1,0:T(8,128)(2,1)} %get-tuple-element.41), channel_id=1, source_target_pairs={{0,64},{1,65},{2,66},{3,67},{4,68},{5,69},{6,70},{7,71},{8,72},{9,... | collective-permute-start | bytes 589832 | tf_op jit(solution)/shard_map/ppermute | solution.py:34
  16.7 17.2 %collective-permute-start.4 = (bf16[768,256]{1,0:T(8,128)(2,1)}, bf16[768,256]{1,0:T(8,128)(2,1)S(1)}, u32[]{:S(2)}, u32[]{:S(2)}) collective-permute-start(bf16[768,256]{1,0:T(8,128)(2,1)} %get-tuple-element.45), channel_id=1, source_target_pairs={{0,8},{1,9},{2,10},{3,11},{4,12},{5,13},{6,14},{7,15},{8,0},{9,1},... | collective-permute-start | bytes 1179656 | tf_op jit(solution)/shard_map/ppermute | solution.py:34
  19.5 14.4 %collective-permute-start.1 = (bf16[384,256]{1,0:T(8,128)(2,1)}, bf16[384,256]{1,0:T(8,128)(2,1)S(1)}, u32[]{:S(2)}, u32[]{:S(2)}) collective-permute-start(bf16[384,256]{1,0:T(8,128)(2,1)} %get-tuple-element.42), channel_id=1, source_target_pairs={{0,72},{1,73},{2,74},{3,75},{4,76},{5,77},{6,78},{7,79},{8,64},{9,... | collective-permute-start | bytes 589832 | tf_op jit(solution)/shard_map/ppermute | solution.py:34
  33.9 1.2 %copy-start.5 = (bf16[384,256]{1,0:T(8,128)(2,1)}, bf16[384,256]{1,0:T(8,128)(2,1)S(1)}, u32[]{:S(2)}) copy-start(bf16[384,256]{1,0:T(8,128)(2,1)S(1)} %collective-permute-done.1.refs_3_) | copy-start | bytes 589828
  35.1 5.4 %copy-start.9 = (bf16[256,512]{1,0:T(8,128)(2,1)S(1)}, bf16[256,512]{1,0:T(8,128)(2,1)}, u32[]{:S(2)}) copy-start(bf16[256,512]{1,0:T(8,128)(2,1)} %get-tuple-element.52.refs_4_) | copy-start | bytes 786436
  35.1 7.0 %copy-start.8 = (bf16[256,512]{1,0:T(8,128)(2,1)S(1)}, bf16[256,512]{1,0:T(8,128)(2,1)}, u32[]{:S(2)}) copy-start(bf16[256,512]{1,0:T(8,128)(2,1)} %get-tuple-element.57.refs_12_) | copy-start | bytes 786436
  35.1 20.2 %all-to-all-start.1 = ((f16[8,264,256]{2,1,0:T(8,128)(2,1)}), f16[8,264,256]{2,1,0:T(8,128)(2,1)}, u32[]{:S(2)}, u32[]{:S(2)}) async-start(f16[8,264,256]{2,1,0:T(8,128)(2,1)} %convert_element_type.44), calls=%async_computation.1 | async-start | bytes 2162688 | tf_op jit(solution)/shard_map/all_to_all | solution.py:428
  40.5 10.7 %copy-start.6 = (bf16[384,256]{1,0:T(8,128)(2,1)S(1)}, bf16[384,256]{1,0:T(8,128)(2,1)}, u32[]{:S(2)}) copy-start(bf16[384,256]{1,0:T(8,128)(2,1)} %copy-done.5) | copy-start | bytes 589828
  40.5 6.5 %collective-permute-start.7 = (bf16[256,512]{1,0:T(8,128)(2,1)S(1)}, bf16[256,512]{1,0:T(8,128)(2,1)S(1)}, u32[]{:S(2)}, u32[]{:S(2)}) collective-permute-start(bf16[256,512]{1,0:T(8,128)(2,1)S(1)} %copy-done.9), channel_id=1, source_target_pairs={{0,64},{1,65},{2,66},{3,67},{4,68},{5,69},{6,70},{7,71},{8,72},{9,... | collective-permute-start | bytes 786440 | tf_op jit(solution)/shard_map/ppermute | solution.py:34
  42.1 7.6 %collective-permute-start.10 = (bf16[256,512]{1,0:T(8,128)(2,1)S(1)}, bf16[256,512]{1,0:T(8,128)(2,1)S(1)}, u32[]{:S(2)}, u32[]{:S(2)}) collective-permute-start(bf16[256,512]{1,0:T(8,128)(2,1)S(1)} %copy-done.8), channel_id=1, source_target_pairs={{0,192},{1,193},{2,194},{3,195},{4,196},{5,197},{6,198},{7,199},{8... | collective-permute-start | bytes 786440 | tf_op jit(solution)/shard_map/ppermute | solution.py:34
  44.2 7.0 %collective-permute-start.6 = (bf16[256,512]{1,0:T(8,128)(2,1)S(1)}, bf16[256,512]{1,0:T(8,128)(2,1)S(1)}, u32[]{:S(2)}, u32[]{:S(2)}) collective-permute-start(bf16[256,512]{1,0:T(8,128)(2,1)S(1)} %copy-done.9), channel_id=1, source_target_pairs={{0,8},{1,9},{2,10},{3,11},{4,12},{5,13},{6,14},{7,15},{8,0},{9,1},... | collective-permute-start | bytes 786440 | tf_op jit(solution)/shard_map/ppermute | solution.py:34
  44.2 7.0 %collective-permute-start.9 = (bf16[256,512]{1,0:T(8,128)(2,1)S(1)}, bf16[256,512]{1,0:T(8,128)(2,1)S(1)}, u32[]{:S(2)}, u32[]{:S(2)}) collective-permute-start(bf16[256,512]{1,0:T(8,128)(2,1)S(1)} %copy-done.8), channel_id=1, source_target_pairs={{0,8},{1,9},{2,10},{3,11},{4,12},{5,13},{6,14},{7,15},{8,0},{9,1},... | collective-permute-start | bytes 786440 | tf_op jit(solution)/shard_map/ppermute | solution.py:34
  47.0 4.2 %collective-permute-start.8 = (bf16[256,512]{1,0:T(8,128)(2,1)S(1)}, bf16[256,512]{1,0:T(8,128)(2,1)S(1)}, u32[]{:S(2)}, u32[]{:S(2)}) collective-permute-start(bf16[256,512]{1,0:T(8,128)(2,1)S(1)} %collective-permute-done.7.refs_6_), channel_id=1, source_target_pairs={{0,8},{1,9},{2,10},{3,11},{4,12},{5,13},{6,14},{7,15},{8,0},{9,1},... | collective-permute-start | bytes 786440 | tf_op jit(solution)/shard_map/ppermute | solution.py:34
  49.7 1.5 %collective-permute-start.11 = (bf16[256,512]{1,0:T(8,128)(2,1)S(1)}, bf16[256,512]{1,0:T(8,128)(2,1)S(1)}, u32[]{:S(2)}, u32[]{:S(2)}) collective-permute-start(bf16[256,512]{1,0:T(8,128)(2,1)S(1)} %collective-permute-done.10.refs_14_), channel_id=1, source_target_pairs={{0,8},{1,9},{2,10},{3,11},{4,12},{5,13},{6,14},{7,15},{8,0},{9,1},... | collective-permute-start | bytes 786440 | tf_op jit(solution)/shard_map/ppermute | solution.py:34
  56.8 2.9 %collective-permute-start.14 = (f32[256,256]{1,0:T(8,128)S(1)}, f32[256,256]{1,0:T(8,128)S(1)}, u32[]{:S(2)}, u32[]{:S(2)}) collective-permute-start(f32[256,256]{1,0:T(8,128)S(1)} %own_terms.1.own_ref), channel_id=1, source_target_pairs={{0,8},{1,9},{2,10},{3,11},{4,12},{5,13},{6,14},{7,15},{8,0},{9,1},... | collective-permute-start | bytes 786440 | tf_op jit(solution)/shard_map/ppermute | solution.py:34
  57.4 7.7 %collective-permute-start.13 = (f16[200,512]{1,0:T(8,128)(2,1)S(1)}, f16[200,512]{1,0:T(8,128)(2,1)S(1)}, u32[]{:S(2)}, u32[]{:S(2)}) collective-permute-start(f16[200,512]{1,0:T(8,128)(2,1)S(1)} %convert_element_type.46), channel_id=1, source_target_pairs={{0,64},{1,65},{2,66},{3,67},{4,68},{5,69},{6,70},{7,71},{8,72},{9,... | collective-permute-start | bytes 614408 | tf_op jit(solution)/shard_map/ppermute | solution.py:34
  57.6 9.5 %collective-permute-start.12 = (f16[200,512]{1,0:T(8,128)(2,1)S(1)}, f16[200,512]{1,0:T(8,128)(2,1)S(1)}, u32[]{:S(2)}, u32[]{:S(2)}) collective-permute-start(f16[200,512]{1,0:T(8,128)(2,1)S(1)} %convert_element_type.45), channel_id=1, source_target_pairs={{0,192},{1,193},{2,194},{3,195},{4,196},{5,197},{6,198},{7,199},{8... | collective-permute-start | bytes 614408 | tf_op jit(solution)/shard_map/ppermute | solution.py:34
  60.8 9.5 %copy-start.4 = (f32[192,1024]{1,0:T(8,128)S(1)}, f32[192,1024]{1,0:T(8,128)}, u32[]{:S(2)}) copy-start(f32[192,1024]{1,0:T(8,128)} %get-tuple-element.61.wide_ref) | copy-start | bytes 2359300
  60.8 9.5 %copy-start.7 = (f32[192,256]{1,0:T(8,128)S(1)}, f32[192,256]{1,0:T(8,128)}, u32[]{:S(2)}) copy-start(f32[192,256]{1,0:T(8,128)} %get-tuple-element.63.narrow_ref) | copy-start | bytes 589828
  60.9 8.2 %collective-permute-start.17 = (f16[200,256]{1,0:T(8,128)(2,1)S(1)}, f16[200,256]{1,0:T(8,128)(2,1)S(1)}, u32[]{:S(2)}, u32[]{:S(2)}) collective-permute-start(f16[200,256]{1,0:T(8,128)(2,1)S(1)} %convert_element_type.52), channel_id=1, source_target_pairs={{0,128},{1,129},{2,130},{3,131},{4,132},{5,133},{6,134},{7,135},{8... | collective-permute-start | bytes 307208 | tf_op jit(solution)/shard_map/ppermute | solution.py:34
  62.8 6.3 %collective-permute-start.16 = (f16[200,256]{1,0:T(8,128)(2,1)S(1)}, f16[200,256]{1,0:T(8,128)(2,1)S(1)}, u32[]{:S(2)}, u32[]{:S(2)}) collective-permute-start(f16[200,256]{1,0:T(8,128)(2,1)S(1)} %convert_element_type.51), channel_id=1, source_target_pairs={{0,64},{1,65},{2,66},{3,67},{4,68},{5,69},{6,70},{7,71},{8,72},{9,... | collective-permute-start | bytes 307208 | tf_op jit(solution)/shard_map/ppermute | solution.py:34
  63.0 7.3 %collective-permute-start.15 = (f16[200,256]{1,0:T(8,128)(2,1)S(1)}, f16[200,256]{1,0:T(8,128)(2,1)S(1)}, u32[]{:S(2)}, u32[]{:S(2)}) collective-permute-start(f16[200,256]{1,0:T(8,128)(2,1)S(1)} %convert_element_type.50), channel_id=1, source_target_pairs={{0,192},{1,193},{2,194},{3,195},{4,196},{5,197},{6,198},{7,199},{8... | collective-permute-start | bytes 307208 | tf_op jit(solution)/shard_map/ppermute | solution.py:34

commit v11 on v10

--- a/solution.py
+++ b/solution.py
@@ -238,14 +238,15 @@
     keep_hbm, *send_refs = refs[16:19]
     sides_ref, factors_ref, keep_ref, in_sems, out_sems = refs[19:]
     rows, cols = keep_ref.shape[0], send_refs[0].shape[1]
+    tokens = factors_ref.shape[1] // 4
     arriving = []
     for i in range(2):
         arriving.append([])
         for n in range(4):
             side, factor = refs[8 * i + n], refs[8 * i + 4 + n]
             copies = (
-                pltpu.make_async_copy(side.at[pl.ds(0, 2 * rows), :], sides_ref.at[i, n], in_sems.at[i, n, 0]),
-                pltpu.make_async_copy(factor, factors_ref.at[i, n], in_sems.at[i, n, 1]),
+                pltpu.make_async_copy(side.at[pl.ds(0, 2 * rows), :], sides_ref.at[i, :, pl.ds(n * tokens, tokens)], in_sems.at[i, n, 0]),
+                pltpu.make_async_copy(factor, factors_ref.at[i, pl.ds(n * tokens, tokens), :], in_sems.at[i, n, 1]),
             )
             for copy in copies:
                 copy.start()
@@ -254,10 +255,7 @@
     for i in range(2):
         for copy in arriving[i]:
             copy.wait()
-        product = None
-        for n in range(4):
-            term = dot(sides_ref[i, n], factors_ref[i, n], ((1,), (0,)))
-            product = term if product is None else product + term
+        product = dot(sides_ref[i], factors_ref[i], ((1,), (0,)))
         here = (slice(None), pl.ds(i * cols, cols))
         keep_ref[:, i * cols : (i + 1) * cols] = product[:rows]
         leaving.append(pltpu.make_async_copy(keep_ref.at[here], keep_hbm.at[here], out_sems.at[i]))
@@ -281,8 +279,8 @@
             jax.ShapeDtypeStruct((rows + 8, cols), jnp.float32),
         ],
         scratch_shapes=[
-            pltpu.VMEM((2, 4, 2 * rows, tokens), jnp.bfloat16),
-            pltpu.VMEM((2, 4, tokens, cols), jnp.bfloat16),
+            pltpu.VMEM((2, 2 * rows, 4 * tokens), jnp.bfloat16),
+            pltpu.VMEM((2, 4 * tokens, cols), jnp.bfloat16),
             pltpu.VMEM((rows, 2 * cols), jnp.float32),
             pltpu.SemaphoreType.DMA((2, 4, 2)),
             pltpu.SemaphoreType.DMA((2,)),

time: 99.7 us -> 98.9 us (level)
  transfers between devices with their start and end apart: 20 -> 20, of which waited for: 8 -> 7; matrix products, arithmetic and copies ran while one was open for 4% -> 4% of each run, Pallas kernels for 18% -> 17%
where the time goes in v11:
time: 98.9 us; the launch traced here: 98.6 us
  starting transfers between devices  28.8 us (29%)
  blocking collectives  26.8 us (27%)
  Pallas kernels  21.5 us (22%)
  waiting for transfers between devices  13.5 us (14%)
  matrix products  4.05 us (4%)
  other arithmetic  3.07 us (3%)
    all_to_all x1, blocking collectives, local(): lax.all_to_all(part.astype(half), AXES, 0, 0, axis_index_groups=YZ_GROUPS...  26.8 us
    ppermute x18, starting transfers between devices, exchange(): return lax.ppermute(value, AXES, [(i, i ^ mask) for i in range(256)])  17.2 us
    ppermute x18, waiting for transfers between devices, exchange(): return lax.ppermute(value, AXES, [(i, i ^ mask) for i in range(256)])  10.4 us
    pallas_call x1, Pallas kernels, attention(): pl.pallas_call(attention_kernel, in_specs=[anywhere] * 3, out_specs=[anyw...  9.49 us
    all_to_all x1, starting transfers between devices, local(): lax.all_to_all(project(hidden, w_key, w_value), AXES, 0, 0, axis_index_gr...  6.11 us
    all_to_all x1, starting transfers between devices, local(): lax.all_to_all(terms.astype(half), AXES, 0, 0, axis_index_groups=SEQ_GROU...  5.41 us
    dot_general x3, matrix products, dot(): lax.dot_general(left, right, (dims, ((), ())), preferred_element_type=jnp...  4.05 us
    pallas_call x2, Pallas kernels, turn(): pl.pallas_call(functools.partial(turn_kernel, pieces), grid_spec=pltpu.Pr...  3.26 us
  transfers between devices with their start and end apart: 20, of which 7 were waited for; matrix products, arithmetic and copies ran while one was open for 4% of the time, Pallas kernels for 17%

profile of v11, /device:TPU:32, one launch (start us, length us, event | category | flops | bytes accessed | tf_op | source)
XLA Modules:
  0.0 98.6 jit_solution(3414788771888216868)
XLA Ops:
  0.6 0.0 copy-start
  0.6 3.0 %project.1 = bf16[8,256,256]{2,1,0:T(8,128)(2,1)} custom-call(bf16[256,1536]{1,0:T(8,128)(2,1)} %bitcast.19, bf16[1536,128]{1,0:T(8,128)(2,1)} %w_key_ref.1, bf16[1536,128]{1,0:T(8,128)(2,1)} %w_value_ref.1), custom_call_target="tpu_custom_call" | custom-call | tf_op jit(solution)/shard_map/project/pallas_call | solution.py:60
  3.6 6.1 %all-to-all-start = ((bf16[8,256,256]{2,1,0:T(8,128)(2,1)}), bf16[8,256,256]{2,1,0:T(8,128)(2,1)}, u32[]{:S(2)}, u32[]{:S(2)}) async-start(bf16[8,256,256]{2,1,0:T(8,128)(2,1)} %project.1), calls=%async_computation | async-start | bytes 2097152 | tf_op jit(solution)/shard_map/all_to_all | solution.py:411
  9.8 0.1 pad_add_fusion.place_ref
  9.8 1.6 %turn.3 = (bf16[384,256]{1,0:T(8,128)(2,1)S(1)}, bf16[384,256]{1,0:T(8,128)(2,1)}, bf16[384,256]{1,0:T(8,128)(2,1)S(1)}, bf16[384,256]{1,0:T(8,128)(2,1)}) custom-call(s32[2]{0:T(128)S(1)} %pad_add_fusion.place_ref, bf16[256,1536]{1,0:T(8,128)(2,1)S(1)} %bitcast.21), custom_call_target="tpu_custom_call" | custom-call | tf_op jit(solution)/shard_map/turn/pallas_call | solution.py:82
  11.4 2.7 %collective-permute-start.2 = (bf16[384,256]{1,0:T(8,128)(2,1)S(1)}, bf16[384,256]{1,0:T(8,128)(2,1)S(1)}, u32[]{:S(2)}, u32[]{:S(2)}) collective-permute-start(bf16[384,256]{1,0:T(8,128)(2,1)S(1)} %get-tuple-element.43), channel_id=1, source_target_pairs={{0,192},{1,193},{2,194},{3,195},{4,196},{5,197},{6,198},{7,199},{8... | collective-permute-start | bytes 589832 | tf_op jit(solution)/shard_map/ppermute | solution.py:34
  14.1 0.0 collective-permute-start.3
  14.1 0.6 collective-permute-start.5
  14.8 1.7 %turn.2 = (bf16[768,256]{1,0:T(8,128)(2,1)S(1)}, bf16[768,256]{1,0:T(8,128)(2,1)}, bf16[384,256]{1,0:T(8,128)(2,1)}, bf16[384,256]{1,0:T(8,128)(2,1)}) custom-call(s32[2]{0:T(128)S(1)} %pad_add_fusion.place_ref, bf16[256,1536]{1,0:T(8,128)(2,1)S(1)} %bitcast.20), custom_call_target="tpu_custom_call" | custom-call | tf_op jit(solution)/shard_map/turn/pallas_call | solution.py:82
  16.5 0.2 collective-permute-start
  16.7 0.0 collective-permute-start.4
  16.7 1.3 %convolution_convert_fusion.2.q_hbm = bf16[256,512]{1,0:T(8,128)(2,1)} fusion(bf16[1536,512]{1,0:T(8,128)(2,1)S(1)} %copy-done.10, bf16[1,256,1536]{2,1,0:T(8,128)(2,1)S(1)} %copy-done.1), kind=kOutput, calls=%fused_computation.2 | convolution fusion | flops 402784256 | bytes 2621440 | tf_op jit(solution)/shard_map/dot_general | solution.py:30
  18.0 1.3 %convolution_convert_fusion.1.da_hbm = bf16[256,512]{1,0:T(8,128)(2,1)} fusion(bf16[1536,512]{1,0:T(8,128)(2,1)S(1)} %copy-done, bf16[1,256,1536]{2,1,0:T(8,128)(2,1)S(1)} %copy-done.3), kind=kOutput, calls=%fused_computation.1 | convolution fusion | flops 402784256 | bytes 2621440 | tf_op jit(solution)/shard_map/dot_general | solution.py:30
  19.3 0.2 collective-permute-done.2.refs_10_
  19.5 1.7 %collective-permute-start.1 = (bf16[384,256]{1,0:T(8,128)(2,1)}, bf16[384,256]{1,0:T(8,128)(2,1)S(1)}, u32[]{:S(2)}, u32[]{:S(2)}) collective-permute-start(bf16[384,256]{1,0:T(8,128)(2,1)} %get-tuple-element.42), channel_id=1, source_target_pairs={{0,72},{1,73},{2,74},{3,75},{4,76},{5,77},{6,78},{7,79},{8,64},{9,... | collective-permute-start | bytes 589832 | tf_op jit(solution)/shard_map/ppermute | solution.py:34
  21.2 3.2 %all-to-all-done = bf16[8,256,256]{2,1,0:T(8,128)(2,1)} async-done(((bf16[8,256,256]{2,1,0:T(8,128)(2,1)}), bf16[8,256,256]{2,1,0:T(8,128)(2,1)}, u32[]{:S(2)}, u32[]{:S(2)}) %all-to-all-start) | async-done | bytes 1048608 | tf_op jit(solution)/shard_map/all_to_all | solution.py:411
  24.3 9.5 %attention.1 = (bf16[256,512]{1,0:T(8,128)(2,1)}, bf16[256,512]{1,0:T(8,128)(2,1)}, f32[8,264,256]{2,1,0:T(8,128)S(1)}) custom-call(bf16[256,512]{1,0:T(8,128)(2,1)} %convolution_convert_fusion.2.q_hbm, bf16[256,512]{1,0:T(8,128)(2,1)} %convolution_convert_fusion.1.da_hbm, bf16[2048,256]{1,0:T(8,128)(2,1)} %bitcast.2.kv_hbm), custom_call_target="tpu_custom_call" | custom-call | flops 3221225472 | bytes 4194304 | tf_op jit(solution)/shard_map/attention/pallas_call | solution.py:212
  33.9 0.0 collective-permute-done.5.refs_9_
  33.9 1.2 %convert_element_type.44 = f16[8,264,256]{2,1,0:T(8,128)(2,1)} convert(f32[8,264,256]{2,1,0:T(8,128)S(1)} %get-tuple-element.47) | non-fusion elementwise | flops 540672 | bytes 3244032 | tf_op jit(solution)/shard_map/convert_element_type | solution.py:426
  35.1 5.4 %all-to-all-start.1 = ((f16[8,264,256]{2,1,0:T(8,128)(2,1)}), f16[8,264,256]{2,1,0:T(8,128)(2,1)}, u32[]{:S(2)}, u32[]{:S(2)}) async-start(f16[8,264,256]{2,1,0:T(8,128)(2,1)} %convert_element_type.44), calls=%async_computation.1 | async-start | bytes 2162688 | tf_op jit(solution)/shard_map/all_to_all | solution.py:426
  40.5 1.6 %collective-permute-start.7 = (bf16[256,512]{1,0:T(8,128)(2,1)S(1)}, bf16[256,512]{1,0:T(8,128)(2,1)S(1)}, u32[]{:S(2)}, u32[]{:S(2)}) collective-permute-start(bf16[256,512]{1,0:T(8,128)(2,1)S(1)} %copy-done.9), channel_id=1, source_target_pairs={{0,64},{1,65},{2,66},{3,67},{4,68},{5,69},{6,70},{7,71},{8,72},{9,... | collective-permute-start | bytes 786440 | tf_op jit(solution)/shard_map/ppermute | solution.py:34
  42.1 2.1 %collective-permute-start.10 = (bf16[256,512]{1,0:T(8,128)(2,1)S(1)}, bf16[256,512]{1,0:T(8,128)(2,1)S(1)}, u32[]{:S(2)}, u32[]{:S(2)}) collective-permute-start(bf16[256,512]{1,0:T(8,128)(2,1)S(1)} %copy-done.8), channel_id=1, source_target_pairs={{0,192},{1,193},{2,194},{3,195},{4,196},{5,197},{6,198},{7,199},{8... | collective-permute-start | bytes 786440 | tf_op jit(solution)/shard_map/ppermute | solution.py:34
  44.2 0.5 collective-permute-start.9
  44.7 2.3 %collective-permute-done.7.refs_6_ = bf16[256,512]{1,0:T(8,128)(2,1)S(1)} collective-permute-done((bf16[256,512]{1,0:T(8,128)(2,1)S(1)}, bf16[256,512]{1,0:T(8,128)(2,1)S(1)}, u32[]{:S(2)}, u32[]{:S(2)}) %collective-permute-start.7) | collective-permute-done | bytes 262176 | tf_op jit(solution)/shard_map/ppermute | solution.py:34
  47.0 2.7 %collective-permute-done.10.refs_14_ = bf16[256,512]{1,0:T(8,128)(2,1)S(1)} collective-permute-done((bf16[256,512]{1,0:T(8,128)(2,1)S(1)}, bf16[256,512]{1,0:T(8,128)(2,1)S(1)}, u32[]{:S(2)}, u32[]{:S(2)}) %collective-permute-start.10) | collective-permute-done | bytes 262176 | tf_op jit(solution)/shard_map/ppermute | solution.py:34
  49.7 0.0 collective-permute-start.11
  49.7 1.5 %convolution_convert_fusion = bf16[256,1536]{1,0:T(8,128)(2,1)} fusion(bf16[256,512]{1,0:T(8,128)(2,1)S(1)} %copy-done.8, bf16[1536,512]{1,0:T(8,128)(2,1)S(1)} %copy-done), kind=kOutput, calls=%fused_computation | convolution fusion | flops 403046400 | bytes 2621440 | tf_op jit(solution)/shard_map/dot_general | solution.py:30
  51.2 0.0 collective-permute-done.11.refs_15_
  51.2 3.2 %wide.1 = (f32[192,1024]{1,0:T(8,128)}, f32[200,512]{1,0:T(8,128)S(1)}, f32[200,512]{1,0:T(8,128)S(1)}) custom-call(bf16[768,256]{1,0:T(8,128)(2,1)S(1)} %get-tuple-element.48.refs_0_.mine_ref, bf16[768,256]{1,0:T(8,128)(2,1)S(1)} %collective-permute-done.4.refs_1_.theirs_ref, bf16[384,256]{1,0:T(8,128)(2,1)} %collective-permute-done.refs_2_, ...), custom_call_target="tpu_custom_call" | custom-call | flops 1073741824 | bytes 5242880 | tf_op jit(solution)/shard_map/wide/pallas_call | solution.py:272
  54.5 1.4 %convert_element_type.49.terms_ref = f32[8,264,256]{2,1,0:T(8,128)S(1)} convert(f16[8,264,256]{2,1,0:T(8,128)(2,1)} %all-to-all-done.1) | non-fusion elementwise | flops 540672 | bytes 3244032 | tf_op jit(solution)/shard_map/convert_element_type | solution.py:442
  55.9 0.1 own_terms.1.own_ref
  56.1 0.6 collective-permute-start.14
  56.7 0.9 collective-permute-start.13
  57.6 2.1 %collective-permute-start.12 = (f16[200,512]{1,0:T(8,128)(2,1)S(1)}, f16[200,512]{1,0:T(8,128)(2,1)S(1)}, u32[]{:S(2)}, u32[]{:S(2)}) collective-permute-start(f16[200,512]{1,0:T(8,128)(2,1)S(1)} %convert_element_type.45), channel_id=1, source_target_pairs={{0,192},{1,193},{2,194},{3,195},{4,196},{5,197},{6,198},{7,199},{8... | collective-permute-start | bytes 614408 | tf_op jit(solution)/shard_map/ppermute | solution.py:34
  59.7 1.2 %narrow.1 = (f32[192,256]{1,0:T(8,128)}, f32[200,256]{1,0:T(8,128)S(1)}, f32[200,256]{1,0:T(8,128)S(1)}, f32[200,256]{1,0:T(8,128)S(1)}) custom-call(bf16[768,256]{1,0:T(8,128)(2,1)S(1)} %get-tuple-element.48.refs_0_.mine_ref, bf16[768,256]{1,0:T(8,128)(2,1)S(1)} %collective-permute-done.4.refs_1_.theirs_ref, f32[256,256]{1,0:T(8,128)S(1)} %own_terms.1.own_ref, ...), custom_call_target="tpu_custom_call" | custom-call | flops 1 | bytes 1 | tf_op jit(solution)/shard_map/narrow/pallas_call | solution.py:318
  60.9 1.2 %collective-permute-start.17 = (f16[200,256]{1,0:T(8,128)(2,1)S(1)}, f16[200,256]{1,0:T(8,128)(2,1)S(1)}, u32[]{:S(2)}, u32[]{:S(2)}) collective-permute-start(f16[200,256]{1,0:T(8,128)(2,1)S(1)} %convert_element_type.52), channel_id=1, source_target_pairs={{0,128},{1,129},{2,130},{3,131},{4,132},{5,133},{6,134},{7,135},{8... | collective-permute-start | bytes 307208 | tf_op jit(solution)/shard_map/ppermute | solution.py:34
  62.1 0.9 collective-permute-start.16
  63.0 2.1 %collective-permute-start.15 = (f16[200,256]{1,0:T(8,128)(2,1)S(1)}, f16[200,256]{1,0:T(8,128)(2,1)S(1)}, u32[]{:S(2)}, u32[]{:S(2)}) collective-permute-start(f16[200,256]{1,0:T(8,128)(2,1)S(1)} %convert_element_type.50), channel_id=1, source_target_pairs={{0,192},{1,193},{2,194},{3,195},{4,196},{5,197},{6,198},{7,199},{8... | collective-permute-start | bytes 307208 | tf_op jit(solution)/shard_map/ppermute | solution.py:34
  65.1 3.1 %collective-permute-done.12 = f16[200,512]{1,0:T(8,128)(2,1)S(1)} collective-permute-done((f16[200,512]{1,0:T(8,128)(2,1)S(1)}, f16[200,512]{1,0:T(8,128)(2,1)S(1)}, u32[]{:S(2)}, u32[]{:S(2)}) %collective-permute-start.12) | collective-permute-done | bytes 204832 | tf_op jit(solution)/shard_map/ppermute | solution.py:34
  68.2 0.1 maximum_convert_fusion.wide_got_ref
  68.3 0.1 collective-permute-done.17
  68.4 1.9 %collective-permute-done.15 = f16[200,256]{1,0:T(8,128)(2,1)S(1)} collective-permute-done((f16[200,256]{1,0:T(8,128)(2,1)S(1)}, f16[200,256]{1,0:T(8,128)(2,1)S(1)}, u32[]{:S(2)}, u32[]{:S(2)}) %collective-permute-start.15) | collective-permute-done | bytes 102432 | tf_op jit(solution)/shard_map/ppermute | solution.py:34
  70.3 0.1 maximum_convert_fusion.1.narrow_got_ref
  70.4 0.5 after_x.1
  70.9 0.1 convert_element_type.54
  71.0 26.8 %all_to_all.15 = f16[32,64,128]{2,1,0:T(8,128)(2,1)S(1)} all-to-all(f16[32,64,128]{2,1,0:T(8,128)(2,1)S(1)} %convert_element_type.54), channel_id=1, replica_groups={{0,17,34,51,4,21,38,55,16,33,50,3,20,37,54,7,32,49,2,19,36,53,6,23,48,1..., dimensions={0} | all-to-all | bytes 1048576 | tf_op jit(solution)/shard_map/all_to_all | solution.py:447
  97.8 0.1 convert_element_type.55.got_ref
  97.9 0.7 last_sum.1
  (39 shorter events, 0.2 us)
Async XLA Ops:
  0.6 17.3 %copy-start = (bf16[1536,512]{1,0:T(8,128)(2,1)S(1)}, bf16[1536,512]{1,0:T(8,128)(2,1)}, u32[]{:S(2)}) copy-start(bf16[1536,512]{1,0:T(8,128)(2,1)} %param.10) | copy-start | bytes 4718596
  3.6 6.2 %copy-start.2 = (bf16[1,256,1536]{2,1,0:T(8,128)(2,1)S(1)}, bf16[1,256,1536]{2,1,0:T(8,128)(2,1)}, u32[]{:S(2)}) copy-start(bf16[1,256,1536]{2,1,0:T(8,128)(2,1)} %param.11) | copy-start | bytes 2359300
  3.6 11.1 %copy-start.1 = (bf16[1,256,1536]{2,1,0:T(8,128)(2,1)S(1)}, bf16[1,256,1536]{2,1,0:T(8,128)(2,1)}, u32[]{:S(2)}) copy-start(bf16[1,256,1536]{2,1,0:T(8,128)(2,1)} %param.6) | copy-start | bytes 2359300
  3.6 20.7 %all-to-all-start = ((bf16[8,256,256]{2,1,0:T(8,128)(2,1)}), bf16[8,256,256]{2,1,0:T(8,128)(2,1)}, u32[]{:S(2)}, u32[]{:S(2)}) async-start(bf16[8,256,256]{2,1,0:T(8,128)(2,1)} %project.1), calls=%async_computation | async-start | bytes 2097152 | tf_op jit(solution)/shard_map/all_to_all | solution.py:411
  9.8 6.9 %copy-start.10 = (bf16[1536,512]{1,0:T(8,128)(2,1)S(1)}, bf16[1536,512]{1,0:T(8,128)(2,1)}, u32[]{:S(2)}) copy-start(bf16[1536,512]{1,0:T(8,128)(2,1)} %param.7) | copy-start | bytes 4718596
  11.4 8.1 %collective-permute-start.2 = (bf16[384,256]{1,0:T(8,128)(2,1)S(1)}, bf16[384,256]{1,0:T(8,128)(2,1)S(1)}, u32[]{:S(2)}, u32[]{:S(2)}) collective-permute-start(bf16[384,256]{1,0:T(8,128)(2,1)S(1)} %get-tuple-element.43), channel_id=1, source_target_pairs={{0,192},{1,193},{2,194},{3,195},{4,196},{5,197},{6,198},{7,199},{8... | collective-permute-start | bytes 589832 | tf_op jit(solution)/shard_map/ppermute | solution.py:34
  14.1 19.7 %collective-permute-start.3 = (bf16[384,256]{1,0:T(8,128)(2,1)}, bf16[384,256]{1,0:T(8,128)(2,1)}, u32[]{:S(2)}, u32[]{:S(2)}) collective-permute-start(bf16[384,256]{1,0:T(8,128)(2,1)} %get-tuple-element.44), channel_id=1, source_target_pairs={{0,200},{1,201},{2,202},{3,203},{4,204},{5,205},{6,206},{7,207},{8... | collective-permute-start | bytes 589832 | tf_op jit(solution)/shard_map/ppermute | solution.py:34
  14.1 3.9 %copy-start.3 = (bf16[1,256,1536]{2,1,0:T(8,128)(2,1)S(1)}, bf16[1,256,1536]{2,1,0:T(8,128)(2,1)}, u32[]{:S(2)}) copy-start(bf16[1,256,1536]{2,1,0:T(8,128)(2,1)} %param.11) | copy-start | bytes 2359300
  14.1 19.7 %collective-permute-start.5 = (bf16[384,256]{1,0:T(8,128)(2,1)}, bf16[384,256]{1,0:T(8,128)(2,1)}, u32[]{:S(2)}, u32[]{:S(2)}) collective-permute-start(bf16[384,256]{1,0:T(8,128)(2,1)} %get-tuple-element.46), channel_id=1, source_target_pairs={{0,8},{1,9},{2,10},{3,11},{4,12},{5,13},{6,14},{7,15},{8,0},{9,1},... | collective-permute-start | bytes 589832 | tf_op jit(solution)/shard_map/ppermute | solution.py:34
  16.5 17.4 %collective-permute-start = (bf16[384,256]{1,0:T(8,128)(2,1)}, bf16[384,256]{1,0:T(8,128)(2,1)}, u32[]{:S(2)}, u32[]{:S(2)}) collective-permute-start(bf16[384,256]{1,0:T(8,128)(2,1)} %get-tuple-element.41), channel_id=1, source_target_pairs={{0,64},{1,65},{2,66},{3,67},{4,68},{5,69},{6,70},{7,71},{8,72},{9,... | collective-permute-start | bytes 589832 | tf_op jit(solution)/shard_map/ppermute | solution.py:34
  16.7 17.2 %collective-permute-start.4 = (bf16[768,256]{1,0:T(8,128)(2,1)}, bf16[768,256]{1,0:T(8,128)(2,1)S(1)}, u32[]{:S(2)}, u32[]{:S(2)}) collective-permute-start(bf16[768,256]{1,0:T(8,128)(2,1)} %get-tuple-element.45), channel_id=1, source_target_pairs={{0,8},{1,9},{2,10},{3,11},{4,12},{5,13},{6,14},{7,15},{8,0},{9,1},... | collective-permute-start | bytes 1179656 | tf_op jit(solution)/shard_map/ppermute | solution.py:34
  19.5 14.4 %collective-permute-start.1 = (bf16[384,256]{1,0:T(8,128)(2,1)}, bf16[384,256]{1,0:T(8,128)(2,1)S(1)}, u32[]{:S(2)}, u32[]{:S(2)}) collective-permute-start(bf16[384,256]{1,0:T(8,128)(2,1)} %get-tuple-element.42), channel_id=1, source_target_pairs={{0,72},{1,73},{2,74},{3,75},{4,76},{5,77},{6,78},{7,79},{8,64},{9,... | collective-permute-start | bytes 589832 | tf_op jit(solution)/shard_map/ppermute | solution.py:34
  33.9 1.2 %copy-start.5 = (bf16[384,256]{1,0:T(8,128)(2,1)}, bf16[384,256]{1,0:T(8,128)(2,1)S(1)}, u32[]{:S(2)}) copy-start(bf16[384,256]{1,0:T(8,128)(2,1)S(1)} %collective-permute-done.1.refs_3_) | copy-start | bytes 589828
  35.1 5.4 %copy-start.9 = (bf16[256,512]{1,0:T(8,128)(2,1)S(1)}, bf16[256,512]{1,0:T(8,128)(2,1)}, u32[]{:S(2)}) copy-start(bf16[256,512]{1,0:T(8,128)(2,1)} %get-tuple-element.52.refs_4_) | copy-start | bytes 786436
  35.1 7.0 %copy-start.8 = (bf16[256,512]{1,0:T(8,128)(2,1)S(1)}, bf16[256,512]{1,0:T(8,128)(2,1)}, u32[]{:S(2)}) copy-start(bf16[256,512]{1,0:T(8,128)(2,1)} %get-tuple-element.57.refs_12_) | copy-start | bytes 786436
  35.1 19.4 %all-to-all-start.1 = ((f16[8,264,256]{2,1,0:T(8,128)(2,1)}), f16[8,264,256]{2,1,0:T(8,128)(2,1)}, u32[]{:S(2)}, u32[]{:S(2)}) async-start(f16[8,264,256]{2,1,0:T(8,128)(2,1)} %convert_element_type.44), calls=%async_computation.1 | async-start | bytes 2162688 | tf_op jit(solution)/shard_map/all_to_all | solution.py:426
  40.5 10.7 %copy-start.6 = (bf16[384,256]{1,0:T(8,128)(2,1)S(1)}, bf16[384,256]{1,0:T(8,128)(2,1)}, u32[]{:S(2)}) copy-start(bf16[384,256]{1,0:T(8,128)(2,1)} %copy-done.5) | copy-start | bytes 589828
  40.5 6.5 %collective-permute-start.7 = (bf16[256,512]{1,0:T(8,128)(2,1)S(1)}, bf16[256,512]{1,0:T(8,128)(2,1)S(1)}, u32[]{:S(2)}, u32[]{:S(2)}) collective-permute-start(bf16[256,512]{1,0:T(8,128)(2,1)S(1)} %copy-done.9), channel_id=1, source_target_pairs={{0,64},{1,65},{2,66},{3,67},{4,68},{5,69},{6,70},{7,71},{8,72},{9,... | collective-permute-start | bytes 786440 | tf_op jit(solution)/shard_map/ppermute | solution.py:34
  42.1 7.6 %collective-permute-start.10 = (bf16[256,512]{1,0:T(8,128)(2,1)S(1)}, bf16[256,512]{1,0:T(8,128)(2,1)S(1)}, u32[]{:S(2)}, u32[]{:S(2)}) collective-permute-start(bf16[256,512]{1,0:T(8,128)(2,1)S(1)} %copy-done.8), channel_id=1, source_target_pairs={{0,192},{1,193},{2,194},{3,195},{4,196},{5,197},{6,198},{7,199},{8... | collective-permute-start | bytes 786440 | tf_op jit(solution)/shard_map/ppermute | solution.py:34
  44.2 7.0 %collective-permute-start.6 = (bf16[256,512]{1,0:T(8,128)(2,1)S(1)}, bf16[256,512]{1,0:T(8,128)(2,1)S(1)}, u32[]{:S(2)}, u32[]{:S(2)}) collective-permute-start(bf16[256,512]{1,0:T(8,128)(2,1)S(1)} %copy-done.9), channel_id=1, source_target_pairs={{0,8},{1,9},{2,10},{3,11},{4,12},{5,13},{6,14},{7,15},{8,0},{9,1},... | collective-permute-start | bytes 786440 | tf_op jit(solution)/shard_map/ppermute | solution.py:34
  44.2 7.0 %collective-permute-start.9 = (bf16[256,512]{1,0:T(8,128)(2,1)S(1)}, bf16[256,512]{1,0:T(8,128)(2,1)S(1)}, u32[]{:S(2)}, u32[]{:S(2)}) collective-permute-start(bf16[256,512]{1,0:T(8,128)(2,1)S(1)} %copy-done.8), channel_id=1, source_target_pairs={{0,8},{1,9},{2,10},{3,11},{4,12},{5,13},{6,14},{7,15},{8,0},{9,1},... | collective-permute-start | bytes 786440 | tf_op jit(solution)/shard_map/ppermute | solution.py:34
  47.0 4.2 %collective-permute-start.8 = (bf16[256,512]{1,0:T(8,128)(2,1)S(1)}, bf16[256,512]{1,0:T(8,128)(2,1)S(1)}, u32[]{:S(2)}, u32[]{:S(2)}) collective-permute-start(bf16[256,512]{1,0:T(8,128)(2,1)S(1)} %collective-permute-done.7.refs_6_), channel_id=1, source_target_pairs={{0,8},{1,9},{2,10},{3,11},{4,12},{5,13},{6,14},{7,15},{8,0},{9,1},... | collective-permute-start | bytes 786440 | tf_op jit(solution)/shard_map/ppermute | solution.py:34
  49.7 1.5 %collective-permute-start.11 = (bf16[256,512]{1,0:T(8,128)(2,1)S(1)}, bf16[256,512]{1,0:T(8,128)(2,1)S(1)}, u32[]{:S(2)}, u32[]{:S(2)}) collective-permute-start(bf16[256,512]{1,0:T(8,128)(2,1)S(1)} %collective-permute-done.10.refs_14_), channel_id=1, source_target_pairs={{0,8},{1,9},{2,10},{3,11},{4,12},{5,13},{6,14},{7,15},{8,0},{9,1},... | collective-permute-start | bytes 786440 | tf_op jit(solution)/shard_map/ppermute | solution.py:34
  56.1 3.6 %collective-permute-start.14 = (f32[256,256]{1,0:T(8,128)S(1)}, f32[256,256]{1,0:T(8,128)S(1)}, u32[]{:S(2)}, u32[]{:S(2)}) collective-permute-start(f32[256,256]{1,0:T(8,128)S(1)} %own_terms.1.own_ref), channel_id=1, source_target_pairs={{0,8},{1,9},{2,10},{3,11},{4,12},{5,13},{6,14},{7,15},{8,0},{9,1},... | collective-permute-start | bytes 786440 | tf_op jit(solution)/shard_map/ppermute | solution.py:34
  56.7 8.4 %collective-permute-start.13 = (f16[200,512]{1,0:T(8,128)(2,1)S(1)}, f16[200,512]{1,0:T(8,128)(2,1)S(1)}, u32[]{:S(2)}, u32[]{:S(2)}) collective-permute-start(f16[200,512]{1,0:T(8,128)(2,1)S(1)} %convert_element_type.46), channel_id=1, source_target_pairs={{0,64},{1,65},{2,66},{3,67},{4,68},{5,69},{6,70},{7,71},{8,72},{9,... | collective-permute-start | bytes 614408 | tf_op jit(solution)/shard_map/ppermute | solution.py:34
  57.6 10.6 %collective-permute-start.12 = (f16[200,512]{1,0:T(8,128)(2,1)S(1)}, f16[200,512]{1,0:T(8,128)(2,1)S(1)}, u32[]{:S(2)}, u32[]{:S(2)}) collective-permute-start(f16[200,512]{1,0:T(8,128)(2,1)S(1)} %convert_element_type.45), channel_id=1, source_target_pairs={{0,192},{1,193},{2,194},{3,195},{4,196},{5,197},{6,198},{7,199},{8... | collective-permute-start | bytes 614408 | tf_op jit(solution)/shard_map/ppermute | solution.py:34
  60.8 9.5 %copy-start.4 = (f32[192,1024]{1,0:T(8,128)S(1)}, f32[192,1024]{1,0:T(8,128)}, u32[]{:S(2)}) copy-start(f32[192,1024]{1,0:T(8,128)} %get-tuple-element.61.wide_ref) | copy-start | bytes 2359300
  60.8 9.5 %copy-start.7 = (f32[192,256]{1,0:T(8,128)S(1)}, f32[192,256]{1,0:T(8,128)}, u32[]{:S(2)}) copy-start(f32[192,256]{1,0:T(8,128)} %get-tuple-element.63.narrow_ref) | copy-start | bytes 589828
  60.9 7.5 %collective-permute-start.17 = (f16[200,256]{1,0:T(8,128)(2,1)S(1)}, f16[200,256]{1,0:T(8,128)(2,1)S(1)}, u32[]{:S(2)}, u32[]{:S(2)}) collective-permute-start(f16[200,256]{1,0:T(8,128)(2,1)S(1)} %convert_element_type.52), channel_id=1, source_target_pairs={{0,128},{1,129},{2,130},{3,131},{4,132},{5,133},{6,134},{7,135},{8... | collective-permute-start | bytes 307208 | tf_op jit(solution)/shard_map/ppermute | solution.py:34
  62.1 6.3 %collective-permute-start.16 = (f16[200,256]{1,0:T(8,128)(2,1)S(1)}, f16[200,256]{1,0:T(8,128)(2,1)S(1)}, u32[]{:S(2)}, u32[]{:S(2)}) collective-permute-start(f16[200,256]{1,0:T(8,128)(2,1)S(1)} %convert_element_type.51), channel_id=1, source_target_pairs={{0,64},{1,65},{2,66},{3,67},{4,68},{5,69},{6,70},{7,71},{8,72},{9,... | collective-permute-start | bytes 307208 | tf_op jit(solution)/shard_map/ppermute | solution.py:34
  63.0 7.3 %collective-permute-start.15 = (f16[200,256]{1,0:T(8,128)(2,1)S(1)}, f16[200,256]{1,0:T(8,128)(2,1)S(1)}, u32[]{:S(2)}, u32[]{:S(2)}) collective-permute-start(f16[200,256]{1,0:T(8,128)(2,1)S(1)} %convert_element_type.50), channel_id=1, source_target_pairs={{0,192},{1,193},{2,194},{3,195},{4,196},{5,197},{6,198},{7,199},{8... | collective-permute-start | bytes 307208 | tf_op jit(solution)/shard_map/ppermute | solution.py:34
